TPU v7x, 32 devices: a whole 2x2x4 slice. The times are simulated.
32 devices in a mesh: dp: 8 (over y, x, core), tp: 4 (over z).
Axes of the slice: x: 2, y: 2, z: 4, core: 2. Of those that a mesh axis runs over, the one named last changes fastest.
Arguments:
- tokens: bfloat16 [16384, 2048], P(('dp', 'tp')), may hold values from -6 to 6
- cotangent: bfloat16 [16384, 2048], P(('dp', 'tp')), may hold values from -6 to 6
- segments: int32 [16, 1024], P('dp'), may hold values from 0 to 3, never falling along the last dimension, each value on 1 to 512 neighbouring positions
- subsets: int32 [16, 4], P('dp'), may hold values from 0 to 21
- packs: int32 [8], P('dp'), may hold values from 1 to 2, as said below
- master_blocks: float32 [768, 256, 256], P(('dp', 'tp'))
- left_stats: float32 [768, 256, 256], P(('dp', 'tp'))
- right_stats: float32 [768, 256, 256], P(('dp', 'tp'))
- local_vecs: float32 [56, 256], P('tp', 'dp'), may hold values from -1.2 to 1.2
- local_vec_stats: float32 [56, 256], P('tp', 'dp')
- shared_vecs: float32 [6, 2048], P(None, ('dp', 'tp'))
- shared_vec_stats: float32 [6, 2048], P(None, ('dp', 'tp'))
Outputs:
- output: bfloat16 [16384, 2048], P(('dp', 'tp'))
- input_grad: float32 [16384, 2048], P(('dp', 'tp'))
- block_grads: float32 [768, 256, 256], P(('dp', 'tp'))
- left_new: float32 [768, 256, 256], P(('dp', 'tp'))
- right_new: float32 [768, 256, 256], P(('dp', 'tp'))
- new_blocks: float32 [768, 256, 256], P(('dp', 'tp'))
- local_vec_grads: float32 [56, 256], P('tp', 'dp')
- local_vec_stats_new: float32 [56, 256], P('tp', 'dp')
- local_vecs_new: float32 [56, 256], P('tp', 'dp')
- shared_vec_grads: float32 [6, 2048], P(None, ('dp', 'tp'))
- shared_vec_stats_new: float32 [6, 2048], P(None, ('dp', 'tp'))
- shared_vecs_new: float32 [6, 2048], P(None, ('dp', 'tp'))
Inputs may be any that keep to these rules, and one draw needn't show every extreme that they name: Each data group holds 1 to 2 packs in its first slots; some group holds 2 and some holds 1. `segments`: document numbers never fall along a pack; each of the 4 documents has 1 to 512 tokens, one exactly 512.
All inputs are finite; a program needn't handle non-finite values.
Results may differ from a plain program's by a relative error of at most 0.011.
Values may be sent and summed in bfloat16 or wider, within the bound.
No kernel may reach another device: no remote copies, remote signals or barrier semaphores. Data moves between devices by JAX's collectives and lax.ppermute only.
A program may use at most 320 MiB of HBM per device.

v0:
```python
import math

import jax
import jax.numpy as jnp
from jax import lax
from jax.sharding import PartitionSpec as P

HEADS = 8
HD = 256
ROT = 64
FF = 8192
SUBSETS = 22
ROOT_ITERS = 8


EPS_NORM = 1e-05
DECAY = 0.5
RATE_BLOCK = 0.6
RATE_VEC = 0.2
NEG_FILL = -1e30
HIGHEST = lax.Precision.HIGHEST
HALF_ROOT = 0.7071067811865476
DENSITY_SCALE = 0.3989422804014327


def apply_layer_norm(values):
    mean_val = jnp.mean(values, axis=-1, keepdims=True)
    centred = values - mean_val
    variance = jnp.mean(centred * centred, axis=-1, keepdims=True)
    inv_std = lax.rsqrt(variance + EPS_NORM)
    return (centred * inv_std, inv_std)


def rotary_tables(row_count, pack_len, rot_dims):
    positions = (jnp.arange(row_count) % pack_len).astype(jnp.float32)
    freqs = 10000.0 ** (-(jnp.arange(rot_dims // 2).astype(jnp.float32) * 2.0) / rot_dims)
    angles = positions[:, None] * freqs[None, :]
    cosines = jnp.cos(angles)
    sines = jnp.sin(angles)
    return (jnp.concatenate([cosines, cosines], -1), jnp.concatenate([sines, sines], -1))


def rotate(values, cosines, sines):
    rot_dims = cosines.shape[-1]
    half_dims = rot_dims // 2
    rotated = values[..., :rot_dims]
    turned = jnp.concatenate([-rotated[..., half_dims:], rotated[..., :half_dims]], -1)
    return jnp.concatenate(
        [rotated * cosines[:, None, :] + turned * sines[:, None, :], values[..., rot_dims:]], -1
    )


def rotate_back(grads, cosines, sines):
    rot_dims = cosines.shape[-1]
    half_dims = rot_dims // 2
    rotated = grads[..., :rot_dims]
    sined = rotated * sines[:, None, :]
    back_turn = jnp.concatenate([sined[..., half_dims:], -sined[..., :half_dims]], -1)
    return jnp.concatenate([rotated * cosines[:, None, :] + back_turn, grads[..., rot_dims:]], -1)


def gelu_slope(values):
    return (
        0.5 * (1.0 + lax.erf(values * HALF_ROOT))
        + values * jnp.exp(-0.5 * values * values) * DENSITY_SCALE
    )


def inverse_fourth_root(matrices):
    order_size = matrices.shape[-1]
    identity = jnp.eye(order_size, dtype=matrices.dtype)
    frob_norms = jnp.sqrt(jnp.sum(matrices * matrices, axis=(1, 2)))
    scaled = matrices / frob_norms[:, None, None]
    root_now = jnp.broadcast_to(identity, matrices.shape)
    for repeat in range(ROOT_ITERS):
        factor = (5.0 * identity - scaled) * 0.25
        root_now = jnp.matmul(root_now, factor, precision=HIGHEST)
        square = jnp.matmul(factor, factor, precision=HIGHEST)
        scaled = jnp.matmul(
            jnp.matmul(square, square, precision=HIGHEST), scaled, precision=HIGHEST
        )
    return root_now * lax.rsqrt(jnp.sqrt(frob_norms))[:, None, None]


def to_matrix(blocks, block_rows, block_cols):
    block_size = blocks.shape[-1]
    return (
        blocks.reshape(block_rows, block_cols, block_size, block_size)
        .transpose(0, 2, 1, 3)
        .reshape(block_rows * block_size, block_cols * block_size)
    )


def to_blocks(matrix, block_size):
    block_rows = matrix.shape[0] // block_size
    block_cols = matrix.shape[1] // block_size
    return (
        matrix.reshape(block_rows, block_size, block_cols, block_size)
        .transpose(0, 2, 1, 3)
        .reshape(block_rows * block_cols, block_size, block_size)
    )


def allow_mask(row_start, seg_keys, query_rows):
    key_pos = jnp.arange(seg_keys.shape[0])
    query_pos = row_start + jnp.arange(query_rows)
    seg_query = lax.dynamic_slice_in_dim(seg_keys, row_start, query_rows, 0)
    return (key_pos[None, :] <= query_pos[:, None]) & (seg_query[:, None] == seg_keys[None, :])


def block_scores(queries, keys, allowed, score_scale):
    scores = (
        jnp.einsum("qhd,khd->hqk", queries, keys, preferred_element_type=jnp.float32) * score_scale
    )
    return jnp.where(allowed[None], scores, NEG_FILL)


def shards(
    tokens,
    cotangent,
    segments,
    subsets,
    packs,
    master_blocks,
    left_stats,
    right_stats,
    local_vecs,
    local_vec_stats,
    shared_vecs,
    shared_vec_stats,
):
    tp_ways = lax.axis_size("tp")
    tp_rank = lax.axis_index("tp")
    tok_dev, model_width = tokens.shape
    group_tok = tok_dev * tp_ways
    pack_count, pack_len = segments.shape
    seg_width = subsets.shape[1]
    heads_dev = HEADS // tp_ways
    ff_dev = FF // tp_ways
    block_size = master_blocks.shape[-1]
    block_rows = model_width // block_size
    qkv_cols = 3 * heads_dev * HD // block_size
    head_rows = heads_dev * HD // block_size
    ff_blocks = ff_dev // block_size
    first_end = block_rows * qkv_cols
    second_end = first_end + head_rows * block_rows
    third_end = second_end + block_rows * ff_blocks
    all_blocks, all_vecs = (
        lax.all_gather(master_blocks.astype(jnp.bfloat16), "dp", axis=0, tiled=True),
        lax.all_gather(local_vecs.astype(jnp.bfloat16), "dp", axis=1, tiled=True),
    )
    norm_params = lax.all_gather(
        shared_vecs.astype(jnp.bfloat16), ("dp", "tp"), axis=1, tiled=True
    ).astype(jnp.float32)
    w_qkv = to_matrix(all_blocks[:first_end], block_rows, qkv_cols)
    w_out = to_matrix(all_blocks[first_end:second_end], head_rows, block_rows)
    w_in = to_matrix(all_blocks[second_end:third_end], block_rows, ff_blocks)
    w_down = to_matrix(all_blocks[third_end:], ff_blocks, block_rows)
    vec_values = all_vecs.astype(jnp.float32)
    bias_qkv = vec_values[: 3 * heads_dev].reshape(-1)
    bias_in = vec_values[3 * heads_dev :].reshape(-1)
    first_gain = norm_params[0]
    first_shift = norm_params[1]
    second_gain = norm_params[2]
    second_shift = norm_params[3]
    own_pos = tp_rank * tok_dev + jnp.arange(tok_dev)
    own_pack = own_pos // pack_len
    valid_own = (own_pack < packs[0]).astype(jnp.float32)
    owned_input_rows = tokens.astype(jnp.float32)
    owned_centred_scaled, owned_inverse_deviation = apply_layer_norm(owned_input_rows)
    owned_first_branch = (owned_centred_scaled * first_gain + first_shift).astype(jnp.bfloat16)
    owned_second_branch = (owned_centred_scaled * second_gain + second_shift).astype(jnp.bfloat16)
    first_normed_input, second_normed_input = (
        lax.all_gather(owned_first_branch, "tp", axis=0, tiled=True),
        lax.all_gather(owned_second_branch, "tp", axis=0, tiled=True),
    )
    seg_flat = segments.reshape(-1)
    cosines, sines = rotary_tables(group_tok, pack_len, ROT)
    qkv_vals = (
        jnp.dot(first_normed_input, w_qkv, preferred_element_type=jnp.float32) + bias_qkv
    ).reshape(group_tok, heads_dev, 3, HD)
    query16 = rotate(qkv_vals[:, :, 0], cosines, sines).astype(jnp.bfloat16)
    key16 = rotate(qkv_vals[:, :, 1], cosines, sines).astype(jnp.bfloat16)
    value16 = qkv_vals[:, :, 2].astype(jnp.bfloat16)
    score_scale = 1.0 / math.sqrt(HD)
    query_rows = min(512, pack_len)
    block_count = pack_len // query_rows

    def forward_pack(pack_idx):
        pack_start = pack_idx * pack_len
        keys = lax.dynamic_slice_in_dim(key16, pack_start, pack_len, 0)
        values = lax.dynamic_slice_in_dim(value16, pack_start, pack_len, 0)
        seg_keys = lax.dynamic_slice_in_dim(seg_flat, pack_start, pack_len, 0)

        def forward_block(block_idx):
            row_start = block_idx * query_rows
            queries = lax.dynamic_slice_in_dim(query16, pack_start + row_start, query_rows, 0)
            masked = block_scores(
                queries, keys, allow_mask(row_start, seg_keys, query_rows), score_scale
            )
            row_max = jnp.max(masked, axis=-1, keepdims=True)
            exp_terms = jnp.exp(masked - row_max)
            row_total = jnp.sum(exp_terms, axis=-1, keepdims=True)
            attn_probs = (exp_terms / row_total).astype(jnp.bfloat16)
            attended = jnp.einsum(
                "hqk,khd->qhd", attn_probs, values, preferred_element_type=jnp.float32
            )
            return (attended.astype(jnp.bfloat16), (row_max + jnp.log(row_total))[..., 0])

        attended, sums_pack = lax.map(forward_block, jnp.arange(block_count))
        return (attended.reshape(pack_len, heads_dev, HD), sums_pack)

    attn_heads, log_sums = lax.map(forward_pack, jnp.arange(pack_count))
    attn16 = attn_heads.reshape(group_tok, heads_dev * HD)
    hidden = jnp.dot(second_normed_input, w_in, preferred_element_type=jnp.float32) + bias_in
    activated = jax.nn.gelu(hidden, approximate=False).astype(jnp.bfloat16)
    partial_value = jnp.dot(attn16, w_out, preferred_element_type=jnp.float32) + jnp.dot(
        activated, w_down, preferred_element_type=jnp.float32
    )
    branch = lax.psum_scatter(partial_value, "tp", scatter_dimension=0, tiled=True)
    output = (
        valid_own[:, None] * (owned_input_rows + branch + norm_params[4] + norm_params[5])
    ).astype(jnp.bfloat16)
    seg_own = lax.dynamic_slice_in_dim(seg_flat, tp_rank * tok_dev, tok_dev, 0)
    lookup_key = own_pack * seg_width + seg_own
    subset_flat = subsets.reshape(-1)
    onehot = lookup_key[:, None] == jnp.arange(pack_count * seg_width)[None, :]
    subset_own = jnp.sum(jnp.where(onehot, subset_flat[None, :], 0), axis=1)
    weight = 0.5 + subset_own.astype(jnp.float32) / (SUBSETS - 1)
    seed16 = (cotangent.astype(jnp.float32) * weight[:, None] * valid_own[:, None]).astype(
        jnp.bfloat16
    )
    seed_all = lax.all_gather(seed16, "tp", axis=0, tiled=True)
    out_bias_grad = jnp.sum(seed16, axis=0, dtype=jnp.float32)
    d_attn16 = jnp.einsum("td,cd->tc", seed_all, w_out, preferred_element_type=jnp.float32).astype(
        jnp.bfloat16
    )
    grad_wout = jnp.einsum("tc,td->cd", attn16, seed_all, preferred_element_type=jnp.float32)
    d_act = jnp.einsum("td,fd->tf", seed_all, w_down, preferred_element_type=jnp.float32)
    grad_wdown = jnp.einsum("tf,td->fd", activated, seed_all, preferred_element_type=jnp.float32)
    d_hidden16 = (d_act * gelu_slope(hidden)).astype(jnp.bfloat16)
    grad_win = jnp.einsum(
        "td,tf->df", second_normed_input, d_hidden16, preferred_element_type=jnp.float32
    )
    grad_bin = jnp.sum(d_hidden16, axis=0, dtype=jnp.float32)
    d_normed_two = jnp.einsum("tf,df->td", d_hidden16, w_in, preferred_element_type=jnp.float32)
    d_attn_heads = d_attn16.reshape(group_tok, heads_dev, HD)

    def backward_pack(pack_idx):
        pack_start = pack_idx * pack_len
        keys = lax.dynamic_slice_in_dim(key16, pack_start, pack_len, 0)
        values = lax.dynamic_slice_in_dim(value16, pack_start, pack_len, 0)
        seg_keys = lax.dynamic_slice_in_dim(seg_flat, pack_start, pack_len, 0)
        query_pack = lax.dynamic_slice_in_dim(query16, pack_start, pack_len, 0)
        d_out_pack = lax.dynamic_slice_in_dim(d_attn_heads, pack_start, pack_len, 0)
        sums_pack = log_sums[pack_idx]

        def backward_block(carry, block_idx):
            key_acc, value_acc = carry
            row_start = block_idx * query_rows
            queries = lax.dynamic_slice_in_dim(query_pack, row_start, query_rows, 0)
            d_out = lax.dynamic_slice_in_dim(d_out_pack, row_start, query_rows, 0)
            masked = block_scores(
                queries, keys, allow_mask(row_start, seg_keys, query_rows), score_scale
            )
            attn_probs = jnp.exp(masked - sums_pack[block_idx][:, :, None])
            d_probs = jnp.einsum("qhd,khd->hqk", d_out, values, preferred_element_type=jnp.float32)
            row_dot = jnp.sum(attn_probs * d_probs, axis=-1, keepdims=True)
            d_scores = (attn_probs * (d_probs - row_dot)).astype(jnp.bfloat16)
            d_query = (
                jnp.einsum("hqk,khd->qhd", d_scores, keys, preferred_element_type=jnp.float32)
                * score_scale
            )
            key_acc = (
                key_acc
                + jnp.einsum("hqk,qhd->khd", d_scores, queries, preferred_element_type=jnp.float32)
                * score_scale
            )
            value_acc = value_acc + jnp.einsum(
                "hqk,qhd->khd",
                attn_probs.astype(jnp.bfloat16),
                d_out,
                preferred_element_type=jnp.float32,
            )
            return ((key_acc, value_acc), d_query)

        zero_acc = jnp.zeros((pack_len, heads_dev, HD), jnp.float32)
        (d_keys, d_values), d_queries = lax.scan(
            backward_block, (zero_acc, zero_acc), jnp.arange(block_count)
        )
        return (d_queries.reshape(pack_len, heads_dev, HD), d_keys, d_values)

    d_queries, d_keys, d_values = lax.map(backward_pack, jnp.arange(pack_count))
    d_queries = rotate_back(d_queries.reshape(group_tok, heads_dev, HD), cosines, sines)
    d_keys = rotate_back(d_keys.reshape(group_tok, heads_dev, HD), cosines, sines)
    d_values = d_values.reshape(group_tok, heads_dev, HD)
    d_qkv16 = (
        jnp.stack([d_queries, d_keys, d_values], 2)
        .reshape(group_tok, 3 * heads_dev * HD)
        .astype(jnp.bfloat16)
    )
    grad_wqkv = jnp.einsum(
        "td,tc->dc", first_normed_input, d_qkv16, preferred_element_type=jnp.float32
    )
    grad_bqkv = jnp.sum(d_qkv16, axis=0, dtype=jnp.float32)
    d_normed_one = jnp.einsum("tc,dc->td", d_qkv16, w_qkv, preferred_element_type=jnp.float32)
    owned_first_gradient, owned_second_gradient = (
        lax.psum_scatter(d_normed_one, "tp", scatter_dimension=0, tiled=True),
        lax.psum_scatter(d_normed_two, "tp", scatter_dimension=0, tiled=True),
    )
    first_gain_gradient = jnp.sum(owned_first_gradient * owned_centred_scaled, axis=0)
    grad_shift_one = jnp.sum(owned_first_gradient, axis=0)
    second_gain_gradient = jnp.sum(owned_second_gradient * owned_centred_scaled, axis=0)
    grad_shift_two = jnp.sum(owned_second_gradient, axis=0)
    norm_input_gradient = owned_first_gradient * first_gain + owned_second_gradient * second_gain
    average_gradient = jnp.mean(norm_input_gradient, axis=-1, keepdims=True)
    average_projection = jnp.mean(
        norm_input_gradient * owned_centred_scaled, axis=-1, keepdims=True
    )
    input_grad = seed16.astype(jnp.float32) + owned_inverse_deviation * (
        norm_input_gradient - average_gradient - owned_centred_scaled * average_projection
    )
    shared_local = jnp.stack(
        [
            first_gain_gradient,
            grad_shift_one,
            second_gain_gradient,
            grad_shift_two,
            out_bias_grad,
            out_bias_grad,
        ],
        0,
    )
    shared_grads = lax.psum_scatter(shared_local, ("dp", "tp"), scatter_dimension=1, tiled=True)
    blocks_local = jnp.concatenate(
        [
            to_blocks(grad_wqkv, block_size),
            to_blocks(grad_wout, block_size),
            to_blocks(grad_win, block_size),
            to_blocks(grad_wdown, block_size),
        ],
        0,
    )
    vecs_local = jnp.concatenate(
        [grad_bqkv.reshape(3 * heads_dev, HD), grad_bin.reshape(ff_dev // HD, HD)], 0
    )
    own_grads, own_vec_grads = (
        lax.psum_scatter(blocks_local, "dp", scatter_dimension=0, tiled=True),
        lax.psum_scatter(vecs_local, "dp", scatter_dimension=1, tiled=True),
    )
    left_new = DECAY * left_stats + jnp.einsum(
        "nij,nkj->nik", own_grads, own_grads, precision=HIGHEST
    )
    right_new = DECAY * right_stats + jnp.einsum(
        "nji,njk->nik", own_grads, own_grads, precision=HIGHEST
    )
    owned_count = own_grads.shape[0]
    roots_all = inverse_fourth_root(jnp.concatenate([left_new, right_new], 0))
    precond = jnp.matmul(
        jnp.matmul(roots_all[:owned_count], own_grads, precision=HIGHEST),
        roots_all[owned_count:],
        precision=HIGHEST,
    )
    new_blocks = master_blocks - RATE_BLOCK * precond
    local_stat_new = DECAY * local_vec_stats + own_vec_grads * own_vec_grads
    local_new = local_vecs - RATE_VEC * own_vec_grads * lax.rsqrt(local_stat_new)
    shared_stat_new = DECAY * shared_vec_stats + shared_grads * shared_grads
    shared_new = shared_vecs - RATE_VEC * shared_grads * lax.rsqrt(shared_stat_new)
    return (
        output,
        input_grad,
        own_grads,
        left_new,
        right_new,
        new_blocks,
        own_vec_grads,
        local_stat_new,
        local_new,
        shared_grads,
        shared_stat_new,
        shared_new,
    )


def solution(mesh):
    placed = (
        P(("dp", "tp"), None),
        P(("dp", "tp"), None),
        P("dp", None),
        P("dp", None),
        P("dp"),
        P(("dp", "tp"), None, None),
        P(("dp", "tp"), None, None),
        P(("dp", "tp"), None, None),
        P("tp", "dp"),
        P("tp", "dp"),
        P(None, ("dp", "tp")),
        P(None, ("dp", "tp")),
    )
    return jax.shard_map(
        shards,
        mesh=mesh,
        in_specs=placed,
        out_specs=(
            P(("dp", "tp"), None),
            P(("dp", "tp"), None),
            P(("dp", "tp"), None, None),
            P(("dp", "tp"), None, None),
            P(("dp", "tp"), None, None),
            P(("dp", "tp"), None, None),
            P("tp", "dp"),
            P("tp", "dp"),
            P("tp", "dp"),
            P(None, ("dp", "tp")),
            P(None, ("dp", "tp")),
            P(None, ("dp", "tp")),
        ),
        check_vma=False,
    )
```

profile of v0, /device:TPU:0, one launch (start us, length us, event | category | flops | bytes accessed | tf_op | source)
XLA Modules:
  0.0 2559.5 jit_solution(7640381051346894925)
XLA Ops:
  12.4 71.4 %all-gather = bf16[32,64,6]{1,2,0:T(8,128)(2,1)S(1)} all-gather(bf16[1,64,6]{1,2,0:T(8,128)(2,1)S(1)} %convert_bitcast_fusion.2), channel_id=1, replica_groups=mesh['dp'=8,'tp'=4] {'dp','tp'}, dimensions={0}, use_global_device_ids=true | all-gather | bytes 25344 | tf_op jit(solution)/shard_map/all_gather | solution.py:152
  108.6 32.2 %all-gather.9.cloned.1.call-done = bf16[192,256,256]{2,1,0:T(8,128)(2,1)} async-done(((bf16[24,256,256]{2,1,0:T(8,128)(2,1)}), bf16[192,256,256]{2,1,0:T(8,128)(2,1)}) %all-gather.9.cloned.1.call-update) | async-done | bytes 25165840 | tf_op jit(solution)/shard_map/all_gather | solution.py:149
  164.7 128.0 %all-gather.7.cloned.1.call-done = bf16[2048,2048]{1,0:T(8,128)(2,1)} async-done(((bf16[512,2048]{1,0:T(8,128)(2,1)}), bf16[2048,2048]{1,0:T(8,128)(2,1)}) %all-gather.7.cloned.1.call-update) | async-done | bytes 8388624 | tf_op jit(solution)/shard_map/all_gather | solution.py:174
  361.1 47.5 %while.54 = (s32[]{:T(128)}, bf16[2,1024,2,256]{3,2,1,0:T(2,128)(2,1)}, f32[2,2,2,512]{3,2,1,0:T(2,128)S(1)}, s32[2]{0:T(128)S(1)}, s32[2048]{0:T(1024)S(1)}, /*...) while((s32[]{:T(128)}, ...), condition=%wide.region_7.8_spmd, body=%wide.region_2.7_spmd.sunk | while | flops 1088159232 | bytes 33626796 | solution.py:213
  408.6 33.5 %all-gather.13.cloned.1.call-done = bf16[2048,2048]{1,0:T(8,128)(2,1)} async-done(((bf16[512,2048]{1,0:T(8,128)(2,1)}), bf16[2048,2048]{1,0:T(8,128)(2,1)}) %all-gather.13.cloned.1.call-update) | async-done | bytes 8388624 | tf_op jit(solution)/shard_map/all_gather | solution.py:233
  451.9 109.2 %while.56 = (s32[]{:T(128)}, f32[2,1024,2,256]{3,1,0,2:T(8,128)}, f32[2,1024,2,256]{3,1,0,2:T(8,128)}, bf16[2,1024,2,256]{3,1,0,2:T(8,128)(2,1)}, s32[2]{0:T(128...) while((s32[]{:T(128)}, f32[2,1024,2,256]{3,1,0,2:T(8,128)}, ...), condition=%wide.region_14.15_spmd, body=%wide.region_10.14_spmd.sunk | while | flops 2704539136 | bytes 122751912 | solution.py:293
  462.0 35.1 %while.58 = (s32[]{:T(128)}, f32[1024,2,256]{0,2,1:T(8,128)S(1)}, f32[1024,2,256]{0,2,1:T(8,128)}, f32[2,512,2,256]{3,2,1,0:T(2,128)}, s32[2]{0:T(128)S(1)}, /*i...) while((s32[]{:T(128)}, f32[1024,2,256]{0,2,1:T(8,128)S(1)}, ...), condition=%wide.region_13.13_spmd.clone, body=%wide.region_11.12_spmd.clone.sunk | while | flops 2704539136 | bytes 79735200 | solution.py:288
  516.3 35.1 %while.58 = (s32[]{:T(128)}, f32[1024,2,256]{0,2,1:T(8,128)S(1)}, f32[1024,2,256]{0,2,1:T(8,128)}, f32[2,512,2,256]{3,2,1,0:T(2,128)}, s32[2]{0:T(128)S(1)}, /*i...) while((s32[]{:T(128)}, f32[1024,2,256]{0,2,1:T(8,128)S(1)}, ...), condition=%wide.region_13.13_spmd.clone, body=%wide.region_11.12_spmd.clone.sunk | while | flops 2704539136 | bytes 79735200 | solution.py:288
  591.4 20.9 fusion.169
  680.0 59.0 %fusion.36 = (bf16[2048,2048]{1,0:T(8,128)(2,1)}, f32[2048,2048]{1,0:T(8,128)}) fusion(f32[2048]{0:T(1024)S(1)} %bitcast.352, bf16[2048,2048]{1,0:T(8,128)(2,1)} %all-gather.11.cloned.1.call-done, bf16[2048,2048]{1,0:T(8,128)(2,1)} %bitcast.311), kind=kOutput, calls=%fused_computation.65 | convolution fusion | flops 17456693248 | bytes 41951232 | tf_op jit(solution)/shard_map/dot_general | solution.py:215
  739.0 24.6 convolution_add_fusion.1
  763.6 30.4 %convert_reduce_fusion = (f32[2048]{0:T(1024)S(1)}, bf16[2048,2048]{1,0:T(8,128)(2,1)S(1)}) fusion(f32[2048,2048]{1,0:T(8,128)} %get-tuple-element.455, f32[2048]{0:T(1024)S(1)} %bitcast.353, bf16[2048,2048]{1,0:T(8,128)(2,1)} %all-gather.13.cloned.1.call-done, bf16[2048,2048]{1,0:T(8,128)(2,1)} %bitcast.308), kind=kOutput, calls=%fused_computation.74 | convolution fusion | flops 17234393088 | bytes 41959424 | tf_op jit(solution)/shard_map/td,fd->tf/dot_general | solution.py:239
  797.4 22.4 fusion.170
  847.3 21.9 fusion.174
  885.2 21.8 fusion.173
  949.6 225.1 %reduce-scatter.11.cloned.1.call-done = f32[512,2048]{1,0:T(8,128)} async-done(((f32[2048,2048]{1,0:T(8,128)}), f32[512,2048]{1,0:T(8,128)}) %reduce-scatter.11.cloned.1.call-update) | async-done | bytes 4194320 | tf_op jit(solution)/shard_map/reduce_scatter | solution.py:220
  1174.6 283.4 %reduce-scatter.15.cloned.1.call-done = f32[512,2048]{1,0:T(8,128)} async-done(((f32[2048,2048]{1,0:T(8,128)}), f32[512,2048]{1,0:T(8,128)}) %reduce-scatter.15.cloned.1.call-update) | async-done | bytes 4194320 | tf_op jit(solution)/shard_map/reduce_scatter | solution.py:309
  1468.7 33.8 %pad_maximum_fusion = f32[192,256,256]{2,1,0:T(8,128)} fusion(f32[64,256,256]{2,1,0:T(8,128)} %bitcast.275, f32[64,256,256]{2,1,0:T(8,128)} %bitcast.276, f32[16,256,256]{2,1,0:T(8,128)} %bitcast.322, f32[48,256,256]{2,1,0:T(8,128)} %bitcast.296), kind=kLoop, calls=%fused_computation.60 | loop fusion | flops 37748736 | bytes 100663296 | tf_op jit(solution)/shard_map/concatenate | solution.py:335
  1509.0 125.2 %reduce-scatter.21.cloned.1.call-done = f32[64,6]{1,0:T(8,128)} async-done(((f32[2048,6]{1,0:T(8,128)}), f32[64,6]{1,0:T(8,128)}) %reduce-scatter.21.cloned.1.call-update) | async-done | bytes 1552
  1635.7 285.7 %reduce-scatter.17.cloned.1.call-done = f32[24,256,256]{2,1,0:T(8,128)} async-done(((f32[192,256,256]{2,1,0:T(8,128)}), f32[24,256,256]{2,1,0:T(8,128)}) %reduce-scatter.17.cloned.1.call-update) | async-done | bytes 6291472 | tf_op jit(solution)/shard_map/reduce_scatter | solution.py:348
  1956.5 25.8 %fusion.53 = f32[48,256,256]{2,1,0:T(8,128)} fusion(f32[256,256]{1,0:T(8,128)S(1)} %fusion.131, f32[24,256,256]{2,1,0:T(8,128)} %multiply_add_fusion, f32[24,256,256]{2,1,0:T(8,128)} %multiply_add_fusion.1, f32[48]{0:T(128)S(1)} %get-tuple-element.452), kind=kOutput, calls=%fused_computation.104 | convolution fusion | flops 9676259328 | bytes 25428160 | tf_op jit(solution)/shard_map/dot_general | solution.py:78
  2040.1 20.7 fusion.55
  2079.4 20.0 fusion.176
  2117.7 20.7 fusion.57
  2157.4 19.8 fusion.178
  2195.6 20.8 fusion.59
  2235.0 19.8 fusion.180
  2273.3 20.7 fusion.61
  2312.7 20.2 fusion.182
  2351.2 20.7 fusion.63
  2428.8 20.9 fusion.65
  2468.3 19.8 fusion.186
  (440 shorter events, 888.7 us)
Async XLA Ops:
  7.2 76.7 %copy-start.7 = (bf16[512,2048]{1,0:T(8,128)(2,1)S(1)}, bf16[512,2048]{1,0:T(8,128)(2,1)}, u32[]{:S(2)}) copy-start(bf16[512,2048]{1,0:T(8,128)(2,1)} %param.20) | copy-start | bytes 6291460
  7.2 133.6 %all-gather.9.cloned.1.call-start = ((), (), s32[]{:S(2)}) async-start(), calls=%async_computation.7 | async-start | bytes 28311552 | tf_op jit(solution)/shard_map/all_gather | solution.py:149
  12.3 77.5 %copy-start.53 = (s32[2,4]{1,0:T(2,128)S(1)}, s32[2,4]{1,0:T(2,128)}, u32[]{:S(2)}) copy-start(s32[2,4]{1,0:T(2,128)} %param.23) | copy-start | bytes 100
  12.3 77.6 %copy-start.50 = (s32[2,1024]{1,0:T(2,128)S(1)}, s32[2,1024]{1,0:T(2,128)}, u32[]{:S(2)}) copy-start(s32[2,1024]{1,0:T(2,128)} %param.22) | copy-start | bytes 24580
  12.3 280.3 %all-gather.7.cloned.1.call-start = ((), (), s32[]{:S(2)}) async-start(), calls=%async_computation.6 | async-start | bytes 10485760 | tf_op jit(solution)/shard_map/all_gather | solution.py:174
  89.1 353.0 %all-gather.13.cloned.1.call-start = ((), (), s32[]{:S(2)}) async-start(), calls=%async_computation.10 | async-start | bytes 10485760 | tf_op jit(solution)/shard_map/all_gather | solution.py:233
  89.9 17.2 copy-start.44
  94.3 585.7 %all-gather.11.cloned.1.call-start = ((), (), s32[]{:S(2)}) async-start(), calls=%async_computation.8 | async-start | bytes 10485760 | tf_op jit(solution)/shard_map/all_gather | solution.py:175
  94.9 854.6 %reduce-scatter.13.cloned.1.call-start = ((), (), s32[]{:S(2)}) async-start(), calls=%async_computation.11 | async-start | bytes 20971520 | tf_op jit(solution)/shard_map/reduce_scatter | solution.py:308
  103.3 43.7 %copy-start.32 = (f32[256,14]{0,1:T(8,128)}, f32[256,14]{0,1:T(8,128)S(1)}, u32[]{:S(2)}) copy-start(f32[256,14]{0,1:T(8,128)S(1)} %reshape.355) | copy-start | bytes 43012
  108.6 241.4 %copy-start.13 = (f32[2048,64]{1,0:T(8,128)}, f32[2048,64]{1,0:T(8,128)S(1)}, u32[]{:S(2)}) copy-start(f32[2048,64]{1,0:T(8,128)S(1)} %get-tuple-element.459) | copy-start | bytes 1572868
  612.3 562.3 %reduce-scatter.11.cloned.1.call-start = ((), (), s32[]{:S(2)}) async-start(), calls=%async_computation.9 | async-start | bytes 20971520 | tf_op jit(solution)/shard_map/reduce_scatter | solution.py:220
  680.0 59.0 %copy-start.18 = (bf16[256,8,8,256]{3,1,2,0:T(8,128)(2,1)S(1)}, bf16[256,8,8,256]{3,1,2,0:T(8,128)(2,1)}, u32[]{:S(2)}) copy-start(bf16[256,8,8,256]{3,1,2,0:T(8,128)(2,1)} %copy.193) | copy-start | bytes 25165828
  763.6 694.5 %reduce-scatter.15.cloned.1.call-start = ((), (), s32[]{:S(2)}) async-start(), calls=%async_computation.12 | async-start | bytes 20971520 | tf_op jit(solution)/shard_map/reduce_scatter | solution.py:309
  819.8 682.8 %reduce-scatter.19.cloned.1.call-start = ((), (), s32[]{:S(2)}) async-start(), calls=%async_computation.14 | async-start | bytes 147456
  914.3 17.9 slice-start.1
  932.2 525.9 %copy-start.8 = (bf16[512,2048]{1,0:T(8,128)(2,1)S(1)}, bf16[512,2048]{1,0:T(8,128)(2,1)}, u32[]{:S(2)}) copy-start(bf16[512,2048]{1,0:T(8,128)(2,1)} %param.20) | copy-start | bytes 6291460
  932.2 525.9 %copy-start.28 = (f32[1,2048]{1,0:T(1,128)S(1)}, f32[1,2048]{1,0:T(1,128)}, u32[]{:S(2)}) copy-start(f32[1,2048]{1,0:T(1,128)} %copy-done.27) | copy-start | bytes 24580
  932.2 525.8 %copy-start.30 = (f32[1,2048]{1,0:T(1,128)S(1)}, f32[1,2048]{1,0:T(1,128)}, u32[]{:S(2)}) copy-start(f32[1,2048]{1,0:T(1,128)} %copy-done.29) | copy-start | bytes 24580
  932.2 525.8 %copy-start.35 = (f32[512]{0:T(512)S(1)}, f32[512]{0:T(512)}, u32[]{:S(2)}) copy-start(f32[512]{0:T(512)} %copy-done.34) | copy-start | bytes 6148
  932.2 525.8 %copy-start.36 = (f32[1,2048]{1,0:T(1,128)S(1)}, f32[1,2048]{1,0:T(1,128)}, u32[]{:S(2)}) copy-start(f32[1,2048]{1,0:T(1,128)} %get-tuple-element.444) | copy-start | bytes 24580
  932.3 525.8 %copy-start.37 = (f32[1,2048]{1,0:T(1,128)S(1)}, f32[1,2048]{1,0:T(1,128)}, u32[]{:S(2)}) copy-start(f32[1,2048]{1,0:T(1,128)} %get-tuple-element.445) | copy-start | bytes 24580
  932.3 525.8 %copy-start.42 = (f32[512]{0:T(512)S(1)}, f32[512]{0:T(512)}, u32[]{:S(2)}) copy-start(f32[512]{0:T(512)} %copy-done.41) | copy-start | bytes 6148
  932.3 525.8 %copy-start.45 = (f32[512]{0:T(512)S(1)}, f32[512]{0:T(512)}, u32[]{:S(2)}) copy-start(f32[512]{0:T(512)} %copy-done.44) | copy-start | bytes 6148
  949.5 684.7 %reduce-scatter.21.cloned.1.call-start = ((), (), s32[]{:S(2)}) async-start(), calls=%async_computation.15 | async-start | bytes 1081344
  1468.6 452.8 %reduce-scatter.17.cloned.1.call-start = ((), (), s32[]{:S(2)}) async-start(), calls=%async_computation.13 | async-start | bytes 56623104 | tf_op jit(solution)/shard_map/reduce_scatter | solution.py:348
  1502.5 132.6 %copy-start.48 = (f32[6,64]{1,0:T(8,128)S(1)}, f32[6,64]{1,0:T(8,128)}, u32[]{:S(2)}) copy-start(f32[6,64]{1,0:T(8,128)} %param.30) | copy-start | bytes 4612
  1502.5 132.6 %copy-start.51 = (f32[6,64]{1,0:T(8,128)S(1)}, f32[6,64]{1,0:T(8,128)}, u32[]{:S(2)}) copy-start(f32[6,64]{1,0:T(8,128)} %param.31) | copy-start | bytes 4612
  1503.4 436.5 %copy-start.38 = (f32[14,32]{1,0:T(8,128)}, f32[14,32]{1,0:T(8,128)S(1)}, u32[]{:S(2)}) copy-start(f32[14,32]{1,0:T(8,128)S(1)} %copy.157) | copy-start | bytes 5380
  1635.1 304.8 %copy-start.46 = (f32[6,64]{1,0:T(8,128)}, f32[6,64]{1,0:T(8,128)S(1)}, u32[]{:S(2)}) copy-start(f32[6,64]{1,0:T(8,128)S(1)} %copy.159) | copy-start | bytes 4612
  1921.4 18.5 copy-start.4
  2488.1 18.7 copy-start.52
  (59 other events, 318.4 us)
Sparse Core Ops, SparseCore 0:
  12.4 128.3 all-gather.8
  143.0 149.6 all-gather.6
  294.2 147.8 all-gather.12
  444.1 147.8 all-gather.10
  612.5 278.7 reduce-scatter.12
  893.6 281.0 reduce-scatter.10
  1177.0 281.0 reduce-scatter.14
  1461.9 34.0 reduce-scatter.18
  1498.8 135.3 reduce-scatter.20
  1638.7 282.6 reduce-scatter.16
where the time goes:
time: 2570 us; the launch traced here: 2560 us
  waiting for transfers between devices  1110 us (43%)
  matrix products  944 us (37%)
  local copies, waits for them, and re-layouts  264 us (10%)
  other arithmetic  122 us (5%)
  blocking collectives  79.6 us (3%)
    reduce_scatter x1, waiting for transfers between devices, shards(): lax.psum_scatter(blocks_local, 'dp', scatter_dimension=0, tiled=True)  286 us
    reduce_scatter x1, waiting for transfers between devices, shards(): lax.psum_scatter(d_normed_two, 'tp', scatter_dimension=0, tiled=True)  283 us
    reduce_scatter x1, waiting for transfers between devices, shards(): lax.psum_scatter(partial_value, 'tp', scatter_dimension=0, tiled=True)  225 us
    dot_general x7, matrix products, inverse_fourth_root(): square = jnp.matmul(factor, factor, precision=HIGHEST)  150 us
    dot_general x8, matrix products, inverse_fourth_root(): root_now = jnp.matmul(root_now, factor, precision=HIGHEST)  150 us
    dot_general x7, matrix products, inverse_fourth_root(): jnp.matmul(square, square, precision=HIGHEST)  139 us
    dot_general x7, matrix products, inverse_fourth_root(): jnp.matmul(jnp.matmul(square, square, precision=HIGHEST), scaled, precisi...  130 us
    all_gather x1, waiting for transfers between devices, shards(): lax.all_gather(owned_first_branch, 'tp', axis=0, tiled=True)  128 us
  transfers between devices with their start and end apart: 10, of which 7 were waited for; matrix products, arithmetic and copies ran while one was open for 26% of the time, Pallas kernels for 0%

commit v1 on v0

--- a/solution.py
+++ b/solution.py
@@ -1,8 +1,11 @@
+import functools
 import math
 
 import jax
 import jax.numpy as jnp
 from jax import lax
+from jax.experimental import pallas as pl
+from jax.experimental.pallas import tpu as pltpu
 from jax.sharding import PartitionSpec as P
 
 HEADS = 8
@@ -66,20 +69,98 @@
     )
 
 
-def inverse_fourth_root(matrices):
-    order_size = matrices.shape[-1]
-    identity = jnp.eye(order_size, dtype=matrices.dtype)
-    frob_norms = jnp.sqrt(jnp.sum(matrices * matrices, axis=(1, 2)))
-    scaled = matrices / frob_norms[:, None, None]
-    root_now = jnp.broadcast_to(identity, matrices.shape)
-    for repeat in range(ROOT_ITERS):
-        factor = (5.0 * identity - scaled) * 0.25
-        root_now = jnp.matmul(root_now, factor, precision=HIGHEST)
-        square = jnp.matmul(factor, factor, precision=HIGHEST)
-        scaled = jnp.matmul(
-            jnp.matmul(square, square, precision=HIGHEST), scaled, precision=HIGHEST
-        )
-    return root_now * lax.rsqrt(jnp.sqrt(frob_norms))[:, None, None]
+def dot32(left_arg, right_arg):
+    return jnp.dot(left_arg, right_arg, preferred_element_type=jnp.float32)
+
+
+def two_terms(values):
+    high = values.astype(jnp.bfloat16)
+    return high, (values - high.astype(jnp.float32)).astype(jnp.bfloat16)
+
+
+def product_three(left_arg, right_arg):
+    left_high, left_low = two_terms(left_arg)
+    right_high, right_low = two_terms(right_arg)
+    return (
+        dot32(left_high, right_high) + dot32(left_high, right_low) + dot32(left_low, right_high)
+    )
+
+
+def next_scaled(quarter, quarter16, scaled):
+    square_rest = 2.0 * quarter + dot32(quarter16, quarter16)
+    square16 = square_rest.astype(jnp.bfloat16)
+    fourth_rest = 2.0 * square_rest + dot32(square16, square16)
+    return scaled + product_three(fourth_rest, scaled)
+
+
+def shampoo_kernel(
+    grad_ref, left_ref, right_ref, master_ref, grad_out, left_out, right_out, new_out, scaled, roots
+):
+    count, size, _ = grad_ref.shape
+    identity = (
+        lax.broadcasted_iota(jnp.int32, (size, size), 0)
+        == lax.broadcasted_iota(jnp.int32, (size, size), 1)
+    ).astype(jnp.float32)
+    factors = []
+    for block in range(count):
+        grad = grad_ref[block]
+        grad_out[block] = grad.astype(jnp.float32)
+        for side, stat_ref, stat_out in ((0, left_ref, left_out), (1, right_ref, right_out)):
+            dims = (((1 - side,), (1 - side,)), ((), ()))
+            stat = DECAY * stat_ref[block] + lax.dot_general(
+                grad, grad, dims, preferred_element_type=jnp.float32
+            )
+            stat_out[block] = stat
+            total = jnp.sum(stat * stat, axis=0, keepdims=True)
+            norm = jnp.sqrt(jnp.sum(total, axis=1, keepdims=True))
+            factors.append(lax.rsqrt(jnp.sqrt(norm)))
+            start = stat / norm
+            quarter = (identity - start) * 0.25
+            roots[2 * block + side] = identity + quarter
+            scaled[2 * block + side] = next_scaled(quarter, quarter.astype(jnp.bfloat16), start)
+
+    def iterate(step, carry):
+        for item in range(2 * count):
+            now = scaled[item]
+            quarter = (identity - now) * 0.25
+            quarter16 = quarter.astype(jnp.bfloat16)
+            root = roots[item]
+            roots[item] = root + dot32(root.astype(jnp.bfloat16), quarter16)
+            scaled[item] = next_scaled(quarter, quarter16, now)
+        return carry
+
+    lax.fori_loop(0, ROOT_ITERS - 2, iterate, 0)
+    for block in range(count):
+        ends = []
+        for side in range(2):
+            item = 2 * block + side
+            quarter16 = ((identity - scaled[item]) * 0.25).astype(jnp.bfloat16)
+            root = roots[item]
+            ends.append(root + dot32(root.astype(jnp.bfloat16), quarter16))
+        grad = grad_ref[block]
+        left_high, left_low = two_terms(ends[0])
+        half = dot32(left_high, grad) + dot32(left_low, grad)
+        rate = RATE_BLOCK * factors[2 * block] * factors[2 * block + 1]
+        new_out[block] = master_ref[block] - rate * product_three(half, ends[1])
+
+
+def shampoo(grads, left_stats, right_stats, master_blocks):
+    owned, size, _ = grads.shape
+    count = next(each for each in (4, 3, 2, 1) if owned % each == 0)
+    spec = pl.BlockSpec((count, size, size), lambda step: (step, 0, 0))
+    result = jax.ShapeDtypeStruct(grads.shape, jnp.float32)
+    return pl.pallas_call(
+        shampoo_kernel,
+        grid=(owned // count,),
+        in_specs=[spec] * 4,
+        out_specs=[spec] * 4,
+        out_shape=[result] * 4,
+        scratch_shapes=[pltpu.VMEM((2 * count, size, size), jnp.float32)] * 2,
+        compiler_params=pltpu.CompilerParams(vmem_limit_bytes=48 << 20),
+        cost_estimate=pl.CostEstimate(
+            flops=owned * 88 * 2 * size**3, bytes_accessed=owned * size * size * 30, transcendentals=0
+        ),
+    )(grads, left_stats, right_stats, master_blocks)
 
 
 def to_matrix(blocks, block_rows, block_cols):
@@ -145,6 +226,7 @@
     first_end = block_rows * qkv_cols
     second_end = first_end + head_rows * block_rows
     third_end = second_end + block_rows * ff_blocks
+    group_tokens = lax.all_gather(tokens, "tp", axis=0, tiled=True)
     all_blocks, all_vecs = (
         lax.all_gather(master_blocks.astype(jnp.bfloat16), "dp", axis=0, tiled=True),
         lax.all_gather(local_vecs.astype(jnp.bfloat16), "dp", axis=1, tiled=True),
@@ -168,12 +250,9 @@
     valid_own = (own_pack < packs[0]).astype(jnp.float32)
     owned_input_rows = tokens.astype(jnp.float32)
     owned_centred_scaled, owned_inverse_deviation = apply_layer_norm(owned_input_rows)
-    owned_first_branch = (owned_centred_scaled * first_gain + first_shift).astype(jnp.bfloat16)
-    owned_second_branch = (owned_centred_scaled * second_gain + second_shift).astype(jnp.bfloat16)
-    first_normed_input, second_normed_input = (
-        lax.all_gather(owned_first_branch, "tp", axis=0, tiled=True),
-        lax.all_gather(owned_second_branch, "tp", axis=0, tiled=True),
-    )
+    group_scaled, _ = apply_layer_norm(group_tokens.astype(jnp.float32))
+    first_normed_input = (group_scaled * first_gain + first_shift).astype(jnp.bfloat16)
+    second_normed_input = (group_scaled * second_gain + second_shift).astype(jnp.bfloat16)
     seg_flat = segments.reshape(-1)
     cosines, sines = rotary_tables(group_tok, pack_len, ROT)
     qkv_vals = (
@@ -217,7 +296,9 @@
     partial_value = jnp.dot(attn16, w_out, preferred_element_type=jnp.float32) + jnp.dot(
         activated, w_down, preferred_element_type=jnp.float32
     )
-    branch = lax.psum_scatter(partial_value, "tp", scatter_dimension=0, tiled=True)
+    branch = lax.psum_scatter(
+        partial_value.astype(jnp.bfloat16), "tp", scatter_dimension=0, tiled=True
+    ).astype(jnp.float32)
     output = (
         valid_own[:, None] * (owned_input_rows + branch + norm_params[4] + norm_params[5])
     ).astype(jnp.bfloat16)
@@ -304,15 +385,16 @@
     )
     grad_bqkv = jnp.sum(d_qkv16, axis=0, dtype=jnp.float32)
     d_normed_one = jnp.einsum("tc,dc->td", d_qkv16, w_qkv, preferred_element_type=jnp.float32)
-    owned_first_gradient, owned_second_gradient = (
-        lax.psum_scatter(d_normed_one, "tp", scatter_dimension=0, tiled=True),
-        lax.psum_scatter(d_normed_two, "tp", scatter_dimension=0, tiled=True),
-    )
-    first_gain_gradient = jnp.sum(owned_first_gradient * owned_centred_scaled, axis=0)
-    grad_shift_one = jnp.sum(owned_first_gradient, axis=0)
-    second_gain_gradient = jnp.sum(owned_second_gradient * owned_centred_scaled, axis=0)
-    grad_shift_two = jnp.sum(owned_second_gradient, axis=0)
-    norm_input_gradient = owned_first_gradient * first_gain + owned_second_gradient * second_gain
+    first_gain_gradient = jnp.sum(d_normed_one * group_scaled, axis=0)
+    grad_shift_one = jnp.sum(d_normed_one, axis=0)
+    second_gain_gradient = jnp.sum(d_normed_two * group_scaled, axis=0)
+    grad_shift_two = jnp.sum(d_normed_two, axis=0)
+    norm_input_gradient = lax.psum_scatter(
+        (d_normed_one * first_gain + d_normed_two * second_gain).astype(jnp.bfloat16),
+        "tp",
+        scatter_dimension=0,
+        tiled=True,
+    ).astype(jnp.float32)
     average_gradient = jnp.mean(norm_input_gradient, axis=-1, keepdims=True)
     average_projection = jnp.mean(
         norm_input_gradient * owned_centred_scaled, axis=-1, keepdims=True
@@ -320,48 +402,46 @@
     input_grad = seed16.astype(jnp.float32) + owned_inverse_deviation * (
         norm_input_gradient - average_gradient - owned_centred_scaled * average_projection
     )
+    dp_ways = lax.axis_size("dp")
+    vec_rows = 3 * heads_dev + ff_dev // HD
     shared_local = jnp.stack(
+        [first_gain_gradient, grad_shift_one, second_gain_gradient, grad_shift_two, out_bias_grad], 0
+    )
+    vecs_local = jnp.concatenate(
+        [grad_bqkv.reshape(3 * heads_dev, HD), grad_bin.reshape(ff_dev // HD, HD)], 0
+    )
+    small = jnp.concatenate(
         [
-            first_gain_gradient,
-            grad_shift_one,
-            second_gain_gradient,
-            grad_shift_two,
-            out_bias_grad,
-            out_bias_grad,
+            shared_local.reshape(5, dp_ways, -1).transpose(1, 0, 2).reshape(dp_ways, -1),
+            vecs_local.reshape(vec_rows, dp_ways, -1).transpose(1, 0, 2).reshape(dp_ways, -1),
+        ],
+        1,
+    )
+    used = small.shape[1]
+    small = jnp.pad(small, ((0, 0), (0, -used % 1024))).reshape(-1, 128)
+    small_own = lax.psum_scatter(small, "dp", scatter_dimension=0, tiled=True).reshape(-1)
+    shared_used = 5 * model_width // dp_ways
+    own_vec_grads = small_own[shared_used:used].reshape(vec_rows, HD // dp_ways)
+    shared_part = small_own[:shared_used].reshape(5, tp_ways, -1).transpose(1, 0, 2)
+    shared_part = jnp.pad(
+        shared_part.reshape(tp_ways, -1), ((0, 0), (0, -(shared_used // tp_ways) % 1024))
+    ).reshape(-1, 128)
+    shared_own = lax.psum_scatter(shared_part, "tp", scatter_dimension=0, tiled=True).reshape(-1)
+    shared_own = shared_own[: shared_used // tp_ways].reshape(5, -1)
+    shared_grads = jnp.concatenate([shared_own, shared_own[4:]], 0)
+    blocks_local = jnp.concatenate(
+        [
+            to_blocks(grad_wqkv.astype(jnp.bfloat16), block_size),
+            to_blocks(grad_wout.astype(jnp.bfloat16), block_size),
+            to_blocks(grad_win.astype(jnp.bfloat16), block_size),
+            to_blocks(grad_wdown.astype(jnp.bfloat16), block_size),
         ],
         0,
     )
-    shared_grads = lax.psum_scatter(shared_local, ("dp", "tp"), scatter_dimension=1, tiled=True)
-    blocks_local = jnp.concatenate(
-        [
-            to_blocks(grad_wqkv, block_size),
-            to_blocks(grad_wout, block_size),
-            to_blocks(grad_win, block_size),
-            to_blocks(grad_wdown, block_size),
-        ],
-        0,
-    )
-    vecs_local = jnp.concatenate(
-        [grad_bqkv.reshape(3 * heads_dev, HD), grad_bin.reshape(ff_dev // HD, HD)], 0
-    )
-    own_grads, own_vec_grads = (
-        lax.psum_scatter(blocks_local, "dp", scatter_dimension=0, tiled=True),
-        lax.psum_scatter(vecs_local, "dp", scatter_dimension=1, tiled=True),
-    )
-    left_new = DECAY * left_stats + jnp.einsum(
-        "nij,nkj->nik", own_grads, own_grads, precision=HIGHEST
-    )
-    right_new = DECAY * right_stats + jnp.einsum(
-        "nji,njk->nik", own_grads, own_grads, precision=HIGHEST
-    )
-    owned_count = own_grads.shape[0]
-    roots_all = inverse_fourth_root(jnp.concatenate([left_new, right_new], 0))
-    precond = jnp.matmul(
-        jnp.matmul(roots_all[:owned_count], own_grads, precision=HIGHEST),
-        roots_all[owned_count:],
-        precision=HIGHEST,
-    )
-    new_blocks = master_blocks - RATE_BLOCK * precond
+    grads16 = lax.psum_scatter(blocks_local, "dp", scatter_dimension=0, tiled=True)
+    own_grads, left_new, right_new, new_blocks = shampoo(
+        grads16, left_stats, right_stats, master_blocks
+    )
     local_stat_new = DECAY * local_vec_stats + own_vec_grads * own_vec_grads
     local_new = local_vecs - RATE_VEC * own_vec_grads * lax.rsqrt(local_stat_new)
     shared_stat_new = DECAY * shared_vec_stats + shared_grads * shared_grads

time: 2570 us -> 1470 us (0.57)
  waiting for transfers between devices: 1110 us -> 452 us
  matrix products: 944 us -> 358 us
  Pallas kernels: 0 us -> 154 us
  other arithmetic: 122 us -> 93.1 us
    dot_general x33 -> x0, matrix products: 625 us -> none  [the longest x7 150 us: inverse_fourth_root(): square = jnp.matmul(factor, factor, precision=HIGHEST)]
    reduce_scatter x3, waiting for transfers between devices: 509 us -> 101 us  [the longest x1 101 us: shards(): lax.psum_scatter(partial_value.astype(jnp.bfloat16), 'tp', scatter_dimens...]
    pallas_call x0 -> x1, Pallas kernels: none -> 154 us  [shampoo(): pl.pallas_call(shampoo_kernel, grid=(owned // count,), in_specs=[spec] *...]
    reduce_scatter x1, waiting for transfers between devices: 286 us -> 156 us  [shards(): lax.psum_scatter(blocks_local, 'dp', scatter_dimension=0, tiled=True)]
    unnamed x12 -> x7, waiting for transfers between devices: 126 us -> 1.3 us
    all_gather x1, waiting for transfers between devices: 32.2 us -> 118 us  [shards(): lax.all_gather(master_blocks.astype(jnp.bfloat16), 'dp', axis=0, tiled=True)]
    all_gather x2 -> x1, waiting for transfers between devices: 128 us -> 52.8 us  [shards(): group_tokens = lax.all_gather(tokens, 'tp', axis=0, tiled=True)]
    dot_general x3 -> x0, local copies, waits for them, and re-layouts: 27.5 us -> none  [the longest x2 14.8 us: shards(): jnp.einsum('tc,td->cd', attn16, seed_all, preferred_element_type=jnp.floa...]
  transfers between devices with their start and end apart: 10 -> 7, of which waited for: 7 -> 5; matrix products, arithmetic and copies ran while one was open for 26% -> 24% of each run, Pallas kernels for 0% -> 0%
where the time goes in v1:
time: 1470 us; the launch traced here: 1460 us
  waiting for transfers between devices  452 us (31%)
  matrix products  358 us (24%)
  local copies, waits for them, and re-layouts  262 us (18%)
  Pallas kernels  154 us (10%)
  blocking collectives  104 us (7%)
  other arithmetic  93.1 us (6%)
  loops' own time  20.6 us (1%)
  between operations  16.8 us (1%)
    reduce_scatter x1, waiting for transfers between devices, shards(): lax.psum_scatter(blocks_local, 'dp', scatter_dimension=0, tiled=True)  156 us
    pallas_call x1, Pallas kernels, shampoo(): pl.pallas_call(shampoo_kernel, grid=(owned // count,), in_specs=[spec] *...  154 us
    all_gather x1, waiting for transfers between devices, shards(): lax.all_gather(master_blocks.astype(jnp.bfloat16), 'dp', axis=0, tiled=True)  118 us
    reduce_scatter x1, waiting for transfers between devices, shards(): lax.psum_scatter(partial_value.astype(jnp.bfloat16), 'tp', scatter_dimens...  101 us
    unnamed x125, local copies, waits for them, and re-layouts  84.6 us
    all_gather x1, blocking collectives, shards(): lax.all_gather(shared_vecs.astype(jnp.bfloat16), ('dp', 'tp'), axis=1, ti...  76.3 us
    dot_general x1, matrix products, shards(): jnp.dot(second_normed_input, w_in, preferred_element_type=jnp.float32)  60.5 us
    all_gather x1, waiting for transfers between devices, shards(): group_tokens = lax.all_gather(tokens, 'tp', axis=0, tiled=True)  52.8 us
  transfers between devices with their start and end apart: 7, of which 5 were waited for; matrix products, arithmetic and copies ran while one was open for 24% of the time, Pallas kernels for 0%

profile of v1, /device:TPU:0, one launch (start us, length us, event | category | flops | bytes accessed | tf_op | source)
XLA Modules:
  0.0 1460.8 jit_solution(4432828649202910636)
XLA Ops:
  16.2 10.5 all-gather.1
  26.9 76.3 %all-gather = bf16[32,64,6]{1,2,0:T(8,128)(2,1)S(1)} all-gather(bf16[1,64,6]{1,2,0:T(8,128)(2,1)S(1)} %convert_bitcast_fusion.2), channel_id=1, replica_groups=mesh['dp'=8,'tp'=4] {'dp','tp'}, dimensions={0}, use_global_device_ids=true | all-gather | bytes 25344 | tf_op jit(solution)/shard_map/all_gather | solution.py:234
  110.4 52.8 %all-gather.6.cloned.1.call-done = bf16[2048,2048]{1,0:T(8,128)(2,1)} async-done(((bf16[512,2048]{1,0:T(8,128)(2,1)}), bf16[2048,2048]{1,0:T(8,128)(2,1)}) %all-gather.6.cloned.1.call-update) | async-done | bytes 8388624 | tf_op jit(solution)/shard_map/all_gather | solution.py:229
  171.3 118.0 %all-gather.8.cloned.1.call-done = bf16[192,256,256]{2,1,0:T(8,128)(2,1)} async-done(((bf16[24,256,256]{2,1,0:T(8,128)(2,1)}), bf16[192,256,256]{2,1,0:T(8,128)(2,1)}) %all-gather.8.cloned.1.call-update) | async-done | bytes 25165840 | tf_op jit(solution)/shard_map/all_gather | solution.py:231
  310.5 18.9 %convolution_add_fusion = f32[2048,1536]{0,1:T(8,128)S(1)} fusion(bf16[2048,1536]{0,1:T(8,128)(2,1)S(1)} %bitcast.253, f32[1536]{0:T(1024)S(1)} %add.271, bf16[2048,2048]{1,0:T(8,128)(2,1)} %all-gather.6.cloned.1.call-done, f32[2048]{0:T(1024)S(1)} %bitcast.279, f32[2048]{0:T(1024)S(1)} %bitcast.281, f32[2048]{0:T(1024)S(1)} %add_rsqrt_fusion, ...), kind=kOutput, calls=%fused_computation.107 | convolution fusion | flops 12913213440 | bytes 27301888 | tf_op jit(solution)/shard_map/dot_general | solution.py:259
  374.1 43.4 %while.54 = (s32[]{:T(128)}, bf16[2,1024,2,256]{3,2,1,0:T(2,128)(2,1)}, f32[2,2,2,512]{3,2,1,0:T(2,128)S(1)}, s32[2]{0:T(128)S(1)}, s32[2048]{0:T(1024)S(1)}, /*...) while((s32[]{:T(128)}, ...), condition=%wide.region_7.8_spmd, body=%wide.region_2.7_spmd.sunk | while | flops 1088159232 | bytes 25239136 | solution.py:292
  377.2 15.7 %while.57 = (s32[]{:T(128)}, bf16[2,512,2,256]{3,2,1,0:T(2,128)(2,1)}, f32[2,2,512]{2,1,0:T(2,128)S(1)}, s32[2]{0:T(128)S(1)}, s32[1024]{0:T(1024)S(1)}, /*index...) while((s32[]{:T(128)}, ...), condition=%wide.region_6.6_spmd, body=%wide.region_3.5_spmd.sunk | while | flops 1088159232 | bytes 18922236 | solution.py:289
  398.9 15.7 %while.57 = (s32[]{:T(128)}, bf16[2,512,2,256]{3,2,1,0:T(2,128)(2,1)}, f32[2,2,512]{2,1,0:T(2,128)S(1)}, s32[2]{0:T(128)S(1)}, s32[1024]{0:T(1024)S(1)}, /*index...) while((s32[]{:T(128)}, ...), condition=%wide.region_6.6_spmd, body=%wide.region_3.5_spmd.sunk | while | flops 1088159232 | bytes 18922236 | solution.py:289
  417.5 23.6 %all-gather.10.cloned.1.call-done = bf16[2048,2048]{1,0:T(8,128)(2,1)} async-done(((bf16[512,2048]{1,0:T(8,128)(2,1)}), bf16[2048,2048]{1,0:T(8,128)(2,1)}) %all-gather.10.cloned.1.call-update) | async-done | bytes 8388624 | tf_op jit(solution)/shard_map/all_gather | solution.py:314
  451.1 130.9 %while.56 = (s32[]{:T(128)}, f32[2,1024,2,256]{3,1,0,2:T(8,128)}, f32[2,1024,2,256]{3,1,0,2:T(8,128)}, bf16[2,1024,2,256]{3,1,0,2:T(8,128)(2,1)}, s32[2]{0:T(128...) while((s32[]{:T(128)}, f32[2,1024,2,256]{3,1,0,2:T(8,128)}, ...), condition=%wide.region_16.17_spmd, body=%wide.region_12.16_spmd.sunk | while | flops 2704539136 | bytes 135336400 | solution.py:374
  460.6 47.1 %while.58 = (s32[]{:T(128)}, f32[1024,2,256]{0,2,1:T(8,128)}, f32[1024,2,256]{0,2,1:T(8,128)}, f32[2,512,2,256]{3,2,1,0:T(2,128)}, s32[2]{0:T(128)S(1)}, /*index...) while((s32[]{:T(128)}, f32[1024,2,256]{0,2,1:T(8,128)}, ...), condition=%wide.region_15.15_spmd.clone, body=%wide.region_13.14_spmd.clone.sunk | while | flops 2704539136 | bytes 100707296 | solution.py:369
  525.9 47.1 %while.58 = (s32[]{:T(128)}, f32[1024,2,256]{0,2,1:T(8,128)}, f32[1024,2,256]{0,2,1:T(8,128)}, f32[2,512,2,256]{3,2,1,0:T(2,128)}, s32[2]{0:T(128)S(1)}, /*index...) while((s32[]{:T(128)}, f32[1024,2,256]{0,2,1:T(8,128)}, ...), condition=%wide.region_15.15_spmd.clone, body=%wide.region_13.14_spmd.clone.sunk | while | flops 2704539136 | bytes 100707296 | solution.py:369
  611.1 21.2 %fusion.98 = f32[2048,2048]{1,0:T(8,128)} fusion(bf16[2048,1536]{0,1:T(8,128)(2,1)} %bitcast.255, bf16[2048,1536]{0,1:T(8,128)(2,1)} %bitcast.254), kind=kOutput, calls=%fused_computation.217 | convolution fusion | flops 12884901888 | bytes 29360128 | tf_op jit(solution)/shard_map/tc,dc->td/dot_general | solution.py:387
  632.3 11.7 fusion.92
  644.0 11.9 copy.161
  655.9 10.4 copy.214
  666.3 12.3 copy.162
  678.6 10.4 copy.216
  689.1 60.5 %fusion.49 = (bf16[2048,2048]{1,0:T(8,128)(2,1)}, f32[2048,2048]{1,0:T(8,128)}) fusion(f32[2048]{0:T(1024)S(1)} %bitcast.285, bf16[2048,2048]{1,0:T(8,128)(2,1)} %bitcast.247, bf16[2048,2048]{1,0:T(8,128)(2,1)} %all-gather.6.cloned.1.call-done, f32[2048]{0:T(1024)S(1)} %bitcast.274, f32[2048]{0:T(1024)S(1)} %bitcast.276, f32[2048]{0:T(1024)S(1)} %copy-done.52, ...), kind=kOutput, calls=%fused_computation.80 | convolution fusion | flops 17481859072 | bytes 41984000 | tf_op jit(solution)/shard_map/dot_general | solution.py:294
  749.5 27.4 %convert_reduce_fusion.1 = (f32[2048]{0:T(1024)S(1)}, bf16[2048,2048]{1,0:T(8,128)(2,1)}) fusion(f32[2048,2048]{1,0:T(8,128)} %get-tuple-element.470, f32[2048]{0:T(1024)S(1)} %bitcast.286, bf16[2048,2048]{1,0:T(8,128)(2,1)} %all-gather.10.cloned.1.call-done, bf16[2048,2048]{1,0:T(8,128)(2,1)S(1)} %bitcast.243), kind=kOutput, calls=%fused_computation.87 | convolution fusion | flops 17234393088 | bytes 41959424 | tf_op jit(solution)/shard_map/td,fd->tf/dot_general | solution.py:320
  776.9 31.1 %fusion.90 = (f32[2048]{0:T(1024)S(1)}, f32[2048]{0:T(1024)S(1)}, bf16[2048,2048]{1,0:T(8,128)(2,1)}, f32[2048]{0:T(1024)S(1)}, f32[2048]{0:T(1024)S(1)}) fusion(f32[2048]{0:T(1024)S(1)} %copy-done.52, f32[2048]{0:T(1024)S(1)} %copy-done.37, bf16[2048,2048]{1,0:T(8,128)(2,1)} %all-gather.6.cloned.1.call-done, f32[2048]{0:T(1024)S(1)} %bitcast.277, ...), kind=kOutput, calls=%fused_computation.209 | convolution fusion | flops 17234386944 | bytes 50397184 | tf_op jit(solution)/shard_map/tf,df->td/dot_general | solution.py:327
  820.8 24.5 %add_convert_fusion.1 = bf16[2048,2048]{1,0:T(8,128)(2,1)} fusion(f32[2048,2048]{1,0:T(8,128)} %fusion.97, bf16[2048,2048]{1,0:T(8,128)(2,1)} %get-tuple-element.469, bf16[2048,2048]{1,0:T(8,128)(2,1)S(1)} %bitcast.246), kind=kOutput, calls=%fused_computation.89 | convolution fusion | flops 17188257792 | bytes 41943040 | tf_op jit(solution)/shard_map/dot_general | solution.py:296
  845.9 22.0 %convolution_convert_fusion.2 = bf16[2048,1536]{1,0:T(8,128)(2,1)} fusion(bf16[2048,1536]{0,1:T(8,128)(2,1)} %bitcast.256, bf16[2048,2048]{1,0:T(8,128)(2,1)} %all-gather.6.cloned.1.call-done, f32[2048]{0:T(1024)S(1)} %bitcast.280, f32[2048]{0:T(1024)S(1)} %bitcast.283, f32[2048]{0:T(1024)S(1)} %copy-done.52, f32[2048]{0:T(1024)S(1)} %copy-done.37), kind=kOutput, calls=%fused_computation.110 | convolution fusion | flops 12913213440 | bytes 21004288 | tf_op jit(solution)/shard_map/td,tc->dc/dot_general | solution.py:383
  903.6 25.2 %convolution_convert_fusion.1 = bf16[2048,2048]{1,0:T(8,128)(2,1)} fusion(bf16[2048,2048]{1,0:T(8,128)(2,1)} %get-tuple-element.472, bf16[2048,2048]{1,0:T(8,128)(2,1)} %all-gather.6.cloned.1.call-done, f32[2048]{0:T(1024)S(1)} %bitcast.275, f32[2048]{0:T(1024)S(1)} %bitcast.278, f32[2048]{0:T(1024)S(1)} %copy-done.52, f32[2048]{0:T(1024)S(1)} %copy-done.37), kind=kOutput, calls=%fused_computation.109 | convolution fusion | flops 17209229312 | bytes 25198592 | tf_op jit(solution)/shard_map/td,tf->df/dot_general | solution.py:323
  928.8 10.4 copy.219
  948.1 24.0 %convolution_convert_fusion = bf16[2048,2048]{1,0:T(8,128)(2,1)} fusion(bf16[2048,2048]{1,0:T(8,128)(2,1)} %get-tuple-element.469, bf16[2048,2048]{1,0:T(8,128)(2,1)} %all-gather.10.cloned.1.call-done), kind=kOutput, calls=%fused_computation.108 | convolution fusion | flops 17184063488 | bytes 25165824 | tf_op jit(solution)/shard_map/tf,td->fd/dot_general | solution.py:321
  972.1 10.4 copy.220
  991.3 17.3 %pad_maximum_fusion = bf16[192,256,256]{2,1,0:T(8,128)(2,1)} fusion(bf16[64,256,256]{2,1,0:T(8,128)(2,1)} %bitcast.225, bf16[64,256,256]{2,1,0:T(8,128)(2,1)} %bitcast.223, bf16[16,256,256]{2,1,0:T(8,128)(2,1)S(1)} %bitcast.242, bf16[48,256,256]{2,1,0:T(8,128)(2,1)} %bitcast.227), kind=kLoop, calls=%fused_computation.60 | loop fusion | flops 37748736 | bytes 50331648 | tf_op jit(solution)/shard_map/concatenate | solution.py:432
  1012.6 16.8 %all-reduce.2 = f32[32,128]{1,0:T(8,128)S(1)} all-reduce(f32[32,128]{1,0:T(8,128)S(1)} %reshape.395), channel_id=6, replica_groups=mesh['dp'=8,'tp'=4] {'tp'}, use_global_device_ids=true, to_apply=%region_29.30.clone | all-reduce | flops 4096 | bytes 32768
  1034.8 100.7 %reduce-scatter.5.cloned.1.call-done = bf16[512,2048]{1,0:T(8,128)(2,1)} async-done(((bf16[2048,2048]{1,0:T(8,128)(2,1)}), bf16[512,2048]{1,0:T(8,128)(2,1)}) %reduce-scatter.5.cloned.1.call-update) | async-done | bytes 2097168 | tf_op jit(solution)/shard_map/reduce_scatter | solution.py:299
  1141.4 155.8 %reduce-scatter.9.cloned.1.call-done.grad_ref = bf16[24,256,256]{2,1,0:T(8,128)(2,1)} async-done(((bf16[192,256,256]{2,1,0:T(8,128)(2,1)}), bf16[24,256,256]{2,1,0:T(8,128)(2,1)}) %reduce-scatter.9.cloned.1.call-update) | async-done | bytes 3145744 | tf_op jit(solution)/shard_map/reduce_scatter | solution.py:441
  1299.1 154.3 %shard_map.211 = (f32[24,256,256]{2,1,0:T(8,128)}, f32[24,256,256]{2,1,0:T(8,128)}, f32[24,256,256]{2,1,0:T(8,128)}, f32[24,256,256]{2,1,0:T(8,128)}) custom-call(bf16[24,256,256]{2,1,0:T(8,128)(2,1)S(1)} %copy-done, f32[24,256,256]{2,1,0:T(8,128)} %left_ref.1, f32[24,256,256]{2,1,0:T(8,128)} %right_ref.1, f32[24,256,256]{2,1,0:T(8,128)} %master_ref.1), custom_call_target="tpu_custom_call" | custom-call | flops 70866960384 | bytes 47185920 | tf_op jit(solution)/shard_map/pallas_call | solution.py:152
  (424 shorter events, 365.1 us)
Async XLA Ops:
  7.2 156.0 %all-gather.6.cloned.1.call-start = ((), (), s32[]{:S(2)}) async-start(), calls=%async_computation.4 | async-start | bytes 10485760 | tf_op jit(solution)/shard_map/all_gather | solution.py:229
  7.9 281.4 %all-gather.8.cloned.1.call-start = ((), (), s32[]{:S(2)}) async-start(), calls=%async_computation.5 | async-start | bytes 28311552 | tf_op jit(solution)/shard_map/all_gather | solution.py:231
  13.0 13.9 copy-start.41
  13.0 428.1 %all-gather.10.cloned.1.call-start = ((), (), s32[]{:S(2)}) async-start(), calls=%async_computation.7 | async-start | bytes 10485760 | tf_op jit(solution)/shard_map/all_gather | solution.py:314
  16.1 995.6 %reduce-scatter.11.cloned.1.call-start = ((), (), s32[]{:S(2)}) async-start(), calls=%async_computation.10 | async-start | bytes 73728 | tf_op jit(solution)/shard_map/reduce_scatter | solution.py:422
  103.9 206.5 %copy-start.46 = (f32[1,2048]{1,0:T(1,128)}, f32[1,2048]{1,0:T(1,128)S(1)}, u32[]{:S(2)}) copy-start(f32[1,2048]{1,0:T(1,128)S(1)} %get-tuple-element.465) | copy-start | bytes 24580
  103.9 206.5 %copy-start.48 = (f32[1,2048]{1,0:T(1,128)}, f32[1,2048]{1,0:T(1,128)S(1)}, u32[]{:S(2)}) copy-start(f32[1,2048]{1,0:T(1,128)S(1)} %get-tuple-element.466) | copy-start | bytes 24580
  110.4 253.4 %copy-start.14 = (f32[2048,64]{1,0:T(8,128)}, f32[2048,64]{1,0:T(8,128)S(1)}, u32[]{:S(2)}) copy-start(f32[2048,64]{1,0:T(8,128)S(1)} %get-tuple-element.474) | copy-start | bytes 1572868
  168.9 141.6 %copy-start.36 = (f32[2048]{0:T(1024)}, f32[2048]{0:T(1024)S(1)}, u32[]{:S(2)}) copy-start(f32[2048]{0:T(1024)S(1)} %broadcast_multiply_fusion) | copy-start | bytes 24580
  171.3 139.2 %copy-start.51 = (f32[2048]{0:T(1024)}, f32[2048]{0:T(1024)S(1)}, u32[]{:S(2)}) copy-start(f32[2048]{0:T(1024)S(1)} %add_rsqrt_fusion) | copy-start | bytes 24580
  310.4 19.0 %copy-start.23 = (bf16[192,8,8,256]{3,1,2,0:T(8,128)(2,1)}, bf16[192,8,8,256]{3,1,2,0:T(8,128)(2,1)S(1)}, u32[]{:S(2)}) copy-start(bf16[192,8,8,256]{3,1,2,0:T(8,128)(2,1)S(1)} %copy.211) | copy-start | bytes 18874372
  460.7 11.2 copy-start.5
  483.0 11.2 copy-start.5
  525.9 11.2 copy-start.5
  548.2 11.2 copy-start.5
  678.5 10.5 copy-start.52
  678.6 10.5 copy-start.53
  689.0 60.5 %copy-start.20 = (bf16[256,8,8,256]{3,1,2,0:T(8,128)(2,1)S(1)}, bf16[256,8,8,256]{3,1,2,0:T(8,128)(2,1)}, u32[]{:S(2)}) copy-start(bf16[256,8,8,256]{3,1,2,0:T(8,128)(2,1)} %copy.216) | copy-start | bytes 25165828
  749.5 27.4 %copy-start.49 = (f32[1,2048]{1,0:T(1,128)S(1)}, f32[1,2048]{1,0:T(1,128)}, u32[]{:S(2)}) copy-start(f32[1,2048]{1,0:T(1,128)} %copy-done.48) | copy-start | bytes 24580
  776.9 31.1 %copy-start.38 = (f32[2,3,256]{2,0,1:T(2,128)S(1)}, f32[2,3,256]{2,0,1:T(2,128)}, u32[]{:S(2)}) copy-start(f32[2,3,256]{2,0,1:T(2,128)} %get-tuple-element.428) | copy-start | bytes 18436
  776.9 31.5 %copy-start.33 = (f32[1,8,256]{2,1,0:T(8,128)S(1)}, f32[1,8,256]{2,1,0:T(8,128)}, u32[]{:S(2)}) copy-start(f32[1,8,256]{2,1,0:T(8,128)} %stack.34) | copy-start | bytes 24580
  809.1 222.4 %reduce-scatter.7.cloned.1.call-start = ((), (), s32[]{:S(2)}) async-start(), calls=%async_computation.8 | async-start | bytes 10485760 | tf_op jit(solution)/shard_map/reduce_scatter | solution.py:392
  809.7 325.9 %reduce-scatter.5.cloned.1.call-start = ((), (), s32[]{:S(2)}) async-start(), calls=%async_computation.6 | async-start | bytes 10485760 | tf_op jit(solution)/shard_map/reduce_scatter | solution.py:299
  809.7 11.0 slice-start.1
  845.3 451.9 %reduce-scatter.9.cloned.1.call-start = ((), (), s32[]{:S(2)}) async-start(), calls=%async_computation.9 | async-start | bytes 28311552 | tf_op jit(solution)/shard_map/reduce_scatter | solution.py:441
  1008.7 21.5 %copy-start.42 = (f32[6,64]{1,0:T(8,128)S(1)}, f32[6,64]{1,0:T(8,128)}, u32[]{:S(2)}) copy-start(f32[6,64]{1,0:T(8,128)} %param.30) | copy-start | bytes 4612
  1008.7 21.5 %copy-start.55 = (f32[6,64]{1,0:T(8,128)S(1)}, f32[6,64]{1,0:T(8,128)}, u32[]{:S(2)}) copy-start(f32[6,64]{1,0:T(8,128)} %param.31) | copy-start | bytes 4612
  1008.7 22.2 %copy-start.35 = (f32[14,32]{1,0:T(8,128)S(1)}, f32[14,32]{1,0:T(8,128)}, u32[]{:S(2)}) copy-start(f32[14,32]{1,0:T(8,128)} %param.28) | copy-start | bytes 5380
  1008.7 22.1 %copy-start.54 = (f32[14,32]{1,0:T(8,128)S(1)}, f32[14,32]{1,0:T(8,128)}, u32[]{:S(2)}) copy-start(f32[14,32]{1,0:T(8,128)} %param.29) | copy-start | bytes 5380
  1010.6 125.0 %copy-start.31 = (f32[1,2048]{1,0:T(1,128)S(1)}, f32[1,2048]{1,0:T(1,128)}, u32[]{:S(2)}) copy-start(f32[1,2048]{1,0:T(1,128)} %get-tuple-element.461) | copy-start | bytes 24580
  1010.6 125.0 %copy-start.32 = (f32[1,2048]{1,0:T(1,128)S(1)}, f32[1,2048]{1,0:T(1,128)}, u32[]{:S(2)}) copy-start(f32[1,2048]{1,0:T(1,128)} %get-tuple-element.462) | copy-start | bytes 24580
  1010.6 125.0 %copy-start.40 = (f32[512]{0:T(512)S(1)}, f32[512]{0:T(512)}, u32[]{:S(2)}) copy-start(f32[512]{0:T(512)} %copy-done.39) | copy-start | bytes 6148
  (58 other events, 262.9 us)
Sparse Core Ops, SparseCore 0:
  9.6 153.5 all-gather.5
  165.6 123.6 all-gather.7
  291.5 149.6 all-gather.9
  809.2 31.4 reduce-scatter.10
  843.0 144.4 reduce-scatter.6
  989.8 145.6 reduce-scatter.4
  1139.6 157.5 reduce-scatter.8

commit v2 on v1

v2 whole, which is shorter than its diff:
```python
import functools
import math

import jax
import jax.numpy as jnp
from jax import lax
from jax.experimental import pallas as pl
from jax.experimental.pallas import tpu as pltpu
from jax.sharding import PartitionSpec as P

HEADS = 8
HD = 256
ROT = 64
FF = 8192
SUBSETS = 22
ROOT_ITERS = 8


EPS_NORM = 1e-05
DECAY = 0.5
RATE_BLOCK = 0.6
RATE_VEC = 0.2
NEG_FILL = -1e30
DOC_MAX = 512
HALF_ROOT = 0.7071067811865476
DENSITY_SCALE = 0.3989422804014327


def apply_layer_norm(values):
    mean_val = jnp.mean(values, axis=-1, keepdims=True)
    centred = values - mean_val
    variance = jnp.mean(centred * centred, axis=-1, keepdims=True)
    inv_std = lax.rsqrt(variance + EPS_NORM)
    return (centred * inv_std, inv_std)


EXTRA_ROWS = 16
VMEM_LIMIT = 60 << 20
NN = (((1,), (0,)), ((), ()))
NT = (((1,), (1,)), ((), ()))
TN = (((0,), (0,)), ((), ()))


def contract(left_arg, right_arg, dims):
    return lax.dot_general(left_arg, right_arg, dims, preferred_element_type=jnp.float32)


def kernel_params():
    return pltpu.CompilerParams(vmem_limit_bytes=VMEM_LIMIT)


def block_row(index, owned, size):
    return index // owned * (owned * size + EXTRA_ROWS) + index % owned * size


def block_copies(blocks_ref, owned, first, rows, cols, target, sems):
    size = blocks_ref.shape[-1]
    return [
        pltpu.make_async_copy(
            blocks_ref.at[pl.ds(block_row(first + row * cols + col, owned, size), size), :],
            target.at[pl.ds(row * size, size), pl.ds(col * size, size)],
            sems.at[row * cols + col],
        )
        for row in range(rows)
        for col in range(cols)
    ]


def begin_copies(copies):
    @pl.when(pl.program_id(0) == 0)
    def _():
        for copy in copies:
            copy.start()


def end_copies(copies):
    @pl.when(pl.program_id(0) == 0)
    def _():
        for copy in copies:
            copy.wait()


def turn(values, cosines, sines):
    lane = lax.broadcasted_iota(jnp.int32, values.shape, 1)
    half = ROT // 2
    wide = values.shape[1]
    swapped = jnp.where(
        lane < half, pltpu.roll(values, wide - half, 1), pltpu.roll(values, half, 1)
    )
    return values * cosines + swapped * sines


def turn_tables(pack_len, lanes):
    half = ROT // 2
    positions = jnp.arange(pack_len).astype(jnp.float32)
    freqs = 10000.0 ** (-(jnp.arange(half).astype(jnp.float32) * 2.0) / ROT)
    angles = positions[:, None] * freqs[None, :]
    cosines = jnp.cos(angles)
    sines = jnp.sin(angles)
    rest = jnp.zeros((pack_len, lanes - ROT), jnp.float32)
    return (
        jnp.concatenate([cosines, cosines, rest + 1.0], -1),
        jnp.concatenate([-sines, sines, rest], -1),
    )


def normed_rows(rows):
    mean = jnp.mean(rows, axis=1, keepdims=True)
    centred = rows - mean
    variance = jnp.mean(centred * centred, axis=1, keepdims=True)
    return mean, lax.rsqrt(variance + EPS_NORM)


def part_copies(part_refs, held, sems):
    return [
        pltpu.make_async_copy(part, held.at[index], sems.at[index])
        for index, part in enumerate(part_refs)
    ]


def await_part(copies, per_part):
    step = pl.program_id(0)
    for index, copy in enumerate(copies):

        @pl.when(step == index * per_part)
        def _():
            copy.wait()


def qkv_kernel(heads, owned, parts, rank_ref, *refs):
    part_refs = refs[:parts]
    blocks_ref, norm_ref, bias_ref, cos_ref, sin_ref = refs[parts : parts + 5]
    qkv_ref, first_ref, second_ref, tokens_ref, weight, held, sems, part_sems = refs[parts + 5 :]
    size = blocks_ref.shape[-1]
    copies = block_copies(blocks_ref, owned, 0, weight.shape[0] // size, weight.shape[1] // size, weight, sems)
    moves = part_copies(part_refs, held, part_sems)
    begin_copies(moves + copies)
    await_part(moves, 1)
    own = held[pl.program_id(0)]
    tokens_ref[...] = own
    rows = own.astype(jnp.float32)
    mean, inverse = normed_rows(rows)
    scaled = (rows - mean) * inverse
    second_ref[...] = (scaled * norm_ref[2:3, :] + norm_ref[3:4, :]).astype(jnp.bfloat16)
    values = (scaled * norm_ref[0:1, :] + norm_ref[1:2, :]).astype(jnp.bfloat16)
    first_ref[...] = values
    end_copies(copies)
    lanes = cos_ref.shape[1]
    for head in range(heads):
        for part in range(3):
            cols = pl.ds((head * 3 + part) * HD, HD)
            result = contract(first_ref[...], weight[:, cols], NN) + bias_ref[:, cols]
            if part < 2:
                first = turn(result[:, :lanes], cos_ref[...], sin_ref[...])
                result = jnp.concatenate([first, result[:, lanes:]], 1)
            if part == 0:
                result = result * (1.0 / math.sqrt(HD))
            qkv_ref[:, cols] = result.astype(jnp.bfloat16)


def project_qkv(parts, rank, blocks, owned, norm_params, bias, cosines, sines, heads):
    ways = len(parts)
    tile, width = parts[0].shape
    tokens = ways * tile
    size = blocks.shape[-1]
    pack_len, lanes = cosines.shape
    cols = 3 * heads * HD
    per_pack = pack_len // tile
    place = lambda i, rank: (rank[0] - i + ways) % ways
    row = lambda n: pl.BlockSpec((tile, n), lambda i, rank: (place(i, rank), 0))
    table = pl.BlockSpec((tile, lanes), lambda i, rank: (place(i, rank) % per_pack, 0))
    anywhere = pl.BlockSpec(memory_space=pl.ANY)
    wide = jax.ShapeDtypeStruct((tokens, width), jnp.bfloat16)
    return pl.pallas_call(
        functools.partial(qkv_kernel, heads, owned, ways),
        grid_spec=pltpu.PrefetchScalarGridSpec(
            num_scalar_prefetch=1,
            grid=(ways,),
            in_specs=[anywhere] * (ways + 1)
            + [
                pl.BlockSpec(norm_params.shape, lambda i, rank: (0, 0)),
                pl.BlockSpec((1, cols), lambda i, rank: (0, 0)),
                table,
                table,
            ],
            out_specs=[row(cols), row(width), row(width), row(width)],
            scratch_shapes=[
                pltpu.VMEM((width, cols), jnp.bfloat16),
                pltpu.VMEM((ways, tile, width), jnp.bfloat16),
                pltpu.SemaphoreType.DMA((width // size * (cols // size),)),
                pltpu.SemaphoreType.DMA((ways,)),
            ],
        ),
        out_shape=[jax.ShapeDtypeStruct((tokens, cols), jnp.bfloat16), wide, wide, wide],
        compiler_params=kernel_params(),
        cost_estimate=pl.CostEstimate(
            flops=2 * tokens * width * cols, bytes_accessed=tokens * (4 * width + cols) * 2 + width * cols * 2, transcendentals=0
        ),
        name="qkv",
    )(rank, *parts, blocks, norm_params, bias, cosines, sines)


def attend_kernel(query_ref, key_ref, value_ref, seg_row, seg_col, out_ref):
    length = key_ref.shape[0]
    step = 256
    for start in range(0, length, step):
        first = max(0, start - DOC_MAX)
        stop = start + step
        scores = contract(query_ref[start:stop, :], key_ref[first:stop, :], NT)
        row = lax.broadcasted_iota(jnp.int32, scores.shape, 0) + start
        col = lax.broadcasted_iota(jnp.int32, scores.shape, 1) + first
        allowed = (col <= row) & (seg_col[0, start:stop, :] == seg_row[0, :, first:stop])
        masked = jnp.where(allowed, scores, NEG_FILL)
        exp_terms = jnp.exp(masked - jnp.max(masked, axis=1, keepdims=True))
        probs = exp_terms * (1.0 / jnp.sum(exp_terms, axis=1, keepdims=True))
        out_ref[start:stop, :] = contract(
            probs.astype(jnp.bfloat16), value_ref[first:stop, :], NN
        ).astype(jnp.bfloat16)


def attend(qkv, segments, heads):
    packs, length = segments.shape
    part = lambda which: pl.BlockSpec((length, HD), lambda p, h: (p, h * 3 + which))
    return pl.pallas_call(
        attend_kernel,
        grid=(packs, heads),
        in_specs=[
            part(0),
            part(1),
            part(2),
            pl.BlockSpec((1, 1, length), lambda p, h: (p, 0, 0)),
            pl.BlockSpec((1, length, 1), lambda p, h: (p, 0, 0)),
        ],
        out_specs=pl.BlockSpec((length, HD), lambda p, h: (p, h)),
        out_shape=jax.ShapeDtypeStruct((packs * length, heads * HD), jnp.bfloat16),
        compiler_params=kernel_params(),
        cost_estimate=pl.CostEstimate(
            flops=packs * heads * length * length * HD * 3, bytes_accessed=packs * length * heads * HD * 8, transcendentals=0
        ),
        name="attend",
    )(qkv, qkv, qkv, segments[:, None, :], segments[:, :, None])


def attend_back_kernel(
    query_ref, key_ref, value_ref, d_out_ref, seg_row, seg_col, cos_ref, sin_ref, grad_ref, d_key, d_value
):
    length = key_ref.shape[0]
    step = 256
    lanes = cos_ref.shape[1]
    d_key[...] = jnp.zeros_like(d_key)
    d_value[...] = jnp.zeros_like(d_value)
    for start in range(0, length, step):
        first = max(0, start - DOC_MAX)
        stop = start + step
        query = query_ref[start:stop, :]
        d_out = d_out_ref[start:stop, :]
        keys = key_ref[first:stop, :]
        scores = contract(keys, query, NT)
        key_pos = lax.broadcasted_iota(jnp.int32, scores.shape, 0) + first
        query_pos = lax.broadcasted_iota(jnp.int32, scores.shape, 1) + start
        allowed = (key_pos <= query_pos) & (seg_col[0, first:stop, :] == seg_row[0, :, start:stop])
        masked = jnp.where(allowed, scores, NEG_FILL)
        exp_terms = jnp.exp(masked - jnp.max(masked, axis=0, keepdims=True))
        probs = exp_terms * (1.0 / jnp.sum(exp_terms, axis=0, keepdims=True))
        d_probs = contract(value_ref[first:stop, :], d_out, NT)
        row_dot = jnp.sum(probs * d_probs, axis=0, keepdims=True)
        d_scores = (probs * (d_probs - row_dot)).astype(jnp.bfloat16)
        d_value[first:stop, :] += contract(probs.astype(jnp.bfloat16), d_out, NN)
        d_key[first:stop, :] += contract(d_scores, query, NN)
        d_query = contract(d_scores, keys, TN) * (1.0 / math.sqrt(HD))
        back = turn(d_query[:, :lanes], cos_ref[start:stop, :], -sin_ref[start:stop, :])
        grad_ref[start:stop, :lanes] = back.astype(jnp.bfloat16)
        grad_ref[start:stop, lanes:HD] = d_query[:, lanes:].astype(jnp.bfloat16)
    back = turn(d_key[:, :lanes], cos_ref[...], -sin_ref[...])
    grad_ref[:, HD : HD + lanes] = back.astype(jnp.bfloat16)
    grad_ref[:, HD + lanes : 2 * HD] = d_key[:, lanes:].astype(jnp.bfloat16)
    grad_ref[:, 2 * HD :] = d_value[...].astype(jnp.bfloat16)


def attend_back(qkv, d_attended, segments, cosines, sines, heads):
    packs, length = segments.shape
    lanes = cosines.shape[1]
    part = lambda which: pl.BlockSpec((length, HD), lambda p, h: (p, h * 3 + which))
    table = pl.BlockSpec((length, lanes), lambda p, h: (0, 0))
    return pl.pallas_call(
        attend_back_kernel,
        grid=(packs, heads),
        in_specs=[
            part(0),
            part(1),
            part(2),
            pl.BlockSpec((length, HD), lambda p, h: (p, h)),
            pl.BlockSpec((1, 1, length), lambda p, h: (p, 0, 0)),
            pl.BlockSpec((1, length, 1), lambda p, h: (p, 0, 0)),
            table,
            table,
        ],
        out_specs=pl.BlockSpec((length, 3 * HD), lambda p, h: (p, h)),
        out_shape=jax.ShapeDtypeStruct((packs * length, 3 * heads * HD), jnp.bfloat16),
        scratch_shapes=[pltpu.VMEM((length, HD), jnp.float32)] * 2,
        compiler_params=kernel_params(),
        cost_estimate=pl.CostEstimate(
            flops=packs * heads * length * length * HD * 7, bytes_accessed=packs * length * heads * HD * 16, transcendentals=0
        ),
        name="attend_back",
    )(qkv, qkv, qkv, d_attended, segments[:, None, :], segments[:, :, None], cosines, sines)


def feed_kernel(
    offsets, owned, x_ref, attended_ref, blocks_ref, bias_ref, act_ref, slope_ref, out_ref, w_in, w_down, sems_in, sems_down
):
    size = blocks_ref.shape[-1]
    width, hidden_units = w_in.shape
    inner = hidden_units // size
    first_out, first_in, first_down = offsets
    head_rows = attended_ref.shape[1] // size
    outer = width // size
    copies_in = block_copies(blocks_ref, owned, first_in, outer, inner, w_in, sems_in)
    copies_down = block_copies(blocks_ref, owned, first_down, inner, outer, w_down.at[pl.ds(0, hidden_units)], sems_down)
    copies_down += block_copies(
        blocks_ref,
        owned,
        first_out,
        head_rows,
        outer,
        w_down.at[pl.ds(hidden_units, head_rows * size)],
        sems_down.at[pl.ds(inner * outer, head_rows * outer)],
    )
    begin_copies(copies_in + copies_down)
    end_copies(copies_in)
    values = x_ref[...]
    for col in range(inner):
        cols = pl.ds(col * size, size)
        hidden = contract(values, w_in[:, cols], NN) + bias_ref[:, cols]
        cdf = 0.5 + 0.5 * lax.erf(hidden * HALF_ROOT)
        density = jnp.exp(-0.5 * hidden * hidden) * DENSITY_SCALE
        act_ref[:, cols] = (hidden * cdf).astype(jnp.bfloat16)
        slope_ref[:, cols] = (cdf + hidden * density).astype(jnp.bfloat16)
    end_copies(copies_down)
    for col in range(outer):
        cols = pl.ds(col * size, size)
        out_ref[:, cols] = (
            contract(act_ref[...], w_down[:hidden_units, cols], NN)
            + contract(attended_ref[...], w_down[hidden_units:, cols], NN)
        ).astype(jnp.bfloat16)


def feed_forward(normed, attended, blocks, owned, bias, offsets):
    tokens, width = normed.shape
    size = blocks.shape[-1]
    hidden_units = bias.shape[1]
    head_cols = attended.shape[1]
    tile = 512
    row = lambda cols: pl.BlockSpec((tile, cols), lambda i: (i, 0))
    inner, outer = hidden_units // size, width // size
    return pl.pallas_call(
        functools.partial(feed_kernel, offsets, owned),
        grid=(tokens // tile,),
        in_specs=[
            row(width),
            row(head_cols),
            pl.BlockSpec(memory_space=pl.ANY),
            pl.BlockSpec((1, hidden_units), lambda i: (0, 0)),
        ],
        out_specs=[row(hidden_units), row(hidden_units), row(width)],
        out_shape=[
            jax.ShapeDtypeStruct((tokens, hidden_units), jnp.bfloat16),
            jax.ShapeDtypeStruct((tokens, hidden_units), jnp.bfloat16),
            jax.ShapeDtypeStruct((tokens, width), jnp.bfloat16),
        ],
        scratch_shapes=[
            pltpu.VMEM((width, hidden_units), jnp.bfloat16),
            pltpu.VMEM((hidden_units + head_cols, width), jnp.bfloat16),
            pltpu.SemaphoreType.DMA((inner * outer,)),
            pltpu.SemaphoreType.DMA((inner * outer + head_cols // size * outer,)),
        ],
        compiler_params=kernel_params(),
        cost_estimate=pl.CostEstimate(
            flops=2 * tokens * width * (2 * hidden_units + head_cols), bytes_accessed=tokens * width * 10 + width * hidden_units * 4, transcendentals=0
        ),
        name="feed",
    )(normed, attended, blocks, bias)


def column_sum(values):
    rows, cols = values.shape
    return jnp.sum(values.reshape(rows // 8, 8, cols), axis=0)


def feed_back_kernel(offsets, owned, parts, held_count, rank_ref, *refs):
    part_refs = refs[:parts]
    factor_ref, slope_ref, tokens_ref, blocks_ref, norm_ref = refs[parts : parts + 5]
    (
        seed_ref, d_attended_ref, d_hidden_ref, dz_ref, norm_sums, hidden_sums,
        w_in, w_down, w_out, held, sems_in, sems_down, sems_out, part_sems,
    ) = refs[parts + 5 + held_count :]
    size = blocks_ref.shape[-1]
    width, hidden_units = w_in.shape
    inner, outer = hidden_units // size, width // size
    first_out, first_in, first_down = offsets
    tile = seed_ref.shape[0]
    per_part = held.shape[1] // tile
    moves = part_copies(part_refs, held, part_sems)
    copies_out = block_copies(blocks_ref, owned, first_out, w_out.shape[0] // size, outer, w_out, sems_out)
    copies_down = block_copies(blocks_ref, owned, first_down, inner, outer, w_down, sems_down)
    copies_in = block_copies(blocks_ref, owned, first_in, outer, inner, w_in, sems_in)
    begin_copies(moves + copies_out + copies_down + copies_in)

    @pl.when(pl.program_id(0) == 0)
    def _():
        norm_sums[...] = jnp.zeros_like(norm_sums)
        hidden_sums[...] = jnp.zeros_like(hidden_sums)

    await_part(moves, per_part)
    step = pl.program_id(0)
    cotangent = held[step // per_part, pl.ds(pl.multiple_of(step % per_part * tile, tile), tile), :]
    seed_ref[...] = (cotangent.astype(jnp.float32) * factor_ref[...]).astype(jnp.bfloat16)
    seed = seed_ref[...]
    end_copies(copies_out)
    d_attended_ref[...] = contract(seed, w_out[...], NT).astype(jnp.bfloat16)
    end_copies(copies_down)
    for col in range(inner):
        cols = pl.ds(col * size, size)
        d_act = contract(seed_ref[...], w_down[cols, :], NT)
        d_hidden = (d_act * slope_ref[:, cols].astype(jnp.float32)).astype(jnp.bfloat16)
        d_hidden_ref[:, cols] = d_hidden
        hidden_sums[:, cols] += column_sum(d_hidden.astype(jnp.float32))
    end_copies(copies_in)
    mean, inverse = normed_rows(tokens_ref[...].astype(jnp.float32))
    for col in range(outer):
        cols = pl.ds(col * size, size)
        scaled = (tokens_ref[:, cols].astype(jnp.float32) - mean) * inverse
        second = contract(d_hidden_ref[...], w_in[cols, :], NT)
        dz_ref[:, cols] = second * norm_ref[2:3, cols]
        norm_sums[0:8, cols] += column_sum(second * scaled)
        norm_sums[8:16, cols] += column_sum(second)


def feed_back(parts, first_part, ways, rank, factor, slope, group_tokens, blocks, owned, norm_params, offsets, head_cols, priors):
    chunk, width = parts[0].shape
    tokens = ways * chunk
    size = blocks.shape[-1]
    hidden_units = slope.shape[1]
    tile = min(256, chunk)
    per_part = chunk // tile
    inner, outer = hidden_units // size, width // size
    place = lambda i, rank: (rank[0] - first_part - i // per_part + ways) % ways * per_part + i % per_part
    row = lambda n: pl.BlockSpec((tile, n), lambda i, rank: (place(i, rank), 0))
    whole = lambda rows, cols: pl.BlockSpec((rows, cols), lambda i, rank: (0, 0))
    anywhere = pl.BlockSpec(memory_space=pl.ANY)
    count = len(parts)
    rows = count * chunk
    return pl.pallas_call(
        functools.partial(feed_back_kernel, offsets, owned, count, len(priors)),
        grid_spec=pltpu.PrefetchScalarGridSpec(
            num_scalar_prefetch=1,
            grid=(count * per_part,),
            in_specs=[anywhere] * count
            + [row(1), row(hidden_units), row(width), anywhere, whole(norm_params.shape[0], width)]
            + [anywhere] * len(priors),
            out_specs=[
                row(width), row(head_cols), row(hidden_units), row(width), whole(16, width), whole(8, hidden_units),
            ],
            scratch_shapes=[
                pltpu.VMEM((width, hidden_units), jnp.bfloat16),
                pltpu.VMEM((hidden_units, width), jnp.bfloat16),
                pltpu.VMEM((head_cols, width), jnp.bfloat16),
                pltpu.VMEM((count, chunk, width), jnp.bfloat16),
                pltpu.SemaphoreType.DMA((inner * outer,)),
                pltpu.SemaphoreType.DMA((inner * outer,)),
                pltpu.SemaphoreType.DMA((head_cols // size * outer,)),
                pltpu.SemaphoreType.DMA((count,)),
            ],
        ),
        out_shape=[
            jax.ShapeDtypeStruct((tokens, width), jnp.bfloat16),
            jax.ShapeDtypeStruct((tokens, head_cols), jnp.bfloat16),
            jax.ShapeDtypeStruct((tokens, hidden_units), jnp.bfloat16),
            jax.ShapeDtypeStruct((tokens, width), jnp.float32),
            jax.ShapeDtypeStruct((16, width), jnp.float32),
            jax.ShapeDtypeStruct((8, hidden_units), jnp.float32),
        ],
        input_output_aliases={1 + count + 5 + index: index for index in range(len(priors))},
        compiler_params=kernel_params(),
        cost_estimate=pl.CostEstimate(
            flops=2 * rows * width * (2 * hidden_units + head_cols), bytes_accessed=rows * width * 14 + width * hidden_units * 4, transcendentals=0
        ),
        name="feed_back",
    )(rank, *parts, factor, slope, group_tokens, blocks, norm_params, *priors)


def qkv_back_kernel(owned, d_qkv_ref, part_ref, tokens_ref, blocks_ref, norm_ref, dz_ref, norm_sums, qkv_sums, w_qkv, sems):
    size = blocks_ref.shape[-1]
    outer = w_qkv.shape[0] // size
    copies = block_copies(blocks_ref, owned, 0, outer, w_qkv.shape[1] // size, w_qkv, sems)
    begin_copies(copies)

    @pl.when(pl.program_id(0) == 0)
    def _():
        norm_sums[...] = jnp.zeros_like(norm_sums)
        qkv_sums[...] = jnp.zeros_like(qkv_sums)

    qkv_sums[...] += column_sum(d_qkv_ref[...].astype(jnp.float32))
    mean, inverse = normed_rows(tokens_ref[...].astype(jnp.float32))
    end_copies(copies)
    for col in range(outer):
        cols = pl.ds(col * size, size)
        scaled = (tokens_ref[:, cols].astype(jnp.float32) - mean) * inverse
        first = contract(d_qkv_ref[...], w_qkv[cols, :], NT)
        dz_ref[:, cols] = (part_ref[:, cols] + first * norm_ref[0:1, cols]).astype(jnp.bfloat16)
        norm_sums[0:8, cols] += column_sum(first * scaled)
        norm_sums[8:16, cols] += column_sum(first)


def qkv_back(d_qkv, dz_part, group_tokens, blocks, owned, norm_params):
    tokens, qkv_cols = d_qkv.shape
    width = dz_part.shape[1]
    size = blocks.shape[-1]
    tile = 512
    row = lambda cols: pl.BlockSpec((tile, cols), lambda i: (i, 0))
    whole = lambda rows, cols: pl.BlockSpec((rows, cols), lambda i: (0, 0))
    outer = width // size
    return pl.pallas_call(
        functools.partial(qkv_back_kernel, owned),
        grid=(tokens // tile,),
        in_specs=[
            row(qkv_cols), row(width), row(width), pl.BlockSpec(memory_space=pl.ANY), whole(norm_params.shape[0], width),
        ],
        out_specs=[row(width), whole(16, width), whole(8, qkv_cols)],
        out_shape=[
            jax.ShapeDtypeStruct((tokens, width), jnp.bfloat16),
            jax.ShapeDtypeStruct((16, width), jnp.float32),
            jax.ShapeDtypeStruct((8, qkv_cols), jnp.float32),
        ],
        scratch_shapes=[
            pltpu.VMEM((width, qkv_cols), jnp.bfloat16),
            pltpu.SemaphoreType.DMA((outer * (qkv_cols // size),)),
        ],
        compiler_params=kernel_params(),
        cost_estimate=pl.CostEstimate(
            flops=2 * tokens * width * qkv_cols, bytes_accessed=tokens * width * 11, transcendentals=0
        ),
        name="qkv_back",
    )(d_qkv, dz_part, group_tokens, blocks, norm_params)


def weight_grad_kernel(table, owned, part_size, core_ref, *refs):
    products = len(table)
    parts = owned // part_size
    left_refs, refs = refs[:products], refs[products:]
    rights, refs = refs[:3], refs[3:]
    outs, refs = refs[: 2 * parts], refs[2 * parts :]
    held, (results, sems, right_sems) = refs[:3], refs[3:]
    size = results.shape[-1]
    step = pl.program_id(0)
    slot = lax.rem(step, 2)
    core = core_ref[0]
    loads = [pltpu.make_async_copy(rights[i], held[i], right_sems.at[i]) for i in range(3)]

    @pl.when(step == 0)
    def _():
        for load in loads:
            load.start()

    def finish(of_slot, amount):
        for index in range(amount):
            pltpu.make_async_copy(
                results.at[of_slot, index], outs[0].at[0], sems.at[of_slot, index]
            ).wait()

    def amount_of(product):
        left, right = left_refs[product], held[table[product][3]]
        return left.shape[1] // size * (right.shape[1] // size)

    made = [product for product in range(products) for _ in range(table[product][1])]
    total = len(made)
    for product, (begin, times, first, which, fresh) in enumerate(table):

        @pl.when((step >= begin) & (step < begin + times))
        def _():
            left_ref, right = left_refs[product], held[which]
            rows, cols = left_ref.shape[1] // size, right.shape[1] // size
            if fresh:

                @pl.when(step == begin)
                def _():
                    loads[which].wait()

            for back in range(begin, begin + times):
                if back >= 2:

                    @pl.when(step == back)
                    def _():
                        finish(back % 2, amount_of(made[back - 2]))

            turned = left_ref[...].T
            for col in range(cols):
                result = contract(turned, right[:, pl.ds(col * size, size)], NN)
                for row in range(rows):
                    results[slot, row * cols + col] = result[
                        row * size : (row + 1) * size
                    ].astype(jnp.bfloat16)
            for row in range(rows):
                for col in range(cols):
                    block = first + ((step - begin) * rows + row) * cols + col
                    owner, within = block // owned, block % owned
                    place = owner // 2 * part_size + within % part_size
                    for part in range(parts):
                        for away in range(2):

                            @pl.when((within // part_size == part) & ((owner % 2 == core) == (away == 0)))
                            def _():
                                pltpu.make_async_copy(
                                    results.at[slot, row * cols + col],
                                    outs[2 * part + away].at[place],
                                    sems.at[slot, row * cols + col],
                                ).start()

    @pl.when(step == total - 1)
    def _():
        if total >= 2:
            finish((total - 2) % 2, amount_of(made[total - 2]))
        finish((total - 1) % 2, amount_of(made[total - 1]))


def weight_grads(lefts, rights, chosen, firsts, core, owned, part_size, dp_ways, size):
    tokens = lefts[0].shape[0]
    groups = [min(512, left.shape[1]) for left in lefts]
    times = [left.shape[1] // group for left, group in zip(lefts, groups)]
    begins = [sum(times[:index]) for index in range(len(times))]
    table = tuple(
        (begins[i], times[i], firsts[i], chosen[i], chosen[i] not in chosen[:i]) for i in range(len(lefts))
    )
    most = max(group // size * (rights[which].shape[1] // size) for group, which in zip(groups, chosen))
    parts = owned // part_size

    def left_spec(index):
        begin, last, group = begins[index], times[index] - 1, groups[index]
        return pl.BlockSpec((tokens, group), lambda i, core: (0, jnp.clip(i - begin, 0, last)))

    anywhere = pl.BlockSpec(memory_space=pl.ANY)
    half = jax.ShapeDtypeStruct((dp_ways // 2 * part_size, size, size), jnp.bfloat16)
    flops = sum(2 * tokens * left.shape[1] * rights[which].shape[1] for left, which in zip(lefts, chosen))
    return pl.pallas_call(
        functools.partial(weight_grad_kernel, table, owned, part_size),
        grid_spec=pltpu.PrefetchScalarGridSpec(
            num_scalar_prefetch=1,
            grid=(sum(times),),
            in_specs=[left_spec(index) for index in range(len(lefts))] + [anywhere] * 3,
            out_specs=[anywhere] * (2 * parts),
            scratch_shapes=[pltpu.VMEM(right.shape, jnp.bfloat16) for right in rights]
            + [
                pltpu.VMEM((2, most, size, size), jnp.bfloat16),
                pltpu.SemaphoreType.DMA((2, most)),
                pltpu.SemaphoreType.DMA((3,)),
            ],
        ),
        out_shape=[half] * (2 * parts),
        compiler_params=kernel_params(),
        cost_estimate=pl.CostEstimate(flops=flops, bytes_accessed=flops // 1000, transcendentals=0),
        name="weight_grads",
    )(core, *lefts, *rights)


def pair_sum_kernel(chip_ref, *refs):
    chips = len(refs) // 3
    for index in range(chips):
        total = refs[index][...].astype(jnp.float32) + refs[chips + index][...].astype(jnp.float32)
        refs[2 * chips + index][...] = total.astype(refs[2 * chips + index].dtype)


def pair_sum(kept, received, chip, chips):
    rows, size, _ = kept.shape
    part = rows // chips
    spec = lambda away: pl.BlockSpec(
        (part, size, size), lambda i, chip: (jnp.bitwise_xor(chip[0], away), 0, 0)
    )
    plain = pl.BlockSpec((part, size, size), lambda i, chip: (0, 0, 0))
    dtypes = [jnp.float32] + [jnp.bfloat16] * (chips - 1)
    return pl.pallas_call(
        pair_sum_kernel,
        grid_spec=pltpu.PrefetchScalarGridSpec(
            num_scalar_prefetch=1,
            grid=(1,),
            in_specs=[spec(away) for away in range(chips)] * 2,
            out_specs=[plain] * chips,
        ),
        out_shape=[jax.ShapeDtypeStruct((part, size, size), dtype) for dtype in dtypes],
        compiler_params=kernel_params(),
        cost_estimate=pl.CostEstimate(flops=rows * size * size, bytes_accessed=rows * size * size * 6, transcendentals=0),
        name="pair_sum",
    )(chip, *([kept] * chips), *([received] * chips))


def dot32(left_arg, right_arg):
    return jnp.dot(left_arg, right_arg, preferred_element_type=jnp.float32)


def two_terms(values):
    high = values.astype(jnp.bfloat16)
    return high, (values - high.astype(jnp.float32)).astype(jnp.bfloat16)


def product_three(left_arg, right_arg):
    left_high, left_low = two_terms(left_arg)
    right_high, right_low = two_terms(right_arg)
    return (
        dot32(left_high, right_high) + dot32(left_high, right_low) + dot32(left_low, right_high)
    )


def next_scaled(quarter, quarter16, scaled):
    square_rest = 2.0 * quarter + dot32(quarter16, quarter16)
    square16 = square_rest.astype(jnp.bfloat16)
    fourth_rest = 2.0 * square_rest + dot32(square16, square16)
    return scaled + product_three(fourth_rest, scaled)


def shampoo_kernel(
    grad_refs, left_ref, right_ref, master_ref, grad_out, left_out, right_out, new_out, scaled, roots
):
    count, size, _ = left_ref.shape
    identity = (
        lax.broadcasted_iota(jnp.int32, (size, size), 0)
        == lax.broadcasted_iota(jnp.int32, (size, size), 1)
    ).astype(jnp.float32)
    factors = []
    for block in range(count):
        total = grad_refs[0][block].astype(jnp.float32)
        for grad_ref in grad_refs[1:]:
            total = total + grad_ref[block].astype(jnp.float32)
        grad_out[block] = total
        grad = total.astype(jnp.bfloat16)
        for side, stat_ref, stat_out in ((0, left_ref, left_out), (1, right_ref, right_out)):
            dims = (((1 - side,), (1 - side,)), ((), ()))
            stat = DECAY * stat_ref[block] + lax.dot_general(
                grad, grad, dims, preferred_element_type=jnp.float32
            )
            stat_out[block] = stat
            squares = jnp.sum(stat * stat, axis=0, keepdims=True)
            norm = jnp.sqrt(jnp.sum(squares, axis=1, keepdims=True))
            factors.append(lax.rsqrt(jnp.sqrt(norm)))
            start = stat / norm
            quarter = (identity - start) * 0.25
            roots[2 * block + side] = identity + quarter
            scaled[2 * block + side] = next_scaled(quarter, quarter.astype(jnp.bfloat16), start)

    def iterate(step, carry):
        for item in range(2 * count):
            now = scaled[item]
            quarter = (identity - now) * 0.25
            quarter16 = quarter.astype(jnp.bfloat16)
            root = roots[item]
            roots[item] = root + dot32(root.astype(jnp.bfloat16), quarter16)
            scaled[item] = next_scaled(quarter, quarter16, now)
        return carry

    lax.fori_loop(0, ROOT_ITERS - 2, iterate, 0)
    for block in range(count):
        ends = []
        for side in range(2):
            item = 2 * block + side
            quarter16 = ((identity - scaled[item]) * 0.25).astype(jnp.bfloat16)
            root = roots[item]
            ends.append(root + dot32(root.astype(jnp.bfloat16), quarter16))
        grad = grad_out[block].astype(jnp.bfloat16)
        left_high, left_low = two_terms(ends[0])
        half = dot32(left_high, grad) + dot32(left_low, grad)
        rate = RATE_BLOCK * factors[2 * block] * factors[2 * block + 1]
        new_out[block] = master_ref[block] - rate * product_three(half, ends[1])


def shampoo(grads, left_stats, right_stats, master_blocks, first, priors):
    part, size, _ = grads[0].shape
    terms = len(grads)
    count = next(each for each in (3, 2, 1) if part % each == 0)
    start = first // count
    spec = pl.BlockSpec((count, size, size), lambda step: (step + start, 0, 0))
    own = pl.BlockSpec((count, size, size), lambda step: (step, 0, 0))
    result = jax.ShapeDtypeStruct(left_stats.shape, jnp.float32)
    held = [] if priors is None else list(priors)

    def kernel(*refs):
        shampoo_kernel(refs[:terms], *refs[terms : terms + 3], *refs[terms + 3 + len(held) :])

    return pl.pallas_call(
        kernel,
        grid=(part // count,),
        in_specs=[own] * terms + [spec] * 3 + [pl.BlockSpec(memory_space=pl.ANY)] * len(held),
        out_specs=[spec] * 4,
        out_shape=[result] * 4,
        input_output_aliases={terms + 3 + index: index for index in range(len(held))},
        scratch_shapes=[pltpu.VMEM((2 * count, size, size), jnp.float32)] * 2,
        compiler_params=kernel_params(),
        cost_estimate=pl.CostEstimate(
            flops=part * 180 * 2 * size**3, bytes_accessed=part * size * size * 30, transcendentals=0
        ),
        name="shampoo",
    )(*grads, left_stats, right_stats, master_blocks, *held)


def after(value, *earlier):
    return lax.optimization_barrier((value,) + earlier)[0]


def onward(part, axis):
    ways = lax.axis_size(axis)
    return lax.ppermute(part, axis, [(each, (each + 1) % ways) for each in range(ways)])


def swap(part, bits):
    ways = lax.axis_size("dp")
    return lax.ppermute(part, "dp", [(each, each ^ bits) for each in range(ways)])


def small_rows(values, ways):
    return jnp.pad(values, ((0, 0), (0, -values.shape[1] % 2048))).reshape(-1, 128)


def shards(
    tokens,
    cotangent,
    segments,
    subsets,
    packs,
    master_blocks,
    left_stats,
    right_stats,
    local_vecs,
    local_vec_stats,
    shared_vecs,
    shared_vec_stats,
):
    tp_ways = lax.axis_size("tp")
    dp_ways = lax.axis_size("dp")
    tp_rank = lax.axis_index("tp")
    tok_dev, model_width = tokens.shape
    group_tok = tok_dev * tp_ways
    pack_count, pack_len = segments.shape
    seg_width = subsets.shape[1]
    heads_dev = HEADS // tp_ways
    ff_dev = FF // tp_ways
    head_cols = heads_dev * HD
    owned, block_size, _ = master_blocks.shape
    block_rows = model_width // block_size
    first_out = block_rows * (3 * head_cols // block_size)
    first_in = first_out + head_cols // block_size * block_rows
    first_down = first_in + block_rows * (ff_dev // block_size)
    all_count = owned * dp_ways
    vec_rows = 3 * heads_dev + ff_dev // HD

    shared16 = shared_vecs.astype(jnp.bfloat16)
    shared_here = [(tp_rank, shared16)] + [
        (
            (tp_rank - step) % tp_ways,
            lax.ppermute(shared16, "tp", [(each, (each + step) % tp_ways) for each in range(tp_ways)]),
        )
        for step in range(1, tp_ways)
    ]
    shared_group = jnp.zeros((tp_ways,) + shared16.shape, jnp.bfloat16)
    for place, part in shared_here:
        shared_group = lax.dynamic_update_slice(shared_group, part[None], (place, 0, 0))
    vec_flat = jnp.concatenate([local_vecs.astype(jnp.bfloat16).reshape(-1), shared_group.reshape(-1)])
    vec_used = local_vecs.size
    shared_used = shared_group.size
    extra = jnp.pad(vec_flat, (0, EXTRA_ROWS * block_size - vec_flat.size)).reshape(EXTRA_ROWS, block_size)
    rows16 = jnp.concatenate([master_blocks.astype(jnp.bfloat16).reshape(-1, block_size), extra], 0)
    blocks = lax.all_gather(rows16, "dp", axis=0, tiled=True)

    token_parts = [tokens]
    for step in range(1, tp_ways):
        token_parts.append(onward(token_parts[-1], "tp"))

    gathered = blocks.reshape(dp_ways, -1, block_size)[:, owned * block_size :].reshape(dp_ways, -1)
    vec_values = (
        gathered[:, :vec_used].reshape(dp_ways, vec_rows, -1).transpose(1, 0, 2).reshape(vec_rows, HD)
    ).astype(jnp.float32)
    norm_params = (
        gathered[:, vec_used : vec_used + shared_used]
        .reshape(dp_ways, tp_ways, 6, -1)
        .transpose(2, 0, 1, 3)
        .reshape(6, model_width)
    ).astype(jnp.float32)
    bias_qkv = vec_values[: 3 * heads_dev].reshape(1, -1)
    bias_in = vec_values[3 * heads_dev :].reshape(1, -1)

    own_pos = tp_rank * tok_dev + jnp.arange(tok_dev)
    own_pack = own_pos // pack_len
    valid_own = (own_pack < packs[0]).astype(jnp.float32)
    owned_input_rows = tokens.astype(jnp.float32)
    owned_centred_scaled, owned_inverse_deviation = apply_layer_norm(owned_input_rows)

    group_pack = jnp.arange(group_tok) // pack_len
    lookup_key = group_pack * seg_width + segments.reshape(-1)
    onehot = lookup_key[:, None] == jnp.arange(pack_count * seg_width)[None, :]
    subset_tok = jnp.sum(jnp.where(onehot, subsets.reshape(-1)[None, :], 0), axis=1)
    weight = 0.5 + subset_tok.astype(jnp.float32) / (SUBSETS - 1)
    factor = (weight * (group_pack < packs[0]).astype(jnp.float32))[:, None]
    own_factor = lax.dynamic_slice_in_dim(factor, tp_rank * tok_dev, tok_dev, 0)
    seed16 = (cotangent.astype(jnp.float32) * own_factor).astype(jnp.bfloat16)
    out_bias_grad = jnp.sum(seed16, axis=0, dtype=jnp.float32)

    rank = tp_rank.astype(jnp.int32)[None]
    cosines, sines = turn_tables(pack_len, 128)
    cotangent_parts = [cotangent, onward(after(cotangent, token_parts[-1]), "tp")]
    qkv16, first_normed, second_normed, group_tokens = project_qkv(
        token_parts, rank, blocks, owned, norm_params, bias_qkv, cosines, sines, heads_dev
    )
    attended = attend(qkv16, segments, heads_dev)
    cotangent_parts.append(onward(after(cotangent_parts[-1], attended), "tp"))
    activated, slope, partial_value = feed_forward(
        second_normed, attended, blocks, owned, bias_in, (first_out, first_in, first_down)
    )
    while len(cotangent_parts) < tp_ways:
        cotangent_parts.append(onward(after(cotangent_parts[-1], slope), "tp"))

    back_args = (
        tp_ways, rank, factor, slope, group_tokens, blocks, owned, norm_params, (first_out, first_in, first_down), head_cols,
    )
    early = feed_back(cotangent_parts[:-1], 0, *back_args, ())
    late = feed_back(cotangent_parts[-1:], tp_ways - 1, *back_args, early[:4])
    seed_all, d_attended, d_hidden16, dz_part = late[:4]
    branch = lax.psum_scatter(
        after(partial_value, cotangent_parts[-1]), "tp", scatter_dimension=0, tiled=True
    )
    output = (
        valid_own[:, None]
        * (owned_input_rows + branch.astype(jnp.float32) + norm_params[4] + norm_params[5])
    ).astype(jnp.bfloat16)
    d_qkv16 = attend_back(qkv16, d_attended, segments, cosines, sines, heads_dev)
    dz16, first_sums, qkv_sums = qkv_back(d_qkv16, dz_part, group_tokens, blocks, owned, norm_params)

    dz_rows = lambda back: lax.dynamic_slice_in_dim(dz16, (tp_rank - back) % tp_ways * tok_dev, tok_dev, 0)
    moving = onward(dz_rows(1), "tp")

    parts = next(each for each in (4, 3, 2, 1) if owned % each == 0)
    part_size = owned // parts
    dp_rank = lax.axis_index("dp").astype(jnp.int32)
    halves = weight_grads(
        (first_normed, attended, second_normed, activated),
        (d_qkv16, seed_all, d_hidden16),
        (0, 1, 2, 1),
        (0, first_out, first_in, first_down),
        (dp_rank % 2)[None],
        owned,
        part_size,
        dp_ways,
        block_size,
    )
    results = None
    last = None
    back = 2

    def pass_on(moving, back):
        total = moving.astype(jnp.float32) + dz_rows(back).astype(jnp.float32)
        return total if back == tp_ways else onward(total.astype(jnp.bfloat16), "tp")

    moving = pass_on(after(moving, halves[0]), back)
    terms = []
    for part in range(parts):
        kept, away = halves[2 * part : 2 * part + 2]
        received = swap(away, 1)
        if dp_ways == 8:
            sums = pair_sum(kept, received, (dp_rank // 2)[None], dp_ways // 2)
            if last is not None:
                sums = [sums[0]] + [after(each, last) for each in sums[1:]]
            terms.append([sums[0]] + [swap(sums[bits], 2 * bits) for bits in range(1, 4)])
            last = terms[-1][3]
        else:
            total = (kept.astype(jnp.float32) + received.astype(jnp.float32)).astype(jnp.bfloat16)
            cores = [[each for each in range(dp_ways) if each % 2 == core] for core in range(2)]
            terms.append(
                [lax.psum_scatter(total, "dp", scatter_dimension=0, tiled=True, axis_index_groups=cores)]
            )
    for part in range(parts):
        results = shampoo(
            terms[part], left_stats, right_stats, master_blocks, part * part_size, results
        )
        while back < tp_ways and (back < part + 3 or part == parts - 1):
            back += 1
            moving, first_result = lax.optimization_barrier((moving, results[0]))
            results = [first_result] + list(results[1:])
            moving = pass_on(moving, back)
    norm_input_gradient = moving
    own_grads, left_new, right_new, new_blocks = results

    average_gradient = jnp.mean(norm_input_gradient, axis=-1, keepdims=True)
    average_projection = jnp.mean(
        norm_input_gradient * owned_centred_scaled, axis=-1, keepdims=True
    )
    input_grad = seed16.astype(jnp.float32) + owned_inverse_deviation * (
        norm_input_gradient - average_gradient - owned_centred_scaled * average_projection
    )

    shared_local = jnp.concatenate(
        [
            jnp.sum(first_sums.reshape(2, 8, model_width), axis=1),
            jnp.sum((early[4] + late[4]).reshape(2, 8, model_width), axis=1),
            out_bias_grad[None],
        ],
        0,
    )
    vecs_local = jnp.concatenate(
        [
            jnp.sum(qkv_sums, axis=0).reshape(3 * heads_dev, HD),
            jnp.sum(early[5] + late[5], axis=0).reshape(ff_dev // HD, HD),
        ],
        0,
    )
    small = jnp.concatenate(
        [
            shared_local.reshape(5, dp_ways, -1).transpose(1, 0, 2).reshape(dp_ways, -1),
            vecs_local.reshape(vec_rows, dp_ways, -1).transpose(1, 0, 2).reshape(dp_ways, -1),
        ],
        1,
    )
    small_own = lax.psum_scatter(
        small_rows(small, dp_ways), "dp", scatter_dimension=0, tiled=True
    ).reshape(-1)
    shared_size = 5 * model_width // dp_ways
    own_vec_grads = small_own[shared_size : small.shape[1]].reshape(vec_rows, HD // dp_ways)
    shared_part = small_own[:shared_size].reshape(5, tp_ways, -1).transpose(1, 0, 2)
    shared_own = lax.psum_scatter(
        small_rows(shared_part.reshape(tp_ways, -1), tp_ways), "tp", scatter_dimension=0, tiled=True
    ).reshape(-1)
    shared_own = shared_own[: shared_size // tp_ways].reshape(5, -1)
    shared_grads = jnp.concatenate([shared_own, shared_own[4:]], 0)
    local_stat_new = DECAY * local_vec_stats + own_vec_grads * own_vec_grads
    local_new = local_vecs - RATE_VEC * own_vec_grads * lax.rsqrt(local_stat_new)
    shared_stat_new = DECAY * shared_vec_stats + shared_grads * shared_grads
    shared_new = shared_vecs - RATE_VEC * shared_grads * lax.rsqrt(shared_stat_new)
    return (
        output,
        input_grad,
        own_grads,
        left_new,
        right_new,
        new_blocks,
        own_vec_grads,
        local_stat_new,
        local_new,
        shared_grads,
        shared_stat_new,
        shared_new,
    )


def solution(mesh):
    placed = (
        P(("dp", "tp"), None),
        P(("dp", "tp"), None),
        P("dp", None),
        P("dp", None),
        P("dp"),
        P(("dp", "tp"), None, None),
        P(("dp", "tp"), None, None),
        P(("dp", "tp"), None, None),
        P("tp", "dp"),
        P("tp", "dp"),
        P(None, ("dp", "tp")),
        P(None, ("dp", "tp")),
    )
    return jax.shard_map(
        shards,
        mesh=mesh,
        in_specs=placed,
        out_specs=(
            P(("dp", "tp"), None),
            P(("dp", "tp"), None),
            P(("dp", "tp"), None, None),
            P(("dp", "tp"), None, None),
            P(("dp", "tp"), None, None),
            P(("dp", "tp"), None, None),
            P("tp", "dp"),
            P("tp", "dp"),
            P("tp", "dp"),
            P(None, ("dp", "tp")),
            P(None, ("dp", "tp")),
            P(None, ("dp", "tp")),
        ),
        check_vma=False,
    )
```

time: 1470 us -> 786 us (0.53)
  matrix products: 358 us -> 0 us
  Pallas kernels: 154 us -> 483 us
  waiting for transfers between devices: 452 us -> 182 us
  local copies, waits for them, and re-layouts: 262 us -> 24.1 us
  blocking collectives: 104 us -> 0 us
  other arithmetic: 93.1 us -> 42.6 us
  starting transfers between devices: 0.28 us -> 31 us
  loops' own time: 20.6 us -> 0 us
    dot_general x40 -> x0, matrix products: 358 us -> none  [the longest x1 60.5 us: shards(): jnp.dot(second_normed_input, w_in, preferred_element_type=jnp.float32)]
    pallas_call x1 -> x16, Pallas kernels: 154 us -> 483 us  [the longest x4 172 us: shampoo(): pl.pallas_call(kernel, grid=(part // count,), in_specs=[own] * terms + [s...]
    reduce_scatter x4 -> x3, waiting for transfers between devices: 257 us -> 15 us  [the longest x1 14.9 us: shards(): lax.psum_scatter(small_rows(shared_part.reshape(tp_ways, -1), tp_ways), '...]
    all_gather x3 -> x1, waiting for transfers between devices: 194 us -> 0.01 us  [shards(): blocks = lax.all_gather(rows16, 'dp', axis=0, tiled=True)]
    ppermute x0 -> x28, waiting for transfers between devices: none -> 167 us  [the longest x9 167 us: onward(): lax.ppermute(part, axis, [(each, (each + 1) % ways) for each in range(way...]
    all_gather x2 -> x0, blocking collectives: 86.8 us -> none  [the longest x1 76.3 us: shards(): lax.all_gather(shared_vecs.astype(jnp.bfloat16), ('dp', 'tp'), axis=1, ti...]
    unnamed x125 -> x68, local copies, waits for them, and re-layouts: 84.6 us -> 7.47 us
    reshape x11 -> x8, local copies, waits for them, and re-layouts: 54.4 us -> 3.57 us  [the longest x2 1.25 us: small_rows(): jnp.pad(values, ((0, 0), (0, -values.shape[1] % 2048))).reshape(-1, 128)]
  transfers between devices with their start and end apart: 7 -> 32, of which waited for: 5 -> 6; matrix products, arithmetic and copies ran while one was open for 24% -> 7% of each run, Pallas kernels for 0% -> 62%
where the time goes in v2:
time: 786 us; the launch traced here: 777 us
  Pallas kernels  483 us (61%)
  waiting for transfers between devices  182 us (23%)
  other arithmetic  42.6 us (5%)
  starting transfers between devices  31 us (4%)
  local copies, waits for them, and re-layouts  24.1 us (3%)
  between operations  15.4 us (2%)
    pallas_call x4, Pallas kernels, shampoo(): pl.pallas_call(kernel, grid=(part // count,), in_specs=[own] * terms + [s...  172 us
    ppermute x9, waiting for transfers between devices, onward(): lax.ppermute(part, axis, [(each, (each + 1) % ways) for each in range(way...  167 us
    pallas_call x2, Pallas kernels, feed_back(): pl.pallas_call(functools.partial(feed_back_kernel, offsets, owned, count,...  78.5 us
    pallas_call x1, Pallas kernels, weight_grads(): pl.pallas_call(functools.partial(weight_grad_kernel, table, owned, part_s...  70 us
    pallas_call x1, Pallas kernels, feed_forward(): pl.pallas_call(functools.partial(feed_kernel, offsets, owned), grid=(toke...  57.2 us
    pallas_call x1, Pallas kernels, project_qkv(): pl.pallas_call(functools.partial(qkv_kernel, heads, owned, ways), grid_sp...  29.5 us
    pallas_call x1, Pallas kernels, qkv_back(): pl.pallas_call(functools.partial(qkv_back_kernel, owned), grid=(tokens //...  29 us
    pallas_call x4, Pallas kernels, pair_sum(): pl.pallas_call(pair_sum_kernel, grid_spec=pltpu.PrefetchScalarGridSpec(nu...  19.7 us
  transfers between devices with their start and end apart: 32, of which 6 were waited for; matrix products, arithmetic and copies ran while one was open for 7% of the time, Pallas kernels for 62%

profile of v2, /device:TPU:0, one launch (start us, length us, event | category | flops | bytes accessed | tf_op | source)
XLA Modules:
  0.0 777.5 jit_solution(14422751821805405493)
XLA Ops:
  7.9 4.0 collective-permute-start.4
  16.6 4.9 convert_element_type.124
  21.7 3.9 pad_maximum_fusion
  25.8 48.3 %collective-permute-done.refs_1_ = bf16[512,2048]{1,0:T(8,128)(2,1)S(1)} collective-permute-done((bf16[512,2048]{1,0:T(8,128)(2,1)S(1)}, bf16[512,2048]{1,0:T(8,128)(2,1)S(1)}, u32[]{:S(2)}, u32[]{:S(2)}) %collective-permute-start) | collective-permute-done | bytes 2097184 | tf_op jit(solution)/shard_map/ppermute | solution.py:808
  75.4 47.5 %collective-permute-done.1.refs_2_ = bf16[512,2048]{1,0:T(8,128)(2,1)} collective-permute-done((bf16[512,2048]{1,0:T(8,128)(2,1)S(1)}, bf16[512,2048]{1,0:T(8,128)(2,1)}, u32[]{:S(2)}, u32[]{:S(2)}) %collective-permute-start.1) | collective-permute-done | bytes 2097184 | tf_op jit(solution)/shard_map/ppermute | solution.py:808
  130.7 39.1 %collective-permute-done.2.refs_3_ = bf16[512,2048]{1,0:T(8,128)(2,1)} collective-permute-done((bf16[512,2048]{1,0:T(8,128)(2,1)}, bf16[512,2048]{1,0:T(8,128)(2,1)}, u32[]{:S(2)}, u32[]{:S(2)}) %collective-permute-start.2) | collective-permute-done | bytes 2097184 | tf_op jit(solution)/shard_map/ppermute | solution.py:808
  173.1 29.5 %qkv.1 = (bf16[2048,1536]{1,0:T(8,128)(2,1)}, bf16[2048,2048]{1,0:T(8,128)(2,1)}, bf16[2048,2048]{1,0:T(8,128)(2,1)}, bf16[2048,2048]{1,0:T(8,128)(2,1)}) custom-call(s32[1]{0:T(128)} %bitcast.1.rank_ref, bf16[512,2048]{1,0:T(8,128)(2,1)} %refs_0_.2, bf16[512,2048]{1,0:T(8,128)(2,1)} %copy-done.25, bf16[512,2048]{1,0:T(8,128)(2,1)} %collective-permute-done.1.refs_2_, ...), custom_call_target="tpu_custom_call" | custom-call | flops 12884901888 | bytes 46137344 | tf_op jit(solution)/shard_map/qkv/pallas_call | solution.py:174
  202.6 10.4 %attend.1.attended_ref.refs_1_ = bf16[2048,512]{1,0:T(8,128)(2,1)} custom-call(bf16[2048,1536]{1,0:T(8,128)(2,1)} %get-tuple-element.93.query_ref.key_ref.value_ref, bf16[2048,1536]{1,0:T(8,128)(2,1)} %get-tuple-element.93.query_ref.key_ref.value_ref, bf16[2048,1536]{1,0:T(8,128)(2,1)} %get-tuple-element.93.query_ref.key_ref.value_ref, ...), custom_call_target="tpu_custom_call" | custom-call | flops 3221225472 | bytes 8388608 | tf_op jit(solution)/shard_map/attend/pallas_call | solution.py:224
  215.6 57.2 %feed.1 = (bf16[2048,2048]{1,0:T(8,128)(2,1)}, bf16[2048,2048]{1,0:T(8,128)(2,1)}, bf16[2048,2048]{1,0:T(8,128)(2,1)}) custom-call(bf16[2048,2048]{1,0:T(8,128)(2,1)} %get-tuple-element.92.x_ref.refs_2_, bf16[2048,512]{1,0:T(8,128)(2,1)} %attend.1.attended_ref.refs_1_, bf16[49280,256]{1,0:T(8,128)(2,1)} %all-gather.2.cloned.1.call-done.refs_4_.blocks_ref.refs_6_, ...), custom_call_target="tpu_custom_call" | custom-call | flops 38654705664 | bytes 58720256 | tf_op jit(solution)/shard_map/feed/pallas_call | solution.py:356
  274.1 52.2 %feed_back.2 = (bf16[2048,2048]{1,0:T(8,128)(2,1)}, bf16[2048,512]{1,0:T(8,128)(2,1)}, bf16[2048,2048]{1,0:T(8,128)(2,1)}, f32[2048,2048]{1,0:T(8,128)}, f32[16,2048]{1,0:T(8,128)}, /*index=5*/f32[8,2048]{1,0:T(8,128)}) custom-call(s32[1]{0:T(128)} %bitcast.1.rank_ref, bf16[512,2048]{1,0:T(8,128)(2,1)} %refs_0_.3, ...), custom_call_target="tpu_custom_call" | custom-call | flops 28991029248 | bytes 60817408 | tf_op jit(solution)/shard_map/feed_back/pallas_call | solution.py:453
  328.0 26.3 %feed_back.3 = (bf16[2048,2048]{1,0:T(8,128)(2,1)}, bf16[2048,512]{1,0:T(8,128)(2,1)}, bf16[2048,2048]{1,0:T(8,128)(2,1)}, f32[2048,2048]{1,0:T(8,128)}, f32[16,2048]{1,0:T(8,128)}, /*index=5*/f32[8,2048]{1,0:T(8,128)}) custom-call(s32[1]{0:T(128)} %bitcast.1.rank_ref, ...), custom_call_target="tpu_custom_call", output_to_operand_aliasing={{0}: (7, {}), {1}: (8, {}), {2}: (9, {}), {3}: (10, {})} | custom-call | flops 9663676416 | bytes 31457280 | tf_op jit(solution)/shard_map/feed_back/pallas_call | solution.py:453
  354.3 16.9 %attend_back.1.d_qkv_ref.refs_4_ = bf16[2048,1536]{1,0:T(8,128)(2,1)} custom-call(bf16[2048,1536]{1,0:T(8,128)(2,1)} %get-tuple-element.93.query_ref.key_ref.value_ref, bf16[2048,1536]{1,0:T(8,128)(2,1)} %get-tuple-element.93.query_ref.key_ref.value_ref, bf16[2048,1536]{1,0:T(8,128)(2,1)} %get-tuple-element.93.query_ref.key_ref.value_ref, ...), custom_call_target="tpu_custom_call" | custom-call | flops 7516192768 | bytes 16777216 | tf_op jit(solution)/shard_map/attend_back/pallas_call | solution.py:285
  371.2 70.0 %weight_grads.1 = (bf16[24,256,256]{2,1,0:T(8,128)(2,1)}, bf16[24,256,256]{2,1,0:T(8,128)(2,1)}, bf16[24,256,256]{2,1,0:T(8,128)(2,1)}, bf16[24,256,256]{2,1,0:T...) custom-call(s32[1]{0:T(128)} %bitcast.12.core_ref, ...), custom_call_target="tpu_custom_call" | custom-call | flops 51539607552 | bytes 51539608 | tf_op jit(solution)/shard_map/weight_grads/pallas_call | solution.py:644
  442.3 29.0 %qkv_back.1 = (bf16[2048,2048]{1,0:T(8,128)(2,1)}, f32[16,2048]{1,0:T(8,128)}, f32[8,1536]{1,0:T(8,128)}) custom-call(bf16[2048,1536]{1,0:T(8,128)(2,1)} %attend_back.1.d_qkv_ref.refs_4_, f32[2048,2048]{1,0:T(8,128)} %get-tuple-element.106.part_ref, bf16[2048,2048]{1,0:T(8,128)(2,1)} %get-tuple-element.100.refs_5_.refs_3_.tokens_ref, ...), custom_call_target="tpu_custom_call" | custom-call | flops 12884901888 | bytes 46137344 | tf_op jit(solution)/shard_map/qkv_back/pallas_call | solution.py:523
  471.3 3.2 constant_dynamic-slice_fusion
  474.5 2.5 collective-permute-start.9
  487.7 5.0 pair_sum.4
  495.2 29.3 %collective-permute-done.9 = bf16[512,2048]{1,0:T(8,128)(2,1)} collective-permute-done((bf16[512,2048]{1,0:T(8,128)(2,1)}, bf16[512,2048]{1,0:T(8,128)(2,1)}, u32[]{:S(2)}, u32[]{:S(2)}) %collective-permute-start.9) | collective-permute-done | bytes 2097184 | tf_op jit(solution)/shard_map/ppermute | solution.py:808
  527.8 4.4 add_convert_fusion.1
  532.2 4.8 pair_sum.5
  537.5 5.0 pair_sum.6
  544.1 4.9 pair_sum.7
  552.5 43.1 %shampoo.4 = (f32[24,256,256]{2,1,0:T(8,128)}, f32[24,256,256]{2,1,0:T(8,128)}, f32[24,256,256]{2,1,0:T(8,128)}, f32[24,256,256]{2,1,0:T(8,128)}) custom-call(f32[6,256,256]{2,1,0:T(8,128)} %get-tuple-element.115.refs_0_, bf16[6,256,256]{2,1,0:T(8,128)(2,1)} %collective-permute-done.12.refs_1_, bf16[6,256,256]{2,1,0:T(8,128)(2,1)} %collective-permute-done.13.refs_2_, ...), custom_call_target="tpu_custom_call" | custom-call | flops 36238786560 | bytes 11796480 | tf_op jit(solution)/shard_map/shampoo/pallas_call | solution.py:786
  595.5 4.4 add_convert_fusion
  600.0 2.5 collective-permute-start.15
  606.9 42.9 %shampoo.5 = (f32[24,256,256]{2,1,0:T(8,128)}, f32[24,256,256]{2,1,0:T(8,128)}, f32[24,256,256]{2,1,0:T(8,128)}, f32[24,256,256]{2,1,0:T(8,128)}) custom-call(f32[6,256,256]{2,1,0:T(8,128)} %get-tuple-element.123.refs_0_, bf16[6,256,256]{2,1,0:T(8,128)(2,1)} %copy-done.30, ...), custom_call_target="tpu_custom_call", output_to_operand_aliasing={{0}: (7, {}), {1}: (8, {}), {2}: (9, {}), {3}: (10, {})} | custom-call | flops 36238786560 | bytes 11796480 | tf_op jit(solution)/shard_map/shampoo/pallas_call | solution.py:786
  650.9 2.4 collective-permute-start.25
  653.3 3.6 fusion.12
  657.0 42.8 %shampoo.6 = (f32[24,256,256]{2,1,0:T(8,128)}, f32[24,256,256]{2,1,0:T(8,128)}, f32[24,256,256]{2,1,0:T(8,128)}, f32[24,256,256]{2,1,0:T(8,128)}) custom-call(f32[6,256,256]{2,1,0:T(8,128)} %get-tuple-element.149.refs_0_, ...), custom_call_target="tpu_custom_call", output_to_operand_aliasing={{0}: (7, {}), {1}: (8, {}), {2}: (9, {}), {3}: (10, {})} | custom-call | flops 36238786560 | bytes 11796480 | tf_op jit(solution)/shard_map/shampoo/pallas_call | solution.py:786
  699.9 7.2 convert_reduce_fusion.1
  707.9 42.8 %shampoo.7 = (f32[24,256,256]{2,1,0:T(8,128)}, f32[24,256,256]{2,1,0:T(8,128)}, f32[24,256,256]{2,1,0:T(8,128)}, f32[24,256,256]{2,1,0:T(8,128)}) custom-call(f32[6,256,256]{2,1,0:T(8,128)} %get-tuple-element.138.refs_0_, ...), custom_call_target="tpu_custom_call", output_to_operand_aliasing={{0}: (7, {}), {1}: (8, {}), {2}: (9, {}), {3}: (10, {})} | custom-call | flops 36238786560 | bytes 11796480 | tf_op jit(solution)/shard_map/shampoo/pallas_call | solution.py:786
  753.7 14.9 %reduce-scatter.8.cloned.1.call-done = f32[16,128]{1,0:T(8,128)} async-done(((f32[64,128]{1,0:T(8,128)}), f32[16,128]{1,0:T(8,128)}) %reduce-scatter.8.cloned.1.call-update) | async-done | bytes 8208 | tf_op jit(solution)/shard_map/reduce_scatter | solution.py:1023
  (201 shorter events, 57.2 us)
Async XLA Ops:
  7.2 162.6 %all-gather.2.cloned.1.call-start = ((), (), s32[]{:S(2)}) async-start(), calls=%async_computation.3 | async-start | bytes 28385280 | tf_op jit(solution)/shard_map/all_gather | solution.py:868
  7.9 13.5 %collective-permute-start.4 = (bf16[6,64]{1,0:T(8,128)(2,1)S(1)}, bf16[6,64]{1,0:T(8,128)(2,1)S(1)}, u32[]{:S(2)}, u32[]{:S(2)}) collective-permute-start(bf16[6,64]{1,0:T(8,128)(2,1)S(1)} %get-tuple-element.183), channel_id=1, source_target_pairs={{0,2},{1,3},{2,0},{3,1},{4,6},{5,7},{6,4},{7,5},{8,10},{9,11},{10,... | collective-permute-start | bytes 2312 | tf_op jit(solution)/shard_map/ppermute | solution.py:856
  12.0 9.5 %collective-permute-start.3 = (bf16[6,64]{1,0:T(8,128)(2,1)S(1)}, bf16[6,64]{1,0:T(8,128)(2,1)S(1)}, u32[]{:S(2)}, u32[]{:S(2)}) collective-permute-start(bf16[6,64]{1,0:T(8,128)(2,1)S(1)} %get-tuple-element.183), channel_id=1, source_target_pairs={{0,1},{1,2},{2,3},{3,0},{4,5},{5,6},{6,7},{7,4},{8,9},{9,10},{10,1... | collective-permute-start | bytes 2312 | tf_op jit(solution)/shard_map/ppermute | solution.py:856
  13.6 7.9 %collective-permute-start.5 = (bf16[6,64]{1,0:T(8,128)(2,1)S(1)}, bf16[6,64]{1,0:T(8,128)(2,1)S(1)}, u32[]{:S(2)}, u32[]{:S(2)}) collective-permute-start(bf16[6,64]{1,0:T(8,128)(2,1)S(1)} %get-tuple-element.183), channel_id=1, source_target_pairs={{0,3},{1,0},{2,1},{3,2},{4,7},{5,4},{6,5},{7,6},{8,11},{9,8},{10,9... | collective-permute-start | bytes 2312 | tf_op jit(solution)/shard_map/ppermute | solution.py:856
  25.7 674.2 %reduce-scatter.4.cloned.1.call-start = ((), (), s32[]{:S(2)}) async-start(), calls=%async_computation.4 | async-start | bytes 10485760 | tf_op jit(solution)/shard_map/reduce_scatter | solution.py:923
  25.7 48.4 %collective-permute-start = (bf16[512,2048]{1,0:T(8,128)(2,1)S(1)}, bf16[512,2048]{1,0:T(8,128)(2,1)S(1)}, u32[]{:S(2)}, u32[]{:S(2)}) collective-permute-start(bf16[512,2048]{1,0:T(8,128)(2,1)S(1)} %copy-done.1), channel_id=1, source_target_pairs={{0,1},{1,2},{2,3},{3,0},{4,5},{5,6},{6,7},{7,4},{8,9},{9,10},{10,1... | collective-permute-start | bytes 6291464 | tf_op jit(solution)/shard_map/ppermute | solution.py:808
  75.4 47.5 %collective-permute-start.1 = (bf16[512,2048]{1,0:T(8,128)(2,1)S(1)}, bf16[512,2048]{1,0:T(8,128)(2,1)}, u32[]{:S(2)}, u32[]{:S(2)}) collective-permute-start(bf16[512,2048]{1,0:T(8,128)(2,1)S(1)} %collective-permute-done.refs_1_), channel_id=1, source_target_pairs={{0,1},{1,2},{2,3},{3,0},{4,5},{5,6},{6,7},{7,4},{8,9},{9,10},{10,1... | collective-permute-start | bytes 6291464 | tf_op jit(solution)/shard_map/ppermute | solution.py:808
  122.9 46.8 %collective-permute-start.2 = (bf16[512,2048]{1,0:T(8,128)(2,1)}, bf16[512,2048]{1,0:T(8,128)(2,1)}, u32[]{:S(2)}, u32[]{:S(2)}) collective-permute-start(bf16[512,2048]{1,0:T(8,128)(2,1)} %collective-permute-done.1.refs_2_), channel_id=1, source_target_pairs={{0,1},{1,2},{2,3},{3,0},{4,5},{5,6},{6,7},{7,4},{8,9},{9,10},{10,1... | collective-permute-start | bytes 6291464 | tf_op jit(solution)/shard_map/ppermute | solution.py:808
  169.7 45.7 %collective-permute-start.6 = (bf16[512,2048]{1,0:T(8,128)(2,1)S(1)}, bf16[512,2048]{1,0:T(8,128)(2,1)}, u32[]{:S(2)}, u32[]{:S(2)}) collective-permute-start(bf16[512,2048]{1,0:T(8,128)(2,1)S(1)} %copy-done.4), channel_id=1, source_target_pairs={{0,1},{1,2},{2,3},{3,0},{4,5},{5,6},{6,7},{7,4},{8,9},{9,10},{10,1... | collective-permute-start | bytes 6291464 | tf_op jit(solution)/shard_map/ppermute | solution.py:808
  215.4 57.4 %collective-permute-start.7 = (bf16[512,2048]{1,0:T(8,128)(2,1)}, bf16[512,2048]{1,0:T(8,128)(2,1)S(1)}, u32[]{:S(2)}, u32[]{:S(2)}) collective-permute-start(bf16[512,2048]{1,0:T(8,128)(2,1)} %collective-permute-done.6.refs_1_), channel_id=1, source_target_pairs={{0,1},{1,2},{2,3},{3,0},{4,5},{5,6},{6,7},{7,4},{8,9},{9,10},{10,1... | collective-permute-start | bytes 6291464 | tf_op jit(solution)/shard_map/ppermute | solution.py:808
  274.1 52.2 %collective-permute-start.8 = (bf16[512,2048]{1,0:T(8,128)(2,1)}, bf16[512,2048]{1,0:T(8,128)(2,1)S(1)}, u32[]{:S(2)}, u32[]{:S(2)}) collective-permute-start(bf16[512,2048]{1,0:T(8,128)(2,1)} %copy-done.26), channel_id=1, source_target_pairs={{0,1},{1,2},{2,3},{3,0},{4,5},{5,6},{6,7},{7,4},{8,9},{9,10},{10,1... | collective-permute-start | bytes 6291464 | tf_op jit(solution)/shard_map/ppermute | solution.py:808
  327.6 423.1 %reduce-scatter.6.cloned.1.call-start = ((), (), s32[]{:S(2)}) async-start(), calls=%async_computation.5 | async-start | bytes 73728 | tf_op jit(solution)/shard_map/reduce_scatter | solution.py:1017
  441.2 46.4 %collective-permute-start.11 = (bf16[24,256,256]{2,1,0:T(8,128)(2,1)}, bf16[24,256,256]{2,1,0:T(8,128)(2,1)}, u32[]{:S(2)}, u32[]{:S(2)}) collective-permute-start(bf16[24,256,256]{2,1,0:T(8,128)(2,1)} %get-tuple-element.114), channel_id=1, source_target_pairs={{0,4},{4,0},{8,12},{12,8},{16,20},{20,16},{24,28},{28,24},{1,5},{5... | collective-permute-start | bytes 9437192 | tf_op jit(solution)/shard_map/ppermute | solution.py:813
  441.3 84.7 %collective-permute-start.16 = (bf16[24,256,256]{2,1,0:T(8,128)(2,1)}, bf16[24,256,256]{2,1,0:T(8,128)(2,1)}, u32[]{:S(2)}, u32[]{:S(2)}) collective-permute-start(bf16[24,256,256]{2,1,0:T(8,128)(2,1)} %get-tuple-element.122), channel_id=1, source_target_pairs={{0,4},{4,0},{8,12},{12,8},{16,20},{20,16},{24,28},{28,24},{1,5},{5... | collective-permute-start | bytes 9437192 | tf_op jit(solution)/shard_map/ppermute | solution.py:813
  441.8 95.3 %collective-permute-start.20 = (bf16[24,256,256]{2,1,0:T(8,128)(2,1)}, bf16[24,256,256]{2,1,0:T(8,128)(2,1)}, u32[]{:S(2)}, u32[]{:S(2)}) collective-permute-start(bf16[24,256,256]{2,1,0:T(8,128)(2,1)} %get-tuple-element.137), channel_id=1, source_target_pairs={{0,4},{4,0},{8,12},{12,8},{16,20},{20,16},{24,28},{28,24},{1,5},{5... | collective-permute-start | bytes 9437192 | tf_op jit(solution)/shard_map/ppermute | solution.py:813
  441.9 100.6 %collective-permute-start.21 = (bf16[24,256,256]{2,1,0:T(8,128)(2,1)}, bf16[24,256,256]{2,1,0:T(8,128)(2,1)S(1)}, u32[]{:S(2)}, u32[]{:S(2)}) collective-permute-start(bf16[24,256,256]{2,1,0:T(8,128)(2,1)} %get-tuple-element.141), channel_id=1, source_target_pairs={{0,4},{4,0},{8,12},{12,8},{16,20},{20,16},{24,28},{28,24},{1,5},{5... | collective-permute-start | bytes 9437192 | tf_op jit(solution)/shard_map/ppermute | solution.py:813
  474.5 50.0 %collective-permute-start.9 = (bf16[512,2048]{1,0:T(8,128)(2,1)}, bf16[512,2048]{1,0:T(8,128)(2,1)}, u32[]{:S(2)}, u32[]{:S(2)}) collective-permute-start(bf16[512,2048]{1,0:T(8,128)(2,1)} %constant_dynamic-slice_fusion), channel_id=1, source_target_pairs={{0,1},{1,2},{2,3},{3,0},{4,5},{5,6},{6,7},{7,4},{8,9},{9,10},{10,1... | collective-permute-start | bytes 6291464 | tf_op jit(solution)/shard_map/ppermute | solution.py:808
  492.7 56.3 %collective-permute-start.14 = (bf16[6,256,256]{2,1,0:T(8,128)(2,1)}, bf16[6,256,256]{2,1,0:T(8,128)(2,1)}, u32[]{:S(2)}, u32[]{:S(2)}) collective-permute-start(bf16[6,256,256]{2,1,0:T(8,128)(2,1)} %get-tuple-element.118), channel_id=1, source_target_pairs={{0,24},{4,28},{8,16},{12,20},{16,8},{20,12},{24,0},{28,4},{1,25},{... | collective-permute-start | bytes 2359304 | tf_op jit(solution)/shard_map/ppermute | solution.py:813
  524.5 26.5 %collective-permute-start.12 = (bf16[6,256,256]{2,1,0:T(8,128)(2,1)}, bf16[6,256,256]{2,1,0:T(8,128)(2,1)}, u32[]{:S(2)}, u32[]{:S(2)}) collective-permute-start(bf16[6,256,256]{2,1,0:T(8,128)(2,1)} %get-tuple-element.116), channel_id=1, source_target_pairs={{0,8},{4,12},{8,0},{12,4},{16,24},{20,28},{24,16},{28,20},{1,9},{5... | collective-permute-start | bytes 2359304 | tf_op jit(solution)/shard_map/ppermute | solution.py:813
  526.0 26.4 %collective-permute-start.13 = (bf16[6,256,256]{2,1,0:T(8,128)(2,1)}, bf16[6,256,256]{2,1,0:T(8,128)(2,1)}, u32[]{:S(2)}, u32[]{:S(2)}) collective-permute-start(bf16[6,256,256]{2,1,0:T(8,128)(2,1)} %get-tuple-element.117), channel_id=1, source_target_pairs={{0,16},{4,20},{8,24},{12,28},{16,0},{20,4},{24,8},{28,12},{1,17},{... | collective-permute-start | bytes 2359304 | tf_op jit(solution)/shard_map/ppermute | solution.py:813
  537.1 58.5 %collective-permute-start.10 = (bf16[512,2048]{1,0:T(8,128)(2,1)}, bf16[512,2048]{1,0:T(8,128)(2,1)}, u32[]{:S(2)}, u32[]{:S(2)}) collective-permute-start(bf16[512,2048]{1,0:T(8,128)(2,1)} %add_convert_fusion.1), channel_id=1, source_target_pairs={{0,1},{1,2},{2,3},{3,0},{4,5},{5,6},{6,7},{7,4},{8,9},{9,10},{10,1... | collective-permute-start | bytes 6291464 | tf_op jit(solution)/shard_map/ppermute | solution.py:808
  549.0 53.5 %collective-permute-start.19 = (bf16[6,256,256]{2,1,0:T(8,128)(2,1)}, bf16[6,256,256]{2,1,0:T(8,128)(2,1)S(1)}, u32[]{:S(2)}, u32[]{:S(2)}) collective-permute-start(bf16[6,256,256]{2,1,0:T(8,128)(2,1)} %get-tuple-element.129), channel_id=1, source_target_pairs={{0,24},{4,28},{8,16},{12,20},{16,8},{20,12},{24,0},{28,4},{1,25},{... | collective-permute-start | bytes 2359304 | tf_op jit(solution)/shard_map/ppermute | solution.py:813
  549.5 54.1 %collective-permute-start.18 = (bf16[6,256,256]{2,1,0:T(8,128)(2,1)}, bf16[6,256,256]{2,1,0:T(8,128)(2,1)S(1)}, u32[]{:S(2)}, u32[]{:S(2)}) collective-permute-start(bf16[6,256,256]{2,1,0:T(8,128)(2,1)} %get-tuple-element.127), channel_id=1, source_target_pairs={{0,16},{4,20},{8,24},{12,28},{16,0},{20,4},{24,8},{28,12},{1,17},{... | collective-permute-start | bytes 2359304 | tf_op jit(solution)/shard_map/ppermute | solution.py:813
  551.0 55.0 %collective-permute-start.17 = (bf16[6,256,256]{2,1,0:T(8,128)(2,1)}, bf16[6,256,256]{2,1,0:T(8,128)(2,1)S(1)}, u32[]{:S(2)}, u32[]{:S(2)}) collective-permute-start(bf16[6,256,256]{2,1,0:T(8,128)(2,1)} %get-tuple-element.125), channel_id=1, source_target_pairs={{0,8},{4,12},{8,0},{12,4},{16,24},{20,28},{24,16},{28,20},{1,9},{5... | collective-permute-start | bytes 2359304 | tf_op jit(solution)/shard_map/ppermute | solution.py:813
  600.0 50.9 %collective-permute-start.15 = (bf16[512,2048]{1,0:T(8,128)(2,1)}, bf16[512,2048]{1,0:T(8,128)(2,1)}, u32[]{:S(2)}, u32[]{:S(2)}) collective-permute-start(bf16[512,2048]{1,0:T(8,128)(2,1)} %add_convert_fusion), channel_id=1, source_target_pairs={{0,1},{1,2},{2,3},{3,0},{4,5},{5,6},{6,7},{7,4},{8,9},{9,10},{10,1... | collective-permute-start | bytes 6291464 | tf_op jit(solution)/shard_map/ppermute | solution.py:808
  602.5 54.5 %collective-permute-start.27 = (bf16[6,256,256]{2,1,0:T(8,128)(2,1)}, bf16[6,256,256]{2,1,0:T(8,128)(2,1)}, u32[]{:S(2)}, u32[]{:S(2)}) collective-permute-start(bf16[6,256,256]{2,1,0:T(8,128)(2,1)} %get-tuple-element.153), channel_id=1, source_target_pairs={{0,16},{4,20},{8,24},{12,28},{16,0},{20,4},{24,8},{28,12},{1,17},{... | collective-permute-start | bytes 2359304 | tf_op jit(solution)/shard_map/ppermute | solution.py:813
  603.0 54.0 %collective-permute-start.26 = (bf16[6,256,256]{2,1,0:T(8,128)(2,1)}, bf16[6,256,256]{2,1,0:T(8,128)(2,1)}, u32[]{:S(2)}, u32[]{:S(2)}) collective-permute-start(bf16[6,256,256]{2,1,0:T(8,128)(2,1)} %get-tuple-element.151), channel_id=1, source_target_pairs={{0,8},{4,12},{8,0},{12,4},{16,24},{20,28},{24,16},{28,20},{1,9},{5... | collective-permute-start | bytes 2359304 | tf_op jit(solution)/shard_map/ppermute | solution.py:813
  603.5 46.2 %collective-permute-start.22 = (bf16[6,256,256]{2,1,0:T(8,128)(2,1)}, bf16[6,256,256]{2,1,0:T(8,128)(2,1)}, u32[]{:S(2)}, u32[]{:S(2)}) collective-permute-start(bf16[6,256,256]{2,1,0:T(8,128)(2,1)} %get-tuple-element.143), channel_id=1, source_target_pairs={{0,24},{4,28},{8,16},{12,20},{16,8},{20,12},{24,0},{28,4},{1,25},{... | collective-permute-start | bytes 2359304 | tf_op jit(solution)/shard_map/ppermute | solution.py:813
  649.8 58.1 %collective-permute-start.23 = (bf16[6,256,256]{2,1,0:T(8,128)(2,1)}, bf16[6,256,256]{2,1,0:T(8,128)(2,1)}, u32[]{:S(2)}, u32[]{:S(2)}) collective-permute-start(bf16[6,256,256]{2,1,0:T(8,128)(2,1)} %get-tuple-element.144), channel_id=1, source_target_pairs={{0,8},{4,12},{8,0},{12,4},{16,24},{20,28},{24,16},{28,20},{1,9},{5... | collective-permute-start | bytes 2359304 | tf_op jit(solution)/shard_map/ppermute | solution.py:813
  650.4 57.5 %collective-permute-start.24 = (bf16[6,256,256]{2,1,0:T(8,128)(2,1)}, bf16[6,256,256]{2,1,0:T(8,128)(2,1)}, u32[]{:S(2)}, u32[]{:S(2)}) collective-permute-start(bf16[6,256,256]{2,1,0:T(8,128)(2,1)} %get-tuple-element.146), channel_id=1, source_target_pairs={{0,16},{4,20},{8,24},{12,28},{16,0},{20,4},{24,8},{28,12},{1,17},{... | collective-permute-start | bytes 2359304 | tf_op jit(solution)/shard_map/ppermute | solution.py:813
  650.9 57.0 %collective-permute-start.25 = (bf16[6,256,256]{2,1,0:T(8,128)(2,1)S(1)}, bf16[6,256,256]{2,1,0:T(8,128)(2,1)}, u32[]{:S(2)}, u32[]{:S(2)}) collective-permute-start(bf16[6,256,256]{2,1,0:T(8,128)(2,1)S(1)} %copy-done.27), channel_id=1, source_target_pairs={{0,24},{4,28},{8,16},{12,20},{16,8},{20,12},{24,0},{28,4},{1,25},{... | collective-permute-start | bytes 2359304 | tf_op jit(solution)/shard_map/ppermute | solution.py:813
  707.8 60.8 %reduce-scatter.8.cloned.1.call-start = ((), (), s32[]{:S(2)}) async-start(), calls=%async_computation.6 | async-start | bytes 40960 | tf_op jit(solution)/shard_map/reduce_scatter | solution.py:1023
  (32 other events, 1050.6 us)
Sparse Core Ops, SparseCore 0:
  25.8 123.8 all-gather.1
  326.5 146.4 reduce-scatter.3
  707.9 30.5 reduce-scatter.5
  752.4 16.1 reduce-scatter.7

commit v3 on v2

--- a/solution.py
+++ b/solution.py
@@ -34,7 +34,19 @@
     return (centred * inv_std, inv_std)
 
 
+def to_blocks(matrix, block_size):
+    block_rows = matrix.shape[0] // block_size
+    block_cols = matrix.shape[1] // block_size
+    return (
+        matrix.reshape(block_rows, block_size, block_cols, block_size)
+        .transpose(0, 2, 1, 3)
+        .reshape(block_rows * block_cols, block_size, block_size)
+    )
+
+
 EXTRA_ROWS = 16
+COST_PART = 16
+FEED_BACK_TILE = 512
 VMEM_LIMIT = 60 << 20
 NN = (((1,), (0,)), ((), ()))
 NT = (((1,), (1,)), ((), ()))
@@ -47,6 +59,12 @@
 
 def kernel_params():
     return pltpu.CompilerParams(vmem_limit_bytes=VMEM_LIMIT)
+
+
+def kernel_cost(flops, bytes_accessed, transcendentals):
+    return pl.CostEstimate(
+        flops=flops // COST_PART, bytes_accessed=bytes_accessed // COST_PART, transcendentals=transcendentals
+    )
 
 
 def block_row(index, owned, size):
@@ -130,7 +148,8 @@
 def qkv_kernel(heads, owned, parts, rank_ref, *refs):
     part_refs = refs[:parts]
     blocks_ref, norm_ref, bias_ref, cos_ref, sin_ref = refs[parts : parts + 5]
-    qkv_ref, first_ref, second_ref, tokens_ref, weight, held, sems, part_sems = refs[parts + 5 :]
+    outs, (normed, weight, held, sems, part_sems) = refs[parts + 5 : parts + 12], refs[parts + 12 :]
+    qkv_ref, first_turned, second_ref, second_turned, tokens_ref, mean_ref, inverse_ref = outs
     size = blocks_ref.shape[-1]
     copies = block_copies(blocks_ref, owned, 0, weight.shape[0] // size, weight.shape[1] // size, weight, sems)
     moves = part_copies(part_refs, held, part_sems)
@@ -140,16 +159,23 @@
     tokens_ref[...] = own
     rows = own.astype(jnp.float32)
     mean, inverse = normed_rows(rows)
-    scaled = (rows - mean) * inverse
-    second_ref[...] = (scaled * norm_ref[2:3, :] + norm_ref[3:4, :]).astype(jnp.bfloat16)
-    values = (scaled * norm_ref[0:1, :] + norm_ref[1:2, :]).astype(jnp.bfloat16)
-    first_ref[...] = values
+    mean_ref[...] = mean
+    inverse_ref[...] = inverse
+    for col in range(rows.shape[1] // size):
+        cols = pl.ds(col * size, size)
+        scaled = (own[:, col * size : (col + 1) * size].astype(jnp.float32) - mean) * inverse
+        second = (scaled * norm_ref[2:3, cols] + norm_ref[3:4, cols]).astype(jnp.bfloat16)
+        second_ref[:, cols] = second
+        second_turned[cols, :] = second.T
+        first = (scaled * norm_ref[0:1, cols] + norm_ref[1:2, cols]).astype(jnp.bfloat16)
+        normed[:, cols] = first
+        first_turned[cols, :] = first.T
     end_copies(copies)
     lanes = cos_ref.shape[1]
     for head in range(heads):
         for part in range(3):
             cols = pl.ds((head * 3 + part) * HD, HD)
-            result = contract(first_ref[...], weight[:, cols], NN) + bias_ref[:, cols]
+            result = contract(normed[...], weight[:, cols], NN) + bias_ref[:, cols]
             if part < 2:
                 first = turn(result[:, :lanes], cos_ref[...], sin_ref[...])
                 result = jnp.concatenate([first, result[:, lanes:]], 1)
@@ -171,6 +197,9 @@
     table = pl.BlockSpec((tile, lanes), lambda i, rank: (place(i, rank) % per_pack, 0))
     anywhere = pl.BlockSpec(memory_space=pl.ANY)
     wide = jax.ShapeDtypeStruct((tokens, width), jnp.bfloat16)
+    tall = jax.ShapeDtypeStruct((width, tokens), jnp.bfloat16)
+    single = jax.ShapeDtypeStruct((tokens, 1), jnp.float32)
+    turned = pl.BlockSpec((width, tile), lambda i, rank: (0, place(i, rank)))
     return pl.pallas_call(
         functools.partial(qkv_kernel, heads, owned, ways),
         grid_spec=pltpu.PrefetchScalarGridSpec(
@@ -183,24 +212,25 @@
                 table,
                 table,
             ],
-            out_specs=[row(cols), row(width), row(width), row(width)],
+            out_specs=[row(cols), turned, row(width), turned, row(width), row(1), row(1)],
             scratch_shapes=[
+                pltpu.VMEM((tile, width), jnp.bfloat16),
                 pltpu.VMEM((width, cols), jnp.bfloat16),
                 pltpu.VMEM((ways, tile, width), jnp.bfloat16),
                 pltpu.SemaphoreType.DMA((width // size * (cols // size),)),
                 pltpu.SemaphoreType.DMA((ways,)),
             ],
         ),
-        out_shape=[jax.ShapeDtypeStruct((tokens, cols), jnp.bfloat16), wide, wide, wide],
+        out_shape=[jax.ShapeDtypeStruct((tokens, cols), jnp.bfloat16), tall, wide, tall, wide, single, single],
         compiler_params=kernel_params(),
-        cost_estimate=pl.CostEstimate(
+        cost_estimate=kernel_cost(
             flops=2 * tokens * width * cols, bytes_accessed=tokens * (4 * width + cols) * 2 + width * cols * 2, transcendentals=0
         ),
         name="qkv",
     )(rank, *parts, blocks, norm_params, bias, cosines, sines)
 
 
-def attend_kernel(query_ref, key_ref, value_ref, seg_row, seg_col, out_ref):
+def attend_kernel(query_ref, key_ref, value_ref, seg_row, seg_col, out_ref, turned_ref):
     length = key_ref.shape[0]
     step = 256
     for start in range(0, length, step):
@@ -213,9 +243,9 @@
         masked = jnp.where(allowed, scores, NEG_FILL)
         exp_terms = jnp.exp(masked - jnp.max(masked, axis=1, keepdims=True))
         probs = exp_terms * (1.0 / jnp.sum(exp_terms, axis=1, keepdims=True))
-        out_ref[start:stop, :] = contract(
-            probs.astype(jnp.bfloat16), value_ref[first:stop, :], NN
-        ).astype(jnp.bfloat16)
+        result = contract(probs.astype(jnp.bfloat16), value_ref[first:stop, :], NN).astype(jnp.bfloat16)
+        out_ref[start:stop, :] = result
+        turned_ref[:, start:stop] = result.T
 
 
 def attend(qkv, segments, heads):
@@ -231,10 +261,16 @@
             pl.BlockSpec((1, 1, length), lambda p, h: (p, 0, 0)),
             pl.BlockSpec((1, length, 1), lambda p, h: (p, 0, 0)),
         ],
-        out_specs=pl.BlockSpec((length, HD), lambda p, h: (p, h)),
-        out_shape=jax.ShapeDtypeStruct((packs * length, heads * HD), jnp.bfloat16),
+        out_specs=[
+            pl.BlockSpec((length, HD), lambda p, h: (p, h)),
+            pl.BlockSpec((HD, length), lambda p, h: (h, p)),
+        ],
+        out_shape=[
+            jax.ShapeDtypeStruct((packs * length, heads * HD), jnp.bfloat16),
+            jax.ShapeDtypeStruct((heads * HD, packs * length), jnp.bfloat16),
+        ],
         compiler_params=kernel_params(),
-        cost_estimate=pl.CostEstimate(
+        cost_estimate=kernel_cost(
             flops=packs * heads * length * length * HD * 3, bytes_accessed=packs * length * heads * HD * 8, transcendentals=0
         ),
         name="attend",
@@ -299,7 +335,7 @@
         out_shape=jax.ShapeDtypeStruct((packs * length, 3 * heads * HD), jnp.bfloat16),
         scratch_shapes=[pltpu.VMEM((length, HD), jnp.float32)] * 2,
         compiler_params=kernel_params(),
-        cost_estimate=pl.CostEstimate(
+        cost_estimate=kernel_cost(
             flops=packs * heads * length * length * HD * 7, bytes_accessed=packs * length * heads * HD * 16, transcendentals=0
         ),
         name="attend_back",
@@ -307,7 +343,7 @@
 
 
 def feed_kernel(
-    offsets, owned, x_ref, attended_ref, blocks_ref, bias_ref, act_ref, slope_ref, out_ref, w_in, w_down, sems_in, sems_down
+    offsets, owned, x_ref, attended_ref, blocks_ref, bias_ref, turned_ref, slope_ref, out_ref, act_ref, w_in, w_down, sems_in, sems_down
 ):
     size = blocks_ref.shape[-1]
     width, hidden_units = w_in.shape
@@ -334,7 +370,9 @@
         hidden = contract(values, w_in[:, cols], NN) + bias_ref[:, cols]
         cdf = 0.5 + 0.5 * lax.erf(hidden * HALF_ROOT)
         density = jnp.exp(-0.5 * hidden * hidden) * DENSITY_SCALE
-        act_ref[:, cols] = (hidden * cdf).astype(jnp.bfloat16)
+        activated = (hidden * cdf).astype(jnp.bfloat16)
+        act_ref[:, cols] = activated
+        turned_ref[cols, :] = activated.T
         slope_ref[:, cols] = (cdf + hidden * density).astype(jnp.bfloat16)
     end_copies(copies_down)
     for col in range(outer):
@@ -362,20 +400,23 @@
             pl.BlockSpec(memory_space=pl.ANY),
             pl.BlockSpec((1, hidden_units), lambda i: (0, 0)),
         ],
-        out_specs=[row(hidden_units), row(hidden_units), row(width)],
+        out_specs=[
+            pl.BlockSpec((hidden_units, tile), lambda i: (0, i)), row(hidden_units), row(width),
+        ],
         out_shape=[
-            jax.ShapeDtypeStruct((tokens, hidden_units), jnp.bfloat16),
+            jax.ShapeDtypeStruct((hidden_units, tokens), jnp.bfloat16),
             jax.ShapeDtypeStruct((tokens, hidden_units), jnp.bfloat16),
             jax.ShapeDtypeStruct((tokens, width), jnp.bfloat16),
         ],
         scratch_shapes=[
+            pltpu.VMEM((tile, hidden_units), jnp.bfloat16),
             pltpu.VMEM((width, hidden_units), jnp.bfloat16),
             pltpu.VMEM((hidden_units + head_cols, width), jnp.bfloat16),
             pltpu.SemaphoreType.DMA((inner * outer,)),
             pltpu.SemaphoreType.DMA((inner * outer + head_cols // size * outer,)),
         ],
         compiler_params=kernel_params(),
-        cost_estimate=pl.CostEstimate(
+        cost_estimate=kernel_cost(
             flops=2 * tokens * width * (2 * hidden_units + head_cols), bytes_accessed=tokens * width * 10 + width * hidden_units * 4, transcendentals=0
         ),
         name="feed",
@@ -387,13 +428,13 @@
     return jnp.sum(values.reshape(rows // 8, 8, cols), axis=0)
 
 
-def feed_back_kernel(offsets, owned, parts, held_count, rank_ref, *refs):
+def feed_back_kernel(offsets, owned, first_part, parts, held_count, rank_ref, *refs):
     part_refs = refs[:parts]
-    factor_ref, slope_ref, tokens_ref, blocks_ref, norm_ref = refs[parts : parts + 5]
+    factor_ref, slope_ref, tokens_ref, mean_ref, inverse_ref, blocks_ref, norm_ref = refs[parts : parts + 7]
     (
         seed_ref, d_attended_ref, d_hidden_ref, dz_ref, norm_sums, hidden_sums,
         w_in, w_down, w_out, held, sems_in, sems_down, sems_out, part_sems,
-    ) = refs[parts + 5 + held_count :]
+    ) = refs[parts + 7 + held_count :]
     size = blocks_ref.shape[-1]
     width, hidden_units = w_in.shape
     inner, outer = hidden_units // size, width // size
@@ -416,6 +457,12 @@
     cotangent = held[step // per_part, pl.ds(pl.multiple_of(step % per_part * tile, tile), tile), :]
     seed_ref[...] = (cotangent.astype(jnp.float32) * factor_ref[...]).astype(jnp.bfloat16)
     seed = seed_ref[...]
+    if first_part == 0:
+
+        @pl.when(step < per_part)
+        def _():
+            norm_sums[16:24, :] += column_sum(seed_ref[...].astype(jnp.float32))
+
     end_copies(copies_out)
     d_attended_ref[...] = contract(seed, w_out[...], NT).astype(jnp.bfloat16)
     end_copies(copies_down)
@@ -426,7 +473,7 @@
         d_hidden_ref[:, cols] = d_hidden
         hidden_sums[:, cols] += column_sum(d_hidden.astype(jnp.float32))
     end_copies(copies_in)
-    mean, inverse = normed_rows(tokens_ref[...].astype(jnp.float32))
+    mean, inverse = mean_ref[...], inverse_ref[...]
     for col in range(outer):
         cols = pl.ds(col * size, size)
         scaled = (tokens_ref[:, cols].astype(jnp.float32) - mean) * inverse
@@ -436,12 +483,12 @@
         norm_sums[8:16, cols] += column_sum(second)
 
 
-def feed_back(parts, first_part, ways, rank, factor, slope, group_tokens, blocks, owned, norm_params, offsets, head_cols, priors):
+def feed_back(parts, first_part, ways, rank, factor, slope, group_tokens, mean, inverse, blocks, owned, norm_params, offsets, head_cols, priors):
     chunk, width = parts[0].shape
     tokens = ways * chunk
     size = blocks.shape[-1]
     hidden_units = slope.shape[1]
-    tile = min(256, chunk)
+    tile = min(FEED_BACK_TILE, chunk)
     per_part = chunk // tile
     inner, outer = hidden_units // size, width // size
     place = lambda i, rank: (rank[0] - first_part - i // per_part + ways) % ways * per_part + i % per_part
@@ -451,15 +498,16 @@
     count = len(parts)
     rows = count * chunk
     return pl.pallas_call(
-        functools.partial(feed_back_kernel, offsets, owned, count, len(priors)),
+        functools.partial(feed_back_kernel, offsets, owned, first_part, count, len(priors)),
         grid_spec=pltpu.PrefetchScalarGridSpec(
             num_scalar_prefetch=1,
             grid=(count * per_part,),
             in_specs=[anywhere] * count
-            + [row(1), row(hidden_units), row(width), anywhere, whole(norm_params.shape[0], width)]
+            + [row(1), row(hidden_units), row(width), row(1), row(1), anywhere]
+            + [whole(norm_params.shape[0], width)]
             + [anywhere] * len(priors),
             out_specs=[
-                row(width), row(head_cols), row(hidden_units), row(width), whole(16, width), whole(8, hidden_units),
+                row(width), row(head_cols), row(hidden_units), row(width), whole(24, width), whole(8, hidden_units),
             ],
             scratch_shapes=[
                 pltpu.VMEM((width, hidden_units), jnp.bfloat16),
@@ -477,19 +525,19 @@
             jax.ShapeDtypeStruct((tokens, head_cols), jnp.bfloat16),
             jax.ShapeDtypeStruct((tokens, hidden_units), jnp.bfloat16),
             jax.ShapeDtypeStruct((tokens, width), jnp.float32),
-            jax.ShapeDtypeStruct((16, width), jnp.float32),
+            jax.ShapeDtypeStruct((24, width), jnp.float32),
             jax.ShapeDtypeStruct((8, hidden_units), jnp.float32),
         ],
-        input_output_aliases={1 + count + 5 + index: index for index in range(len(priors))},
+        input_output_aliases={1 + count + 7 + index: index for index in range(len(priors))},
         compiler_params=kernel_params(),
-        cost_estimate=pl.CostEstimate(
+        cost_estimate=kernel_cost(
             flops=2 * rows * width * (2 * hidden_units + head_cols), bytes_accessed=rows * width * 14 + width * hidden_units * 4, transcendentals=0
         ),
         name="feed_back",
-    )(rank, *parts, factor, slope, group_tokens, blocks, norm_params, *priors)
-
-
-def qkv_back_kernel(owned, d_qkv_ref, part_ref, tokens_ref, blocks_ref, norm_ref, dz_ref, norm_sums, qkv_sums, w_qkv, sems):
+    )(rank, *parts, factor, slope, group_tokens, mean, inverse, blocks, norm_params, *priors)
+
+
+def qkv_back_kernel(owned, d_qkv_ref, part_ref, tokens_ref, mean_ref, inverse_ref, blocks_ref, norm_ref, dz_ref, norm_sums, qkv_sums, w_qkv, sems):
     size = blocks_ref.shape[-1]
     outer = w_qkv.shape[0] // size
     copies = block_copies(blocks_ref, owned, 0, outer, w_qkv.shape[1] // size, w_qkv, sems)
@@ -501,7 +549,7 @@
         qkv_sums[...] = jnp.zeros_like(qkv_sums)
 
     qkv_sums[...] += column_sum(d_qkv_ref[...].astype(jnp.float32))
-    mean, inverse = normed_rows(tokens_ref[...].astype(jnp.float32))
+    mean, inverse = mean_ref[...], inverse_ref[...]
     end_copies(copies)
     for col in range(outer):
         cols = pl.ds(col * size, size)
@@ -512,7 +560,7 @@
         norm_sums[8:16, cols] += column_sum(first)
 
 
-def qkv_back(d_qkv, dz_part, group_tokens, blocks, owned, norm_params):
+def qkv_back(d_qkv, dz_part, group_tokens, mean, inverse, blocks, owned, norm_params):
     tokens, qkv_cols = d_qkv.shape
     width = dz_part.shape[1]
     size = blocks.shape[-1]
@@ -524,7 +572,7 @@
         functools.partial(qkv_back_kernel, owned),
         grid=(tokens // tile,),
         in_specs=[
-            row(qkv_cols), row(width), row(width), pl.BlockSpec(memory_space=pl.ANY), whole(norm_params.shape[0], width),
+            row(qkv_cols), row(width), row(width), row(1), row(1), pl.BlockSpec(memory_space=pl.ANY), whole(norm_params.shape[0], width),
         ],
         out_specs=[row(width), whole(16, width), whole(8, qkv_cols)],
         out_shape=[
@@ -537,127 +585,122 @@
             pltpu.SemaphoreType.DMA((outer * (qkv_cols // size),)),
         ],
         compiler_params=kernel_params(),
-        cost_estimate=pl.CostEstimate(
+        cost_estimate=kernel_cost(
             flops=2 * tokens * width * qkv_cols, bytes_accessed=tokens * width * 11, transcendentals=0
         ),
         name="qkv_back",
-    )(d_qkv, dz_part, group_tokens, blocks, norm_params)
-
-
-def weight_grad_kernel(table, owned, part_size, core_ref, *refs):
-    products = len(table)
-    parts = owned // part_size
-    left_refs, refs = refs[:products], refs[products:]
-    rights, refs = refs[:3], refs[3:]
-    outs, refs = refs[: 2 * parts], refs[2 * parts :]
-    held, (results, sems, right_sems) = refs[:3], refs[3:]
+    )(d_qkv, dz_part, group_tokens, mean, inverse, blocks, norm_params)
+
+
+def weight_grad_kernel(steps, core_ref, *refs):
+    lefts, rights, outs = refs[:4], refs[4:7], refs[7:9]
+    rows_held, rights_held, (results, left_sems, right_sems, sems) = refs[9], refs[10:13], refs[13:]
     size = results.shape[-1]
-    step = pl.program_id(0)
-    slot = lax.rem(step, 2)
     core = core_ref[0]
-    loads = [pltpu.make_async_copy(rights[i], held[i], right_sems.at[i]) for i in range(3)]
-
-    @pl.when(step == 0)
-    def _():
-        for load in loads:
-            load.start()
-
-    def finish(of_slot, amount):
-        for index in range(amount):
+
+    def left_copy(index):
+        left, first, rows, _, _, _ = steps[index]
+        return pltpu.make_async_copy(
+            lefts[left].at[pl.ds(first, rows), :],
+            rows_held.at[index % 2, pl.ds(0, rows), :],
+            left_sems.at[index % 2],
+        )
+
+    def right_copy(right, first):
+        held = rights_held[right]
+        return pltpu.make_async_copy(
+            rights[right].at[:, pl.ds(first, held.shape[1])], held, right_sems.at[right]
+        )
+
+    def finish(index):
+        for place in range(len(steps[index][5])):
             pltpu.make_async_copy(
-                results.at[of_slot, index], outs[0].at[0], sems.at[of_slot, index]
+                results.at[index % 2, place], outs[0].at[0], sems.at[index % 2, place]
             ).wait()
 
-    def amount_of(product):
-        left, right = left_refs[product], held[table[product][3]]
-        return left.shape[1] // size * (right.shape[1] // size)
-
-    made = [product for product in range(products) for _ in range(table[product][1])]
-    total = len(made)
-    for product, (begin, times, first, which, fresh) in enumerate(table):
-
-        @pl.when((step >= begin) & (step < begin + times))
-        def _():
-            left_ref, right = left_refs[product], held[which]
-            rows, cols = left_ref.shape[1] // size, right.shape[1] // size
-            if fresh:
-
-                @pl.when(step == begin)
+    order = []
+    for step in steps:
+        if step[3:5] not in order:
+            order.append(step[3:5])
+    left_copy(0).start()
+    for right in order:
+        right_copy(*right).start()
+    for index, (left, first, rows, right, right_first, places) in enumerate(steps):
+        left_copy(index).wait()
+        if index + 1 < len(steps):
+            left_copy(index + 1).start()
+        if all(step[3:5] != (right, right_first) for step in steps[:index]):
+            right_copy(right, right_first).wait()
+        if index >= 2:
+            finish(index - 2)
+        held = rights_held[right]
+        cols = held.shape[1] // size
+        for col in range(cols):
+            result = contract(rows_held[index % 2, :rows, :], held[:, col * size : (col + 1) * size], NN)
+            for row in range(rows // size):
+                results[index % 2, row * cols + col] = result[row * size : (row + 1) * size].astype(jnp.bfloat16)
+        for number, (owner, place) in enumerate(places):
+            for away in range(2):
+
+                @pl.when((core == owner % 2) == (away == 0))
                 def _():
-                    loads[which].wait()
-
-            for back in range(begin, begin + times):
-                if back >= 2:
-
-                    @pl.when(step == back)
-                    def _():
-                        finish(back % 2, amount_of(made[back - 2]))
-
-            turned = left_ref[...].T
-            for col in range(cols):
-                result = contract(turned, right[:, pl.ds(col * size, size)], NN)
-                for row in range(rows):
-                    results[slot, row * cols + col] = result[
-                        row * size : (row + 1) * size
-                    ].astype(jnp.bfloat16)
-            for row in range(rows):
-                for col in range(cols):
-                    block = first + ((step - begin) * rows + row) * cols + col
+                    pltpu.make_async_copy(
+                        results.at[index % 2, number], outs[away].at[place], sems.at[index % 2, number]
+                    ).start()
+
+    for index in range(max(0, len(steps) - 2), len(steps)):
+        finish(index)
+
+
+def weight_grads(part, parts, lefts, rights, firsts, core, owned, dp_ways, size):
+    first_normed, second_normed, activated, attended = lefts
+    d_hidden, seed, d_qkv = rights
+    tokens = d_qkv.shape[0]
+    width = seed.shape[1]
+    part_size = owned // parts
+    qkv_blocks = d_qkv.shape[1] // size
+    per_row = width // size
+    span = per_row // parts
+    steps = []
+    for left, right, first, rows_all in (
+        (1, 0, firsts[2], second_normed.shape[0]),
+        (2, 1, firsts[3], activated.shape[0]),
+        (3, 1, firsts[1], attended.shape[0]),
+    ):
+        rows = min(512, rows_all)
+        for begin in range(0, rows_all, rows):
+            places = []
+            for row in range(begin // size, (begin + rows) // size):
+                for col in range(span):
+                    block = first + row * per_row + part * span + col
                     owner, within = block // owned, block % owned
-                    place = owner // 2 * part_size + within % part_size
-                    for part in range(parts):
-                        for away in range(2):
-
-                            @pl.when((within // part_size == part) & ((owner % 2 == core) == (away == 0)))
-                            def _():
-                                pltpu.make_async_copy(
-                                    results.at[slot, row * cols + col],
-                                    outs[2 * part + away].at[place],
-                                    sems.at[slot, row * cols + col],
-                                ).start()
-
-    @pl.when(step == total - 1)
-    def _():
-        if total >= 2:
-            finish((total - 2) % 2, amount_of(made[total - 2]))
-        finish((total - 1) % 2, amount_of(made[total - 1]))
-
-
-def weight_grads(lefts, rights, chosen, firsts, core, owned, part_size, dp_ways, size):
-    tokens = lefts[0].shape[0]
-    groups = [min(512, left.shape[1]) for left in lefts]
-    times = [left.shape[1] // group for left, group in zip(lefts, groups)]
-    begins = [sum(times[:index]) for index in range(len(times))]
-    table = tuple(
-        (begins[i], times[i], firsts[i], chosen[i], chosen[i] not in chosen[:i]) for i in range(len(lefts))
-    )
-    most = max(group // size * (rights[which].shape[1] // size) for group, which in zip(groups, chosen))
-    parts = owned // part_size
-
-    def left_spec(index):
-        begin, last, group = begins[index], times[index] - 1, groups[index]
-        return pl.BlockSpec((tokens, group), lambda i, core: (0, jnp.clip(i - begin, 0, last)))
-
+                    places.append((owner, owner // 2 * part_size + within // per_row * span + col))
+            steps.append((left, begin, rows, right, part * span * size, tuple(places)))
+    for owner in range(per_row // parts):
+        row = owner * parts + part
+        places = [(owner, owner // 2 * part_size + col) for col in range(qkv_blocks)]
+        steps.append((0, row * size, size, 2, 0, tuple(places)))
+    most = max(len(step[5]) for step in steps)
     anywhere = pl.BlockSpec(memory_space=pl.ANY)
     half = jax.ShapeDtypeStruct((dp_ways // 2 * part_size, size, size), jnp.bfloat16)
-    flops = sum(2 * tokens * left.shape[1] * rights[which].shape[1] for left, which in zip(lefts, chosen))
+    flops = 2 * tokens * size * size * dp_ways * part_size
     return pl.pallas_call(
-        functools.partial(weight_grad_kernel, table, owned, part_size),
-        grid_spec=pltpu.PrefetchScalarGridSpec(
-            num_scalar_prefetch=1,
-            grid=(sum(times),),
-            in_specs=[left_spec(index) for index in range(len(lefts))] + [anywhere] * 3,
-            out_specs=[anywhere] * (2 * parts),
-            scratch_shapes=[pltpu.VMEM(right.shape, jnp.bfloat16) for right in rights]
-            + [
-                pltpu.VMEM((2, most, size, size), jnp.bfloat16),
-                pltpu.SemaphoreType.DMA((2, most)),
-                pltpu.SemaphoreType.DMA((3,)),
-            ],
-        ),
-        out_shape=[half] * (2 * parts),
+        functools.partial(weight_grad_kernel, tuple(steps)),
+        in_specs=[pl.BlockSpec(memory_space=pltpu.SMEM)] + [anywhere] * 7,
+        out_specs=[anywhere] * 2,
+        out_shape=[half] * 2,
+        scratch_shapes=[
+            pltpu.VMEM((2, max(step[2] for step in steps), tokens), jnp.bfloat16),
+            pltpu.VMEM((tokens, span * size), jnp.bfloat16),
+            pltpu.VMEM((tokens, span * size), jnp.bfloat16),
+            pltpu.VMEM((tokens, d_qkv.shape[1]), jnp.bfloat16),
+            pltpu.VMEM((2, most, size, size), jnp.bfloat16),
+            pltpu.SemaphoreType.DMA((2,)),
+            pltpu.SemaphoreType.DMA((3,)),
+            pltpu.SemaphoreType.DMA((2, most)),
+        ],
         compiler_params=kernel_params(),
-        cost_estimate=pl.CostEstimate(flops=flops, bytes_accessed=flops // 1000, transcendentals=0),
+        cost_estimate=kernel_cost(flops=flops, bytes_accessed=flops // 500, transcendentals=0),
         name="weight_grads",
     )(core, *lefts, *rights)
 
@@ -687,7 +730,7 @@
         ),
         out_shape=[jax.ShapeDtypeStruct((part, size, size), dtype) for dtype in dtypes],
         compiler_params=kernel_params(),
-        cost_estimate=pl.CostEstimate(flops=rows * size * size, bytes_accessed=rows * size * size * 6, transcendentals=0),
+        cost_estimate=kernel_cost(flops=rows * size * size, bytes_accessed=rows * size * size * 6, transcendentals=0),
         name="pair_sum",
     )(chip, *([kept] * chips), *([received] * chips))
 
@@ -701,102 +744,169 @@
     return high, (values - high.astype(jnp.float32)).astype(jnp.bfloat16)
 
 
-def product_three(left_arg, right_arg):
-    left_high, left_low = two_terms(left_arg)
-    right_high, right_low = two_terms(right_arg)
-    return (
-        dot32(left_high, right_high) + dot32(left_high, right_low) + dot32(left_low, right_high)
-    )
-
-
-def next_scaled(quarter, quarter16, scaled):
-    square_rest = 2.0 * quarter + dot32(quarter16, quarter16)
-    square16 = square_rest.astype(jnp.bfloat16)
-    fourth_rest = 2.0 * square_rest + dot32(square16, square16)
-    return scaled + product_three(fourth_rest, scaled)
-
-
-def shampoo_kernel(
-    grad_refs, left_ref, right_ref, master_ref, grad_out, left_out, right_out, new_out, scaled, roots
-):
-    count, size, _ = left_ref.shape
+def shampoo_kernel(count, terms, held, places_ref, *refs):
+    grads, refs = refs[:terms], refs[terms:]
+    left_refs, right_refs, master_refs = (refs[side * count : (side + 1) * count] for side in range(3))
+    outs, refs = refs[3 * count + held : 3 * count + held + 4], refs[3 * count + held + 4 :]
+    results, scaled, roots, pairs, powers, high, low, sems = refs
+    size = results.shape[-1]
+    step, steps = pl.program_id(0), pl.num_programs(0)
+    slot = lax.rem(step, 2)
+    chains = range(2 * count)
+    stat_refs = (left_refs, right_refs)
     identity = (
         lax.broadcasted_iota(jnp.int32, (size, size), 0)
         == lax.broadcasted_iota(jnp.int32, (size, size), 1)
     ).astype(jnp.float32)
-    factors = []
+
+    def copies(of_step, of_slot):
+        return [
+            pltpu.make_async_copy(
+                results.at[of_slot, kind, block],
+                outs[kind].at[places_ref[of_step * count + block]],
+                sems.at[of_slot, kind, block],
+            )
+            for kind in range(4)
+            for block in range(count)
+        ]
+
+    @pl.when(step >= 2)
+    def _():
+        for copy in copies(step - 2, slot):
+            copy.wait()
+
+    grad16 = []
     for block in range(count):
-        total = grad_refs[0][block].astype(jnp.float32)
-        for grad_ref in grad_refs[1:]:
-            total = total + grad_ref[block].astype(jnp.float32)
-        grad_out[block] = total
-        grad = total.astype(jnp.bfloat16)
-        for side, stat_ref, stat_out in ((0, left_ref, left_out), (1, right_ref, right_out)):
-            dims = (((1 - side,), (1 - side,)), ((), ()))
-            stat = DECAY * stat_ref[block] + lax.dot_general(
-                grad, grad, dims, preferred_element_type=jnp.float32
+        total = grads[0][block].astype(jnp.float32)
+        for grad in grads[1:]:
+            total = total + grad[block].astype(jnp.float32)
+        results[slot, 0, block] = total
+        grad16.append(total.astype(jnp.bfloat16))
+    for item in chains:
+        block, side = item // 2, item % 2
+        dims = (((1 - side,), (1 - side,)), ((), ()))
+        results[slot, 1 + side, block] = DECAY * stat_refs[side][block][0] + lax.dot_general(
+            grad16[block], grad16[block], dims, preferred_element_type=jnp.float32
+        )
+    sums = []
+    for item in chains:
+        stat = results[slot, 1 + item % 2, item // 2]
+        sums.append(jnp.sum(stat * stat, axis=0, keepdims=True))
+    norms = [jnp.sqrt(jnp.sum(each, axis=1, keepdims=True)) for each in sums]
+    for item in chains:
+        scaled[item] = results[slot, 1 + item % 2, item // 2] * (1.0 / norms[item])
+    factors = [lax.rsqrt(jnp.sqrt(norm)) for norm in norms]
+
+    for repeat in range(ROOT_ITERS - 1):
+        for item in chains:
+            quarter = (identity - scaled[item]) * 0.25
+            pairs[item, size:] = quarter.astype(jnp.bfloat16)
+            if repeat == 0:
+                roots[item] = identity + quarter
+            else:
+                pairs[item, :size] = roots[item].astype(jnp.bfloat16)
+        if repeat == 0:
+            squares = [dot32(pairs[item, size:], pairs[item, size:]) for item in chains]
+        else:
+            both = [dot32(pairs[item], pairs[item, size:]) for item in chains]
+            for item in chains:
+                roots[item] = roots[item] + both[item][:size]
+            squares = [each[size:] for each in both]
+        seconds = [(identity - scaled[item]) * 0.5 + squares[item] for item in chains]
+        seconds16 = [second.astype(jnp.bfloat16) for second in seconds]
+        fourths = [2.0 * seconds[item] + dot32(seconds16[item], seconds16[item]) for item in chains]
+        for item in chains:
+            high[item], low[item] = two_terms(scaled[item])
+            powers[item, :size], powers[item, size:] = two_terms(fourths[item])
+        for item in chains:
+            both_terms = dot32(powers[item], high[item])
+            scaled[item] = scaled[item] + (
+                both_terms[:size] + both_terms[size:] + dot32(powers[item, :size], low[item])
             )
-            stat_out[block] = stat
-            squares = jnp.sum(stat * stat, axis=0, keepdims=True)
-            norm = jnp.sqrt(jnp.sum(squares, axis=1, keepdims=True))
-            factors.append(lax.rsqrt(jnp.sqrt(norm)))
-            start = stat / norm
-            quarter = (identity - start) * 0.25
-            roots[2 * block + side] = identity + quarter
-            scaled[2 * block + side] = next_scaled(quarter, quarter.astype(jnp.bfloat16), start)
-
-    def iterate(step, carry):
-        for item in range(2 * count):
-            now = scaled[item]
-            quarter = (identity - now) * 0.25
-            quarter16 = quarter.astype(jnp.bfloat16)
-            root = roots[item]
-            roots[item] = root + dot32(root.astype(jnp.bfloat16), quarter16)
-            scaled[item] = next_scaled(quarter, quarter16, now)
-        return carry
-
-    lax.fori_loop(0, ROOT_ITERS - 2, iterate, 0)
+    for item in chains:
+        pairs[item, size:] = ((identity - scaled[item]) * 0.25).astype(jnp.bfloat16)
+        pairs[item, :size] = roots[item].astype(jnp.bfloat16)
+    for item in chains:
+        ends = two_terms(roots[item] + dot32(pairs[item, :size], pairs[item, size:]))
+        if item % 2 == 0:
+            powers[item, :size], powers[item, size:] = ends
+        else:
+            high[item], low[item] = ends
+    halves = []
     for block in range(count):
-        ends = []
-        for side in range(2):
-            item = 2 * block + side
-            quarter16 = ((identity - scaled[item]) * 0.25).astype(jnp.bfloat16)
-            root = roots[item]
-            ends.append(root + dot32(root.astype(jnp.bfloat16), quarter16))
-        grad = grad_out[block].astype(jnp.bfloat16)
-        left_high, left_low = two_terms(ends[0])
-        half = dot32(left_high, grad) + dot32(left_low, grad)
-        rate = RATE_BLOCK * factors[2 * block] * factors[2 * block + 1]
-        new_out[block] = master_ref[block] - rate * product_three(half, ends[1])
-
-
-def shampoo(grads, left_stats, right_stats, master_blocks, first, priors):
+        both_terms = dot32(powers[2 * block], grad16[block])
+        halves.append(both_terms[:size] + both_terms[size:])
+    for block in range(count):
+        pairs[block, :size], pairs[block, size:] = two_terms(halves[block])
+    for block in range(count):
+        item = 2 * block + 1
+        both_terms = dot32(pairs[block], high[item])
+        product = both_terms[:size] + both_terms[size:] + dot32(pairs[block, :size], low[item])
+        rate = RATE_BLOCK * factors[2 * block] * factors[item]
+        results[slot, 3, block] = master_refs[block][0] - rate * product
+    for copy in copies(step, slot):
+        copy.start()
+
+    @pl.when(step == steps - 1)
+    def _():
+        @pl.when(steps >= 2)
+        def _():
+            for copy in copies(step - 1, 1 - slot):
+                copy.wait()
+
+        for copy in copies(step, slot):
+            copy.wait()
+
+
+def shampoo(grads, left_stats, right_stats, master_blocks, places, priors):
     part, size, _ = grads[0].shape
-    terms = len(grads)
     count = next(each for each in (3, 2, 1) if part % each == 0)
-    start = first // count
-    spec = pl.BlockSpec((count, size, size), lambda step: (step + start, 0, 0))
-    own = pl.BlockSpec((count, size, size), lambda step: (step, 0, 0))
+    own = pl.BlockSpec((count, size, size), lambda step, places: (step, 0, 0))
+    anywhere = pl.BlockSpec(memory_space=pl.ANY)
+
+    def single(block):
+        return pl.BlockSpec((1, size, size), lambda step, places: (places[step * count + block], 0, 0))
+
     result = jax.ShapeDtypeStruct(left_stats.shape, jnp.float32)
-    held = [] if priors is None else list(priors)
-
-    def kernel(*refs):
-        shampoo_kernel(refs[:terms], *refs[terms : terms + 3], *refs[terms + 3 + len(held) :])
-
+    held = len(priors)
+    first_prior = 1 + len(grads) + 3 * count
+    wide = pltpu.VMEM((2 * count, 2 * size, size), jnp.bfloat16)
+    plain = pltpu.VMEM((2 * count, size, size), jnp.bfloat16)
     return pl.pallas_call(
-        kernel,
-        grid=(part // count,),
-        in_specs=[own] * terms + [spec] * 3 + [pl.BlockSpec(memory_space=pl.ANY)] * len(held),
-        out_specs=[spec] * 4,
+        functools.partial(shampoo_kernel, count, len(grads), held),
+        grid_spec=pltpu.PrefetchScalarGridSpec(
+            num_scalar_prefetch=1,
+            grid=(part // count,),
+            in_specs=[own] * len(grads)
+            + [single(block) for block in range(count)] * 3
+            + [anywhere] * held,
+            out_specs=[anywhere] * 4,
+            scratch_shapes=[
+                pltpu.VMEM((2, 4, count, size, size), jnp.float32),
+                pltpu.VMEM((2 * count, size, size), jnp.float32),
+                pltpu.VMEM((2 * count, size, size), jnp.float32),
+                wide,
+                wide,
+                plain,
+                plain,
+                pltpu.SemaphoreType.DMA((2, 4, count)),
+            ],
+        ),
         out_shape=[result] * 4,
-        input_output_aliases={terms + 3 + index: index for index in range(len(held))},
-        scratch_shapes=[pltpu.VMEM((2 * count, size, size), jnp.float32)] * 2,
+        input_output_aliases={first_prior + index: index for index in range(held)},
         compiler_params=kernel_params(),
-        cost_estimate=pl.CostEstimate(
-            flops=part * 180 * 2 * size**3, bytes_accessed=part * size * size * 30, transcendentals=0
+        cost_estimate=kernel_cost(
+            flops=part * 130 * 2 * size**3, bytes_accessed=part * size * size * 30, transcendentals=0
         ),
         name="shampoo",
-    )(*grads, left_stats, right_stats, master_blocks, *held)
+    )(
+        places,
+        *grads,
+        *([left_stats] * count),
+        *([right_stats] * count),
+        *([master_blocks] * count),
+        *priors,
+    )
 
 
 def after(value, *earlier):
@@ -849,22 +959,11 @@
     all_count = owned * dp_ways
     vec_rows = 3 * heads_dev + ff_dev // HD
 
-    shared16 = shared_vecs.astype(jnp.bfloat16)
-    shared_here = [(tp_rank, shared16)] + [
-        (
-            (tp_rank - step) % tp_ways,
-            lax.ppermute(shared16, "tp", [(each, (each + step) % tp_ways) for each in range(tp_ways)]),
-        )
-        for step in range(1, tp_ways)
-    ]
-    shared_group = jnp.zeros((tp_ways,) + shared16.shape, jnp.bfloat16)
-    for place, part in shared_here:
-        shared_group = lax.dynamic_update_slice(shared_group, part[None], (place, 0, 0))
-    vec_flat = jnp.concatenate([local_vecs.astype(jnp.bfloat16).reshape(-1), shared_group.reshape(-1)])
     vec_used = local_vecs.size
-    shared_used = shared_group.size
+    shared_used = shared_vecs.size
+    vec_flat = jnp.concatenate([local_vecs.reshape(-1), shared_vecs.reshape(-1)])
     extra = jnp.pad(vec_flat, (0, EXTRA_ROWS * block_size - vec_flat.size)).reshape(EXTRA_ROWS, block_size)
-    rows16 = jnp.concatenate([master_blocks.astype(jnp.bfloat16).reshape(-1, block_size), extra], 0)
+    rows16 = jnp.concatenate([master_blocks.reshape(-1, block_size), extra], 0).astype(jnp.bfloat16)
     blocks = lax.all_gather(rows16, "dp", axis=0, tiled=True)
 
     token_parts = [tokens]
@@ -875,11 +974,19 @@
     vec_values = (
         gathered[:, :vec_used].reshape(dp_ways, vec_rows, -1).transpose(1, 0, 2).reshape(vec_rows, HD)
     ).astype(jnp.float32)
+    shared_mine = gathered[:, vec_used : vec_used + shared_used]
+    shared_all = jnp.zeros((tp_ways,) + shared_mine.shape, jnp.bfloat16)
+    for step in range(tp_ways):
+        part = shared_mine
+        if step:
+            part = lax.ppermute(
+                part, "tp", [(each, (each + step) % tp_ways) for each in range(tp_ways)]
+            )
+        shared_all = lax.dynamic_update_slice(
+            shared_all, part[None], ((tp_rank - step) % tp_ways, 0, 0)
+        )
     norm_params = (
-        gathered[:, vec_used : vec_used + shared_used]
-        .reshape(dp_ways, tp_ways, 6, -1)
-        .transpose(2, 0, 1, 3)
-        .reshape(6, model_width)
+        shared_all.reshape(tp_ways, dp_ways, 6, -1).transpose(2, 1, 0, 3).reshape(6, model_width)
     ).astype(jnp.float32)
     bias_qkv = vec_values[: 3 * heads_dev].reshape(1, -1)
     bias_in = vec_values[3 * heads_dev :].reshape(1, -1)
@@ -898,91 +1005,121 @@
     factor = (weight * (group_pack < packs[0]).astype(jnp.float32))[:, None]
     own_factor = lax.dynamic_slice_in_dim(factor, tp_rank * tok_dev, tok_dev, 0)
     seed16 = (cotangent.astype(jnp.float32) * own_factor).astype(jnp.bfloat16)
-    out_bias_grad = jnp.sum(seed16, axis=0, dtype=jnp.float32)
 
     rank = tp_rank.astype(jnp.int32)[None]
     cosines, sines = turn_tables(pack_len, 128)
     cotangent_parts = [cotangent, onward(after(cotangent, token_parts[-1]), "tp")]
-    qkv16, first_normed, second_normed, group_tokens = project_qkv(
+    qkv16, first_turned, second_normed, second_turned, group_tokens, mean, inverse = project_qkv(
         token_parts, rank, blocks, owned, norm_params, bias_qkv, cosines, sines, heads_dev
     )
-    attended = attend(qkv16, segments, heads_dev)
+    attended, attended_turned = attend(qkv16, segments, heads_dev)
     cotangent_parts.append(onward(after(cotangent_parts[-1], attended), "tp"))
-    activated, slope, partial_value = feed_forward(
+    active_turned, slope, partial_value = feed_forward(
         second_normed, attended, blocks, owned, bias_in, (first_out, first_in, first_down)
     )
     while len(cotangent_parts) < tp_ways:
         cotangent_parts.append(onward(after(cotangent_parts[-1], slope), "tp"))
 
     back_args = (
-        tp_ways, rank, factor, slope, group_tokens, blocks, owned, norm_params, (first_out, first_in, first_down), head_cols,
+        tp_ways, rank, factor, slope, group_tokens, mean, inverse, blocks, owned, norm_params,
+        (first_out, first_in, first_down), head_cols,
     )
     early = feed_back(cotangent_parts[:-1], 0, *back_args, ())
     late = feed_back(cotangent_parts[-1:], tp_ways - 1, *back_args, early[:4])
     seed_all, d_attended, d_hidden16, dz_part = late[:4]
     branch = lax.psum_scatter(
-        after(partial_value, cotangent_parts[-1]), "tp", scatter_dimension=0, tiled=True
-    )
+        after(partial_value, cotangent_parts[-1], early[5]), "tp", scatter_dimension=0, tiled=True
+    )
+    d_qkv16 = attend_back(qkv16, d_attended, segments, cosines, sines, heads_dev)
+    dz16, first_sums, qkv_sums = qkv_back(
+        d_qkv16, dz_part, group_tokens, mean, inverse, blocks, owned, norm_params
+    )
+
+    dz_rows = lambda back: lax.dynamic_slice_in_dim(dz16, (tp_rank - back) % tp_ways * tok_dev, tok_dev, 0)
+    back = 2
+
+    def pass_on(moving, back):
+        total = moving.astype(jnp.float32) + dz_rows(back).astype(jnp.float32)
+        return total if back == tp_ways else onward(total.astype(jnp.bfloat16), "tp")
+
+    dp_rank = lax.axis_index("dp").astype(jnp.int32)
+    lefts = (first_turned, second_turned, active_turned, attended_turned)
+    d_qkv_late, first_rows = lax.optimization_barrier((d_qkv16, dz_rows(1)))
+    moving = onward(first_rows, "tp")
+    rights = (d_hidden16, seed_all, d_qkv_late)
+    firsts = (0, first_out, first_in, first_down)
+    qkv_blocks = 3 * head_cols // block_size
+    parts = 4
+    by_part = (
+        dp_ways == 8
+        and owned == parts * qkv_blocks
+        and block_rows == 2 * parts
+        and ff_dev == model_width
+        and owned % block_rows == 0
+        and first_out % block_rows == 0
+        and first_in % block_rows == 0
+    )
+    results = ()
+    if by_part:
+        part_size = owned // parts
+        span = block_rows // parts
+        sums = []
+        for part in range(parts):
+            core = (dp_rank % 2)[None]
+            if part >= 2:
+                core = after(core, sums[part - 2][0])
+            kept, away = weight_grads(
+                part, parts, lefts, rights, firsts, core, owned, dp_ways, block_size
+            )
+            sums.append(pair_sum(kept, swap(away, 1), (dp_rank // 2)[None], dp_ways // 2))
+        moving = pass_on(after(moving, kept), back)
+        back += 1
+        terms = []
+        ready = []
+        for part in range(parts):
+            if part:
+                sums[part] = [sums[part][0]] + [after(each, terms[-1][3]) for each in sums[part][1:]]
+                ready.append(sums[part][3])
+            terms.append([sums[part][0]] + [swap(sums[part][bits], 2 * bits) for bits in range(1, 4)])
+        count = jnp.arange(part_size, dtype=jnp.int32)
+        in_qkv = dp_rank * owned < first_out
+        for part in range(parts):
+            places = jnp.where(
+                in_qkv,
+                part * part_size + count,
+                count // span * block_rows + part * span + count % span,
+            )
+            if part < parts - 1:
+                places = after(places, ready[part])
+            results = shampoo(terms[part], left_stats, right_stats, master_blocks, places, results)
+            if part % 2 == 1 and back <= tp_ways:
+                moving, first_result = lax.optimization_barrier((moving, results[0]))
+                results = [first_result] + list(results[1:])
+                moving = pass_on(moving, back)
+                back += 1
+    else:
+        local = [
+            to_blocks(jnp.dot(left, right, preferred_element_type=jnp.float32).astype(jnp.bfloat16), block_size)
+            for left, right in (
+                (first_turned, d_qkv_late),
+                (attended_turned, seed_all),
+                (second_turned, d_hidden16),
+                (active_turned, seed_all),
+            )
+        ]
+        grads16 = lax.psum_scatter(jnp.concatenate(local, 0), "dp", scatter_dimension=0, tiled=True)
+        results = shampoo(
+            [grads16], left_stats, right_stats, master_blocks, jnp.arange(owned, dtype=jnp.int32), results
+        )
+    while back <= tp_ways:
+        moving = pass_on(moving, back)
+        back += 1
+    norm_input_gradient = moving
+    own_grads, left_new, right_new, new_blocks = results
     output = (
         valid_own[:, None]
         * (owned_input_rows + branch.astype(jnp.float32) + norm_params[4] + norm_params[5])
     ).astype(jnp.bfloat16)
-    d_qkv16 = attend_back(qkv16, d_attended, segments, cosines, sines, heads_dev)
-    dz16, first_sums, qkv_sums = qkv_back(d_qkv16, dz_part, group_tokens, blocks, owned, norm_params)
-
-    dz_rows = lambda back: lax.dynamic_slice_in_dim(dz16, (tp_rank - back) % tp_ways * tok_dev, tok_dev, 0)
-    moving = onward(dz_rows(1), "tp")
-
-    parts = next(each for each in (4, 3, 2, 1) if owned % each == 0)
-    part_size = owned // parts
-    dp_rank = lax.axis_index("dp").astype(jnp.int32)
-    halves = weight_grads(
-        (first_normed, attended, second_normed, activated),
-        (d_qkv16, seed_all, d_hidden16),
-        (0, 1, 2, 1),
-        (0, first_out, first_in, first_down),
-        (dp_rank % 2)[None],
-        owned,
-        part_size,
-        dp_ways,
-        block_size,
-    )
-    results = None
-    last = None
-    back = 2
-
-    def pass_on(moving, back):
-        total = moving.astype(jnp.float32) + dz_rows(back).astype(jnp.float32)
-        return total if back == tp_ways else onward(total.astype(jnp.bfloat16), "tp")
-
-    moving = pass_on(after(moving, halves[0]), back)
-    terms = []
-    for part in range(parts):
-        kept, away = halves[2 * part : 2 * part + 2]
-        received = swap(away, 1)
-        if dp_ways == 8:
-            sums = pair_sum(kept, received, (dp_rank // 2)[None], dp_ways // 2)
-            if last is not None:
-                sums = [sums[0]] + [after(each, last) for each in sums[1:]]
-            terms.append([sums[0]] + [swap(sums[bits], 2 * bits) for bits in range(1, 4)])
-            last = terms[-1][3]
-        else:
-            total = (kept.astype(jnp.float32) + received.astype(jnp.float32)).astype(jnp.bfloat16)
-            cores = [[each for each in range(dp_ways) if each % 2 == core] for core in range(2)]
-            terms.append(
-                [lax.psum_scatter(total, "dp", scatter_dimension=0, tiled=True, axis_index_groups=cores)]
-            )
-    for part in range(parts):
-        results = shampoo(
-            terms[part], left_stats, right_stats, master_blocks, part * part_size, results
-        )
-        while back < tp_ways and (back < part + 3 or part == parts - 1):
-            back += 1
-            moving, first_result = lax.optimization_barrier((moving, results[0]))
-            results = [first_result] + list(results[1:])
-            moving = pass_on(moving, back)
-    norm_input_gradient = moving
-    own_grads, left_new, right_new, new_blocks = results
 
     average_gradient = jnp.mean(norm_input_gradient, axis=-1, keepdims=True)
     average_projection = jnp.mean(
@@ -995,8 +1132,8 @@
     shared_local = jnp.concatenate(
         [
             jnp.sum(first_sums.reshape(2, 8, model_width), axis=1),
-            jnp.sum((early[4] + late[4]).reshape(2, 8, model_width), axis=1),
-            out_bias_grad[None],
+            jnp.sum((early[4][:16] + late[4][:16]).reshape(2, 8, model_width), axis=1),
+            jnp.sum(early[4][16:], axis=0)[None],
         ],
         0,
     )

time: 786 us -> 871 us (1.11)
  waiting for transfers between devices: 182 us -> 290 us
  Pallas kernels: 483 us -> 440 us
  starting transfers between devices: 31 us -> 55.8 us
    pallas_call x7 -> x10, Pallas kernels: 320 us -> 276 us  [the longest x4 112 us: shampoo(): pl.pallas_call(functools.partial(shampoo_kernel, count, len(grads), held)...]
    ppermute x16, waiting for transfers between devices: 0.04 us -> 41.5 us  [swap(): lax.ppermute(part, 'dp', [(each, each ^ bits) for each in range(ways)])]
    ppermute x3, waiting for transfers between devices: 0.01 us -> 35.9 us  [shards(): lax.ppermute(part, 'tp', [(each, (each + step) % tp_ways) for each in ran...]
    reduce_scatter x1, waiting for transfers between devices: 0.01 us -> 33.7 us  [shards(): lax.psum_scatter(small_rows(small, dp_ways), 'dp', scatter_dimension=0, t...]
    ppermute x9, starting transfers between devices: 5.62 us -> 34.6 us  [onward(): lax.ppermute(part, axis, [(each, (each + 1) % ways) for each in range(way...]
    reduce_scatter x1, waiting for transfers between devices: 14.9 us -> 0.01 us  [shards(): lax.psum_scatter(small_rows(shared_part.reshape(tp_ways, -1), tp_ways), '...]
    ppermute x9, waiting for transfers between devices: 167 us -> 178 us  [onward(): lax.ppermute(part, axis, [(each, (each + 1) % ways) for each in range(way...]
  transfers between devices with their start and end apart: 32 -> 32, of which waited for: 6 -> 10; matrix products, arithmetic and copies ran while one was open for 7% -> 4% of each run, Pallas kernels for 62% -> 43%
where the time goes in v3:
time: 871 us; the launch traced here: 861 us
  Pallas kernels  440 us (51%)
  waiting for transfers between devices  290 us (33%)
  starting transfers between devices  55.8 us (6%)
  other arithmetic  38 us (4%)
  local copies, waits for them, and re-layouts  22 us (3%)
  between operations  15.3 us (2%)
    ppermute x9, waiting for transfers between devices, onward(): lax.ppermute(part, axis, [(each, (each + 1) % ways) for each in range(way...  178 us
    pallas_call x4, Pallas kernels, shampoo(): pl.pallas_call(functools.partial(shampoo_kernel, count, len(grads), held)...  112 us
    pallas_call x4, Pallas kernels, weight_grads(): pl.pallas_call(functools.partial(weight_grad_kernel, tuple(steps)), in_sp...  91.4 us
    pallas_call x2, Pallas kernels, feed_back(): pl.pallas_call(functools.partial(feed_back_kernel, offsets, owned, first_...  73.4 us
    pallas_call x1, Pallas kernels, feed_forward(): pl.pallas_call(functools.partial(feed_kernel, offsets, owned), grid=(toke...  57.1 us
    ppermute x16, waiting for transfers between devices, swap(): lax.ppermute(part, 'dp', [(each, each ^ bits) for each in range(ways)])  41.5 us
    ppermute x3, waiting for transfers between devices, shards(): lax.ppermute(part, 'tp', [(each, (each + step) % tp_ways) for each in ran...  35.9 us
    ppermute x9, starting transfers between devices, onward(): lax.ppermute(part, axis, [(each, (each + 1) % ways) for each in range(way...  34.6 us
  transfers between devices with their start and end apart: 32, of which 10 were waited for; matrix products, arithmetic and copies ran while one was open for 4% of the time, Pallas kernels for 43%

profile of v3, /device:TPU:0, one launch (start us, length us, event | category | flops | bytes accessed | tf_op | source)
XLA Modules:
  0.0 860.6 jit_solution(2041615017916888144)
XLA Ops:
  17.7 47.7 %collective-permute-done.refs_1_ = bf16[512,2048]{1,0:T(8,128)(2,1)S(1)} collective-permute-done((bf16[512,2048]{1,0:T(8,128)(2,1)S(1)}, bf16[512,2048]{1,0:T(8,128)(2,1)S(1)}, u32[]{:S(2)}, u32[]{:S(2)}) %collective-permute-start) | collective-permute-done | bytes 2097184 | tf_op jit(solution)/shard_map/ppermute | solution.py:918
  66.7 48.6 %collective-permute-done.1.refs_2_ = bf16[512,2048]{1,0:T(8,128)(2,1)S(1)} collective-permute-done((bf16[512,2048]{1,0:T(8,128)(2,1)S(1)}, bf16[512,2048]{1,0:T(8,128)(2,1)S(1)}, u32[]{:S(2)}, u32[]{:S(2)}) %collective-permute-start.1) | collective-permute-done | bytes 2097184 | tf_op jit(solution)/shard_map/ppermute | solution.py:918
  115.3 47.7 %collective-permute-done.2.refs_3_ = bf16[512,2048]{1,0:T(8,128)(2,1)S(1)} collective-permute-done((bf16[512,2048]{1,0:T(8,128)(2,1)S(1)}, bf16[512,2048]{1,0:T(8,128)(2,1)S(1)}, u32[]{:S(2)}, u32[]{:S(2)}) %collective-permute-start.2) | collective-permute-done | bytes 2097184 | tf_op jit(solution)/shard_map/ppermute | solution.py:918
  175.9 35.8 %collective-permute-done.3 = bf16[8,384]{1,0:T(8,128)(2,1)S(1)} collective-permute-done((bf16[8,384]{1,0:T(8,128)(2,1)S(1)}, bf16[8,384]{1,0:T(8,128)(2,1)S(1)}, u32[]{:S(2)}, u32[]{:S(2)}) %collective-permute-start.3) | collective-permute-done | bytes 6176 | tf_op jit(solution)/shard_map/ppermute | solution.py:982
  212.7 33.0 %qkv.1 = (bf16[2048,1536]{1,0:T(8,128)(2,1)}, bf16[2048,2048]{1,0:T(8,128)(2,1)}, bf16[2048,2048]{1,0:T(8,128)(2,1)}, bf16[2048,2048]{1,0:T(8,128)(2,1)}, bf16[2...) custom-call(s32[1]{0:T(128)} %bitcast.1.rank_ref, bf16[512,2048]{1,0:T(8,128)(2,1)} %refs_0_.2, ...), custom_call_target="tpu_custom_call" | custom-call | flops 805306368 | bytes 2883584 | tf_op jit(solution)/shard_map/qkv/pallas_call | solution.py:203
  245.7 10.8 %attend.1 = (bf16[2048,512]{1,0:T(8,128)(2,1)}, bf16[512,2048]{1,0:T(8,128)(2,1)}) custom-call(bf16[2048,1536]{1,0:T(8,128)(2,1)} %get-tuple-element.105.query_ref.key_ref.value_ref, bf16[2048,1536]{1,0:T(8,128)(2,1)} %get-tuple-element.105.query_ref.key_ref.value_ref, bf16[2048,1536]{1,0:T(8,128)(2,1)} %get-tuple-element.105.query_ref.key_ref.value_ref, ...), custom_call_target="tpu_custom_call" | custom-call | flops 201326592 | bytes 524288 | tf_op jit(solution)/shard_map/attend/pallas_call | solution.py:254
  258.1 57.1 %feed.1 = (bf16[2048,2048]{1,0:T(8,128)(2,1)}, bf16[2048,2048]{1,0:T(8,128)(2,1)}, bf16[2048,2048]{1,0:T(8,128)(2,1)}) custom-call(bf16[2048,2048]{1,0:T(8,128)(2,1)} %get-tuple-element.104.x_ref, bf16[2048,512]{1,0:T(8,128)(2,1)} %get-tuple-element.106.attended_ref, bf16[49280,256]{1,0:T(8,128)(2,1)} %all-gather.2.cloned.1.call-done.refs_4_.blocks_ref.refs_8_.refs_6_, ...), custom_call_target="tpu_custom_call" | custom-call | flops 2415919104 | bytes 3670016 | tf_op jit(solution)/shard_map/feed/pallas_call | solution.py:394
  319.8 49.0 %feed_back.2 = (bf16[2048,2048]{1,0:T(8,128)(2,1)}, bf16[2048,512]{1,0:T(8,128)(2,1)}, bf16[2048,2048]{1,0:T(8,128)(2,1)}, f32[2048,2048]{1,0:T(8,128)}, f32[24,2048]{1,0:T(8,128)}, /*index=5*/f32[8,2048]{1,0:T(8,128)}) custom-call(s32[1]{0:T(128)} %bitcast.1.rank_ref, bf16[512,2048]{1,0:T(8,128)(2,1)} %refs_0_.3, ...), custom_call_target="tpu_custom_call" | custom-call | flops 1811939328 | bytes 3801088 | tf_op jit(solution)/shard_map/feed_back/pallas_call | solution.py:500
  371.1 24.3 %feed_back.3 = (bf16[2048,2048]{1,0:T(8,128)(2,1)}, bf16[2048,512]{1,0:T(8,128)(2,1)}, bf16[2048,2048]{1,0:T(8,128)(2,1)}, f32[2048,2048]{1,0:T(8,128)}, f32[24,2048]{1,0:T(8,128)}, /*index=5*/f32[8,2048]{1,0:T(8,128)}) custom-call(s32[1]{0:T(128)} %bitcast.1.rank_ref, ...), custom_call_target="tpu_custom_call", output_to_operand_aliasing={{0}: (9, {}), {1}: (10, {}), {2}: (11, {}), {3}: (12, {})} | custom-call | flops 603979776 | bytes 1966080 | tf_op jit(solution)/shard_map/feed_back/pallas_call | solution.py:500
  395.4 17.0 %attend_back.1.d_qkv_ref.refs_6_ = bf16[2048,1536]{1,0:T(8,128)(2,1)} custom-call(bf16[2048,1536]{1,0:T(8,128)(2,1)} %get-tuple-element.105.query_ref.key_ref.value_ref, bf16[2048,1536]{1,0:T(8,128)(2,1)} %get-tuple-element.105.query_ref.key_ref.value_ref, bf16[2048,1536]{1,0:T(8,128)(2,1)} %get-tuple-element.105.query_ref.key_ref.value_ref, ...), custom_call_target="tpu_custom_call" | custom-call | flops 469762048 | bytes 1048576 | tf_op jit(solution)/shard_map/attend_back/pallas_call | solution.py:321
  412.5 25.9 %qkv_back.1 = (bf16[2048,2048]{1,0:T(8,128)(2,1)}, f32[16,2048]{1,0:T(8,128)}, f32[8,1536]{1,0:T(8,128)}) custom-call(bf16[2048,1536]{1,0:T(8,128)(2,1)} %attend_back.1.d_qkv_ref.refs_6_, f32[2048,2048]{1,0:T(8,128)} %get-tuple-element.122.part_ref, bf16[2048,2048]{1,0:T(8,128)(2,1)} %get-tuple-element.112.refs_5_.refs_3_.tokens_ref, ...), custom_call_target="tpu_custom_call" | custom-call | flops 805306368 | bytes 2883584 | tf_op jit(solution)/shard_map/qkv_back/pallas_call | solution.py:571
  441.3 33.7 %reduce-scatter.6.cloned.1.call-done = f32[16,128]{1,0:T(8,128)} async-done(((f32[128,128]{1,0:T(8,128)}), f32[16,128]{1,0:T(8,128)}) %reduce-scatter.6.cloned.1.call-update) | async-done | bytes 8208 | tf_op jit(solution)/shard_map/reduce_scatter | solution.py:1154
  480.2 22.8 %weight_grads.6 = (bf16[24,256,256]{2,1,0:T(8,128)(2,1)}, bf16[24,256,256]{2,1,0:T(8,128)(2,1)}) custom-call(s32[1]{0:T(128)} %bitcast.12.core_ref, bf16[2048,2048]{1,0:T(8,128)(2,1)} %get-tuple-element.125.refs_0_, bf16[2048,2048]{1,0:T(8,128)(2,1)} %get-tuple-element.126.refs_1_, bf16[2048,2048]{1,0:T(8,128)(2,1)} %get-tuple-element.127.refs_2_, ...), custom_call_target="tpu_custom_call" | custom-call | flops 805306368 | bytes 1610612 | tf_op jit(solution)/shard_map/weight_grads/pallas_call | solution.py:687
  503.1 22.8 %weight_grads.4 = (bf16[24,256,256]{2,1,0:T(8,128)(2,1)}, bf16[24,256,256]{2,1,0:T(8,128)(2,1)}) custom-call(s32[1]{0:T(128)} %bitcast.12.core_ref, bf16[2048,2048]{1,0:T(8,128)(2,1)} %get-tuple-element.125.refs_0_, bf16[2048,2048]{1,0:T(8,128)(2,1)} %get-tuple-element.126.refs_1_, bf16[2048,2048]{1,0:T(8,128)(2,1)} %get-tuple-element.127.refs_2_, ...), custom_call_target="tpu_custom_call" | custom-call | flops 805306368 | bytes 1610612 | tf_op jit(solution)/shard_map/weight_grads/pallas_call | solution.py:687
  528.0 4.9 pair_sum.5
  532.9 22.8 %weight_grads.7 = (bf16[24,256,256]{2,1,0:T(8,128)(2,1)}, bf16[24,256,256]{2,1,0:T(8,128)(2,1)}) custom-call(s32[1]{0:T(128)} %bitcast.12.core_ref, bf16[2048,2048]{1,0:T(8,128)(2,1)} %get-tuple-element.125.refs_0_, bf16[2048,2048]{1,0:T(8,128)(2,1)} %get-tuple-element.126.refs_1_, bf16[2048,2048]{1,0:T(8,128)(2,1)} %get-tuple-element.127.refs_2_, ...), custom_call_target="tpu_custom_call" | custom-call | flops 805306368 | bytes 1610612 | tf_op jit(solution)/shard_map/weight_grads/pallas_call | solution.py:687
  559.4 5.0 pair_sum.4
  564.4 23.0 %weight_grads.5 = (bf16[24,256,256]{2,1,0:T(8,128)(2,1)}, bf16[24,256,256]{2,1,0:T(8,128)(2,1)}) custom-call(s32[1]{0:T(128)} %bitcast.12.core_ref, bf16[2048,2048]{1,0:T(8,128)(2,1)} %get-tuple-element.125.refs_0_, bf16[2048,2048]{1,0:T(8,128)(2,1)} %get-tuple-element.126.refs_1_, bf16[2048,2048]{1,0:T(8,128)(2,1)} %get-tuple-element.127.refs_2_, ...), custom_call_target="tpu_custom_call" | custom-call | flops 805306368 | bytes 1610612 | tf_op jit(solution)/shard_map/weight_grads/pallas_call | solution.py:687
  587.5 34.3 %collective-permute-done.9 = bf16[512,2048]{1,0:T(8,128)(2,1)} collective-permute-done((bf16[512,2048]{1,0:T(8,128)(2,1)}, bf16[512,2048]{1,0:T(8,128)(2,1)}, u32[]{:S(2)}, u32[]{:S(2)}) %collective-permute-start.9) | collective-permute-done | bytes 2097184 | tf_op jit(solution)/shard_map/ppermute | solution.py:918
  621.8 4.4 add_convert_fusion.1
  626.3 25.9 %collective-permute-start.11 = (bf16[512,2048]{1,0:T(8,128)(2,1)}, bf16[512,2048]{1,0:T(8,128)(2,1)}, u32[]{:S(2)}, u32[]{:S(2)}) collective-permute-start(bf16[512,2048]{1,0:T(8,128)(2,1)} %add_convert_fusion.1), channel_id=1, source_target_pairs={{0,1},{1,2},{2,3},{3,0},{4,5},{5,6},{6,7},{7,4},{8,9},{9,10},{10,1... | collective-permute-start | bytes 6291464 | tf_op jit(solution)/shard_map/ppermute | solution.py:918
  654.8 16.8 %collective-permute-done.18.refs_1_ = bf16[6,256,256]{2,1,0:T(8,128)(2,1)S(1)} collective-permute-done((bf16[6,256,256]{2,1,0:T(8,128)(2,1)}, bf16[6,256,256]{2,1,0:T(8,128)(2,1)S(1)}, u32[]{:S(2)}, u32[]{:S(2)}) %collective-permute-start.18) | collective-permute-done | bytes 786464 | tf_op jit(solution)/shard_map/ppermute | solution.py:923
  677.0 28.1 %shampoo.4 = (f32[24,256,256]{2,1,0:T(8,128)}, f32[24,256,256]{2,1,0:T(8,128)}, f32[24,256,256]{2,1,0:T(8,128)}, f32[24,256,256]{2,1,0:T(8,128)}) custom-call(s32[6]{0:T(128)} %get-tuple-element.154.places_ref, f32[6,256,256]{2,1,0:T(8,128)} %get-tuple-element.140.refs_0_, bf16[6,256,256]{2,1,0:T(8,128)(2,1)} %copy-done.8, ...), custom_call_target="tpu_custom_call" | custom-call | flops 1635778560 | bytes 737280 | tf_op jit(solution)/shard_map/shampoo/pallas_call | solution.py:875
  705.1 4.9 pair_sum.6
  710.0 27.9 %shampoo.5 = (f32[24,256,256]{2,1,0:T(8,128)}, f32[24,256,256]{2,1,0:T(8,128)}, f32[24,256,256]{2,1,0:T(8,128)}, f32[24,256,256]{2,1,0:T(8,128)}) custom-call(s32[6]{0:T(128)} %broadcast_select_fusion.3.places_ref, f32[6,256,256]{2,1,0:T(8,128)} %get-tuple-element.134.refs_0_, ...), custom_call_target="tpu_custom_call", output_to_operand_aliasing={{0}: (14, {}), {1}: (15, {}), {2}: (16, {}), {3}: (17, {})} | custom-call | flops 1635778560 | bytes 737280 | tf_op jit(solution)/shard_map/shampoo/pallas_call | solution.py:875
  738.0 4.4 add_convert_fusion
  751.6 5.0 pair_sum.7
  756.6 10.6 %collective-permute-done.22.refs_3_ = bf16[6,256,256]{2,1,0:T(8,128)(2,1)S(1)} collective-permute-done((bf16[6,256,256]{2,1,0:T(8,128)(2,1)}, bf16[6,256,256]{2,1,0:T(8,128)(2,1)S(1)}, u32[]{:S(2)}, u32[]{:S(2)}) %collective-permute-start.22) | collective-permute-done | bytes 786464 | tf_op jit(solution)/shard_map/ppermute | solution.py:923
  769.7 14.0 %collective-permute-done.26.refs_1_ = bf16[6,256,256]{2,1,0:T(8,128)(2,1)} collective-permute-done((bf16[6,256,256]{2,1,0:T(8,128)(2,1)}, bf16[6,256,256]{2,1,0:T(8,128)(2,1)}, u32[]{:S(2)}, u32[]{:S(2)}) %collective-permute-start.26) | collective-permute-done | bytes 786464 | tf_op jit(solution)/shard_map/ppermute | solution.py:923
  787.6 27.5 %shampoo.6 = (f32[24,256,256]{2,1,0:T(8,128)}, f32[24,256,256]{2,1,0:T(8,128)}, f32[24,256,256]{2,1,0:T(8,128)}, f32[24,256,256]{2,1,0:T(8,128)}) custom-call(s32[6]{0:T(128)} %get-tuple-element.171.places_ref, f32[6,256,256]{2,1,0:T(8,128)} %get-tuple-element.172.refs_0_, ...), custom_call_target="tpu_custom_call", output_to_operand_aliasing={{0}: (14, {}), {1}: (15, {}), {2}: (16, {}), {3}: (17, {})} | custom-call | flops 1635778560 | bytes 737280 | tf_op jit(solution)/shard_map/shampoo/pallas_call | solution.py:875
  815.2 27.9 %shampoo.7 = (f32[24,256,256]{2,1,0:T(8,128)}, f32[24,256,256]{2,1,0:T(8,128)}, f32[24,256,256]{2,1,0:T(8,128)}, f32[24,256,256]{2,1,0:T(8,128)}) custom-call(s32[6]{0:T(128)} %broadcast_select_fusion.1.places_ref, f32[6,256,256]{2,1,0:T(8,128)} %get-tuple-element.164.refs_0_, ...), custom_call_target="tpu_custom_call", output_to_operand_aliasing={{0}: (14, {}), {1}: (15, {}), {2}: (16, {}), {3}: (17, {})} | custom-call | flops 1635778560 | bytes 737280 | tf_op jit(solution)/shard_map/shampoo/pallas_call | solution.py:875
  846.8 7.1 fusion.7
  (193 shorter events, 74.3 us)
Async XLA Ops:
  7.2 162.6 %all-gather.2.cloned.1.call-start = ((), (), s32[]{:S(2)}) async-start(), calls=%async_computation.3 | async-start | bytes 28385280 | tf_op jit(solution)/shard_map/all_gather | solution.py:967
  14.0 460.9 %reduce-scatter.6.cloned.1.call-start = ((), (), s32[]{:S(2)}) async-start(), calls=%async_computation.5 | async-start | bytes 73728 | tf_op jit(solution)/shard_map/reduce_scatter | solution.py:1154
  14.7 50.7 %collective-permute-start = (bf16[512,2048]{1,0:T(8,128)(2,1)S(1)}, bf16[512,2048]{1,0:T(8,128)(2,1)S(1)}, u32[]{:S(2)}, u32[]{:S(2)}) collective-permute-start(bf16[512,2048]{1,0:T(8,128)(2,1)S(1)} %copy-done), channel_id=1, source_target_pairs={{0,1},{1,2},{2,3},{3,0},{4,5},{5,6},{6,7},{7,4},{8,9},{9,10},{10,1... | collective-permute-start | bytes 6291464 | tf_op jit(solution)/shard_map/ppermute | solution.py:918
  66.7 48.6 %collective-permute-start.1 = (bf16[512,2048]{1,0:T(8,128)(2,1)S(1)}, bf16[512,2048]{1,0:T(8,128)(2,1)S(1)}, u32[]{:S(2)}, u32[]{:S(2)}) collective-permute-start(bf16[512,2048]{1,0:T(8,128)(2,1)S(1)} %collective-permute-done.refs_1_), channel_id=1, source_target_pairs={{0,1},{1,2},{2,3},{3,0},{4,5},{5,6},{6,7},{7,4},{8,9},{9,10},{10,1... | collective-permute-start | bytes 6291464 | tf_op jit(solution)/shard_map/ppermute | solution.py:918
  115.3 47.7 %collective-permute-start.2 = (bf16[512,2048]{1,0:T(8,128)(2,1)S(1)}, bf16[512,2048]{1,0:T(8,128)(2,1)S(1)}, u32[]{:S(2)}, u32[]{:S(2)}) collective-permute-start(bf16[512,2048]{1,0:T(8,128)(2,1)S(1)} %collective-permute-done.1.refs_2_), channel_id=1, source_target_pairs={{0,1},{1,2},{2,3},{3,0},{4,5},{5,6},{6,7},{7,4},{8,9},{9,10},{10,1... | collective-permute-start | bytes 6291464 | tf_op jit(solution)/shard_map/ppermute | solution.py:918
  164.3 92.2 %collective-permute-start.6 = (bf16[512,2048]{1,0:T(8,128)(2,1)}, bf16[512,2048]{1,0:T(8,128)(2,1)}, u32[]{:S(2)}, u32[]{:S(2)}) collective-permute-start(bf16[512,2048]{1,0:T(8,128)(2,1)} %refs_0_.3), channel_id=1, source_target_pairs={{0,1},{1,2},{2,3},{3,0},{4,5},{5,6},{6,7},{7,4},{8,9},{9,10},{10,1... | collective-permute-start | bytes 6291464 | tf_op jit(solution)/shard_map/ppermute | solution.py:918
  170.7 41.1 %collective-permute-start.4 = (bf16[8,384]{1,0:T(8,128)(2,1)S(1)}, bf16[8,384]{1,0:T(8,128)(2,1)S(1)}, u32[]{:S(2)}, u32[]{:S(2)}) collective-permute-start(bf16[8,384]{1,0:T(8,128)(2,1)S(1)} %slice.75), channel_id=1, source_target_pairs={{0,2},{1,3},{2,0},{3,1},{4,6},{5,7},{6,4},{7,5},{8,10},{9,11},{10,... | collective-permute-start | bytes 18440 | tf_op jit(solution)/shard_map/ppermute | solution.py:982
  170.7 41.0 %collective-permute-start.3 = (bf16[8,384]{1,0:T(8,128)(2,1)S(1)}, bf16[8,384]{1,0:T(8,128)(2,1)S(1)}, u32[]{:S(2)}, u32[]{:S(2)}) collective-permute-start(bf16[8,384]{1,0:T(8,128)(2,1)S(1)} %slice.75), channel_id=1, source_target_pairs={{0,1},{1,2},{2,3},{3,0},{4,5},{5,6},{6,7},{7,4},{8,9},{9,10},{10,1... | collective-permute-start | bytes 18440 | tf_op jit(solution)/shard_map/ppermute | solution.py:982
  175.0 36.8 %collective-permute-start.5 = (bf16[8,384]{1,0:T(8,128)(2,1)S(1)}, bf16[8,384]{1,0:T(8,128)(2,1)S(1)}, u32[]{:S(2)}, u32[]{:S(2)}) collective-permute-start(bf16[8,384]{1,0:T(8,128)(2,1)S(1)} %slice.75), channel_id=1, source_target_pairs={{0,3},{1,0},{2,1},{3,2},{4,7},{5,4},{6,5},{7,6},{8,11},{9,8},{10,9... | collective-permute-start | bytes 18440 | tf_op jit(solution)/shard_map/ppermute | solution.py:982
  256.5 58.7 %collective-permute-start.7 = (bf16[512,2048]{1,0:T(8,128)(2,1)}, bf16[512,2048]{1,0:T(8,128)(2,1)S(1)}, u32[]{:S(2)}, u32[]{:S(2)}) collective-permute-start(bf16[512,2048]{1,0:T(8,128)(2,1)} %collective-permute-done.6.refs_1_), channel_id=1, source_target_pairs={{0,1},{1,2},{2,3},{3,0},{4,5},{5,6},{6,7},{7,4},{8,9},{9,10},{10,1... | collective-permute-start | bytes 6291464 | tf_op jit(solution)/shard_map/ppermute | solution.py:918
  316.6 53.2 %collective-permute-start.8 = (bf16[512,2048]{1,0:T(8,128)(2,1)}, bf16[512,2048]{1,0:T(8,128)(2,1)S(1)}, u32[]{:S(2)}, u32[]{:S(2)}) collective-permute-start(bf16[512,2048]{1,0:T(8,128)(2,1)} %copy-done.7), channel_id=1, source_target_pairs={{0,1},{1,2},{2,3},{3,0},{4,5},{5,6},{6,7},{7,4},{8,9},{9,10},{10,1... | collective-permute-start | bytes 6291464 | tf_op jit(solution)/shard_map/ppermute | solution.py:918
  441.2 344.4 %reduce-scatter.8.cloned.1.call-start = ((), (), s32[]{:S(2)}) async-start(), calls=%async_computation.6 | async-start | bytes 40960 | tf_op jit(solution)/shard_map/reduce_scatter | solution.py:1160
  476.4 370.3 %reduce-scatter.4.cloned.1.call-start = ((), (), s32[]{:S(2)}) async-start(), calls=%async_computation.4 | async-start | bytes 10485760 | tf_op jit(solution)/shard_map/reduce_scatter | solution.py:1030
  503.0 25.0 %collective-permute-start.12 = (bf16[24,256,256]{2,1,0:T(8,128)(2,1)}, bf16[24,256,256]{2,1,0:T(8,128)(2,1)}, u32[]{:S(2)}, u32[]{:S(2)}) collective-permute-start(bf16[24,256,256]{2,1,0:T(8,128)(2,1)} %get-tuple-element.139), channel_id=1, source_target_pairs={{0,4},{4,0},{8,12},{12,8},{16,20},{20,16},{24,28},{28,24},{1,5},{5... | collective-permute-start | bytes 9437192 | tf_op jit(solution)/shard_map/ppermute | solution.py:923
  525.9 31.9 %collective-permute-start.10 = (bf16[24,256,256]{2,1,0:T(8,128)(2,1)}, bf16[24,256,256]{2,1,0:T(8,128)(2,1)S(1)}, u32[]{:S(2)}, u32[]{:S(2)}) collective-permute-start(bf16[24,256,256]{2,1,0:T(8,128)(2,1)} %get-tuple-element.133), channel_id=1, source_target_pairs={{0,4},{4,0},{8,12},{12,8},{16,20},{20,16},{24,28},{28,24},{1,5},{5... | collective-permute-start | bytes 9437192 | tf_op jit(solution)/shard_map/ppermute | solution.py:923
  526.4 95.4 %collective-permute-start.9 = (bf16[512,2048]{1,0:T(8,128)(2,1)}, bf16[512,2048]{1,0:T(8,128)(2,1)}, u32[]{:S(2)}, u32[]{:S(2)}) collective-permute-start(bf16[512,2048]{1,0:T(8,128)(2,1)} %constant_dynamic-slice_fusion), channel_id=1, source_target_pairs={{0,1},{1,2},{2,3},{3,0},{4,5},{5,6},{6,7},{7,4},{8,9},{9,10},{10,1... | collective-permute-start | bytes 6291464 | tf_op jit(solution)/shard_map/ppermute | solution.py:918
  555.7 118.4 %collective-permute-start.13 = (bf16[24,256,256]{2,1,0:T(8,128)(2,1)}, bf16[24,256,256]{2,1,0:T(8,128)(2,1)}, u32[]{:S(2)}, u32[]{:S(2)}) collective-permute-start(bf16[24,256,256]{2,1,0:T(8,128)(2,1)} %get-tuple-element.143), channel_id=1, source_target_pairs={{0,4},{4,0},{8,12},{12,8},{16,20},{20,16},{24,28},{28,24},{1,5},{5... | collective-permute-start | bytes 9437192 | tf_op jit(solution)/shard_map/ppermute | solution.py:923
  555.8 98.9 %collective-permute-start.14 = (bf16[6,256,256]{2,1,0:T(8,128)(2,1)}, bf16[6,256,256]{2,1,0:T(8,128)(2,1)}, u32[]{:S(2)}, u32[]{:S(2)}) collective-permute-start(bf16[6,256,256]{2,1,0:T(8,128)(2,1)} %get-tuple-element.146), channel_id=1, source_target_pairs={{0,24},{4,28},{8,16},{12,20},{16,8},{20,12},{24,0},{28,4},{1,25},{... | collective-permute-start | bytes 2359304 | tf_op jit(solution)/shard_map/ppermute | solution.py:923
  626.3 111.7 %collective-permute-start.11 = (bf16[512,2048]{1,0:T(8,128)(2,1)}, bf16[512,2048]{1,0:T(8,128)(2,1)}, u32[]{:S(2)}, u32[]{:S(2)}) collective-permute-start(bf16[512,2048]{1,0:T(8,128)(2,1)} %add_convert_fusion.1), channel_id=1, source_target_pairs={{0,1},{1,2},{2,3},{3,0},{4,5},{5,6},{6,7},{7,4},{8,9},{9,10},{10,1... | collective-permute-start | bytes 6291464 | tf_op jit(solution)/shard_map/ppermute | solution.py:918
  652.1 19.4 %collective-permute-start.18 = (bf16[6,256,256]{2,1,0:T(8,128)(2,1)}, bf16[6,256,256]{2,1,0:T(8,128)(2,1)S(1)}, u32[]{:S(2)}, u32[]{:S(2)}) collective-permute-start(bf16[6,256,256]{2,1,0:T(8,128)(2,1)} %get-tuple-element.155), channel_id=1, source_target_pairs={{0,8},{4,12},{8,0},{12,4},{16,24},{20,28},{24,16},{28,20},{1,9},{5... | collective-permute-start | bytes 2359304 | tf_op jit(solution)/shard_map/ppermute | solution.py:923
  653.3 19.6 %collective-permute-start.19 = (bf16[6,256,256]{2,1,0:T(8,128)(2,1)}, bf16[6,256,256]{2,1,0:T(8,128)(2,1)}, u32[]{:S(2)}, u32[]{:S(2)}) collective-permute-start(bf16[6,256,256]{2,1,0:T(8,128)(2,1)} %get-tuple-element.156), channel_id=1, source_target_pairs={{0,16},{4,20},{8,24},{12,28},{16,0},{20,4},{24,8},{28,12},{1,17},{... | collective-permute-start | bytes 2359304 | tf_op jit(solution)/shard_map/ppermute | solution.py:923
  654.8 96.9 %collective-permute-start.21 = (bf16[24,256,256]{2,1,0:T(8,128)(2,1)}, bf16[24,256,256]{2,1,0:T(8,128)(2,1)}, u32[]{:S(2)}, u32[]{:S(2)}) collective-permute-start(bf16[24,256,256]{2,1,0:T(8,128)(2,1)} %get-tuple-element.163), channel_id=1, source_target_pairs={{0,4},{4,0},{8,12},{12,8},{16,20},{20,16},{24,28},{28,24},{1,5},{5... | collective-permute-start | bytes 9437192 | tf_op jit(solution)/shard_map/ppermute | solution.py:923
  671.5 38.5 %collective-permute-start.17 = (bf16[6,256,256]{2,1,0:T(8,128)(2,1)}, bf16[6,256,256]{2,1,0:T(8,128)(2,1)}, u32[]{:S(2)}, u32[]{:S(2)}) collective-permute-start(bf16[6,256,256]{2,1,0:T(8,128)(2,1)} %get-tuple-element.153), channel_id=1, source_target_pairs={{0,16},{4,20},{8,24},{12,28},{16,0},{20,4},{24,8},{28,12},{1,17},{... | collective-permute-start | bytes 2359304 | tf_op jit(solution)/shard_map/ppermute | solution.py:923
  672.9 37.1 %collective-permute-start.16 = (bf16[6,256,256]{2,1,0:T(8,128)(2,1)}, bf16[6,256,256]{2,1,0:T(8,128)(2,1)}, u32[]{:S(2)}, u32[]{:S(2)}) collective-permute-start(bf16[6,256,256]{2,1,0:T(8,128)(2,1)} %get-tuple-element.151), channel_id=1, source_target_pairs={{0,8},{4,12},{8,0},{12,4},{16,24},{20,28},{24,16},{28,20},{1,9},{5... | collective-permute-start | bytes 2359304 | tf_op jit(solution)/shard_map/ppermute | solution.py:923
  674.2 35.9 %collective-permute-start.15 = (bf16[6,256,256]{2,1,0:T(8,128)(2,1)}, bf16[6,256,256]{2,1,0:T(8,128)(2,1)}, u32[]{:S(2)}, u32[]{:S(2)}) collective-permute-start(bf16[6,256,256]{2,1,0:T(8,128)(2,1)} %get-tuple-element.147), channel_id=1, source_target_pairs={{0,24},{4,28},{8,16},{12,20},{16,8},{20,12},{24,0},{28,4},{1,25},{... | collective-permute-start | bytes 2359304 | tf_op jit(solution)/shard_map/ppermute | solution.py:923
  742.4 100.7 %collective-permute-start.20 = (bf16[512,2048]{1,0:T(8,128)(2,1)}, bf16[512,2048]{1,0:T(8,128)(2,1)}, u32[]{:S(2)}, u32[]{:S(2)}) collective-permute-start(bf16[512,2048]{1,0:T(8,128)(2,1)} %add_convert_fusion), channel_id=1, source_target_pairs={{0,1},{1,2},{2,3},{3,0},{4,5},{5,6},{6,7},{7,4},{8,9},{9,10},{10,1... | collective-permute-start | bytes 6291464 | tf_op jit(solution)/shard_map/ppermute | solution.py:918
  745.6 21.6 %collective-permute-start.22 = (bf16[6,256,256]{2,1,0:T(8,128)(2,1)}, bf16[6,256,256]{2,1,0:T(8,128)(2,1)S(1)}, u32[]{:S(2)}, u32[]{:S(2)}) collective-permute-start(bf16[6,256,256]{2,1,0:T(8,128)(2,1)} %get-tuple-element.148), channel_id=1, source_target_pairs={{0,24},{4,28},{8,16},{12,20},{16,8},{20,12},{24,0},{28,4},{1,25},{... | collective-permute-start | bytes 2359304 | tf_op jit(solution)/shard_map/ppermute | solution.py:923
  747.3 36.4 %collective-permute-start.26 = (bf16[6,256,256]{2,1,0:T(8,128)(2,1)}, bf16[6,256,256]{2,1,0:T(8,128)(2,1)}, u32[]{:S(2)}, u32[]{:S(2)}) collective-permute-start(bf16[6,256,256]{2,1,0:T(8,128)(2,1)} %get-tuple-element.174), channel_id=1, source_target_pairs={{0,8},{4,12},{8,0},{12,4},{16,24},{20,28},{24,16},{28,20},{1,9},{5... | collective-permute-start | bytes 2359304 | tf_op jit(solution)/shard_map/ppermute | solution.py:923
  749.2 38.4 %collective-permute-start.27 = (bf16[6,256,256]{2,1,0:T(8,128)(2,1)}, bf16[6,256,256]{2,1,0:T(8,128)(2,1)}, u32[]{:S(2)}, u32[]{:S(2)}) collective-permute-start(bf16[6,256,256]{2,1,0:T(8,128)(2,1)} %get-tuple-element.176), channel_id=1, source_target_pairs={{0,16},{4,20},{8,24},{12,28},{16,0},{20,4},{24,8},{28,12},{1,17},{... | collective-permute-start | bytes 2359304 | tf_op jit(solution)/shard_map/ppermute | solution.py:923
  767.2 47.9 %collective-permute-start.25 = (bf16[6,256,256]{2,1,0:T(8,128)(2,1)}, bf16[6,256,256]{2,1,0:T(8,128)(2,1)}, u32[]{:S(2)}, u32[]{:S(2)}) collective-permute-start(bf16[6,256,256]{2,1,0:T(8,128)(2,1)} %get-tuple-element.170), channel_id=1, source_target_pairs={{0,24},{4,28},{8,16},{12,20},{16,8},{20,12},{24,0},{28,4},{1,25},{... | collective-permute-start | bytes 2359304 | tf_op jit(solution)/shard_map/ppermute | solution.py:923
  768.9 46.3 %collective-permute-start.24 = (bf16[6,256,256]{2,1,0:T(8,128)(2,1)}, bf16[6,256,256]{2,1,0:T(8,128)(2,1)}, u32[]{:S(2)}, u32[]{:S(2)}) collective-permute-start(bf16[6,256,256]{2,1,0:T(8,128)(2,1)} %get-tuple-element.168), channel_id=1, source_target_pairs={{0,16},{4,20},{8,24},{12,28},{16,0},{20,4},{24,8},{28,12},{1,17},{... | collective-permute-start | bytes 2359304 | tf_op jit(solution)/shard_map/ppermute | solution.py:923
  783.7 31.5 %collective-permute-start.23 = (bf16[6,256,256]{2,1,0:T(8,128)(2,1)}, bf16[6,256,256]{2,1,0:T(8,128)(2,1)}, u32[]{:S(2)}, u32[]{:S(2)}) collective-permute-start(bf16[6,256,256]{2,1,0:T(8,128)(2,1)} %get-tuple-element.166), channel_id=1, source_target_pairs={{0,8},{4,12},{8,0},{12,4},{16,24},{20,28},{24,16},{28,20},{1,9},{5... | collective-permute-start | bytes 2359304 | tf_op jit(solution)/shard_map/ppermute | solution.py:923
  (23 other events, 780.8 us)
Sparse Core Ops, SparseCore 0:
  14.1 128.2 all-gather.1
  441.3 33.5 reduce-scatter.5
  477.3 18.8 reduce-scatter.7
  498.4 216.2 reduce-scatter.3

commit v4 on v3

--- a/solution.py
+++ b/solution.py
@@ -45,7 +45,6 @@
 
 
 EXTRA_ROWS = 16
-COST_PART = 16
 FEED_BACK_TILE = 512
 VMEM_LIMIT = 60 << 20
 NN = (((1,), (0,)), ((), ()))
@@ -59,12 +58,6 @@
 
 def kernel_params():
     return pltpu.CompilerParams(vmem_limit_bytes=VMEM_LIMIT)
-
-
-def kernel_cost(flops, bytes_accessed, transcendentals):
-    return pl.CostEstimate(
-        flops=flops // COST_PART, bytes_accessed=bytes_accessed // COST_PART, transcendentals=transcendentals
-    )
 
 
 def block_row(index, owned, size):
@@ -223,7 +216,7 @@
         ),
         out_shape=[jax.ShapeDtypeStruct((tokens, cols), jnp.bfloat16), tall, wide, tall, wide, single, single],
         compiler_params=kernel_params(),
-        cost_estimate=kernel_cost(
+        cost_estimate=pl.CostEstimate(
             flops=2 * tokens * width * cols, bytes_accessed=tokens * (4 * width + cols) * 2 + width * cols * 2, transcendentals=0
         ),
         name="qkv",
@@ -270,7 +263,7 @@
             jax.ShapeDtypeStruct((heads * HD, packs * length), jnp.bfloat16),
         ],
         compiler_params=kernel_params(),
-        cost_estimate=kernel_cost(
+        cost_estimate=pl.CostEstimate(
             flops=packs * heads * length * length * HD * 3, bytes_accessed=packs * length * heads * HD * 8, transcendentals=0
         ),
         name="attend",
@@ -335,7 +328,7 @@
         out_shape=jax.ShapeDtypeStruct((packs * length, 3 * heads * HD), jnp.bfloat16),
         scratch_shapes=[pltpu.VMEM((length, HD), jnp.float32)] * 2,
         compiler_params=kernel_params(),
-        cost_estimate=kernel_cost(
+        cost_estimate=pl.CostEstimate(
             flops=packs * heads * length * length * HD * 7, bytes_accessed=packs * length * heads * HD * 16, transcendentals=0
         ),
         name="attend_back",
@@ -416,7 +409,7 @@
             pltpu.SemaphoreType.DMA((inner * outer + head_cols // size * outer,)),
         ],
         compiler_params=kernel_params(),
-        cost_estimate=kernel_cost(
+        cost_estimate=pl.CostEstimate(
             flops=2 * tokens * width * (2 * hidden_units + head_cols), bytes_accessed=tokens * width * 10 + width * hidden_units * 4, transcendentals=0
         ),
         name="feed",
@@ -478,7 +471,7 @@
         cols = pl.ds(col * size, size)
         scaled = (tokens_ref[:, cols].astype(jnp.float32) - mean) * inverse
         second = contract(d_hidden_ref[...], w_in[cols, :], NT)
-        dz_ref[:, cols] = second * norm_ref[2:3, cols]
+        dz_ref[:, cols] = (second * norm_ref[2:3, cols]).astype(jnp.bfloat16)
         norm_sums[0:8, cols] += column_sum(second * scaled)
         norm_sums[8:16, cols] += column_sum(second)
 
@@ -524,13 +517,13 @@
             jax.ShapeDtypeStruct((tokens, width), jnp.bfloat16),
             jax.ShapeDtypeStruct((tokens, head_cols), jnp.bfloat16),
             jax.ShapeDtypeStruct((tokens, hidden_units), jnp.bfloat16),
-            jax.ShapeDtypeStruct((tokens, width), jnp.float32),
+            jax.ShapeDtypeStruct((tokens, width), jnp.bfloat16),
             jax.ShapeDtypeStruct((24, width), jnp.float32),
             jax.ShapeDtypeStruct((8, hidden_units), jnp.float32),
         ],
         input_output_aliases={1 + count + 7 + index: index for index in range(len(priors))},
         compiler_params=kernel_params(),
-        cost_estimate=kernel_cost(
+        cost_estimate=pl.CostEstimate(
             flops=2 * rows * width * (2 * hidden_units + head_cols), bytes_accessed=rows * width * 14 + width * hidden_units * 4, transcendentals=0
         ),
         name="feed_back",
@@ -555,7 +548,7 @@
         cols = pl.ds(col * size, size)
         scaled = (tokens_ref[:, cols].astype(jnp.float32) - mean) * inverse
         first = contract(d_qkv_ref[...], w_qkv[cols, :], NT)
-        dz_ref[:, cols] = (part_ref[:, cols] + first * norm_ref[0:1, cols]).astype(jnp.bfloat16)
+        dz_ref[:, cols] = (part_ref[:, cols].astype(jnp.float32) + first * norm_ref[0:1, cols]).astype(jnp.bfloat16)
         norm_sums[0:8, cols] += column_sum(first * scaled)
         norm_sums[8:16, cols] += column_sum(first)
 
@@ -585,25 +578,27 @@
             pltpu.SemaphoreType.DMA((outer * (qkv_cols // size),)),
         ],
         compiler_params=kernel_params(),
-        cost_estimate=kernel_cost(
+        cost_estimate=pl.CostEstimate(
             flops=2 * tokens * width * qkv_cols, bytes_accessed=tokens * width * 11, transcendentals=0
         ),
         name="qkv_back",
     )(d_qkv, dz_part, group_tokens, mean, inverse, blocks, norm_params)
 
 
-def weight_grad_kernel(steps, core_ref, *refs):
-    lefts, rights, outs = refs[:4], refs[4:7], refs[7:9]
-    rows_held, rights_held, (results, left_sems, right_sems, sems) = refs[9], refs[10:13], refs[13:]
+def weight_grad_kernel(steps, waits, core_ref, *refs):
+    lefts, rights, refs = refs[:4], refs[4:7], refs[7 + waits :]
+    outs, rows_held, rights_held = refs[:2], refs[2], refs[3:6]
+    results, left_sems, right_sems, sems = refs[6:]
     size = results.shape[-1]
     core = core_ref[0]
+    depth = rows_held.shape[0]
 
     def left_copy(index):
         left, first, rows, _, _, _ = steps[index]
         return pltpu.make_async_copy(
             lefts[left].at[pl.ds(first, rows), :],
-            rows_held.at[index % 2, pl.ds(0, rows), :],
-            left_sems.at[index % 2],
+            rows_held.at[index % depth, pl.ds(0, rows), :],
+            left_sems.at[index % depth],
         )
 
     def right_copy(right, first):
@@ -622,13 +617,15 @@
     for step in steps:
         if step[3:5] not in order:
             order.append(step[3:5])
-    left_copy(0).start()
-    for right in order:
+    right_copy(*order[0]).start()
+    for index in range(min(depth - 1, len(steps))):
+        left_copy(index).start()
+    for right in order[1:]:
         right_copy(*right).start()
     for index, (left, first, rows, right, right_first, places) in enumerate(steps):
         left_copy(index).wait()
-        if index + 1 < len(steps):
-            left_copy(index + 1).start()
+        if index + depth - 1 < len(steps):
+            left_copy(index + depth - 1).start()
         if all(step[3:5] != (right, right_first) for step in steps[:index]):
             right_copy(right, right_first).wait()
         if index >= 2:
@@ -636,7 +633,7 @@
         held = rights_held[right]
         cols = held.shape[1] // size
         for col in range(cols):
-            result = contract(rows_held[index % 2, :rows, :], held[:, col * size : (col + 1) * size], NN)
+            result = contract(rows_held[index % depth, :rows, :], held[:, col * size : (col + 1) * size], NN)
             for row in range(rows // size):
                 results[index % 2, row * cols + col] = result[row * size : (row + 1) * size].astype(jnp.bfloat16)
         for number, (owner, place) in enumerate(places):
@@ -652,7 +649,7 @@
         finish(index)
 
 
-def weight_grads(part, parts, lefts, rights, firsts, core, owned, dp_ways, size):
+def weight_grads(part, parts, lefts, rights, firsts, core, owned, dp_ways, size, waits):
     first_normed, second_normed, activated, attended = lefts
     d_hidden, seed, d_qkv = rights
     tokens = d_qkv.shape[0]
@@ -685,24 +682,24 @@
     half = jax.ShapeDtypeStruct((dp_ways // 2 * part_size, size, size), jnp.bfloat16)
     flops = 2 * tokens * size * size * dp_ways * part_size
     return pl.pallas_call(
-        functools.partial(weight_grad_kernel, tuple(steps)),
-        in_specs=[pl.BlockSpec(memory_space=pltpu.SMEM)] + [anywhere] * 7,
+        functools.partial(weight_grad_kernel, tuple(steps), len(waits)),
+        in_specs=[pl.BlockSpec(memory_space=pltpu.SMEM)] + [anywhere] * (7 + len(waits)),
         out_specs=[anywhere] * 2,
         out_shape=[half] * 2,
         scratch_shapes=[
-            pltpu.VMEM((2, max(step[2] for step in steps), tokens), jnp.bfloat16),
+            pltpu.VMEM((4, max(step[2] for step in steps), tokens), jnp.bfloat16),
             pltpu.VMEM((tokens, span * size), jnp.bfloat16),
             pltpu.VMEM((tokens, span * size), jnp.bfloat16),
             pltpu.VMEM((tokens, d_qkv.shape[1]), jnp.bfloat16),
             pltpu.VMEM((2, most, size, size), jnp.bfloat16),
-            pltpu.SemaphoreType.DMA((2,)),
+            pltpu.SemaphoreType.DMA((4,)),
             pltpu.SemaphoreType.DMA((3,)),
             pltpu.SemaphoreType.DMA((2, most)),
         ],
         compiler_params=kernel_params(),
-        cost_estimate=kernel_cost(flops=flops, bytes_accessed=flops // 500, transcendentals=0),
+        cost_estimate=pl.CostEstimate(flops=flops, bytes_accessed=flops // 500, transcendentals=0),
         name="weight_grads",
-    )(core, *lefts, *rights)
+    )(core, *lefts, *rights, *waits)
 
 
 def pair_sum_kernel(chip_ref, *refs):
@@ -730,7 +727,7 @@
         ),
         out_shape=[jax.ShapeDtypeStruct((part, size, size), dtype) for dtype in dtypes],
         compiler_params=kernel_params(),
-        cost_estimate=kernel_cost(flops=rows * size * size, bytes_accessed=rows * size * size * 6, transcendentals=0),
+        cost_estimate=pl.CostEstimate(flops=rows * size * size, bytes_accessed=rows * size * size * 6, transcendentals=0),
         name="pair_sum",
     )(chip, *([kept] * chips), *([received] * chips))
 
@@ -858,7 +855,7 @@
             copy.wait()
 
 
-def shampoo(grads, left_stats, right_stats, master_blocks, places, priors):
+def shampoo(grads, left_stats, right_stats, master_blocks, places, priors, waits=()):
     part, size, _ = grads[0].shape
     count = next(each for each in (3, 2, 1) if part % each == 0)
     own = pl.BlockSpec((count, size, size), lambda step, places: (step, 0, 0))
@@ -873,13 +870,13 @@
     wide = pltpu.VMEM((2 * count, 2 * size, size), jnp.bfloat16)
     plain = pltpu.VMEM((2 * count, size, size), jnp.bfloat16)
     return pl.pallas_call(
-        functools.partial(shampoo_kernel, count, len(grads), held),
+        functools.partial(shampoo_kernel, count, len(grads), held + len(waits)),
         grid_spec=pltpu.PrefetchScalarGridSpec(
             num_scalar_prefetch=1,
             grid=(part // count,),
             in_specs=[own] * len(grads)
             + [single(block) for block in range(count)] * 3
-            + [anywhere] * held,
+            + [anywhere] * (held + len(waits)),
             out_specs=[anywhere] * 4,
             scratch_shapes=[
                 pltpu.VMEM((2, 4, count, size, size), jnp.float32),
@@ -895,7 +892,7 @@
         out_shape=[result] * 4,
         input_output_aliases={first_prior + index: index for index in range(held)},
         compiler_params=kernel_params(),
-        cost_estimate=kernel_cost(
+        cost_estimate=pl.CostEstimate(
             flops=part * 130 * 2 * size**3, bytes_accessed=part * size * size * 30, transcendentals=0
         ),
         name="shampoo",
@@ -906,6 +903,7 @@
         *([right_stats] * count),
         *([master_blocks] * count),
         *priors,
+        *waits,
     )
 
 
@@ -1008,7 +1006,7 @@
 
     rank = tp_rank.astype(jnp.int32)[None]
     cosines, sines = turn_tables(pack_len, 128)
-    cotangent_parts = [cotangent, onward(after(cotangent, token_parts[-1]), "tp")]
+    cotangent_parts = [cotangent, onward(after(cotangent, token_parts[-1], shared_all), "tp")]
     qkv16, first_turned, second_normed, second_turned, group_tokens, mean, inverse = project_qkv(
         token_parts, rank, blocks, owned, norm_params, bias_qkv, cosines, sines, heads_dev
     )
@@ -1042,6 +1040,43 @@
         total = moving.astype(jnp.float32) + dz_rows(back).astype(jnp.float32)
         return total if back == tp_ways else onward(total.astype(jnp.bfloat16), "tp")
 
+    shared_local = jnp.concatenate(
+        [
+            jnp.sum(first_sums.reshape(2, 8, model_width), axis=1),
+            jnp.sum((early[4][:16] + late[4][:16]).reshape(2, 8, model_width), axis=1),
+            jnp.sum(early[4][16:], axis=0)[None],
+        ],
+        0,
+    )
+    vecs_local = jnp.concatenate(
+        [
+            jnp.sum(qkv_sums, axis=0).reshape(3 * heads_dev, HD),
+            jnp.sum(early[5] + late[5], axis=0).reshape(ff_dev // HD, HD),
+        ],
+        0,
+    )
+    small = jnp.concatenate(
+        [
+            shared_local.reshape(5, dp_ways, -1).transpose(1, 0, 2).reshape(dp_ways, -1),
+            vecs_local.reshape(vec_rows, dp_ways, -1).transpose(1, 0, 2).reshape(dp_ways, -1),
+        ],
+        1,
+    )
+    small_in = after(small_rows(small, dp_ways), branch)
+    small_own = lax.psum_scatter(small_in, "dp", scatter_dimension=0, tiled=True).reshape(-1)
+    output = (
+        valid_own[:, None]
+        * (owned_input_rows + branch.astype(jnp.float32) + norm_params[4] + norm_params[5])
+    ).astype(jnp.bfloat16)
+
+    shared_size = 5 * model_width // dp_ways
+    own_vec_grads = small_own[shared_size : small.shape[1]].reshape(vec_rows, HD // dp_ways)
+    shared_part = small_own[:shared_size].reshape(5, tp_ways, -1).transpose(1, 0, 2)
+    shared_own = lax.psum_scatter(
+        small_rows(shared_part.reshape(tp_ways, -1), tp_ways), "tp", scatter_dimension=0, tiled=True
+    ).reshape(-1)
+    shared_own = shared_own[: shared_size // tp_ways].reshape(5, -1)
+    shared_grads = jnp.concatenate([shared_own, shared_own[4:]], 0)
     dp_rank = lax.axis_index("dp").astype(jnp.int32)
     lefts = (first_turned, second_turned, active_turned, attended_turned)
     d_qkv_late, first_rows = lax.optimization_barrier((d_qkv16, dz_rows(1)))
@@ -1064,23 +1099,28 @@
         part_size = owned // parts
         span = block_rows // parts
         sums = []
+        terms = []
+        ready = []
+
+        def send_on(part):
+            if part:
+                sums[part] = [sums[part][0]] + [after(each, terms[-1][3]) for each in sums[part][1:]]
+                ready.append(sums[part][3])
+            terms.append([sums[part][0]] + [swap(sums[part][bits], 2 * bits) for bits in range(1, 4)])
+
         for part in range(parts):
-            core = (dp_rank % 2)[None]
-            if part >= 2:
-                core = after(core, sums[part - 2][0])
+            waits = (sums[part - 2][0],) if part >= 2 else ()
+            if part == parts - 1:
+                send_on(0)
+                waits += tuple(terms[0][1:])
             kept, away = weight_grads(
-                part, parts, lefts, rights, firsts, core, owned, dp_ways, block_size
+                part, parts, lefts, rights, firsts, (dp_rank % 2)[None], owned, dp_ways, block_size, waits
             )
             sums.append(pair_sum(kept, swap(away, 1), (dp_rank // 2)[None], dp_ways // 2))
         moving = pass_on(after(moving, kept), back)
         back += 1
-        terms = []
-        ready = []
-        for part in range(parts):
-            if part:
-                sums[part] = [sums[part][0]] + [after(each, terms[-1][3]) for each in sums[part][1:]]
-                ready.append(sums[part][3])
-            terms.append([sums[part][0]] + [swap(sums[part][bits], 2 * bits) for bits in range(1, 4)])
+        for part in range(1, parts):
+            send_on(part)
         count = jnp.arange(part_size, dtype=jnp.int32)
         in_qkv = dp_rank * owned < first_out
         for part in range(parts):
@@ -1089,9 +1129,18 @@
                 part * part_size + count,
                 count // span * block_rows + part * span + count % span,
             )
+            waits = []
             if part < parts - 1:
-                places = after(places, ready[part])
-            results = shampoo(terms[part], left_stats, right_stats, master_blocks, places, results)
+                waits.append(ready[part])
+            if part == 1:
+                waits.append(small_in)
+            if part == 2:
+                waits.append(small_own)
+            if part == 3:
+                waits += [output, shared_own]
+            results = shampoo(
+                terms[part], left_stats, right_stats, master_blocks, places, results, waits
+            )
             if part % 2 == 1 and back <= tp_ways:
                 moving, first_result = lax.optimization_barrier((moving, results[0]))
                 results = [first_result] + list(results[1:])
@@ -1116,11 +1165,6 @@
         back += 1
     norm_input_gradient = moving
     own_grads, left_new, right_new, new_blocks = results
-    output = (
-        valid_own[:, None]
-        * (owned_input_rows + branch.astype(jnp.float32) + norm_params[4] + norm_params[5])
-    ).astype(jnp.bfloat16)
-
     average_gradient = jnp.mean(norm_input_gradient, axis=-1, keepdims=True)
     average_projection = jnp.mean(
         norm_input_gradient * owned_centred_scaled, axis=-1, keepdims=True
@@ -1129,39 +1173,6 @@
         norm_input_gradient - average_gradient - owned_centred_scaled * average_projection
     )
 
-    shared_local = jnp.concatenate(
-        [
-            jnp.sum(first_sums.reshape(2, 8, model_width), axis=1),
-            jnp.sum((early[4][:16] + late[4][:16]).reshape(2, 8, model_width), axis=1),
-            jnp.sum(early[4][16:], axis=0)[None],
-        ],
-        0,
-    )
-    vecs_local = jnp.concatenate(
-        [
-            jnp.sum(qkv_sums, axis=0).reshape(3 * heads_dev, HD),
-            jnp.sum(early[5] + late[5], axis=0).reshape(ff_dev // HD, HD),
-        ],
-        0,
-    )
-    small = jnp.concatenate(
-        [
-            shared_local.reshape(5, dp_ways, -1).transpose(1, 0, 2).reshape(dp_ways, -1),
-            vecs_local.reshape(vec_rows, dp_ways, -1).transpose(1, 0, 2).reshape(dp_ways, -1),
-        ],
-        1,
-    )
-    small_own = lax.psum_scatter(
-        small_rows(small, dp_ways), "dp", scatter_dimension=0, tiled=True
-    ).reshape(-1)
-    shared_size = 5 * model_width // dp_ways
-    own_vec_grads = small_own[shared_size : small.shape[1]].reshape(vec_rows, HD // dp_ways)
-    shared_part = small_own[:shared_size].reshape(5, tp_ways, -1).transpose(1, 0, 2)
-    shared_own = lax.psum_scatter(
-        small_rows(shared_part.reshape(tp_ways, -1), tp_ways), "tp", scatter_dimension=0, tiled=True
-    ).reshape(-1)
-    shared_own = shared_own[: shared_size // tp_ways].reshape(5, -1)
-    shared_grads = jnp.concatenate([shared_own, shared_own[4:]], 0)
     local_stat_new = DECAY * local_vec_stats + own_vec_grads * own_vec_grads
     local_new = local_vecs - RATE_VEC * own_vec_grads * lax.rsqrt(local_stat_new)
     shared_stat_new = DECAY * shared_vec_stats + shared_grads * shared_grads

time: 871 us -> 705 us (0.81)
  waiting for transfers between devices: 290 us -> 156 us
  starting transfers between devices: 55.8 us -> 31.6 us
  Pallas kernels: 440 us -> 425 us
    ppermute x9, waiting for transfers between devices: 178 us -> 97.4 us  [onward(): lax.ppermute(part, axis, [(each, (each + 1) % ways) for each in range(way...]
    reduce_scatter x1, waiting for transfers between devices: 33.7 us -> 0.01 us  [shards(): lax.psum_scatter(small_in, 'dp', scatter_dimension=0, tiled=True)]
    all_gather x1, waiting for transfers between devices: 0.01 us -> 25.8 us  [shards(): blocks = lax.all_gather(rows16, 'dp', axis=0, tiled=True)]
    ppermute x9, starting transfers between devices: 34.6 us -> 10.7 us  [onward(): lax.ppermute(part, axis, [(each, (each + 1) % ways) for each in range(way...]
    ppermute x16, waiting for transfers between devices: 41.5 us -> 18.9 us  [swap(): lax.ppermute(part, 'dp', [(each, each ^ bits) for each in range(ways)])]
    ppermute x3, waiting for transfers between devices: 35.9 us -> 13.9 us  [shards(): lax.ppermute(part, 'tp', [(each, (each + step) % tp_ways) for each in ran...]
    pallas_call x8, Pallas kernels: 203 us -> 190 us  [the longest x4 112 us: shampoo(): pl.pallas_call(functools.partial(shampoo_kernel, count, len(grads), held...]
  transfers between devices with their start and end apart: 32 -> 32, of which waited for: 10 -> 7; matrix products, arithmetic and copies ran while one was open for 4% -> 7% of each run, Pallas kernels for 43% -> 61%
where the time goes in v4:
time: 705 us; the launch traced here: 696 us
  Pallas kernels  425 us (60%)
  waiting for transfers between devices  156 us (22%)
  other arithmetic  44.2 us (6%)
  starting transfers between devices  31.6 us (4%)
  local copies, waits for them, and re-layouts  23 us (3%)
  between operations  15.4 us (2%)
    pallas_call x4, Pallas kernels, shampoo(): pl.pallas_call(functools.partial(shampoo_kernel, count, len(grads), held...  112 us
    ppermute x9, waiting for transfers between devices, onward(): lax.ppermute(part, axis, [(each, (each + 1) % ways) for each in range(way...  97.4 us
    pallas_call x4, Pallas kernels, weight_grads(): pl.pallas_call(functools.partial(weight_grad_kernel, tuple(steps), len(wa...  78.4 us
    pallas_call x2, Pallas kernels, feed_back(): pl.pallas_call(functools.partial(feed_back_kernel, offsets, owned, first_...  72.7 us
    pallas_call x1, Pallas kernels, feed_forward(): pl.pallas_call(functools.partial(feed_kernel, offsets, owned), grid=(toke...  57.2 us
    pallas_call x1, Pallas kernels, project_qkv(): pl.pallas_call(functools.partial(qkv_kernel, heads, owned, ways), grid_sp...  32.9 us
    all_gather x1, waiting for transfers between devices, shards(): blocks = lax.all_gather(rows16, 'dp', axis=0, tiled=True)  25.8 us
    pallas_call x1, Pallas kernels, qkv_back(): pl.pallas_call(functools.partial(qkv_back_kernel, owned), grid=(tokens //...  25.1 us
  transfers between devices with their start and end apart: 32, of which 7 were waited for; matrix products, arithmetic and copies ran while one was open for 7% of the time, Pallas kernels for 61%

profile of v4, /device:TPU:0, one launch (start us, length us, event | category | flops | bytes accessed | tf_op | source)
XLA Modules:
  0.0 695.6 jit_solution(13374302476921441102)
XLA Ops:
  8.9 3.2 convert.20
  14.6 3.0 collective-permute-start
  17.7 47.8 %collective-permute-done.refs_1_ = bf16[512,2048]{1,0:T(8,128)(2,1)} collective-permute-done((bf16[512,2048]{1,0:T(8,128)(2,1)S(1)}, bf16[512,2048]{1,0:T(8,128)(2,1)}, u32[]{:S(2)}, u32[]{:S(2)}) %collective-permute-start) | collective-permute-done | bytes 2097184 | tf_op jit(solution)/shard_map/ppermute | solution.py:916
  65.5 48.8 %collective-permute-done.1.refs_2_ = bf16[512,2048]{1,0:T(8,128)(2,1)} collective-permute-done((bf16[512,2048]{1,0:T(8,128)(2,1)}, bf16[512,2048]{1,0:T(8,128)(2,1)}, u32[]{:S(2)}, u32[]{:S(2)}) %collective-permute-start.1) | collective-permute-done | bytes 2097184 | tf_op jit(solution)/shard_map/ppermute | solution.py:916
  116.7 25.8 %all-gather.2.cloned.1.call-done.refs_4_.blocks_ref.refs_8_.refs_6_ = bf16[49280,256]{1,0:T(8,128)(2,1)} async-done(((bf16[6160,256]{1,0:T(8,128)(2,1)}), bf16[49280,256]{1,0:T(8,128)(2,1)}) %all-gather.2.cloned.1.call-update) | async-done | bytes 25231376 | tf_op jit(solution)/shard_map/all_gather | solution.py:965
  148.8 13.8 %collective-permute-done.3 = bf16[8,384]{1,0:T(8,128)(2,1)S(1)} collective-permute-done((bf16[8,384]{1,0:T(8,128)(2,1)S(1)}, bf16[8,384]{1,0:T(8,128)(2,1)S(1)}, u32[]{:S(2)}, u32[]{:S(2)}) %collective-permute-start.3) | collective-permute-done | bytes 6176 | tf_op jit(solution)/shard_map/ppermute | solution.py:980
  171.2 32.9 %qkv.1 = (bf16[2048,1536]{1,0:T(8,128)(2,1)}, bf16[2048,2048]{1,0:T(8,128)(2,1)}, bf16[2048,2048]{1,0:T(8,128)(2,1)}, bf16[2048,2048]{1,0:T(8,128)(2,1)}, bf16[2...) custom-call(s32[1]{0:T(128)} %bitcast.1.rank_ref, bf16[512,2048]{1,0:T(8,128)(2,1)} %refs_0_.2, ...), custom_call_target="tpu_custom_call" | custom-call | flops 12884901888 | bytes 46137344 | tf_op jit(solution)/shard_map/qkv/pallas_call | solution.py:196
  204.2 10.8 %attend.1 = (bf16[2048,512]{1,0:T(8,128)(2,1)}, bf16[512,2048]{1,0:T(8,128)(2,1)}) custom-call(bf16[2048,1536]{1,0:T(8,128)(2,1)} %get-tuple-element.101.query_ref.key_ref.value_ref, bf16[2048,1536]{1,0:T(8,128)(2,1)} %get-tuple-element.101.query_ref.key_ref.value_ref, bf16[2048,1536]{1,0:T(8,128)(2,1)} %get-tuple-element.101.query_ref.key_ref.value_ref, ...), custom_call_target="tpu_custom_call" | custom-call | flops 3221225472 | bytes 8388608 | tf_op jit(solution)/shard_map/attend/pallas_call | solution.py:247
  216.0 57.2 %feed.1 = (bf16[2048,2048]{1,0:T(8,128)(2,1)}, bf16[2048,2048]{1,0:T(8,128)(2,1)}, bf16[2048,2048]{1,0:T(8,128)(2,1)}) custom-call(bf16[2048,2048]{1,0:T(8,128)(2,1)} %get-tuple-element.100.x_ref, bf16[2048,512]{1,0:T(8,128)(2,1)} %get-tuple-element.102.attended_ref, bf16[49280,256]{1,0:T(8,128)(2,1)} %all-gather.2.cloned.1.call-done.refs_4_.blocks_ref.refs_8_.refs_6_, ...), custom_call_target="tpu_custom_call" | custom-call | flops 38654705664 | bytes 58720256 | tf_op jit(solution)/shard_map/feed/pallas_call | solution.py:387
  274.8 47.9 %feed_back.2 = (bf16[2048,2048]{1,0:T(8,128)(2,1)}, bf16[2048,512]{1,0:T(8,128)(2,1)}, bf16[2048,2048]{1,0:T(8,128)(2,1)}, bf16[2048,2048]{1,0:T(8,128)(2,1)}, f32[24,2048]{1,0:T(8,128)}, /*index=5*/f32[8,2048]{1,0:T(8,128)}) custom-call(s32[1]{0:T(128)} %bitcast.1.rank_ref, bf16[512,2048]{1,0:T(8,128)(2,1)} %refs_0_.3, ...), custom_call_target="tpu_custom_call" | custom-call | flops 28991029248 | bytes 60817408 | tf_op jit(solution)/shard_map/feed_back/pallas_call | solution.py:493
  325.3 24.8 %feed_back.3 = (bf16[2048,2048]{1,0:T(8,128)(2,1)}, bf16[2048,512]{1,0:T(8,128)(2,1)}, bf16[2048,2048]{1,0:T(8,128)(2,1)}, bf16[2048,2048]{1,0:T(8,128)(2,1)}, f32[24,2048]{1,0:T(8,128)}, /*index=5*/f32[8,2048]{1,0:T(8,128)}) custom-call(s32[1]{0:T(128)} %bitcast.1.rank_ref, ...), custom_call_target="tpu_custom_call", output_to_operand_aliasing={{0}: (9, {}), {1}: (10, {}), {2}: (11, {}), {3}: (12, {})} | custom-call | flops 9663676416 | bytes 31457280 | tf_op jit(solution)/shard_map/feed_back/pallas_call | solution.py:493
  350.1 16.8 %attend_back.1.d_qkv_ref.refs_6_ = bf16[2048,1536]{1,0:T(8,128)(2,1)} custom-call(bf16[2048,1536]{1,0:T(8,128)(2,1)} %get-tuple-element.101.query_ref.key_ref.value_ref, bf16[2048,1536]{1,0:T(8,128)(2,1)} %get-tuple-element.101.query_ref.key_ref.value_ref, bf16[2048,1536]{1,0:T(8,128)(2,1)} %get-tuple-element.101.query_ref.key_ref.value_ref, ...), custom_call_target="tpu_custom_call" | custom-call | flops 7516192768 | bytes 16777216 | tf_op jit(solution)/shard_map/attend_back/pallas_call | solution.py:314
  366.9 25.1 %qkv_back.1 = (bf16[2048,2048]{1,0:T(8,128)(2,1)}, f32[16,2048]{1,0:T(8,128)}, f32[8,1536]{1,0:T(8,128)}) custom-call(bf16[2048,1536]{1,0:T(8,128)(2,1)} %attend_back.1.d_qkv_ref.refs_6_, bf16[2048,2048]{1,0:T(8,128)(2,1)} %get-tuple-element.118.part_ref, bf16[2048,2048]{1,0:T(8,128)(2,1)} %get-tuple-element.108.refs_5_.refs_3_.tokens_ref, ...), custom_call_target="tpu_custom_call" | custom-call | flops 12884901888 | bytes 46137344 | tf_op jit(solution)/shard_map/qkv_back/pallas_call | solution.py:564
  392.1 3.2 constant_dynamic-slice_fusion
  395.2 19.8 %weight_grads.5 = (bf16[24,256,256]{2,1,0:T(8,128)(2,1)}, bf16[24,256,256]{2,1,0:T(8,128)(2,1)}) custom-call(s32[1]{0:T(128)} %bitcast.12.core_ref, bf16[2048,2048]{1,0:T(8,128)(2,1)} %get-tuple-element.121.refs_0_, bf16[2048,2048]{1,0:T(8,128)(2,1)} %get-tuple-element.122.refs_1_, bf16[2048,2048]{1,0:T(8,128)(2,1)} %get-tuple-element.123.refs_2_, ...), custom_call_target="tpu_custom_call" | custom-call | flops 12884901888 | bytes 25769804 | tf_op jit(solution)/shard_map/weight_grads/pallas_call | solution.py:684
  415.1 19.7 %weight_grads.4 = (bf16[24,256,256]{2,1,0:T(8,128)(2,1)}, bf16[24,256,256]{2,1,0:T(8,128)(2,1)}) custom-call(s32[1]{0:T(128)} %bitcast.12.core_ref, bf16[2048,2048]{1,0:T(8,128)(2,1)} %get-tuple-element.121.refs_0_, bf16[2048,2048]{1,0:T(8,128)(2,1)} %get-tuple-element.122.refs_1_, bf16[2048,2048]{1,0:T(8,128)(2,1)} %get-tuple-element.123.refs_2_, ...), custom_call_target="tpu_custom_call" | custom-call | flops 12884901888 | bytes 25769804 | tf_op jit(solution)/shard_map/weight_grads/pallas_call | solution.py:684
  442.6 5.0 pair_sum.5
  447.6 19.6 %weight_grads.7 = (bf16[24,256,256]{2,1,0:T(8,128)(2,1)}, bf16[24,256,256]{2,1,0:T(8,128)(2,1)}) custom-call(s32[1]{0:T(128)} %bitcast.12.core_ref, bf16[2048,2048]{1,0:T(8,128)(2,1)} %get-tuple-element.121.refs_0_, bf16[2048,2048]{1,0:T(8,128)(2,1)} %get-tuple-element.122.refs_1_, bf16[2048,2048]{1,0:T(8,128)(2,1)} %get-tuple-element.123.refs_2_, ...), custom_call_target="tpu_custom_call" | custom-call | flops 12884901888 | bytes 25769804 | tf_op jit(solution)/shard_map/weight_grads/pallas_call | solution.py:684
  482.3 4.9 pair_sum.4
  487.2 18.8 %collective-permute-done.14.refs_10_.refs_3_ = bf16[6,256,256]{2,1,0:T(8,128)(2,1)} collective-permute-done((bf16[6,256,256]{2,1,0:T(8,128)(2,1)}, bf16[6,256,256]{2,1,0:T(8,128)(2,1)}, u32[]{:S(2)}, u32[]{:S(2)}) %collective-permute-start.14) | collective-permute-done | bytes 786464 | tf_op jit(solution)/shard_map/ppermute | solution.py:921
  507.6 19.3 %weight_grads.6 = (bf16[24,256,256]{2,1,0:T(8,128)(2,1)}, bf16[24,256,256]{2,1,0:T(8,128)(2,1)}) custom-call(s32[1]{0:T(128)} %bitcast.12.core_ref, bf16[2048,2048]{1,0:T(8,128)(2,1)} %get-tuple-element.121.refs_0_, bf16[2048,2048]{1,0:T(8,128)(2,1)} %get-tuple-element.122.refs_1_, bf16[2048,2048]{1,0:T(8,128)(2,1)} %get-tuple-element.123.refs_2_, ...), custom_call_target="tpu_custom_call" | custom-call | flops 12884901888 | bytes 25769804 | tf_op jit(solution)/shard_map/weight_grads/pallas_call | solution.py:684
  527.6 4.5 add_convert_fusion.1
  537.1 4.9 pair_sum.6
  543.9 28.1 %shampoo.4 = (f32[24,256,256]{2,1,0:T(8,128)}, f32[24,256,256]{2,1,0:T(8,128)}, f32[24,256,256]{2,1,0:T(8,128)}, f32[24,256,256]{2,1,0:T(8,128)}) custom-call(s32[6]{0:T(128)} %broadcast_select_fusion.2.places_ref, f32[6,256,256]{2,1,0:T(8,128)} %get-tuple-element.144.refs_0_.refs_7_, bf16[6,256,256]{2,1,0:T(8,128)(2,1)} %collective-permute-done.12.refs_8_.refs_1_, ...), custom_call_target="tpu_custom_call" | custom-call | flops 26172456960 | bytes 11796480 | tf_op jit(solution)/shard_map/shampoo/pallas_call | solution.py:872
  572.7 4.9 pair_sum.7
  581.2 28.1 %shampoo.5 = (f32[24,256,256]{2,1,0:T(8,128)}, f32[24,256,256]{2,1,0:T(8,128)}, f32[24,256,256]{2,1,0:T(8,128)}, f32[24,256,256]{2,1,0:T(8,128)}) custom-call(s32[6]{0:T(128)} %broadcast_select_fusion.3.places_ref, f32[6,256,256]{2,1,0:T(8,128)} %get-tuple-element.130.refs_7_.refs_0_, ...), custom_call_target="tpu_custom_call", output_to_operand_aliasing={{0}: (14, {}), {1}: (15, {}), {2}: (16, {}), {3}: (17, {})} | custom-call | flops 26172456960 | bytes 11796480 | tf_op jit(solution)/shard_map/shampoo/pallas_call | solution.py:872
  609.4 4.3 fusion.8
  614.8 4.4 add_convert_fusion
  621.6 27.7 %shampoo.6 = (f32[24,256,256]{2,1,0:T(8,128)}, f32[24,256,256]{2,1,0:T(8,128)}, f32[24,256,256]{2,1,0:T(8,128)}, f32[24,256,256]{2,1,0:T(8,128)}) custom-call(s32[6]{0:T(128)} %broadcast_select_fusion.places_ref, f32[6,256,256]{2,1,0:T(8,128)} %get-tuple-element.169.refs_0_, ...), custom_call_target="tpu_custom_call", output_to_operand_aliasing={{0}: (14, {}), {1}: (15, {}), {2}: (16, {}), {3}: (17, {})} | custom-call | flops 26172456960 | bytes 11796480 | tf_op jit(solution)/shard_map/shampoo/pallas_call | solution.py:872
  652.1 27.9 %shampoo.7 = (f32[24,256,256]{2,1,0:T(8,128)}, f32[24,256,256]{2,1,0:T(8,128)}, f32[24,256,256]{2,1,0:T(8,128)}, f32[24,256,256]{2,1,0:T(8,128)}) custom-call(s32[6]{0:T(128)} %broadcast_select_fusion.1.places_ref, f32[6,256,256]{2,1,0:T(8,128)} %get-tuple-element.162.refs_0_, ...), custom_call_target="tpu_custom_call", output_to_operand_aliasing={{0}: (14, {}), {1}: (15, {}), {2}: (16, {}), {3}: (17, {})} | custom-call | flops 26172456960 | bytes 11796480 | tf_op jit(solution)/shard_map/shampoo/pallas_call | solution.py:872
  680.1 3.7 fusion.13
  683.8 5.0 fusion.7
  (200 shorter events, 68.4 us)
Async XLA Ops:
  7.2 135.3 %all-gather.2.cloned.1.call-start = ((), (), s32[]{:S(2)}) async-start(), calls=%async_computation.3 | async-start | bytes 28385280 | tf_op jit(solution)/shard_map/all_gather | solution.py:965
  14.0 564.6 %reduce-scatter.4.cloned.1.call-start = ((), (), s32[]{:S(2)}) async-start(), calls=%async_computation.4 | async-start | bytes 10485760 | tf_op jit(solution)/shard_map/reduce_scatter | solution.py:1028
  14.6 50.8 %collective-permute-start = (bf16[512,2048]{1,0:T(8,128)(2,1)S(1)}, bf16[512,2048]{1,0:T(8,128)(2,1)}, u32[]{:S(2)}, u32[]{:S(2)}) collective-permute-start(bf16[512,2048]{1,0:T(8,128)(2,1)S(1)} %copy-done.2), channel_id=1, source_target_pairs={{0,1},{1,2},{2,3},{3,0},{4,5},{5,6},{6,7},{7,4},{8,9},{9,10},{10,1... | collective-permute-start | bytes 6291464 | tf_op jit(solution)/shard_map/ppermute | solution.py:916
  65.4 48.9 %collective-permute-start.1 = (bf16[512,2048]{1,0:T(8,128)(2,1)}, bf16[512,2048]{1,0:T(8,128)(2,1)}, u32[]{:S(2)}, u32[]{:S(2)}) collective-permute-start(bf16[512,2048]{1,0:T(8,128)(2,1)} %collective-permute-done.refs_1_), channel_id=1, source_target_pairs={{0,1},{1,2},{2,3},{3,0},{4,5},{5,6},{6,7},{7,4},{8,9},{9,10},{10,1... | collective-permute-start | bytes 6291464 | tf_op jit(solution)/shard_map/ppermute | solution.py:916
  114.3 48.4 %collective-permute-start.2 = (bf16[512,2048]{1,0:T(8,128)(2,1)}, bf16[512,2048]{1,0:T(8,128)(2,1)}, u32[]{:S(2)}, u32[]{:S(2)}) collective-permute-start(bf16[512,2048]{1,0:T(8,128)(2,1)} %collective-permute-done.1.refs_2_), channel_id=1, source_target_pairs={{0,1},{1,2},{2,3},{3,0},{4,5},{5,6},{6,7},{7,4},{8,9},{9,10},{10,1... | collective-permute-start | bytes 6291464 | tf_op jit(solution)/shard_map/ppermute | solution.py:916
  143.4 19.2 %collective-permute-start.3 = (bf16[8,384]{1,0:T(8,128)(2,1)S(1)}, bf16[8,384]{1,0:T(8,128)(2,1)S(1)}, u32[]{:S(2)}, u32[]{:S(2)}) collective-permute-start(bf16[8,384]{1,0:T(8,128)(2,1)S(1)} %slice.75), channel_id=1, source_target_pairs={{0,1},{1,2},{2,3},{3,0},{4,5},{5,6},{6,7},{7,4},{8,9},{9,10},{10,1... | collective-permute-start | bytes 18440 | tf_op jit(solution)/shard_map/ppermute | solution.py:980
  144.9 17.8 %collective-permute-start.4 = (bf16[8,384]{1,0:T(8,128)(2,1)S(1)}, bf16[8,384]{1,0:T(8,128)(2,1)S(1)}, u32[]{:S(2)}, u32[]{:S(2)}) collective-permute-start(bf16[8,384]{1,0:T(8,128)(2,1)S(1)} %slice.75), channel_id=1, source_target_pairs={{0,2},{1,3},{2,0},{3,1},{4,6},{5,7},{6,4},{7,5},{8,10},{9,11},{10,... | collective-permute-start | bytes 18440 | tf_op jit(solution)/shard_map/ppermute | solution.py:980
  147.3 15.4 %collective-permute-start.5 = (bf16[8,384]{1,0:T(8,128)(2,1)S(1)}, bf16[8,384]{1,0:T(8,128)(2,1)S(1)}, u32[]{:S(2)}, u32[]{:S(2)}) collective-permute-start(bf16[8,384]{1,0:T(8,128)(2,1)S(1)} %slice.75), channel_id=1, source_target_pairs={{0,3},{1,0},{2,1},{3,2},{4,7},{5,4},{6,5},{7,6},{8,11},{9,8},{10,9... | collective-permute-start | bytes 18440 | tf_op jit(solution)/shard_map/ppermute | solution.py:980
  162.8 52.1 %collective-permute-start.6 = (bf16[512,2048]{1,0:T(8,128)(2,1)}, bf16[512,2048]{1,0:T(8,128)(2,1)}, u32[]{:S(2)}, u32[]{:S(2)}) collective-permute-start(bf16[512,2048]{1,0:T(8,128)(2,1)} %refs_0_.3), channel_id=1, source_target_pairs={{0,1},{1,2},{2,3},{3,0},{4,5},{5,6},{6,7},{7,4},{8,9},{9,10},{10,1... | collective-permute-start | bytes 6291464 | tf_op jit(solution)/shard_map/ppermute | solution.py:916
  214.9 58.2 %collective-permute-start.7 = (bf16[512,2048]{1,0:T(8,128)(2,1)}, bf16[512,2048]{1,0:T(8,128)(2,1)S(1)}, u32[]{:S(2)}, u32[]{:S(2)}) collective-permute-start(bf16[512,2048]{1,0:T(8,128)(2,1)} %collective-permute-done.6.refs_1_), channel_id=1, source_target_pairs={{0,1},{1,2},{2,3},{3,0},{4,5},{5,6},{6,7},{7,4},{8,9},{9,10},{10,1... | collective-permute-start | bytes 6291464 | tf_op jit(solution)/shard_map/ppermute | solution.py:916
  274.5 49.0 %collective-permute-start.8 = (bf16[512,2048]{1,0:T(8,128)(2,1)}, bf16[512,2048]{1,0:T(8,128)(2,1)S(1)}, u32[]{:S(2)}, u32[]{:S(2)}) collective-permute-start(bf16[512,2048]{1,0:T(8,128)(2,1)} %copy-done.23), channel_id=1, source_target_pairs={{0,1},{1,2},{2,3},{3,0},{4,5},{5,6},{6,7},{7,4},{8,9},{9,10},{10,1... | collective-permute-start | bytes 6291464 | tf_op jit(solution)/shard_map/ppermute | solution.py:916
  324.8 294.4 %reduce-scatter.6.cloned.1.call-start = ((), (), s32[]{:S(2)}) async-start(), calls=%async_computation.5 | async-start | bytes 73728 | tf_op jit(solution)/shard_map/reduce_scatter | solution.py:1066
  415.0 25.9 %collective-permute-start.11 = (bf16[24,256,256]{2,1,0:T(8,128)(2,1)}, bf16[24,256,256]{2,1,0:T(8,128)(2,1)S(1)}, u32[]{:S(2)}, u32[]{:S(2)}) collective-permute-start(bf16[24,256,256]{2,1,0:T(8,128)(2,1)} %get-tuple-element.132), channel_id=1, source_target_pairs={{0,4},{4,0},{8,12},{12,8},{16,20},{20,16},{24,28},{28,24},{1,5},{5... | collective-permute-start | bytes 9437192 | tf_op jit(solution)/shard_map/ppermute | solution.py:921
  434.8 40.7 %collective-permute-start.10 = (bf16[24,256,256]{2,1,0:T(8,128)(2,1)}, bf16[24,256,256]{2,1,0:T(8,128)(2,1)}, u32[]{:S(2)}, u32[]{:S(2)}) collective-permute-start(bf16[24,256,256]{2,1,0:T(8,128)(2,1)} %get-tuple-element.129), channel_id=1, source_target_pairs={{0,4},{4,0},{8,12},{12,8},{16,20},{20,16},{24,28},{28,24},{1,5},{5... | collective-permute-start | bytes 9437192 | tf_op jit(solution)/shard_map/ppermute | solution.py:921
  467.2 68.3 %collective-permute-start.19 = (bf16[24,256,256]{2,1,0:T(8,128)(2,1)}, bf16[24,256,256]{2,1,0:T(8,128)(2,1)S(1)}, u32[]{:S(2)}, u32[]{:S(2)}) collective-permute-start(bf16[24,256,256]{2,1,0:T(8,128)(2,1)} %get-tuple-element.150), channel_id=1, source_target_pairs={{0,4},{4,0},{8,12},{12,8},{16,20},{20,16},{24,28},{28,24},{1,5},{5... | collective-permute-start | bytes 9437192 | tf_op jit(solution)/shard_map/ppermute | solution.py:921
  468.4 39.2 %collective-permute-start.12 = (bf16[6,256,256]{2,1,0:T(8,128)(2,1)}, bf16[6,256,256]{2,1,0:T(8,128)(2,1)}, u32[]{:S(2)}, u32[]{:S(2)}) collective-permute-start(bf16[6,256,256]{2,1,0:T(8,128)(2,1)} %get-tuple-element.133), channel_id=1, source_target_pairs={{0,8},{4,12},{8,0},{12,4},{16,24},{20,28},{24,16},{28,20},{1,9},{5... | collective-permute-start | bytes 2359304 | tf_op jit(solution)/shard_map/ppermute | solution.py:921
  469.5 38.1 %collective-permute-start.13 = (bf16[6,256,256]{2,1,0:T(8,128)(2,1)}, bf16[6,256,256]{2,1,0:T(8,128)(2,1)}, u32[]{:S(2)}, u32[]{:S(2)}) collective-permute-start(bf16[6,256,256]{2,1,0:T(8,128)(2,1)} %get-tuple-element.134), channel_id=1, source_target_pairs={{0,16},{4,20},{8,24},{12,28},{16,0},{20,4},{24,8},{28,12},{1,17},{... | collective-permute-start | bytes 2359304 | tf_op jit(solution)/shard_map/ppermute | solution.py:921
  471.0 35.0 %collective-permute-start.14 = (bf16[6,256,256]{2,1,0:T(8,128)(2,1)}, bf16[6,256,256]{2,1,0:T(8,128)(2,1)}, u32[]{:S(2)}, u32[]{:S(2)}) collective-permute-start(bf16[6,256,256]{2,1,0:T(8,128)(2,1)} %get-tuple-element.135), channel_id=1, source_target_pairs={{0,24},{4,28},{8,16},{12,20},{16,8},{20,12},{24,0},{28,4},{1,25},{... | collective-permute-start | bytes 2359304 | tf_op jit(solution)/shard_map/ppermute | solution.py:921
  475.6 52.1 %collective-permute-start.9 = (bf16[512,2048]{1,0:T(8,128)(2,1)}, bf16[512,2048]{1,0:T(8,128)(2,1)}, u32[]{:S(2)}, u32[]{:S(2)}) collective-permute-start(bf16[512,2048]{1,0:T(8,128)(2,1)} %constant_dynamic-slice_fusion), channel_id=1, source_target_pairs={{0,1},{1,2},{2,3},{3,0},{4,5},{5,6},{6,7},{7,4},{8,9},{9,10},{10,1... | collective-permute-start | bytes 6291464 | tf_op jit(solution)/shard_map/ppermute | solution.py:916
  506.1 35.9 %collective-permute-start.18 = (bf16[6,256,256]{2,1,0:T(8,128)(2,1)}, bf16[6,256,256]{2,1,0:T(8,128)(2,1)}, u32[]{:S(2)}, u32[]{:S(2)}) collective-permute-start(bf16[6,256,256]{2,1,0:T(8,128)(2,1)} %get-tuple-element.143.refs_13_), channel_id=1, source_target_pairs={{0,24},{4,28},{8,16},{12,20},{16,8},{20,12},{24,0},{28,4},{1,25},{... | collective-permute-start | bytes 2359304 | tf_op jit(solution)/shard_map/ppermute | solution.py:921
  526.9 45.1 %collective-permute-start.21 = (bf16[24,256,256]{2,1,0:T(8,128)(2,1)}, bf16[24,256,256]{2,1,0:T(8,128)(2,1)}, u32[]{:S(2)}, u32[]{:S(2)}) collective-permute-start(bf16[24,256,256]{2,1,0:T(8,128)(2,1)} %get-tuple-element.161), channel_id=1, source_target_pairs={{0,4},{4,0},{8,12},{12,8},{16,20},{20,16},{24,28},{28,24},{1,5},{5... | collective-permute-start | bytes 9437192 | tf_op jit(solution)/shard_map/ppermute | solution.py:921
  532.1 81.7 %collective-permute-start.15 = (bf16[512,2048]{1,0:T(8,128)(2,1)}, bf16[512,2048]{1,0:T(8,128)(2,1)}, u32[]{:S(2)}, u32[]{:S(2)}) collective-permute-start(bf16[512,2048]{1,0:T(8,128)(2,1)} %add_convert_fusion.1), channel_id=1, source_target_pairs={{0,1},{1,2},{2,3},{3,0},{4,5},{5,6},{6,7},{7,4},{8,9},{9,10},{10,1... | collective-permute-start | bytes 6291464 | tf_op jit(solution)/shard_map/ppermute | solution.py:916
  534.5 44.2 %collective-permute-start.16 = (bf16[6,256,256]{2,1,0:T(8,128)(2,1)}, bf16[6,256,256]{2,1,0:T(8,128)(2,1)}, u32[]{:S(2)}, u32[]{:S(2)}) collective-permute-start(bf16[6,256,256]{2,1,0:T(8,128)(2,1)} %get-tuple-element.139), channel_id=1, source_target_pairs={{0,8},{4,12},{8,0},{12,4},{16,24},{20,28},{24,16},{28,20},{1,9},{5... | collective-permute-start | bytes 2359304 | tf_op jit(solution)/shard_map/ppermute | solution.py:921
  535.4 44.4 %collective-permute-start.17 = (bf16[6,256,256]{2,1,0:T(8,128)(2,1)}, bf16[6,256,256]{2,1,0:T(8,128)(2,1)}, u32[]{:S(2)}, u32[]{:S(2)}) collective-permute-start(bf16[6,256,256]{2,1,0:T(8,128)(2,1)} %get-tuple-element.141), channel_id=1, source_target_pairs={{0,16},{4,20},{8,24},{12,28},{16,0},{20,4},{24,8},{28,12},{1,17},{... | collective-permute-start | bytes 2359304 | tf_op jit(solution)/shard_map/ppermute | solution.py:921
  542.0 35.7 %collective-permute-start.22 = (bf16[6,256,256]{2,1,0:T(8,128)(2,1)}, bf16[6,256,256]{2,1,0:T(8,128)(2,1)}, u32[]{:S(2)}, u32[]{:S(2)}) collective-permute-start(bf16[6,256,256]{2,1,0:T(8,128)(2,1)} %get-tuple-element.152.refs_17_), channel_id=1, source_target_pairs={{0,24},{4,28},{8,16},{12,20},{16,8},{20,12},{24,0},{28,4},{1,25},{... | collective-permute-start | bytes 2359304 | tf_op jit(solution)/shard_map/ppermute | solution.py:921
  572.0 48.8 %collective-permute-start.26 = (bf16[6,256,256]{2,1,0:T(8,128)(2,1)}, bf16[6,256,256]{2,1,0:T(8,128)(2,1)}, u32[]{:S(2)}, u32[]{:S(2)}) collective-permute-start(bf16[6,256,256]{2,1,0:T(8,128)(2,1)} %get-tuple-element.171), channel_id=1, source_target_pairs={{0,8},{4,12},{8,0},{12,4},{16,24},{20,28},{24,16},{28,20},{1,9},{5... | collective-permute-start | bytes 2359304 | tf_op jit(solution)/shard_map/ppermute | solution.py:921
  577.7 43.9 %collective-permute-start.27 = (bf16[6,256,256]{2,1,0:T(8,128)(2,1)}, bf16[6,256,256]{2,1,0:T(8,128)(2,1)}, u32[]{:S(2)}, u32[]{:S(2)}) collective-permute-start(bf16[6,256,256]{2,1,0:T(8,128)(2,1)} %get-tuple-element.173), channel_id=1, source_target_pairs={{0,16},{4,20},{8,24},{12,28},{16,0},{20,4},{24,8},{28,12},{1,17},{... | collective-permute-start | bytes 2359304 | tf_op jit(solution)/shard_map/ppermute | solution.py:921
  578.6 71.4 %reduce-scatter.8.cloned.1.call-start = ((), (), s32[]{:S(2)}) async-start(), calls=%async_computation.6 | async-start | bytes 40960 | tf_op jit(solution)/shard_map/reduce_scatter | solution.py:1075
  578.7 73.4 %collective-permute-start.23 = (bf16[6,256,256]{2,1,0:T(8,128)(2,1)}, bf16[6,256,256]{2,1,0:T(8,128)(2,1)}, u32[]{:S(2)}, u32[]{:S(2)}) collective-permute-start(bf16[6,256,256]{2,1,0:T(8,128)(2,1)} %get-tuple-element.164), channel_id=1, source_target_pairs={{0,8},{4,12},{8,0},{12,4},{16,24},{20,28},{24,16},{28,20},{1,9},{5... | collective-permute-start | bytes 2359304 | tf_op jit(solution)/shard_map/ppermute | solution.py:921
  579.8 72.3 %collective-permute-start.24 = (bf16[6,256,256]{2,1,0:T(8,128)(2,1)}, bf16[6,256,256]{2,1,0:T(8,128)(2,1)}, u32[]{:S(2)}, u32[]{:S(2)}) collective-permute-start(bf16[6,256,256]{2,1,0:T(8,128)(2,1)} %get-tuple-element.166), channel_id=1, source_target_pairs={{0,16},{4,20},{8,24},{12,28},{16,0},{20,4},{24,8},{28,12},{1,17},{... | collective-permute-start | bytes 2359304 | tf_op jit(solution)/shard_map/ppermute | solution.py:921
  613.8 38.3 %collective-permute-start.25 = (bf16[6,256,256]{2,1,0:T(8,128)(2,1)S(1)}, bf16[6,256,256]{2,1,0:T(8,128)(2,1)}, u32[]{:S(2)}, u32[]{:S(2)}) collective-permute-start(bf16[6,256,256]{2,1,0:T(8,128)(2,1)S(1)} %copy-done.24), channel_id=1, source_target_pairs={{0,24},{4,28},{8,16},{12,20},{16,8},{20,12},{24,0},{28,4},{1,25},{... | collective-permute-start | bytes 2359304 | tf_op jit(solution)/shard_map/ppermute | solution.py:921
  620.8 59.3 %collective-permute-start.20 = (bf16[512,2048]{1,0:T(8,128)(2,1)}, bf16[512,2048]{1,0:T(8,128)(2,1)}, u32[]{:S(2)}, u32[]{:S(2)}) collective-permute-start(bf16[512,2048]{1,0:T(8,128)(2,1)} %add_convert_fusion), channel_id=1, source_target_pairs={{0,1},{1,2},{2,3},{3,0},{4,5},{5,6},{6,7},{7,4},{8,9},{9,10},{10,1... | collective-permute-start | bytes 6291464 | tf_op jit(solution)/shard_map/ppermute | solution.py:916
  (26 other events, 589.7 us)
Sparse Core Ops, SparseCore 0:
  14.1 128.2 all-gather.1
  323.7 144.5 reduce-scatter.3
  578.7 31.9 reduce-scatter.5
  620.9 17.9 reduce-scatter.7

commit v5 on v4

--- a/solution.py
+++ b/solution.py
@@ -24,14 +24,6 @@
 DOC_MAX = 512
 HALF_ROOT = 0.7071067811865476
 DENSITY_SCALE = 0.3989422804014327
-
-
-def apply_layer_norm(values):
-    mean_val = jnp.mean(values, axis=-1, keepdims=True)
-    centred = values - mean_val
-    variance = jnp.mean(centred * centred, axis=-1, keepdims=True)
-    inv_std = lax.rsqrt(variance + EPS_NORM)
-    return (centred * inv_std, inv_std)
 
 
 def to_blocks(matrix, block_size):
@@ -91,6 +83,26 @@
             copy.wait()
 
 
+def wait_for(copies):
+    for copy in copies:
+        copy.wait()
+
+
+def both_ways(steps, work):
+    if steps == 1:
+        work(True)
+        return
+    step = pl.program_id(0)
+
+    @pl.when(step == 0)
+    def _():
+        work(True)
+
+    @pl.when(step > 0)
+    def _():
+        work(False)
+
+
 def turn(values, cosines, sines):
     lane = lax.broadcasted_iota(jnp.int32, values.shape, 1)
     half = ROT // 2
@@ -146,7 +158,8 @@
     size = blocks_ref.shape[-1]
     copies = block_copies(blocks_ref, owned, 0, weight.shape[0] // size, weight.shape[1] // size, weight, sems)
     moves = part_copies(part_refs, held, part_sems)
-    begin_copies(moves + copies)
+    cols_all = weight.shape[1] // size
+    begin_copies(moves + [copy for col in range(cols_all) for copy in copies[col::cols_all]])
     await_part(moves, 1)
     own = held[pl.program_id(0)]
     tokens_ref[...] = own
@@ -163,18 +176,24 @@
         first = (scaled * norm_ref[0:1, cols] + norm_ref[1:2, cols]).astype(jnp.bfloat16)
         normed[:, cols] = first
         first_turned[cols, :] = first.T
-    end_copies(copies)
     lanes = cos_ref.shape[1]
-    for head in range(heads):
-        for part in range(3):
-            cols = pl.ds((head * 3 + part) * HD, HD)
-            result = contract(normed[...], weight[:, cols], NN) + bias_ref[:, cols]
-            if part < 2:
-                first = turn(result[:, :lanes], cos_ref[...], sin_ref[...])
-                result = jnp.concatenate([first, result[:, lanes:]], 1)
-            if part == 0:
-                result = result * (1.0 / math.sqrt(HD))
-            qkv_ref[:, cols] = result.astype(jnp.bfloat16)
+
+    def work(fresh):
+        for head in range(heads):
+            for part in range(3):
+                index = head * 3 + part
+                if fresh:
+                    wait_for(copies[index::cols_all])
+                cols = pl.ds(index * HD, HD)
+                result = contract(normed[...], weight[:, cols], NN) + bias_ref[:, cols]
+                if part < 2:
+                    first = turn(result[:, :lanes], cos_ref[...], sin_ref[...])
+                    result = jnp.concatenate([first, result[:, lanes:]], 1)
+                if part == 0:
+                    result = result * (1.0 / math.sqrt(HD))
+                qkv_ref[:, cols] = result.astype(jnp.bfloat16)
+
+    both_ways(parts, work)
 
 
 def project_qkv(parts, rank, blocks, owned, norm_params, bias, cosines, sines, heads):
@@ -336,7 +355,7 @@
 
 
 def feed_kernel(
-    offsets, owned, x_ref, attended_ref, blocks_ref, bias_ref, turned_ref, slope_ref, out_ref, act_ref, w_in, w_down, sems_in, sems_down
+    steps, offsets, owned, x_ref, attended_ref, blocks_ref, bias_ref, turned_ref, slope_ref, out_ref, act_ref, w_in, w_down, sems_in, sems_down
 ):
     size = blocks_ref.shape[-1]
     width, hidden_units = w_in.shape
@@ -355,25 +374,33 @@
         w_down.at[pl.ds(hidden_units, head_rows * size)],
         sems_down.at[pl.ds(inner * outer, head_rows * outer)],
     )
-    begin_copies(copies_in + copies_down)
-    end_copies(copies_in)
-    values = x_ref[...]
-    for col in range(inner):
-        cols = pl.ds(col * size, size)
-        hidden = contract(values, w_in[:, cols], NN) + bias_ref[:, cols]
-        cdf = 0.5 + 0.5 * lax.erf(hidden * HALF_ROOT)
-        density = jnp.exp(-0.5 * hidden * hidden) * DENSITY_SCALE
-        activated = (hidden * cdf).astype(jnp.bfloat16)
-        act_ref[:, cols] = activated
-        turned_ref[cols, :] = activated.T
-        slope_ref[:, cols] = (cdf + hidden * density).astype(jnp.bfloat16)
-    end_copies(copies_down)
-    for col in range(outer):
-        cols = pl.ds(col * size, size)
-        out_ref[:, cols] = (
-            contract(act_ref[...], w_down[:hidden_units, cols], NN)
-            + contract(attended_ref[...], w_down[hidden_units:, cols], NN)
-        ).astype(jnp.bfloat16)
+    begin_copies(
+        [copy for col in range(inner) for copy in copies_in[col::inner]]
+        + [copy for col in range(outer) for copy in copies_down[col::outer]]
+    )
+
+    def work(fresh):
+        for col in range(inner):
+            if fresh:
+                wait_for(copies_in[col::inner])
+            cols = pl.ds(col * size, size)
+            hidden = contract(x_ref[...], w_in[:, cols], NN) + bias_ref[:, cols]
+            cdf = 0.5 + 0.5 * lax.erf(hidden * HALF_ROOT)
+            density = jnp.exp(-0.5 * hidden * hidden) * DENSITY_SCALE
+            activated = (hidden * cdf).astype(jnp.bfloat16)
+            act_ref[:, cols] = activated
+            turned_ref[cols, :] = activated.T
+            slope_ref[:, cols] = (cdf + hidden * density).astype(jnp.bfloat16)
+        for col in range(outer):
+            if fresh:
+                wait_for(copies_down[col::outer])
+            cols = pl.ds(col * size, size)
+            out_ref[:, cols] = (
+                contract(act_ref[...], w_down[:hidden_units, cols], NN)
+                + contract(attended_ref[...], w_down[hidden_units:, cols], NN)
+            ).astype(jnp.bfloat16)
+
+    both_ways(steps, work)
 
 
 def feed_forward(normed, attended, blocks, owned, bias, offsets):
@@ -385,7 +412,7 @@
     row = lambda cols: pl.BlockSpec((tile, cols), lambda i: (i, 0))
     inner, outer = hidden_units // size, width // size
     return pl.pallas_call(
-        functools.partial(feed_kernel, offsets, owned),
+        functools.partial(feed_kernel, tokens // tile, offsets, owned),
         grid=(tokens // tile,),
         in_specs=[
             row(width),
@@ -449,31 +476,36 @@
     step = pl.program_id(0)
     cotangent = held[step // per_part, pl.ds(pl.multiple_of(step % per_part * tile, tile), tile), :]
     seed_ref[...] = (cotangent.astype(jnp.float32) * factor_ref[...]).astype(jnp.bfloat16)
-    seed = seed_ref[...]
     if first_part == 0:
 
         @pl.when(step < per_part)
         def _():
             norm_sums[16:24, :] += column_sum(seed_ref[...].astype(jnp.float32))
 
-    end_copies(copies_out)
-    d_attended_ref[...] = contract(seed, w_out[...], NT).astype(jnp.bfloat16)
-    end_copies(copies_down)
-    for col in range(inner):
-        cols = pl.ds(col * size, size)
-        d_act = contract(seed_ref[...], w_down[cols, :], NT)
-        d_hidden = (d_act * slope_ref[:, cols].astype(jnp.float32)).astype(jnp.bfloat16)
-        d_hidden_ref[:, cols] = d_hidden
-        hidden_sums[:, cols] += column_sum(d_hidden.astype(jnp.float32))
-    end_copies(copies_in)
-    mean, inverse = mean_ref[...], inverse_ref[...]
-    for col in range(outer):
-        cols = pl.ds(col * size, size)
-        scaled = (tokens_ref[:, cols].astype(jnp.float32) - mean) * inverse
-        second = contract(d_hidden_ref[...], w_in[cols, :], NT)
-        dz_ref[:, cols] = (second * norm_ref[2:3, cols]).astype(jnp.bfloat16)
-        norm_sums[0:8, cols] += column_sum(second * scaled)
-        norm_sums[8:16, cols] += column_sum(second)
+    def work(fresh):
+        if fresh:
+            wait_for(copies_out)
+        d_attended_ref[...] = contract(seed_ref[...], w_out[...], NT).astype(jnp.bfloat16)
+        for col in range(inner):
+            if fresh:
+                wait_for(copies_down[col * outer : (col + 1) * outer])
+            cols = pl.ds(col * size, size)
+            d_act = contract(seed_ref[...], w_down[cols, :], NT)
+            d_hidden = (d_act * slope_ref[:, cols].astype(jnp.float32)).astype(jnp.bfloat16)
+            d_hidden_ref[:, cols] = d_hidden
+            hidden_sums[:, cols] += column_sum(d_hidden.astype(jnp.float32))
+        mean, inverse = mean_ref[...], inverse_ref[...]
+        for col in range(outer):
+            if fresh:
+                wait_for(copies_in[col * inner : (col + 1) * inner])
+            cols = pl.ds(col * size, size)
+            scaled = (tokens_ref[:, cols].astype(jnp.float32) - mean) * inverse
+            second = contract(d_hidden_ref[...], w_in[cols, :], NT)
+            dz_ref[:, cols] = (second * norm_ref[2:3, cols]).astype(jnp.bfloat16)
+            norm_sums[0:8, cols] += column_sum(second * scaled)
+            norm_sums[8:16, cols] += column_sum(second)
+
+    both_ways(parts * per_part, work)
 
 
 def feed_back(parts, first_part, ways, rank, factor, slope, group_tokens, mean, inverse, blocks, owned, norm_params, offsets, head_cols, priors):
@@ -530,7 +562,10 @@
     )(rank, *parts, factor, slope, group_tokens, mean, inverse, blocks, norm_params, *priors)
 
 
-def qkv_back_kernel(owned, d_qkv_ref, part_ref, tokens_ref, mean_ref, inverse_ref, blocks_ref, norm_ref, dz_ref, norm_sums, qkv_sums, w_qkv, sems):
+def qkv_back_kernel(
+    steps, owned, waits, d_qkv_ref, part_ref, tokens_ref, mean_ref, inverse_ref, blocks_ref, norm_ref, *refs
+):
+    dz_ref, norm_sums, qkv_sums, w_qkv, sems = refs[waits:]
     size = blocks_ref.shape[-1]
     outer = w_qkv.shape[0] // size
     copies = block_copies(blocks_ref, owned, 0, outer, w_qkv.shape[1] // size, w_qkv, sems)
@@ -543,17 +578,23 @@
 
     qkv_sums[...] += column_sum(d_qkv_ref[...].astype(jnp.float32))
     mean, inverse = mean_ref[...], inverse_ref[...]
-    end_copies(copies)
-    for col in range(outer):
-        cols = pl.ds(col * size, size)
-        scaled = (tokens_ref[:, cols].astype(jnp.float32) - mean) * inverse
-        first = contract(d_qkv_ref[...], w_qkv[cols, :], NT)
-        dz_ref[:, cols] = (part_ref[:, cols].astype(jnp.float32) + first * norm_ref[0:1, cols]).astype(jnp.bfloat16)
-        norm_sums[0:8, cols] += column_sum(first * scaled)
-        norm_sums[8:16, cols] += column_sum(first)
-
-
-def qkv_back(d_qkv, dz_part, group_tokens, mean, inverse, blocks, owned, norm_params):
+    inner = w_qkv.shape[1] // size
+
+    def work(fresh):
+        for col in range(outer):
+            if fresh:
+                wait_for(copies[col * inner : (col + 1) * inner])
+            cols = pl.ds(col * size, size)
+            scaled = (tokens_ref[:, cols].astype(jnp.float32) - mean) * inverse
+            first = contract(d_qkv_ref[...], w_qkv[cols, :], NT)
+            dz_ref[:, cols] = (part_ref[:, cols].astype(jnp.float32) + first * norm_ref[0:1, cols]).astype(jnp.bfloat16)
+            norm_sums[0:8, cols] += column_sum(first * scaled)
+            norm_sums[8:16, cols] += column_sum(first)
+
+    both_ways(steps, work)
+
+
+def qkv_back(d_qkv, dz_part, group_tokens, mean, inverse, blocks, owned, norm_params, waits):
     tokens, qkv_cols = d_qkv.shape
     width = dz_part.shape[1]
     size = blocks.shape[-1]
@@ -562,11 +603,12 @@
     whole = lambda rows, cols: pl.BlockSpec((rows, cols), lambda i: (0, 0))
     outer = width // size
     return pl.pallas_call(
-        functools.partial(qkv_back_kernel, owned),
+        functools.partial(qkv_back_kernel, tokens // tile, owned, len(waits)),
         grid=(tokens // tile,),
         in_specs=[
             row(qkv_cols), row(width), row(width), row(1), row(1), pl.BlockSpec(memory_space=pl.ANY), whole(norm_params.shape[0], width),
-        ],
+        ]
+        + [pl.BlockSpec(memory_space=pl.ANY)] * len(waits),
         out_specs=[row(width), whole(16, width), whole(8, qkv_cols)],
         out_shape=[
             jax.ShapeDtypeStruct((tokens, width), jnp.bfloat16),
@@ -582,7 +624,7 @@
             flops=2 * tokens * width * qkv_cols, bytes_accessed=tokens * width * 11, transcendentals=0
         ),
         name="qkv_back",
-    )(d_qkv, dz_part, group_tokens, mean, inverse, blocks, norm_params)
+    )(d_qkv, dz_part, group_tokens, mean, inverse, blocks, norm_params, *waits)
 
 
 def weight_grad_kernel(steps, waits, core_ref, *refs):
@@ -730,6 +772,41 @@
         cost_estimate=pl.CostEstimate(flops=rows * size * size, bytes_accessed=rows * size * size * 6, transcendentals=0),
         name="pair_sum",
     )(chip, *([kept] * chips), *([received] * chips))
+
+
+def input_grad_kernel(moved_ref, last_ref, tokens_ref, seed_ref, mean_ref, inverse_ref, out_ref):
+    d_scaled = moved_ref[...].astype(jnp.float32) + last_ref[...].astype(jnp.float32)
+    inverse = inverse_ref[...]
+    scaled = (tokens_ref[...].astype(jnp.float32) - mean_ref[...]) * inverse
+    average = jnp.mean(d_scaled, axis=1, keepdims=True)
+    projection = jnp.mean(d_scaled * scaled, axis=1, keepdims=True)
+    out_ref[...] = seed_ref[...].astype(jnp.float32) + inverse * (d_scaled - average - scaled * projection)
+
+
+def input_gradient(moved, dz, tokens, seed, mean, inverse, rank, waits):
+    rows, width = moved.shape
+    tile = min(128, rows)
+    per = rows // tile
+    own = lambda n: pl.BlockSpec((tile, n), lambda i, rank: (i, 0))
+    ranked = lambda n: pl.BlockSpec((tile, n), lambda i, rank: (rank[0] * per + i, 0))
+
+    def kernel(rank_ref, *refs):
+        input_grad_kernel(*refs[:6], refs[-1])
+
+    return pl.pallas_call(
+        kernel,
+        grid_spec=pltpu.PrefetchScalarGridSpec(
+            num_scalar_prefetch=1,
+            grid=(per,),
+            in_specs=[own(width), ranked(width), own(width), ranked(width), ranked(1), ranked(1)]
+            + [pl.BlockSpec(memory_space=pl.ANY)] * len(waits),
+            out_specs=own(width),
+        ),
+        out_shape=jax.ShapeDtypeStruct((rows, width), jnp.float32),
+        compiler_params=kernel_params(),
+        cost_estimate=pl.CostEstimate(flops=rows * width * 12, bytes_accessed=rows * width * 12, transcendentals=0),
+        name="input_gradient",
+    )(rank, moved, dz, tokens, seed, mean, inverse, *waits)
 
 
 def dot32(left_arg, right_arg):
@@ -993,7 +1070,6 @@
     own_pack = own_pos // pack_len
     valid_own = (own_pack < packs[0]).astype(jnp.float32)
     owned_input_rows = tokens.astype(jnp.float32)
-    owned_centred_scaled, owned_inverse_deviation = apply_layer_norm(owned_input_rows)
 
     group_pack = jnp.arange(group_tok) // pack_len
     lookup_key = group_pack * seg_width + segments.reshape(-1)
@@ -1001,8 +1077,6 @@
     subset_tok = jnp.sum(jnp.where(onehot, subsets.reshape(-1)[None, :], 0), axis=1)
     weight = 0.5 + subset_tok.astype(jnp.float32) / (SUBSETS - 1)
     factor = (weight * (group_pack < packs[0]).astype(jnp.float32))[:, None]
-    own_factor = lax.dynamic_slice_in_dim(factor, tp_rank * tok_dev, tok_dev, 0)
-    seed16 = (cotangent.astype(jnp.float32) * own_factor).astype(jnp.bfloat16)
 
     rank = tp_rank.astype(jnp.int32)[None]
     cosines, sines = turn_tables(pack_len, 128)
@@ -1029,59 +1103,9 @@
         after(partial_value, cotangent_parts[-1], early[5]), "tp", scatter_dimension=0, tiled=True
     )
     d_qkv16 = attend_back(qkv16, d_attended, segments, cosines, sines, heads_dev)
-    dz16, first_sums, qkv_sums = qkv_back(
-        d_qkv16, dz_part, group_tokens, mean, inverse, blocks, owned, norm_params
-    )
-
-    dz_rows = lambda back: lax.dynamic_slice_in_dim(dz16, (tp_rank - back) % tp_ways * tok_dev, tok_dev, 0)
-    back = 2
-
-    def pass_on(moving, back):
-        total = moving.astype(jnp.float32) + dz_rows(back).astype(jnp.float32)
-        return total if back == tp_ways else onward(total.astype(jnp.bfloat16), "tp")
-
-    shared_local = jnp.concatenate(
-        [
-            jnp.sum(first_sums.reshape(2, 8, model_width), axis=1),
-            jnp.sum((early[4][:16] + late[4][:16]).reshape(2, 8, model_width), axis=1),
-            jnp.sum(early[4][16:], axis=0)[None],
-        ],
-        0,
-    )
-    vecs_local = jnp.concatenate(
-        [
-            jnp.sum(qkv_sums, axis=0).reshape(3 * heads_dev, HD),
-            jnp.sum(early[5] + late[5], axis=0).reshape(ff_dev // HD, HD),
-        ],
-        0,
-    )
-    small = jnp.concatenate(
-        [
-            shared_local.reshape(5, dp_ways, -1).transpose(1, 0, 2).reshape(dp_ways, -1),
-            vecs_local.reshape(vec_rows, dp_ways, -1).transpose(1, 0, 2).reshape(dp_ways, -1),
-        ],
-        1,
-    )
-    small_in = after(small_rows(small, dp_ways), branch)
-    small_own = lax.psum_scatter(small_in, "dp", scatter_dimension=0, tiled=True).reshape(-1)
-    output = (
-        valid_own[:, None]
-        * (owned_input_rows + branch.astype(jnp.float32) + norm_params[4] + norm_params[5])
-    ).astype(jnp.bfloat16)
-
-    shared_size = 5 * model_width // dp_ways
-    own_vec_grads = small_own[shared_size : small.shape[1]].reshape(vec_rows, HD // dp_ways)
-    shared_part = small_own[:shared_size].reshape(5, tp_ways, -1).transpose(1, 0, 2)
-    shared_own = lax.psum_scatter(
-        small_rows(shared_part.reshape(tp_ways, -1), tp_ways), "tp", scatter_dimension=0, tiled=True
-    ).reshape(-1)
-    shared_own = shared_own[: shared_size // tp_ways].reshape(5, -1)
-    shared_grads = jnp.concatenate([shared_own, shared_own[4:]], 0)
     dp_rank = lax.axis_index("dp").astype(jnp.int32)
     lefts = (first_turned, second_turned, active_turned, attended_turned)
-    d_qkv_late, first_rows = lax.optimization_barrier((d_qkv16, dz_rows(1)))
-    moving = onward(first_rows, "tp")
-    rights = (d_hidden16, seed_all, d_qkv_late)
+    rights = (d_hidden16, seed_all, d_qkv16)
     firsts = (0, first_out, first_in, first_down)
     qkv_blocks = 3 * head_cols // block_size
     parts = 4
@@ -1094,11 +1118,71 @@
         and first_out % block_rows == 0
         and first_in % block_rows == 0
     )
+    sums = []
+
+    def quarter(part, waits):
+        kept, away = weight_grads(
+            part, parts, lefts, rights, firsts, (dp_rank % 2)[None], owned, dp_ways, block_size, waits
+        )
+        sums.append(pair_sum(kept, swap(away, 1), (dp_rank // 2)[None], dp_ways // 2))
+        return kept
+
+    first_waits = ()
+    if by_part:
+        quarter(0, ())
+        quarter(1, ())
+        first_waits = (sums[0][0],)
+    dz16, first_sums, qkv_sums = qkv_back(
+        d_qkv16, dz_part, group_tokens, mean, inverse, blocks, owned, norm_params, first_waits
+    )
+    dz_rows = lambda back: lax.dynamic_slice_in_dim(dz16, (tp_rank - back) % tp_ways * tok_dev, tok_dev, 0)
+    back = 2
+
+    def pass_on(moving, back):
+        total = moving.astype(jnp.float32) + dz_rows(back).astype(jnp.float32)
+        return total.astype(jnp.bfloat16)
+
+    moving = onward(dz_rows(1), "tp")
+    shared_local = jnp.concatenate(
+        [
+            jnp.sum(first_sums.reshape(2, 8, model_width), axis=1),
+            jnp.sum((early[4][:16] + late[4][:16]).reshape(2, 8, model_width), axis=1),
+            jnp.sum(early[4][16:], axis=0)[None],
+        ],
+        0,
+    )
+    vecs_local = jnp.concatenate(
+        [
+            jnp.sum(qkv_sums, axis=0).reshape(3 * heads_dev, HD),
+            jnp.sum(early[5] + late[5], axis=0).reshape(ff_dev // HD, HD),
+        ],
+        0,
+    )
+    small = jnp.concatenate(
+        [
+            shared_local.reshape(5, dp_ways, -1).transpose(1, 0, 2).reshape(dp_ways, -1),
+            vecs_local.reshape(vec_rows, dp_ways, -1).transpose(1, 0, 2).reshape(dp_ways, -1),
+        ],
+        1,
+    )
+    small_in = after(small_rows(small, dp_ways), branch)
+    small_own = lax.psum_scatter(small_in, "dp", scatter_dimension=0, tiled=True).reshape(-1)
+    output = (
+        valid_own[:, None]
+        * (owned_input_rows + branch.astype(jnp.float32) + norm_params[4] + norm_params[5])
+    ).astype(jnp.bfloat16)
+
+    shared_size = 5 * model_width // dp_ways
+    own_vec_grads = small_own[shared_size : small.shape[1]].reshape(vec_rows, HD // dp_ways)
+    shared_part = small_own[:shared_size].reshape(5, tp_ways, -1).transpose(1, 0, 2)
+    shared_in = small_rows(shared_part.reshape(tp_ways, -1), tp_ways)
+    shared_own = lax.psum_scatter(shared_in, "tp", scatter_dimension=0, tiled=True).reshape(-1)
+    shared_own = shared_own[: shared_size // tp_ways].reshape(5, -1)
+    shared_grads = jnp.concatenate([shared_own, shared_own[4:]], 0)
     results = ()
     if by_part:
         part_size = owned // parts
         span = block_rows // parts
-        sums = []
         terms = []
         ready = []
 
@@ -1108,17 +1192,9 @@
                 ready.append(sums[part][3])
             terms.append([sums[part][0]] + [swap(sums[part][bits], 2 * bits) for bits in range(1, 4)])
 
-        for part in range(parts):
-            waits = (sums[part - 2][0],) if part >= 2 else ()
-            if part == parts - 1:
-                send_on(0)
-                waits += tuple(terms[0][1:])
-            kept, away = weight_grads(
-                part, parts, lefts, rights, firsts, (dp_rank % 2)[None], owned, dp_ways, block_size, waits
-            )
-            sums.append(pair_sum(kept, swap(away, 1), (dp_rank // 2)[None], dp_ways // 2))
-        moving = pass_on(after(moving, kept), back)
-        back += 1
+        send_on(0)
+        quarter(2, (dz16, sums[1][0]) + tuple(terms[0][1:]))
+        quarter(3, tuple(terms[0][1:]))
         for part in range(1, parts):
             send_on(part)
         count = jnp.arange(part_size, dtype=jnp.int32)
@@ -1132,25 +1208,30 @@
             waits = []
             if part < parts - 1:
                 waits.append(ready[part])
+            if part == 0:
+                waits += terms[1][1:]
+            if part % 2 == 1 and back < tp_ways:
+                if part:
+                    moving, first_result = lax.optimization_barrier((moving, results[0]))
+                    results = [first_result] + list(results[1:])
+                total = pass_on(moving, back)
+                waits.append(total)
+                moving = onward(total, "tp")
+                back += 1
             if part == 1:
                 waits.append(small_in)
             if part == 2:
-                waits.append(small_own)
+                waits += [small_own, shared_in]
             if part == 3:
                 waits += [output, shared_own]
             results = shampoo(
                 terms[part], left_stats, right_stats, master_blocks, places, results, waits
             )
-            if part % 2 == 1 and back <= tp_ways:
-                moving, first_result = lax.optimization_barrier((moving, results[0]))
-                results = [first_result] + list(results[1:])
-                moving = pass_on(moving, back)
-                back += 1
     else:
         local = [
             to_blocks(jnp.dot(left, right, preferred_element_type=jnp.float32).astype(jnp.bfloat16), block_size)
             for left, right in (
-                (first_turned, d_qkv_late),
+                (first_turned, d_qkv16),
                 (attended_turned, seed_all),
                 (second_turned, d_hidden16),
                 (active_turned, seed_all),
@@ -1160,19 +1241,11 @@
         results = shampoo(
             [grads16], left_stats, right_stats, master_blocks, jnp.arange(owned, dtype=jnp.int32), results
         )
-    while back <= tp_ways:
-        moving = pass_on(moving, back)
+    while back < tp_ways:
+        moving = onward(pass_on(moving, back), "tp")
         back += 1
-    norm_input_gradient = moving
+    input_grad = input_gradient(moving, dz16, tokens, seed_all, mean, inverse, rank, results[:1])
     own_grads, left_new, right_new, new_blocks = results
-    average_gradient = jnp.mean(norm_input_gradient, axis=-1, keepdims=True)
-    average_projection = jnp.mean(
-        norm_input_gradient * owned_centred_scaled, axis=-1, keepdims=True
-    )
-    input_grad = seed16.astype(jnp.float32) + owned_inverse_deviation * (
-        norm_input_gradient - average_gradient - owned_centred_scaled * average_projection
-    )
-
     local_stat_new = DECAY * local_vec_stats + own_vec_grads * own_vec_grads
     local_new = local_vecs - RATE_VEC * own_vec_grads * lax.rsqrt(local_stat_new)
     shared_stat_new = DECAY * shared_vec_stats + shared_grads * shared_grads

time: 705 us -> 771 us (1.094)
  Pallas kernels: 425 us -> 498 us
  other arithmetic: 44.2 us -> 31.3 us
  waiting for transfers between devices: 156 us -> 166 us
    pallas_call x2 -> x3, Pallas kernels: 82.3 us -> 128 us  [the longest x1 93.7 us: feed_forward(): pl.pallas_call(functools.partial(feed_kernel, tokens // tile, offsets, ow...]
    ppermute x9, waiting for transfers between devices: 97.4 us -> 120 us  [onward(): lax.ppermute(part, axis, [(each, (each + 1) % ways) for each in range(way...]
    pallas_call x2, Pallas kernels: 72.7 us -> 94.8 us  [feed_back(): pl.pallas_call(functools.partial(feed_back_kernel, offsets, owned, first_...]
    ppermute x16, waiting for transfers between devices: 18.9 us -> 5.4 us  [swap(): lax.ppermute(part, 'dp', [(each, each ^ bits) for each in range(ways)])]
    reduce_sum x3 -> x0, other arithmetic: 10 us -> none  [the longest x1 4.34 us: apply_layer_norm(): variance = jnp.mean(centred * centred, axis=-1, keepdims=True)]
  transfers between devices with their start and end apart: 32 -> 32, of which waited for: 7 -> 9; matrix products, arithmetic and copies ran while one was open for 7% -> 5% of each run, Pallas kernels for 61% -> 64%
where the time goes in v5:
time: 771 us; the launch traced here: 766 us
  Pallas kernels  498 us (65%)
  waiting for transfers between devices  166 us (22%)
  other arithmetic  31.3 us (4%)
  starting transfers between devices  31.2 us (4%)
  local copies, waits for them, and re-layouts  24.9 us (3%)
  between operations  15.3 us (2%)
    ppermute x9, waiting for transfers between devices, onward(): lax.ppermute(part, axis, [(each, (each + 1) % ways) for each in range(way...  120 us
    pallas_call x4, Pallas kernels, shampoo(): pl.pallas_call(functools.partial(shampoo_kernel, count, len(grads), held...  111 us
    pallas_call x2, Pallas kernels, feed_back(): pl.pallas_call(functools.partial(feed_back_kernel, offsets, owned, first_...  94.8 us
    pallas_call x1, Pallas kernels, feed_forward(): pl.pallas_call(functools.partial(feed_kernel, tokens // tile, offsets, ow...  93.7 us
    pallas_call x4, Pallas kernels, weight_grads(): pl.pallas_call(functools.partial(weight_grad_kernel, tuple(steps), len(wa...  78.5 us
    pallas_call x1, Pallas kernels, project_qkv(): pl.pallas_call(functools.partial(qkv_kernel, heads, owned, ways), grid_sp...  37.6 us
    pallas_call x1, Pallas kernels, qkv_back(): pl.pallas_call(functools.partial(qkv_back_kernel, tokens // tile, owned,...  27.6 us
    all_gather x1, waiting for transfers between devices, shards(): blocks = lax.all_gather(rows16, 'dp', axis=0, tiled=True)  25.8 us
  transfers between devices with their start and end apart: 32, of which 9 were waited for; matrix products, arithmetic and copies ran while one was open for 5% of the time, Pallas kernels for 64%

profile of v5, /device:TPU:0, one launch (start us, length us, event | category | flops | bytes accessed | tf_op | source)
XLA Modules:
  0.0 766.3 jit_solution(8011664639408116297)
XLA Ops:
  8.9 3.2 convert.20
  17.7 47.8 %collective-permute-done.refs_1_ = bf16[512,2048]{1,0:T(8,128)(2,1)} collective-permute-done((bf16[512,2048]{1,0:T(8,128)(2,1)S(1)}, bf16[512,2048]{1,0:T(8,128)(2,1)}, u32[]{:S(2)}, u32[]{:S(2)}) %collective-permute-start) | collective-permute-done | bytes 2097184 | tf_op jit(solution)/shard_map/ppermute | solution.py:993
  65.5 48.8 %collective-permute-done.1.refs_2_ = bf16[512,2048]{1,0:T(8,128)(2,1)} collective-permute-done((bf16[512,2048]{1,0:T(8,128)(2,1)}, bf16[512,2048]{1,0:T(8,128)(2,1)}, u32[]{:S(2)}, u32[]{:S(2)}) %collective-permute-start.1) | collective-permute-done | bytes 2097184 | tf_op jit(solution)/shard_map/ppermute | solution.py:993
  116.7 25.8 %all-gather.2.cloned.1.call-done.refs_4_.blocks_ref.refs_8_.refs_6_ = bf16[49280,256]{1,0:T(8,128)(2,1)} async-done(((bf16[6160,256]{1,0:T(8,128)(2,1)}), bf16[49280,256]{1,0:T(8,128)(2,1)}) %all-gather.2.cloned.1.call-update) | async-done | bytes 25231376 | tf_op jit(solution)/shard_map/all_gather | solution.py:1042
  148.8 13.8 %collective-permute-done.3 = bf16[8,384]{1,0:T(8,128)(2,1)S(1)} collective-permute-done((bf16[8,384]{1,0:T(8,128)(2,1)S(1)}, bf16[8,384]{1,0:T(8,128)(2,1)S(1)}, u32[]{:S(2)}, u32[]{:S(2)}) %collective-permute-start.3) | collective-permute-done | bytes 6176 | tf_op jit(solution)/shard_map/ppermute | solution.py:1057
  171.1 37.6 %qkv.1 = (bf16[2048,1536]{1,0:T(8,128)(2,1)}, bf16[2048,2048]{1,0:T(8,128)(2,1)}, bf16[2048,2048]{1,0:T(8,128)(2,1)}, bf16[2048,2048]{1,0:T(8,128)(2,1)}, bf16[2...) custom-call(s32[1]{0:T(128)} %bitcast.1.rank_ref, bf16[512,2048]{1,0:T(8,128)(2,1)} %refs_2_.1, ...), custom_call_target="tpu_custom_call" | custom-call | flops 12884901888 | bytes 46137344 | tf_op jit(solution)/shard_map/qkv/pallas_call | solution.py:215
  208.7 10.8 %attend.1 = (bf16[2048,512]{1,0:T(8,128)(2,1)}, bf16[512,2048]{1,0:T(8,128)(2,1)}) custom-call(bf16[2048,1536]{1,0:T(8,128)(2,1)} %get-tuple-element.98.query_ref.key_ref.value_ref, bf16[2048,1536]{1,0:T(8,128)(2,1)} %get-tuple-element.98.query_ref.key_ref.value_ref, bf16[2048,1536]{1,0:T(8,128)(2,1)} %get-tuple-element.98.query_ref.key_ref.value_ref, ...), custom_call_target="tpu_custom_call" | custom-call | flops 3221225472 | bytes 8388608 | tf_op jit(solution)/shard_map/attend/pallas_call | solution.py:266
  220.0 93.7 %feed.1 = (bf16[2048,2048]{1,0:T(8,128)(2,1)}, bf16[2048,2048]{1,0:T(8,128)(2,1)}, bf16[2048,2048]{1,0:T(8,128)(2,1)}) custom-call(bf16[2048,2048]{1,0:T(8,128)(2,1)} %get-tuple-element.97.x_ref, bf16[2048,512]{1,0:T(8,128)(2,1)} %get-tuple-element.99.attended_ref, bf16[49280,256]{1,0:T(8,128)(2,1)} %all-gather.2.cloned.1.call-done.refs_4_.blocks_ref.refs_8_.refs_6_, ...), custom_call_target="tpu_custom_call" | custom-call | flops 38654705664 | bytes 58720256 | tf_op jit(solution)/shard_map/feed/pallas_call | solution.py:414
  315.4 59.1 %feed_back.2 = (bf16[2048,2048]{1,0:T(8,128)(2,1)}, bf16[2048,512]{1,0:T(8,128)(2,1)}, bf16[2048,2048]{1,0:T(8,128)(2,1)}, bf16[2048,2048]{1,0:T(8,128)(2,1)}, f32[24,2048]{1,0:T(8,128)}, /*index=5*/f32[8,2048]{1,0:T(8,128)}) custom-call(s32[1]{0:T(128)} %bitcast.1.rank_ref, bf16[512,2048]{1,0:T(8,128)(2,1)} %refs_0_.3, ...), custom_call_target="tpu_custom_call" | custom-call | flops 28991029248 | bytes 60817408 | tf_op jit(solution)/shard_map/feed_back/pallas_call | solution.py:525
  375.9 35.7 %feed_back.3 = (bf16[2048,2048]{1,0:T(8,128)(2,1)}, bf16[2048,512]{1,0:T(8,128)(2,1)}, bf16[2048,2048]{1,0:T(8,128)(2,1)}, bf16[2048,2048]{1,0:T(8,128)(2,1)}, f32[24,2048]{1,0:T(8,128)}, /*index=5*/f32[8,2048]{1,0:T(8,128)}) custom-call(s32[1]{0:T(128)} %bitcast.1.rank_ref, ...), custom_call_target="tpu_custom_call", output_to_operand_aliasing={{0}: (9, {}), {1}: (10, {}), {2}: (11, {}), {3}: (12, {})} | custom-call | flops 9663676416 | bytes 31457280 | tf_op jit(solution)/shard_map/feed_back/pallas_call | solution.py:525
  411.6 17.0 %attend_back.1.refs_6_.d_qkv_ref = bf16[2048,1536]{1,0:T(8,128)(2,1)} custom-call(bf16[2048,1536]{1,0:T(8,128)(2,1)} %get-tuple-element.98.query_ref.key_ref.value_ref, bf16[2048,1536]{1,0:T(8,128)(2,1)} %get-tuple-element.98.query_ref.key_ref.value_ref, bf16[2048,1536]{1,0:T(8,128)(2,1)} %get-tuple-element.98.query_ref.key_ref.value_ref, ...), custom_call_target="tpu_custom_call" | custom-call | flops 7516192768 | bytes 16777216 | tf_op jit(solution)/shard_map/attend_back/pallas_call | solution.py:333
  428.6 19.3 %weight_grads.4 = (bf16[24,256,256]{2,1,0:T(8,128)(2,1)}, bf16[24,256,256]{2,1,0:T(8,128)(2,1)}) custom-call(s32[1]{0:T(128)} %bitcast.13.core_ref, bf16[2048,2048]{1,0:T(8,128)(2,1)} %get-tuple-element.116.refs_0_, bf16[2048,2048]{1,0:T(8,128)(2,1)} %get-tuple-element.117.refs_1_, bf16[2048,2048]{1,0:T(8,128)(2,1)} %get-tuple-element.118.refs_2_, ...), custom_call_target="tpu_custom_call" | custom-call | flops 12884901888 | bytes 25769804 | tf_op jit(solution)/shard_map/weight_grads/pallas_call | solution.py:726
  447.9 20.2 %weight_grads.5 = (bf16[24,256,256]{2,1,0:T(8,128)(2,1)}, bf16[24,256,256]{2,1,0:T(8,128)(2,1)}) custom-call(s32[1]{0:T(128)} %bitcast.13.core_ref, bf16[2048,2048]{1,0:T(8,128)(2,1)} %get-tuple-element.116.refs_0_, bf16[2048,2048]{1,0:T(8,128)(2,1)} %get-tuple-element.117.refs_1_, bf16[2048,2048]{1,0:T(8,128)(2,1)} %get-tuple-element.118.refs_2_, ...), custom_call_target="tpu_custom_call" | custom-call | flops 12884901888 | bytes 25769804 | tf_op jit(solution)/shard_map/weight_grads/pallas_call | solution.py:726
  468.6 5.0 pair_sum.4
  478.8 5.0 pair_sum.5
  483.7 27.6 %qkv_back.1 = (bf16[2048,2048]{1,0:T(8,128)(2,1)}, f32[16,2048]{1,0:T(8,128)}, f32[8,1536]{1,0:T(8,128)}) custom-call(bf16[2048,1536]{1,0:T(8,128)(2,1)} %attend_back.1.refs_6_.d_qkv_ref, bf16[2048,2048]{1,0:T(8,128)(2,1)} %get-tuple-element.115.part_ref, bf16[2048,2048]{1,0:T(8,128)(2,1)} %get-tuple-element.105.refs_5_.refs_3_.tokens_ref, ...), custom_call_target="tpu_custom_call" | custom-call | flops 12884901888 | bytes 46137344 | tf_op jit(solution)/shard_map/qkv_back/pallas_call | solution.py:605
  511.4 19.4 %weight_grads.6 = (bf16[24,256,256]{2,1,0:T(8,128)(2,1)}, bf16[24,256,256]{2,1,0:T(8,128)(2,1)}) custom-call(s32[1]{0:T(128)} %bitcast.13.core_ref, bf16[2048,2048]{1,0:T(8,128)(2,1)} %get-tuple-element.116.refs_0_, bf16[2048,2048]{1,0:T(8,128)(2,1)} %get-tuple-element.117.refs_1_, bf16[2048,2048]{1,0:T(8,128)(2,1)} %get-tuple-element.118.refs_2_, ...), custom_call_target="tpu_custom_call" | custom-call | flops 12884901888 | bytes 25769804 | tf_op jit(solution)/shard_map/weight_grads/pallas_call | solution.py:726
  547.6 19.7 %weight_grads.7 = (bf16[24,256,256]{2,1,0:T(8,128)(2,1)}, bf16[24,256,256]{2,1,0:T(8,128)(2,1)}) custom-call(s32[1]{0:T(128)} %bitcast.13.core_ref, bf16[2048,2048]{1,0:T(8,128)(2,1)} %get-tuple-element.116.refs_0_, bf16[2048,2048]{1,0:T(8,128)(2,1)} %get-tuple-element.117.refs_1_, bf16[2048,2048]{1,0:T(8,128)(2,1)} %get-tuple-element.118.refs_2_, ...), custom_call_target="tpu_custom_call" | custom-call | flops 12884901888 | bytes 25769804 | tf_op jit(solution)/shard_map/weight_grads/pallas_call | solution.py:726
  568.1 3.5 collective-permute-start.10
  571.6 4.9 pair_sum.6
  576.6 5.4 collective-permute-done.17.refs_16_.refs_3_
  583.3 27.6 %shampoo.4 = (f32[24,256,256]{2,1,0:T(8,128)}, f32[24,256,256]{2,1,0:T(8,128)}, f32[24,256,256]{2,1,0:T(8,128)}, f32[24,256,256]{2,1,0:T(8,128)}) custom-call(s32[6]{0:T(128)} %broadcast_select_fusion.3.places_ref, f32[6,256,256]{2,1,0:T(8,128)} %get-tuple-element.124.refs_0_, bf16[6,256,256]{2,1,0:T(8,128)(2,1)} %collective-permute-done.11.refs_1_.refs_9_.refs_7_, ...), custom_call_target="tpu_custom_call" | custom-call | flops 26172456960 | bytes 11796480 | tf_op jit(solution)/shard_map/shampoo/pallas_call | solution.py:949
  610.9 7.5 collective-permute-done.10
  618.4 4.5 add_convert_fusion.1.refs_18_
  627.1 4.9 pair_sum.7
  634.4 27.9 %shampoo.5 = (f32[24,256,256]{2,1,0:T(8,128)}, f32[24,256,256]{2,1,0:T(8,128)}, f32[24,256,256]{2,1,0:T(8,128)}, f32[24,256,256]{2,1,0:T(8,128)}) custom-call(s32[6]{0:T(128)} %broadcast_select_fusion.1.places_ref, f32[6,256,256]{2,1,0:T(8,128)} %get-tuple-element.139.refs_8_.refs_0_, ...), custom_call_target="tpu_custom_call", output_to_operand_aliasing={{0}: (14, {}), {1}: (15, {}), {2}: (16, {}), {3}: (17, {})} | custom-call | flops 26172456960 | bytes 11796480 | tf_op jit(solution)/shard_map/shampoo/pallas_call | solution.py:949
  662.3 4.1 multiply_convert_fusion.refs_18_
  670.2 27.9 %shampoo.6 = (f32[24,256,256]{2,1,0:T(8,128)}, f32[24,256,256]{2,1,0:T(8,128)}, f32[24,256,256]{2,1,0:T(8,128)}, f32[24,256,256]{2,1,0:T(8,128)}) custom-call(s32[6]{0:T(128)} %broadcast_select_fusion.2.places_ref, f32[6,256,256]{2,1,0:T(8,128)} %get-tuple-element.142.refs_0_, ...), custom_call_target="tpu_custom_call", output_to_operand_aliasing={{0}: (14, {}), {1}: (15, {}), {2}: (16, {}), {3}: (17, {})} | custom-call | flops 26172456960 | bytes 11796480 | tf_op jit(solution)/shard_map/shampoo/pallas_call | solution.py:949
  698.2 4.5 add_convert_fusion.refs_17_
  707.8 27.7 %shampoo.7 = (f32[24,256,256]{2,1,0:T(8,128)}, f32[24,256,256]{2,1,0:T(8,128)}, f32[24,256,256]{2,1,0:T(8,128)}, f32[24,256,256]{2,1,0:T(8,128)}) custom-call(s32[6]{0:T(128)} %broadcast_select_fusion.places_ref, f32[6,256,256]{2,1,0:T(8,128)} %get-tuple-element.169.refs_0_, ...), custom_call_target="tpu_custom_call", output_to_operand_aliasing={{0}: (14, {}), {1}: (15, {}), {2}: (16, {}), {3}: (17, {})} | custom-call | flops 26172456960 | bytes 11796480 | tf_op jit(solution)/shard_map/shampoo/pallas_call | solution.py:949
  735.6 16.0 %collective-permute-done.24.refs_0_ = bf16[512,2048]{1,0:T(8,128)(2,1)S(1)} collective-permute-done((bf16[512,2048]{1,0:T(8,128)(2,1)}, bf16[512,2048]{1,0:T(8,128)(2,1)S(1)}, u32[]{:S(2)}, u32[]{:S(2)}) %collective-permute-start.24) | collective-permute-done | bytes 2097184 | tf_op jit(solution)/shard_map/ppermute | solution.py:993
  752.9 6.7 input_gradient.1
  (188 shorter events, 68.5 us)
Async XLA Ops:
  7.2 135.3 %all-gather.2.cloned.1.call-start = ((), (), s32[]{:S(2)}) async-start(), calls=%async_computation.3 | async-start | bytes 28385280 | tf_op jit(solution)/shard_map/all_gather | solution.py:1042
  14.0 620.3 %reduce-scatter.4.cloned.1.call-start = ((), (), s32[]{:S(2)}) async-start(), calls=%async_computation.4 | async-start | bytes 10485760 | tf_op jit(solution)/shard_map/reduce_scatter | solution.py:1102
  14.6 50.8 %collective-permute-start = (bf16[512,2048]{1,0:T(8,128)(2,1)S(1)}, bf16[512,2048]{1,0:T(8,128)(2,1)}, u32[]{:S(2)}, u32[]{:S(2)}) collective-permute-start(bf16[512,2048]{1,0:T(8,128)(2,1)S(1)} %copy-done.2), channel_id=1, source_target_pairs={{0,1},{1,2},{2,3},{3,0},{4,5},{5,6},{6,7},{7,4},{8,9},{9,10},{10,1... | collective-permute-start | bytes 6291464 | tf_op jit(solution)/shard_map/ppermute | solution.py:993
  65.4 48.9 %collective-permute-start.1 = (bf16[512,2048]{1,0:T(8,128)(2,1)}, bf16[512,2048]{1,0:T(8,128)(2,1)}, u32[]{:S(2)}, u32[]{:S(2)}) collective-permute-start(bf16[512,2048]{1,0:T(8,128)(2,1)} %collective-permute-done.refs_1_), channel_id=1, source_target_pairs={{0,1},{1,2},{2,3},{3,0},{4,5},{5,6},{6,7},{7,4},{8,9},{9,10},{10,1... | collective-permute-start | bytes 6291464 | tf_op jit(solution)/shard_map/ppermute | solution.py:993
  114.3 48.4 %collective-permute-start.2 = (bf16[512,2048]{1,0:T(8,128)(2,1)}, bf16[512,2048]{1,0:T(8,128)(2,1)}, u32[]{:S(2)}, u32[]{:S(2)}) collective-permute-start(bf16[512,2048]{1,0:T(8,128)(2,1)} %collective-permute-done.1.refs_2_), channel_id=1, source_target_pairs={{0,1},{1,2},{2,3},{3,0},{4,5},{5,6},{6,7},{7,4},{8,9},{9,10},{10,1... | collective-permute-start | bytes 6291464 | tf_op jit(solution)/shard_map/ppermute | solution.py:993
  143.4 19.2 %collective-permute-start.3 = (bf16[8,384]{1,0:T(8,128)(2,1)S(1)}, bf16[8,384]{1,0:T(8,128)(2,1)S(1)}, u32[]{:S(2)}, u32[]{:S(2)}) collective-permute-start(bf16[8,384]{1,0:T(8,128)(2,1)S(1)} %slice.75), channel_id=1, source_target_pairs={{0,1},{1,2},{2,3},{3,0},{4,5},{5,6},{6,7},{7,4},{8,9},{9,10},{10,1... | collective-permute-start | bytes 18440 | tf_op jit(solution)/shard_map/ppermute | solution.py:1057
  144.9 17.8 %collective-permute-start.4 = (bf16[8,384]{1,0:T(8,128)(2,1)S(1)}, bf16[8,384]{1,0:T(8,128)(2,1)S(1)}, u32[]{:S(2)}, u32[]{:S(2)}) collective-permute-start(bf16[8,384]{1,0:T(8,128)(2,1)S(1)} %slice.75), channel_id=1, source_target_pairs={{0,2},{1,3},{2,0},{3,1},{4,6},{5,7},{6,4},{7,5},{8,10},{9,11},{10,... | collective-permute-start | bytes 18440 | tf_op jit(solution)/shard_map/ppermute | solution.py:1057
  147.3 15.4 %collective-permute-start.5 = (bf16[8,384]{1,0:T(8,128)(2,1)S(1)}, bf16[8,384]{1,0:T(8,128)(2,1)S(1)}, u32[]{:S(2)}, u32[]{:S(2)}) collective-permute-start(bf16[8,384]{1,0:T(8,128)(2,1)S(1)} %slice.75), channel_id=1, source_target_pairs={{0,3},{1,0},{2,1},{3,2},{4,7},{5,4},{6,5},{7,6},{8,11},{9,8},{10,9... | collective-permute-start | bytes 18440 | tf_op jit(solution)/shard_map/ppermute | solution.py:1057
  162.7 56.7 %collective-permute-start.6 = (bf16[512,2048]{1,0:T(8,128)(2,1)}, bf16[512,2048]{1,0:T(8,128)(2,1)}, u32[]{:S(2)}, u32[]{:S(2)}) collective-permute-start(bf16[512,2048]{1,0:T(8,128)(2,1)} %refs_0_.3), channel_id=1, source_target_pairs={{0,1},{1,2},{2,3},{3,0},{4,5},{5,6},{6,7},{7,4},{8,9},{9,10},{10,1... | collective-permute-start | bytes 6291464 | tf_op jit(solution)/shard_map/ppermute | solution.py:993
  219.5 94.2 %collective-permute-start.7 = (bf16[512,2048]{1,0:T(8,128)(2,1)}, bf16[512,2048]{1,0:T(8,128)(2,1)S(1)}, u32[]{:S(2)}, u32[]{:S(2)}) collective-permute-start(bf16[512,2048]{1,0:T(8,128)(2,1)} %collective-permute-done.6.refs_1_), channel_id=1, source_target_pairs={{0,1},{1,2},{2,3},{3,0},{4,5},{5,6},{6,7},{7,4},{8,9},{9,10},{10,1... | collective-permute-start | bytes 6291464 | tf_op jit(solution)/shard_map/ppermute | solution.py:993
  315.0 59.5 %collective-permute-start.8 = (bf16[512,2048]{1,0:T(8,128)(2,1)}, bf16[512,2048]{1,0:T(8,128)(2,1)S(1)}, u32[]{:S(2)}, u32[]{:S(2)}) collective-permute-start(bf16[512,2048]{1,0:T(8,128)(2,1)} %copy-done.20), channel_id=1, source_target_pairs={{0,1},{1,2},{2,3},{3,0},{4,5},{5,6},{6,7},{7,4},{8,9},{9,10},{10,1... | collective-permute-start | bytes 6291464 | tf_op jit(solution)/shard_map/ppermute | solution.py:993
  375.9 291.3 %reduce-scatter.6.cloned.1.call-start = ((), (), s32[]{:S(2)}) async-start(), calls=%async_computation.5 | async-start | bytes 73728 | tf_op jit(solution)/shard_map/reduce_scatter | solution.py:1169
  447.8 20.8 %collective-permute-start.9 = (bf16[24,256,256]{2,1,0:T(8,128)(2,1)}, bf16[24,256,256]{2,1,0:T(8,128)(2,1)}, u32[]{:S(2)}, u32[]{:S(2)}) collective-permute-start(bf16[24,256,256]{2,1,0:T(8,128)(2,1)} %get-tuple-element.123), channel_id=1, source_target_pairs={{0,4},{4,0},{8,12},{12,8},{16,20},{20,16},{24,28},{28,24},{1,5},{5... | collective-permute-start | bytes 9437192 | tf_op jit(solution)/shard_map/ppermute | solution.py:998
  468.1 9.0 %collective-permute-start.14 = (bf16[24,256,256]{2,1,0:T(8,128)(2,1)}, bf16[24,256,256]{2,1,0:T(8,128)(2,1)S(1)}, u32[]{:S(2)}, u32[]{:S(2)}) collective-permute-start(bf16[24,256,256]{2,1,0:T(8,128)(2,1)} %get-tuple-element.130), channel_id=1, source_target_pairs={{0,4},{4,0},{8,12},{12,8},{16,20},{20,16},{24,28},{28,24},{1,5},{5... | collective-permute-start | bytes 9437192 | tf_op jit(solution)/shard_map/ppermute | solution.py:998
  473.6 37.7 %collective-permute-start.11 = (bf16[6,256,256]{2,1,0:T(8,128)(2,1)}, bf16[6,256,256]{2,1,0:T(8,128)(2,1)}, u32[]{:S(2)}, u32[]{:S(2)}) collective-permute-start(bf16[6,256,256]{2,1,0:T(8,128)(2,1)} %get-tuple-element.126), channel_id=1, source_target_pairs={{0,8},{4,12},{8,0},{12,4},{16,24},{20,28},{24,16},{28,20},{1,9},{5... | collective-permute-start | bytes 2359304 | tf_op jit(solution)/shard_map/ppermute | solution.py:998
  474.6 36.7 %collective-permute-start.12 = (bf16[6,256,256]{2,1,0:T(8,128)(2,1)}, bf16[6,256,256]{2,1,0:T(8,128)(2,1)}, u32[]{:S(2)}, u32[]{:S(2)}) collective-permute-start(bf16[6,256,256]{2,1,0:T(8,128)(2,1)} %get-tuple-element.127), channel_id=1, source_target_pairs={{0,16},{4,20},{8,24},{12,28},{16,0},{20,4},{24,8},{28,12},{1,17},{... | collective-permute-start | bytes 2359304 | tf_op jit(solution)/shard_map/ppermute | solution.py:998
  476.1 35.2 %collective-permute-start.13 = (bf16[6,256,256]{2,1,0:T(8,128)(2,1)}, bf16[6,256,256]{2,1,0:T(8,128)(2,1)}, u32[]{:S(2)}, u32[]{:S(2)}) collective-permute-start(bf16[6,256,256]{2,1,0:T(8,128)(2,1)} %get-tuple-element.128), channel_id=1, source_target_pairs={{0,24},{4,28},{8,16},{12,20},{16,8},{20,12},{24,0},{28,4},{1,25},{... | collective-permute-start | bytes 2359304 | tf_op jit(solution)/shard_map/ppermute | solution.py:998
  530.8 37.3 %collective-permute-start.19 = (bf16[24,256,256]{2,1,0:T(8,128)(2,1)}, bf16[24,256,256]{2,1,0:T(8,128)(2,1)S(1)}, u32[]{:S(2)}, u32[]{:S(2)}) collective-permute-start(bf16[24,256,256]{2,1,0:T(8,128)(2,1)} %get-tuple-element.141), channel_id=1, source_target_pairs={{0,4},{4,0},{8,12},{12,8},{16,20},{20,16},{24,28},{28,24},{1,5},{5... | collective-permute-start | bytes 9437192 | tf_op jit(solution)/shard_map/ppermute | solution.py:998
  544.1 39.2 %collective-permute-start.15 = (bf16[6,256,256]{2,1,0:T(8,128)(2,1)}, bf16[6,256,256]{2,1,0:T(8,128)(2,1)}, u32[]{:S(2)}, u32[]{:S(2)}) collective-permute-start(bf16[6,256,256]{2,1,0:T(8,128)(2,1)} %get-tuple-element.134), channel_id=1, source_target_pairs={{0,8},{4,12},{8,0},{12,4},{16,24},{20,28},{24,16},{28,20},{1,9},{5... | collective-permute-start | bytes 2359304 | tf_op jit(solution)/shard_map/ppermute | solution.py:998
  545.2 38.1 %collective-permute-start.16 = (bf16[6,256,256]{2,1,0:T(8,128)(2,1)}, bf16[6,256,256]{2,1,0:T(8,128)(2,1)}, u32[]{:S(2)}, u32[]{:S(2)}) collective-permute-start(bf16[6,256,256]{2,1,0:T(8,128)(2,1)} %get-tuple-element.136), channel_id=1, source_target_pairs={{0,16},{4,20},{8,24},{12,28},{16,0},{20,4},{24,8},{28,12},{1,17},{... | collective-permute-start | bytes 2359304 | tf_op jit(solution)/shard_map/ppermute | solution.py:998
  546.7 35.2 %collective-permute-start.17 = (bf16[6,256,256]{2,1,0:T(8,128)(2,1)}, bf16[6,256,256]{2,1,0:T(8,128)(2,1)}, u32[]{:S(2)}, u32[]{:S(2)}) collective-permute-start(bf16[6,256,256]{2,1,0:T(8,128)(2,1)} %get-tuple-element.132.refs_13_), channel_id=1, source_target_pairs={{0,24},{4,28},{8,16},{12,20},{16,8},{20,12},{24,0},{28,4},{1,25},{... | collective-permute-start | bytes 2359304 | tf_op jit(solution)/shard_map/ppermute | solution.py:998
  567.3 59.8 %collective-permute-start.23 = (bf16[24,256,256]{2,1,0:T(8,128)(2,1)}, bf16[24,256,256]{2,1,0:T(8,128)(2,1)}, u32[]{:S(2)}, u32[]{:S(2)}) collective-permute-start(bf16[24,256,256]{2,1,0:T(8,128)(2,1)} %get-tuple-element.164), channel_id=1, source_target_pairs={{0,4},{4,0},{8,12},{12,8},{16,20},{20,16},{24,28},{28,24},{1,5},{5... | collective-permute-start | bytes 9437192 | tf_op jit(solution)/shard_map/ppermute | solution.py:998
  568.1 50.4 %collective-permute-start.10 = (bf16[512,2048]{1,0:T(8,128)(2,1)}, bf16[512,2048]{1,0:T(8,128)(2,1)}, u32[]{:S(2)}, u32[]{:S(2)}) collective-permute-start(bf16[512,2048]{1,0:T(8,128)(2,1)} %constant_dynamic-slice_fusion), channel_id=1, source_target_pairs={{0,1},{1,2},{2,3},{3,0},{4,5},{5,6},{6,7},{7,4},{8,9},{9,10},{10,1... | collective-permute-start | bytes 6291464 | tf_op jit(solution)/shard_map/ppermute | solution.py:993
  581.9 50.1 %collective-permute-start.22 = (bf16[6,256,256]{2,1,0:T(8,128)(2,1)}, bf16[6,256,256]{2,1,0:T(8,128)(2,1)S(1)}, u32[]{:S(2)}, u32[]{:S(2)}) collective-permute-start(bf16[6,256,256]{2,1,0:T(8,128)(2,1)} %get-tuple-element.148.refs_17_), channel_id=1, source_target_pairs={{0,24},{4,28},{8,16},{12,20},{16,8},{20,12},{24,0},{28,4},{1,25},{... | collective-permute-start | bytes 2359304 | tf_op jit(solution)/shard_map/ppermute | solution.py:998
  622.9 75.3 %collective-permute-start.18 = (bf16[512,2048]{1,0:T(8,128)(2,1)}, bf16[512,2048]{1,0:T(8,128)(2,1)}, u32[]{:S(2)}, u32[]{:S(2)}) collective-permute-start(bf16[512,2048]{1,0:T(8,128)(2,1)} %add_convert_fusion.1.refs_18_), channel_id=1, source_target_pairs={{0,1},{1,2},{2,3},{3,0},{4,5},{5,6},{6,7},{7,4},{8,9},{9,10},{10,1... | collective-permute-start | bytes 6291464 | tf_op jit(solution)/shard_map/ppermute | solution.py:993
  624.5 44.2 %collective-permute-start.20 = (bf16[6,256,256]{2,1,0:T(8,128)(2,1)}, bf16[6,256,256]{2,1,0:T(8,128)(2,1)}, u32[]{:S(2)}, u32[]{:S(2)}) collective-permute-start(bf16[6,256,256]{2,1,0:T(8,128)(2,1)} %get-tuple-element.144), channel_id=1, source_target_pairs={{0,8},{4,12},{8,0},{12,4},{16,24},{20,28},{24,16},{28,20},{1,9},{5... | collective-permute-start | bytes 2359304 | tf_op jit(solution)/shard_map/ppermute | solution.py:998
  625.6 44.6 %collective-permute-start.21 = (bf16[6,256,256]{2,1,0:T(8,128)(2,1)}, bf16[6,256,256]{2,1,0:T(8,128)(2,1)}, u32[]{:S(2)}, u32[]{:S(2)}) collective-permute-start(bf16[6,256,256]{2,1,0:T(8,128)(2,1)} %get-tuple-element.146), channel_id=1, source_target_pairs={{0,16},{4,20},{8,24},{12,28},{16,0},{20,4},{24,8},{28,12},{1,17},{... | collective-permute-start | bytes 2359304 | tf_op jit(solution)/shard_map/ppermute | solution.py:998
  632.9 74.0 %collective-permute-start.25 = (bf16[6,256,256]{2,1,0:T(8,128)(2,1)}, bf16[6,256,256]{2,1,0:T(8,128)(2,1)S(1)}, u32[]{:S(2)}, u32[]{:S(2)}) collective-permute-start(bf16[6,256,256]{2,1,0:T(8,128)(2,1)} %get-tuple-element.171), channel_id=1, source_target_pairs={{0,8},{4,12},{8,0},{12,4},{16,24},{20,28},{24,16},{28,20},{1,9},{5... | collective-permute-start | bytes 2359304 | tf_op jit(solution)/shard_map/ppermute | solution.py:998
  633.5 73.4 %collective-permute-start.26 = (bf16[6,256,256]{2,1,0:T(8,128)(2,1)}, bf16[6,256,256]{2,1,0:T(8,128)(2,1)}, u32[]{:S(2)}, u32[]{:S(2)}) collective-permute-start(bf16[6,256,256]{2,1,0:T(8,128)(2,1)} %get-tuple-element.173), channel_id=1, source_target_pairs={{0,16},{4,20},{8,24},{12,28},{16,0},{20,4},{24,8},{28,12},{1,17},{... | collective-permute-start | bytes 2359304 | tf_op jit(solution)/shard_map/ppermute | solution.py:998
  634.3 70.5 %reduce-scatter.8.cloned.1.call-start = ((), (), s32[]{:S(2)}) async-start(), calls=%async_computation.6 | async-start | bytes 40960 | tf_op jit(solution)/shard_map/reduce_scatter | solution.py:1179
  668.7 38.3 %collective-permute-start.27 = (bf16[6,256,256]{2,1,0:T(8,128)(2,1)}, bf16[6,256,256]{2,1,0:T(8,128)(2,1)}, u32[]{:S(2)}, u32[]{:S(2)}) collective-permute-start(bf16[6,256,256]{2,1,0:T(8,128)(2,1)} %get-tuple-element.166.refs_17_), channel_id=1, source_target_pairs={{0,24},{4,28},{8,16},{12,20},{16,8},{20,12},{24,0},{28,4},{1,25},{... | collective-permute-start | bytes 2359304 | tf_op jit(solution)/shard_map/ppermute | solution.py:998
  702.7 48.9 %collective-permute-start.24 = (bf16[512,2048]{1,0:T(8,128)(2,1)}, bf16[512,2048]{1,0:T(8,128)(2,1)S(1)}, u32[]{:S(2)}, u32[]{:S(2)}) collective-permute-start(bf16[512,2048]{1,0:T(8,128)(2,1)} %add_convert_fusion.refs_17_), channel_id=1, source_target_pairs={{0,1},{1,2},{2,3},{3,0},{4,5},{5,6},{6,7},{7,4},{8,9},{9,10},{10,1... | collective-permute-start | bytes 6291464 | tf_op jit(solution)/shard_map/ppermute | solution.py:993
  (24 other events, 388.1 us)
Sparse Core Ops, SparseCore 0:
  14.1 128.2 all-gather.1
  374.7 145.4 reduce-scatter.3
  634.5 32.6 reduce-scatter.5
  669.3 18.9 reduce-scatter.7

commit v6 on v4

--- a/solution.py
+++ b/solution.py
@@ -24,14 +24,6 @@
 DOC_MAX = 512
 HALF_ROOT = 0.7071067811865476
 DENSITY_SCALE = 0.3989422804014327
-
-
-def apply_layer_norm(values):
-    mean_val = jnp.mean(values, axis=-1, keepdims=True)
-    centred = values - mean_val
-    variance = jnp.mean(centred * centred, axis=-1, keepdims=True)
-    inv_std = lax.rsqrt(variance + EPS_NORM)
-    return (centred * inv_std, inv_std)
 
 
 def to_blocks(matrix, block_size):
@@ -530,7 +522,10 @@
     )(rank, *parts, factor, slope, group_tokens, mean, inverse, blocks, norm_params, *priors)
 
 
-def qkv_back_kernel(owned, d_qkv_ref, part_ref, tokens_ref, mean_ref, inverse_ref, blocks_ref, norm_ref, dz_ref, norm_sums, qkv_sums, w_qkv, sems):
+def qkv_back_kernel(
+    owned, waits, d_qkv_ref, part_ref, tokens_ref, mean_ref, inverse_ref, blocks_ref, norm_ref, *refs
+):
+    dz_ref, norm_sums, qkv_sums, w_qkv, sems = refs[waits:]
     size = blocks_ref.shape[-1]
     outer = w_qkv.shape[0] // size
     copies = block_copies(blocks_ref, owned, 0, outer, w_qkv.shape[1] // size, w_qkv, sems)
@@ -553,7 +548,7 @@
         norm_sums[8:16, cols] += column_sum(first)
 
 
-def qkv_back(d_qkv, dz_part, group_tokens, mean, inverse, blocks, owned, norm_params):
+def qkv_back(d_qkv, dz_part, group_tokens, mean, inverse, blocks, owned, norm_params, waits):
     tokens, qkv_cols = d_qkv.shape
     width = dz_part.shape[1]
     size = blocks.shape[-1]
@@ -562,11 +557,12 @@
     whole = lambda rows, cols: pl.BlockSpec((rows, cols), lambda i: (0, 0))
     outer = width // size
     return pl.pallas_call(
-        functools.partial(qkv_back_kernel, owned),
+        functools.partial(qkv_back_kernel, owned, len(waits)),
         grid=(tokens // tile,),
         in_specs=[
             row(qkv_cols), row(width), row(width), row(1), row(1), pl.BlockSpec(memory_space=pl.ANY), whole(norm_params.shape[0], width),
-        ],
+        ]
+        + [pl.BlockSpec(memory_space=pl.ANY)] * len(waits),
         out_specs=[row(width), whole(16, width), whole(8, qkv_cols)],
         out_shape=[
             jax.ShapeDtypeStruct((tokens, width), jnp.bfloat16),
@@ -582,7 +578,7 @@
             flops=2 * tokens * width * qkv_cols, bytes_accessed=tokens * width * 11, transcendentals=0
         ),
         name="qkv_back",
-    )(d_qkv, dz_part, group_tokens, mean, inverse, blocks, norm_params)
+    )(d_qkv, dz_part, group_tokens, mean, inverse, blocks, norm_params, *waits)
 
 
 def weight_grad_kernel(steps, waits, core_ref, *refs):
@@ -730,6 +726,41 @@
         cost_estimate=pl.CostEstimate(flops=rows * size * size, bytes_accessed=rows * size * size * 6, transcendentals=0),
         name="pair_sum",
     )(chip, *([kept] * chips), *([received] * chips))
+
+
+def input_grad_kernel(moved_ref, last_ref, tokens_ref, seed_ref, mean_ref, inverse_ref, out_ref):
+    d_scaled = moved_ref[...].astype(jnp.float32) + last_ref[...].astype(jnp.float32)
+    inverse = inverse_ref[...]
+    scaled = (tokens_ref[...].astype(jnp.float32) - mean_ref[...]) * inverse
+    average = jnp.mean(d_scaled, axis=1, keepdims=True)
+    projection = jnp.mean(d_scaled * scaled, axis=1, keepdims=True)
+    out_ref[...] = seed_ref[...].astype(jnp.float32) + inverse * (d_scaled - average - scaled * projection)
+
+
+def input_gradient(moved, dz, tokens, seed, mean, inverse, rank, waits):
+    rows, width = moved.shape
+    tile = min(128, rows)
+    per = rows // tile
+    own = lambda n: pl.BlockSpec((tile, n), lambda i, rank: (i, 0))
+    ranked = lambda n: pl.BlockSpec((tile, n), lambda i, rank: (rank[0] * per + i, 0))
+
+    def kernel(rank_ref, *refs):
+        input_grad_kernel(*refs[:6], refs[-1])
+
+    return pl.pallas_call(
+        kernel,
+        grid_spec=pltpu.PrefetchScalarGridSpec(
+            num_scalar_prefetch=1,
+            grid=(per,),
+            in_specs=[own(width), ranked(width), own(width), ranked(width), ranked(1), ranked(1)]
+            + [pl.BlockSpec(memory_space=pl.ANY)] * len(waits),
+            out_specs=own(width),
+        ),
+        out_shape=jax.ShapeDtypeStruct((rows, width), jnp.float32),
+        compiler_params=kernel_params(),
+        cost_estimate=pl.CostEstimate(flops=rows * width * 12, bytes_accessed=rows * width * 12, transcendentals=0),
+        name="input_gradient",
+    )(rank, moved, dz, tokens, seed, mean, inverse, *waits)
 
 
 def dot32(left_arg, right_arg):
@@ -993,7 +1024,6 @@
     own_pack = own_pos // pack_len
     valid_own = (own_pack < packs[0]).astype(jnp.float32)
     owned_input_rows = tokens.astype(jnp.float32)
-    owned_centred_scaled, owned_inverse_deviation = apply_layer_norm(owned_input_rows)
 
     group_pack = jnp.arange(group_tok) // pack_len
     lookup_key = group_pack * seg_width + segments.reshape(-1)
@@ -1001,8 +1031,6 @@
     subset_tok = jnp.sum(jnp.where(onehot, subsets.reshape(-1)[None, :], 0), axis=1)
     weight = 0.5 + subset_tok.astype(jnp.float32) / (SUBSETS - 1)
     factor = (weight * (group_pack < packs[0]).astype(jnp.float32))[:, None]
-    own_factor = lax.dynamic_slice_in_dim(factor, tp_rank * tok_dev, tok_dev, 0)
-    seed16 = (cotangent.astype(jnp.float32) * own_factor).astype(jnp.bfloat16)
 
     rank = tp_rank.astype(jnp.int32)[None]
     cosines, sines = turn_tables(pack_len, 128)
@@ -1029,59 +1057,9 @@
         after(partial_value, cotangent_parts[-1], early[5]), "tp", scatter_dimension=0, tiled=True
     )
     d_qkv16 = attend_back(qkv16, d_attended, segments, cosines, sines, heads_dev)
-    dz16, first_sums, qkv_sums = qkv_back(
-        d_qkv16, dz_part, group_tokens, mean, inverse, blocks, owned, norm_params
-    )
-
-    dz_rows = lambda back: lax.dynamic_slice_in_dim(dz16, (tp_rank - back) % tp_ways * tok_dev, tok_dev, 0)
-    back = 2
-
-    def pass_on(moving, back):
-        total = moving.astype(jnp.float32) + dz_rows(back).astype(jnp.float32)
-        return total if back == tp_ways else onward(total.astype(jnp.bfloat16), "tp")
-
-    shared_local = jnp.concatenate(
-        [
-            jnp.sum(first_sums.reshape(2, 8, model_width), axis=1),
-            jnp.sum((early[4][:16] + late[4][:16]).reshape(2, 8, model_width), axis=1),
-            jnp.sum(early[4][16:], axis=0)[None],
-        ],
-        0,
-    )
-    vecs_local = jnp.concatenate(
-        [
-            jnp.sum(qkv_sums, axis=0).reshape(3 * heads_dev, HD),
-            jnp.sum(early[5] + late[5], axis=0).reshape(ff_dev // HD, HD),
-        ],
-        0,
-    )
-    small = jnp.concatenate(
-        [
-            shared_local.reshape(5, dp_ways, -1).transpose(1, 0, 2).reshape(dp_ways, -1),
-            vecs_local.reshape(vec_rows, dp_ways, -1).transpose(1, 0, 2).reshape(dp_ways, -1),
-        ],
-        1,
-    )
-    small_in = after(small_rows(small, dp_ways), branch)
-    small_own = lax.psum_scatter(small_in, "dp", scatter_dimension=0, tiled=True).reshape(-1)
-    output = (
-        valid_own[:, None]
-        * (owned_input_rows + branch.astype(jnp.float32) + norm_params[4] + norm_params[5])
-    ).astype(jnp.bfloat16)
-
-    shared_size = 5 * model_width // dp_ways
-    own_vec_grads = small_own[shared_size : small.shape[1]].reshape(vec_rows, HD // dp_ways)
-    shared_part = small_own[:shared_size].reshape(5, tp_ways, -1).transpose(1, 0, 2)
-    shared_own = lax.psum_scatter(
-        small_rows(shared_part.reshape(tp_ways, -1), tp_ways), "tp", scatter_dimension=0, tiled=True
-    ).reshape(-1)
-    shared_own = shared_own[: shared_size // tp_ways].reshape(5, -1)
-    shared_grads = jnp.concatenate([shared_own, shared_own[4:]], 0)
     dp_rank = lax.axis_index("dp").astype(jnp.int32)
     lefts = (first_turned, second_turned, active_turned, attended_turned)
-    d_qkv_late, first_rows = lax.optimization_barrier((d_qkv16, dz_rows(1)))
-    moving = onward(first_rows, "tp")
-    rights = (d_hidden16, seed_all, d_qkv_late)
+    rights = (d_hidden16, seed_all, d_qkv16)
     firsts = (0, first_out, first_in, first_down)
     qkv_blocks = 3 * head_cols // block_size
     parts = 4
@@ -1094,11 +1072,71 @@
         and first_out % block_rows == 0
         and first_in % block_rows == 0
     )
+    sums = []
+
+    def quarter(part, waits):
+        kept, away = weight_grads(
+            part, parts, lefts, rights, firsts, (dp_rank % 2)[None], owned, dp_ways, block_size, waits
+        )
+        sums.append(pair_sum(kept, swap(away, 1), (dp_rank // 2)[None], dp_ways // 2))
+        return kept
+
+    first_waits = ()
+    if by_part:
+        quarter(0, ())
+        quarter(1, ())
+        first_waits = (sums[0][0],)
+    dz16, first_sums, qkv_sums = qkv_back(
+        d_qkv16, dz_part, group_tokens, mean, inverse, blocks, owned, norm_params, first_waits
+    )
+    dz_rows = lambda back: lax.dynamic_slice_in_dim(dz16, (tp_rank - back) % tp_ways * tok_dev, tok_dev, 0)
+    back = 2
+
+    def pass_on(moving, back):
+        total = moving.astype(jnp.float32) + dz_rows(back).astype(jnp.float32)
+        return total.astype(jnp.bfloat16)
+
+    moving = onward(dz_rows(1), "tp")
+    shared_local = jnp.concatenate(
+        [
+            jnp.sum(first_sums.reshape(2, 8, model_width), axis=1),
+            jnp.sum((early[4][:16] + late[4][:16]).reshape(2, 8, model_width), axis=1),
+            jnp.sum(early[4][16:], axis=0)[None],
+        ],
+        0,
+    )
+    vecs_local = jnp.concatenate(
+        [
+            jnp.sum(qkv_sums, axis=0).reshape(3 * heads_dev, HD),
+            jnp.sum(early[5] + late[5], axis=0).reshape(ff_dev // HD, HD),
+        ],
+        0,
+    )
+    small = jnp.concatenate(
+        [
+            shared_local.reshape(5, dp_ways, -1).transpose(1, 0, 2).reshape(dp_ways, -1),
+            vecs_local.reshape(vec_rows, dp_ways, -1).transpose(1, 0, 2).reshape(dp_ways, -1),
+        ],
+        1,
+    )
+    small_in = after(small_rows(small, dp_ways), branch)
+    small_own = lax.psum_scatter(small_in, "dp", scatter_dimension=0, tiled=True).reshape(-1)
+    output = (
+        valid_own[:, None]
+        * (owned_input_rows + branch.astype(jnp.float32) + norm_params[4] + norm_params[5])
+    ).astype(jnp.bfloat16)
+
+    shared_size = 5 * model_width // dp_ways
+    own_vec_grads = small_own[shared_size : small.shape[1]].reshape(vec_rows, HD // dp_ways)
+    shared_part = small_own[:shared_size].reshape(5, tp_ways, -1).transpose(1, 0, 2)
+    shared_in = small_rows(shared_part.reshape(tp_ways, -1), tp_ways)
+    shared_own = lax.psum_scatter(shared_in, "tp", scatter_dimension=0, tiled=True).reshape(-1)
+    shared_own = shared_own[: shared_size // tp_ways].reshape(5, -1)
+    shared_grads = jnp.concatenate([shared_own, shared_own[4:]], 0)
     results = ()
     if by_part:
         part_size = owned // parts
         span = block_rows // parts
-        sums = []
         terms = []
         ready = []
 
@@ -1108,17 +1146,9 @@
                 ready.append(sums[part][3])
             terms.append([sums[part][0]] + [swap(sums[part][bits], 2 * bits) for bits in range(1, 4)])
 
-        for part in range(parts):
-            waits = (sums[part - 2][0],) if part >= 2 else ()
-            if part == parts - 1:
-                send_on(0)
-                waits += tuple(terms[0][1:])
-            kept, away = weight_grads(
-                part, parts, lefts, rights, firsts, (dp_rank % 2)[None], owned, dp_ways, block_size, waits
-            )
-            sums.append(pair_sum(kept, swap(away, 1), (dp_rank // 2)[None], dp_ways // 2))
-        moving = pass_on(after(moving, kept), back)
-        back += 1
+        send_on(0)
+        quarter(2, (dz16, sums[1][0]) + tuple(terms[0][1:]))
+        quarter(3, tuple(terms[0][1:]))
         for part in range(1, parts):
             send_on(part)
         count = jnp.arange(part_size, dtype=jnp.int32)
@@ -1132,25 +1162,30 @@
             waits = []
             if part < parts - 1:
                 waits.append(ready[part])
+            if part == 0:
+                waits += terms[1][1:]
+            if part % 2 == 0 and back < tp_ways:
+                if part:
+                    moving, first_result = lax.optimization_barrier((moving, results[0]))
+                    results = [first_result] + list(results[1:])
+                total = pass_on(moving, back)
+                waits.append(total)
+                moving = onward(total, "tp")
+                back += 1
             if part == 1:
                 waits.append(small_in)
             if part == 2:
-                waits.append(small_own)
+                waits += [small_own, shared_in]
             if part == 3:
                 waits += [output, shared_own]
             results = shampoo(
                 terms[part], left_stats, right_stats, master_blocks, places, results, waits
             )
-            if part % 2 == 1 and back <= tp_ways:
-                moving, first_result = lax.optimization_barrier((moving, results[0]))
-                results = [first_result] + list(results[1:])
-                moving = pass_on(moving, back)
-                back += 1
     else:
         local = [
             to_blocks(jnp.dot(left, right, preferred_element_type=jnp.float32).astype(jnp.bfloat16), block_size)
             for left, right in (
-                (first_turned, d_qkv_late),
+                (first_turned, d_qkv16),
                 (attended_turned, seed_all),
                 (second_turned, d_hidden16),
                 (active_turned, seed_all),
@@ -1160,19 +1195,11 @@
         results = shampoo(
             [grads16], left_stats, right_stats, master_blocks, jnp.arange(owned, dtype=jnp.int32), results
         )
-    while back <= tp_ways:
-        moving = pass_on(moving, back)
+    while back < tp_ways:
+        moving = onward(pass_on(moving, back), "tp")
         back += 1
-    norm_input_gradient = moving
+    input_grad = input_gradient(moving, dz16, tokens, seed_all, mean, inverse, rank, results[:1])
     own_grads, left_new, right_new, new_blocks = results
-    average_gradient = jnp.mean(norm_input_gradient, axis=-1, keepdims=True)
-    average_projection = jnp.mean(
-        norm_input_gradient * owned_centred_scaled, axis=-1, keepdims=True
-    )
-    input_grad = seed16.astype(jnp.float32) + owned_inverse_deviation * (
-        norm_input_gradient - average_gradient - owned_centred_scaled * average_projection
-    )
-
     local_stat_new = DECAY * local_vec_stats + own_vec_grads * own_vec_grads
     local_new = local_vecs - RATE_VEC * own_vec_grads * lax.rsqrt(local_stat_new)
     shared_stat_new = DECAY * shared_vec_stats + shared_grads * shared_grads

time: 705 us -> 697 us (0.989)
  other arithmetic: 44.2 us -> 29.9 us
    ppermute x9, waiting for transfers between devices: 97.4 us -> 115 us  [onward(): lax.ppermute(part, axis, [(each, (each + 1) % ways) for each in range(way...]
    ppermute x16, waiting for transfers between devices: 18.9 us -> 2.45 us  [swap(): lax.ppermute(part, 'dp', [(each, each ^ bits) for each in range(ways)])]
    reduce_sum x3 -> x0, other arithmetic: 10 us -> none  [the longest x1 4.34 us: apply_layer_norm(): variance = jnp.mean(centred * centred, axis=-1, keepdims=True)]
    pallas_call x1 -> x2, Pallas kernels: 25.1 us -> 31.8 us  [the longest x1 25.1 us: qkv_back(): pl.pallas_call(functools.partial(qkv_back_kernel, owned, len(waits)), gri...]
  transfers between devices with their start and end apart: 32 -> 32, of which waited for: 7 -> 9; matrix products, arithmetic and copies ran while one was open for 7% -> 6% of each run, Pallas kernels for 61% -> 62%
where the time goes in v6:
time: 697 us; the launch traced here: 688 us
  Pallas kernels  432 us (62%)
  waiting for transfers between devices  157 us (23%)
  other arithmetic  29.9 us (4%)
  starting transfers between devices  29.4 us (4%)
  local copies, waits for them, and re-layouts  24.7 us (4%)
  between operations  15.3 us (2%)
    ppermute x9, waiting for transfers between devices, onward(): lax.ppermute(part, axis, [(each, (each + 1) % ways) for each in range(way...  115 us
    pallas_call x4, Pallas kernels, shampoo(): pl.pallas_call(functools.partial(shampoo_kernel, count, len(grads), held...  112 us
    pallas_call x4, Pallas kernels, weight_grads(): pl.pallas_call(functools.partial(weight_grad_kernel, tuple(steps), len(wa...  78.1 us
    pallas_call x2, Pallas kernels, feed_back(): pl.pallas_call(functools.partial(feed_back_kernel, offsets, owned, first_...  72.7 us
    pallas_call x1, Pallas kernels, feed_forward(): pl.pallas_call(functools.partial(feed_kernel, offsets, owned), grid=(toke...  57.1 us
    pallas_call x1, Pallas kernels, project_qkv(): pl.pallas_call(functools.partial(qkv_kernel, heads, owned, ways), grid_sp...  32.9 us
    all_gather x1, waiting for transfers between devices, shards(): blocks = lax.all_gather(rows16, 'dp', axis=0, tiled=True)  25.8 us
    pallas_call x1, Pallas kernels, qkv_back(): pl.pallas_call(functools.partial(qkv_back_kernel, owned, len(waits)), gri...  25.1 us
  transfers between devices with their start and end apart: 32, of which 9 were waited for; matrix products, arithmetic and copies ran while one was open for 6% of the time, Pallas kernels for 62%

profile of v6, /device:TPU:0, one launch (start us, length us, event | category | flops | bytes accessed | tf_op | source)
XLA Modules:
  0.0 688.2 jit_solution(8412031780127219251)
XLA Ops:
  8.9 3.2 convert.20
  14.6 3.0 collective-permute-start
  17.7 47.8 %collective-permute-done.refs_1_ = bf16[512,2048]{1,0:T(8,128)(2,1)} collective-permute-done((bf16[512,2048]{1,0:T(8,128)(2,1)S(1)}, bf16[512,2048]{1,0:T(8,128)(2,1)}, u32[]{:S(2)}, u32[]{:S(2)}) %collective-permute-start) | collective-permute-done | bytes 2097184 | tf_op jit(solution)/shard_map/ppermute | solution.py:947
  65.5 48.8 %collective-permute-done.1.refs_2_ = bf16[512,2048]{1,0:T(8,128)(2,1)} collective-permute-done((bf16[512,2048]{1,0:T(8,128)(2,1)}, bf16[512,2048]{1,0:T(8,128)(2,1)}, u32[]{:S(2)}, u32[]{:S(2)}) %collective-permute-start.1) | collective-permute-done | bytes 2097184 | tf_op jit(solution)/shard_map/ppermute | solution.py:947
  116.7 25.8 %all-gather.2.cloned.1.call-done.refs_4_.blocks_ref.refs_8_.refs_6_ = bf16[49280,256]{1,0:T(8,128)(2,1)} async-done(((bf16[6160,256]{1,0:T(8,128)(2,1)}), bf16[49280,256]{1,0:T(8,128)(2,1)}) %all-gather.2.cloned.1.call-update) | async-done | bytes 25231376 | tf_op jit(solution)/shard_map/all_gather | solution.py:996
  148.8 13.8 %collective-permute-done.3 = bf16[8,384]{1,0:T(8,128)(2,1)S(1)} collective-permute-done((bf16[8,384]{1,0:T(8,128)(2,1)S(1)}, bf16[8,384]{1,0:T(8,128)(2,1)S(1)}, u32[]{:S(2)}, u32[]{:S(2)}) %collective-permute-start.3) | collective-permute-done | bytes 6176 | tf_op jit(solution)/shard_map/ppermute | solution.py:1011
  171.1 32.9 %qkv.1 = (bf16[2048,1536]{1,0:T(8,128)(2,1)}, bf16[2048,2048]{1,0:T(8,128)(2,1)}, bf16[2048,2048]{1,0:T(8,128)(2,1)}, bf16[2048,2048]{1,0:T(8,128)(2,1)}, bf16[2...) custom-call(s32[1]{0:T(128)} %bitcast.1.rank_ref, bf16[512,2048]{1,0:T(8,128)(2,1)} %refs_2_.1, ...), custom_call_target="tpu_custom_call" | custom-call | flops 12884901888 | bytes 46137344 | tf_op jit(solution)/shard_map/qkv/pallas_call | solution.py:188
  204.1 10.8 %attend.1 = (bf16[2048,512]{1,0:T(8,128)(2,1)}, bf16[512,2048]{1,0:T(8,128)(2,1)}) custom-call(bf16[2048,1536]{1,0:T(8,128)(2,1)} %get-tuple-element.96.query_ref.key_ref.value_ref, bf16[2048,1536]{1,0:T(8,128)(2,1)} %get-tuple-element.96.query_ref.key_ref.value_ref, bf16[2048,1536]{1,0:T(8,128)(2,1)} %get-tuple-element.96.query_ref.key_ref.value_ref, ...), custom_call_target="tpu_custom_call" | custom-call | flops 3221225472 | bytes 8388608 | tf_op jit(solution)/shard_map/attend/pallas_call | solution.py:239
  215.6 57.1 %feed.1 = (bf16[2048,2048]{1,0:T(8,128)(2,1)}, bf16[2048,2048]{1,0:T(8,128)(2,1)}, bf16[2048,2048]{1,0:T(8,128)(2,1)}) custom-call(bf16[2048,2048]{1,0:T(8,128)(2,1)} %get-tuple-element.95.x_ref, bf16[2048,512]{1,0:T(8,128)(2,1)} %get-tuple-element.97.attended_ref, bf16[49280,256]{1,0:T(8,128)(2,1)} %all-gather.2.cloned.1.call-done.refs_4_.blocks_ref.refs_8_.refs_6_, ...), custom_call_target="tpu_custom_call" | custom-call | flops 38654705664 | bytes 58720256 | tf_op jit(solution)/shard_map/feed/pallas_call | solution.py:379
  274.7 47.8 %feed_back.2 = (bf16[2048,2048]{1,0:T(8,128)(2,1)}, bf16[2048,512]{1,0:T(8,128)(2,1)}, bf16[2048,2048]{1,0:T(8,128)(2,1)}, bf16[2048,2048]{1,0:T(8,128)(2,1)}, f32[24,2048]{1,0:T(8,128)}, /*index=5*/f32[8,2048]{1,0:T(8,128)}) custom-call(s32[1]{0:T(128)} %bitcast.1.rank_ref, bf16[512,2048]{1,0:T(8,128)(2,1)} %refs_0_.3, ...), custom_call_target="tpu_custom_call" | custom-call | flops 28991029248 | bytes 60817408 | tf_op jit(solution)/shard_map/feed_back/pallas_call | solution.py:485
  324.9 24.8 %feed_back.3 = (bf16[2048,2048]{1,0:T(8,128)(2,1)}, bf16[2048,512]{1,0:T(8,128)(2,1)}, bf16[2048,2048]{1,0:T(8,128)(2,1)}, bf16[2048,2048]{1,0:T(8,128)(2,1)}, f32[24,2048]{1,0:T(8,128)}, /*index=5*/f32[8,2048]{1,0:T(8,128)}) custom-call(s32[1]{0:T(128)} %bitcast.1.rank_ref, ...), custom_call_target="tpu_custom_call", output_to_operand_aliasing={{0}: (9, {}), {1}: (10, {}), {2}: (11, {}), {3}: (12, {})} | custom-call | flops 9663676416 | bytes 31457280 | tf_op jit(solution)/shard_map/feed_back/pallas_call | solution.py:485
  349.7 17.1 %attend_back.1.refs_6_.d_qkv_ref = bf16[2048,1536]{1,0:T(8,128)(2,1)} custom-call(bf16[2048,1536]{1,0:T(8,128)(2,1)} %get-tuple-element.96.query_ref.key_ref.value_ref, bf16[2048,1536]{1,0:T(8,128)(2,1)} %get-tuple-element.96.query_ref.key_ref.value_ref, bf16[2048,1536]{1,0:T(8,128)(2,1)} %get-tuple-element.96.query_ref.key_ref.value_ref, ...), custom_call_target="tpu_custom_call" | custom-call | flops 7516192768 | bytes 16777216 | tf_op jit(solution)/shard_map/attend_back/pallas_call | solution.py:306
  366.8 19.4 %weight_grads.4 = (bf16[24,256,256]{2,1,0:T(8,128)(2,1)}, bf16[24,256,256]{2,1,0:T(8,128)(2,1)}) custom-call(s32[1]{0:T(128)} %bitcast.13.core_ref, bf16[2048,2048]{1,0:T(8,128)(2,1)} %get-tuple-element.114.refs_0_, bf16[2048,2048]{1,0:T(8,128)(2,1)} %get-tuple-element.115.refs_1_, bf16[2048,2048]{1,0:T(8,128)(2,1)} %get-tuple-element.116.refs_2_, ...), custom_call_target="tpu_custom_call" | custom-call | flops 12884901888 | bytes 25769804 | tf_op jit(solution)/shard_map/weight_grads/pallas_call | solution.py:680
  386.2 20.1 %weight_grads.5 = (bf16[24,256,256]{2,1,0:T(8,128)(2,1)}, bf16[24,256,256]{2,1,0:T(8,128)(2,1)}) custom-call(s32[1]{0:T(128)} %bitcast.13.core_ref, bf16[2048,2048]{1,0:T(8,128)(2,1)} %get-tuple-element.114.refs_0_, bf16[2048,2048]{1,0:T(8,128)(2,1)} %get-tuple-element.115.refs_1_, bf16[2048,2048]{1,0:T(8,128)(2,1)} %get-tuple-element.116.refs_2_, ...), custom_call_target="tpu_custom_call" | custom-call | flops 12884901888 | bytes 25769804 | tf_op jit(solution)/shard_map/weight_grads/pallas_call | solution.py:680
  409.6 4.9 pair_sum.4
  419.7 5.0 pair_sum.5
  424.7 25.1 %qkv_back.1 = (bf16[2048,2048]{1,0:T(8,128)(2,1)}, f32[16,2048]{1,0:T(8,128)}, f32[8,1536]{1,0:T(8,128)}) custom-call(bf16[2048,1536]{1,0:T(8,128)(2,1)} %attend_back.1.refs_6_.d_qkv_ref, bf16[2048,2048]{1,0:T(8,128)(2,1)} %get-tuple-element.113.part_ref, bf16[2048,2048]{1,0:T(8,128)(2,1)} %get-tuple-element.103.refs_5_.refs_3_.tokens_ref, ...), custom_call_target="tpu_custom_call" | custom-call | flops 12884901888 | bytes 46137344 | tf_op jit(solution)/shard_map/qkv_back/pallas_call | solution.py:559
  452.2 19.4 %weight_grads.6 = (bf16[24,256,256]{2,1,0:T(8,128)(2,1)}, bf16[24,256,256]{2,1,0:T(8,128)(2,1)}) custom-call(s32[1]{0:T(128)} %bitcast.13.core_ref, bf16[2048,2048]{1,0:T(8,128)(2,1)} %get-tuple-element.114.refs_0_, bf16[2048,2048]{1,0:T(8,128)(2,1)} %get-tuple-element.115.refs_1_, bf16[2048,2048]{1,0:T(8,128)(2,1)} %get-tuple-element.116.refs_2_, ...), custom_call_target="tpu_custom_call" | custom-call | flops 12884901888 | bytes 25769804 | tf_op jit(solution)/shard_map/weight_grads/pallas_call | solution.py:680
  471.7 3.2 constant_dynamic-slice_fusion
  474.9 2.7 collective-permute-start.10
  488.4 19.3 %weight_grads.7 = (bf16[24,256,256]{2,1,0:T(8,128)(2,1)}, bf16[24,256,256]{2,1,0:T(8,128)(2,1)}) custom-call(s32[1]{0:T(128)} %bitcast.13.core_ref, bf16[2048,2048]{1,0:T(8,128)(2,1)} %get-tuple-element.114.refs_0_, bf16[2048,2048]{1,0:T(8,128)(2,1)} %get-tuple-element.115.refs_1_, bf16[2048,2048]{1,0:T(8,128)(2,1)} %get-tuple-element.116.refs_2_, ...), custom_call_target="tpu_custom_call" | custom-call | flops 12884901888 | bytes 25769804 | tf_op jit(solution)/shard_map/weight_grads/pallas_call | solution.py:680
  507.7 17.5 %collective-permute-done.10 = bf16[512,2048]{1,0:T(8,128)(2,1)} collective-permute-done((bf16[512,2048]{1,0:T(8,128)(2,1)}, bf16[512,2048]{1,0:T(8,128)(2,1)}, u32[]{:S(2)}, u32[]{:S(2)}) %collective-permute-start.10) | collective-permute-done | bytes 2097184 | tf_op jit(solution)/shard_map/ppermute | solution.py:947
  525.9 4.5 add_convert_fusion.1.refs_17_
  532.0 4.9 pair_sum.6
  538.8 28.2 %shampoo.4 = (f32[24,256,256]{2,1,0:T(8,128)}, f32[24,256,256]{2,1,0:T(8,128)}, f32[24,256,256]{2,1,0:T(8,128)}, f32[24,256,256]{2,1,0:T(8,128)}) custom-call(s32[6]{0:T(128)} %broadcast_select_fusion.2.places_ref, f32[6,256,256]{2,1,0:T(8,128)} %get-tuple-element.122.refs_0_, bf16[6,256,256]{2,1,0:T(8,128)(2,1)} %collective-permute-done.17.refs_1_.refs_9_.refs_7_, ...), custom_call_target="tpu_custom_call" | custom-call | flops 26172456960 | bytes 11796480 | tf_op jit(solution)/shard_map/shampoo/pallas_call | solution.py:903
  568.6 4.8 pair_sum.7
  577.0 28.1 %shampoo.5 = (f32[24,256,256]{2,1,0:T(8,128)}, f32[24,256,256]{2,1,0:T(8,128)}, f32[24,256,256]{2,1,0:T(8,128)}, f32[24,256,256]{2,1,0:T(8,128)}) custom-call(s32[6]{0:T(128)} %broadcast_select_fusion.3.places_ref, f32[6,256,256]{2,1,0:T(8,128)} %get-tuple-element.126.refs_8_.refs_0_, ...), custom_call_target="tpu_custom_call", output_to_operand_aliasing={{0}: (14, {}), {1}: (15, {}), {2}: (16, {}), {3}: (17, {})} | custom-call | flops 26172456960 | bytes 11796480 | tf_op jit(solution)/shard_map/shampoo/pallas_call | solution.py:903
  605.2 4.1 multiply_convert_fusion.refs_17_
  610.2 3.0 add_convert_fusion.refs_18_
  615.7 27.7 %shampoo.6 = (f32[24,256,256]{2,1,0:T(8,128)}, f32[24,256,256]{2,1,0:T(8,128)}, f32[24,256,256]{2,1,0:T(8,128)}, f32[24,256,256]{2,1,0:T(8,128)}) custom-call(s32[6]{0:T(128)} %broadcast_select_fusion.places_ref, f32[6,256,256]{2,1,0:T(8,128)} %get-tuple-element.161.refs_0_, ...), custom_call_target="tpu_custom_call", output_to_operand_aliasing={{0}: (14, {}), {1}: (15, {}), {2}: (16, {}), {3}: (17, {})} | custom-call | flops 26172456960 | bytes 11796480 | tf_op jit(solution)/shard_map/shampoo/pallas_call | solution.py:903
  647.0 27.7 %shampoo.7 = (f32[24,256,256]{2,1,0:T(8,128)}, f32[24,256,256]{2,1,0:T(8,128)}, f32[24,256,256]{2,1,0:T(8,128)}, f32[24,256,256]{2,1,0:T(8,128)}) custom-call(s32[6]{0:T(128)} %broadcast_select_fusion.1.places_ref, f32[6,256,256]{2,1,0:T(8,128)} %get-tuple-element.154.refs_0_, ...), custom_call_target="tpu_custom_call", output_to_operand_aliasing={{0}: (14, {}), {1}: (15, {}), {2}: (16, {}), {3}: (17, {})} | custom-call | flops 26172456960 | bytes 11796480 | tf_op jit(solution)/shard_map/shampoo/pallas_call | solution.py:903
  674.7 6.7 input_gradient.1
  (188 shorter events, 63.6 us)
Async XLA Ops:
  7.2 135.3 %all-gather.2.cloned.1.call-start = ((), (), s32[]{:S(2)}) async-start(), calls=%async_computation.3 | async-start | bytes 28385280 | tf_op jit(solution)/shard_map/all_gather | solution.py:996
  14.0 562.9 %reduce-scatter.4.cloned.1.call-start = ((), (), s32[]{:S(2)}) async-start(), calls=%async_computation.4 | async-start | bytes 10485760 | tf_op jit(solution)/shard_map/reduce_scatter | solution.py:1056
  14.6 50.8 %collective-permute-start = (bf16[512,2048]{1,0:T(8,128)(2,1)S(1)}, bf16[512,2048]{1,0:T(8,128)(2,1)}, u32[]{:S(2)}, u32[]{:S(2)}) collective-permute-start(bf16[512,2048]{1,0:T(8,128)(2,1)S(1)} %copy-done.2), channel_id=1, source_target_pairs={{0,1},{1,2},{2,3},{3,0},{4,5},{5,6},{6,7},{7,4},{8,9},{9,10},{10,1... | collective-permute-start | bytes 6291464 | tf_op jit(solution)/shard_map/ppermute | solution.py:947
  65.4 48.9 %collective-permute-start.1 = (bf16[512,2048]{1,0:T(8,128)(2,1)}, bf16[512,2048]{1,0:T(8,128)(2,1)}, u32[]{:S(2)}, u32[]{:S(2)}) collective-permute-start(bf16[512,2048]{1,0:T(8,128)(2,1)} %collective-permute-done.refs_1_), channel_id=1, source_target_pairs={{0,1},{1,2},{2,3},{3,0},{4,5},{5,6},{6,7},{7,4},{8,9},{9,10},{10,1... | collective-permute-start | bytes 6291464 | tf_op jit(solution)/shard_map/ppermute | solution.py:947
  114.3 48.4 %collective-permute-start.2 = (bf16[512,2048]{1,0:T(8,128)(2,1)}, bf16[512,2048]{1,0:T(8,128)(2,1)}, u32[]{:S(2)}, u32[]{:S(2)}) collective-permute-start(bf16[512,2048]{1,0:T(8,128)(2,1)} %collective-permute-done.1.refs_2_), channel_id=1, source_target_pairs={{0,1},{1,2},{2,3},{3,0},{4,5},{5,6},{6,7},{7,4},{8,9},{9,10},{10,1... | collective-permute-start | bytes 6291464 | tf_op jit(solution)/shard_map/ppermute | solution.py:947
  143.4 19.2 %collective-permute-start.3 = (bf16[8,384]{1,0:T(8,128)(2,1)S(1)}, bf16[8,384]{1,0:T(8,128)(2,1)S(1)}, u32[]{:S(2)}, u32[]{:S(2)}) collective-permute-start(bf16[8,384]{1,0:T(8,128)(2,1)S(1)} %slice.75), channel_id=1, source_target_pairs={{0,1},{1,2},{2,3},{3,0},{4,5},{5,6},{6,7},{7,4},{8,9},{9,10},{10,1... | collective-permute-start | bytes 18440 | tf_op jit(solution)/shard_map/ppermute | solution.py:1011
  144.9 17.8 %collective-permute-start.4 = (bf16[8,384]{1,0:T(8,128)(2,1)S(1)}, bf16[8,384]{1,0:T(8,128)(2,1)S(1)}, u32[]{:S(2)}, u32[]{:S(2)}) collective-permute-start(bf16[8,384]{1,0:T(8,128)(2,1)S(1)} %slice.75), channel_id=1, source_target_pairs={{0,2},{1,3},{2,0},{3,1},{4,6},{5,7},{6,4},{7,5},{8,10},{9,11},{10,... | collective-permute-start | bytes 18440 | tf_op jit(solution)/shard_map/ppermute | solution.py:1011
  147.3 15.4 %collective-permute-start.5 = (bf16[8,384]{1,0:T(8,128)(2,1)S(1)}, bf16[8,384]{1,0:T(8,128)(2,1)S(1)}, u32[]{:S(2)}, u32[]{:S(2)}) collective-permute-start(bf16[8,384]{1,0:T(8,128)(2,1)S(1)} %slice.75), channel_id=1, source_target_pairs={{0,3},{1,0},{2,1},{3,2},{4,7},{5,4},{6,5},{7,6},{8,11},{9,8},{10,9... | collective-permute-start | bytes 18440 | tf_op jit(solution)/shard_map/ppermute | solution.py:1011
  162.7 52.1 %collective-permute-start.6 = (bf16[512,2048]{1,0:T(8,128)(2,1)}, bf16[512,2048]{1,0:T(8,128)(2,1)}, u32[]{:S(2)}, u32[]{:S(2)}) collective-permute-start(bf16[512,2048]{1,0:T(8,128)(2,1)} %refs_0_.3), channel_id=1, source_target_pairs={{0,1},{1,2},{2,3},{3,0},{4,5},{5,6},{6,7},{7,4},{8,9},{9,10},{10,1... | collective-permute-start | bytes 6291464 | tf_op jit(solution)/shard_map/ppermute | solution.py:947
  214.9 57.9 %collective-permute-start.7 = (bf16[512,2048]{1,0:T(8,128)(2,1)}, bf16[512,2048]{1,0:T(8,128)(2,1)S(1)}, u32[]{:S(2)}, u32[]{:S(2)}) collective-permute-start(bf16[512,2048]{1,0:T(8,128)(2,1)} %collective-permute-done.6.refs_1_), channel_id=1, source_target_pairs={{0,1},{1,2},{2,3},{3,0},{4,5},{5,6},{6,7},{7,4},{8,9},{9,10},{10,1... | collective-permute-start | bytes 6291464 | tf_op jit(solution)/shard_map/ppermute | solution.py:947
  274.1 49.3 %collective-permute-start.8 = (bf16[512,2048]{1,0:T(8,128)(2,1)}, bf16[512,2048]{1,0:T(8,128)(2,1)S(1)}, u32[]{:S(2)}, u32[]{:S(2)}) collective-permute-start(bf16[512,2048]{1,0:T(8,128)(2,1)} %copy-done.20), channel_id=1, source_target_pairs={{0,1},{1,2},{2,3},{3,0},{4,5},{5,6},{6,7},{7,4},{8,9},{9,10},{10,1... | collective-permute-start | bytes 6291464 | tf_op jit(solution)/shard_map/ppermute | solution.py:947
  324.7 288.6 %reduce-scatter.6.cloned.1.call-start = ((), (), s32[]{:S(2)}) async-start(), calls=%async_computation.5 | async-start | bytes 73728 | tf_op jit(solution)/shard_map/reduce_scatter | solution.py:1123
  386.1 23.5 %collective-permute-start.9 = (bf16[24,256,256]{2,1,0:T(8,128)(2,1)}, bf16[24,256,256]{2,1,0:T(8,128)(2,1)}, u32[]{:S(2)}, u32[]{:S(2)}) collective-permute-start(bf16[24,256,256]{2,1,0:T(8,128)(2,1)} %get-tuple-element.121), channel_id=1, source_target_pairs={{0,4},{4,0},{8,12},{12,8},{16,20},{20,16},{24,28},{28,24},{1,5},{5... | collective-permute-start | bytes 9437192 | tf_op jit(solution)/shard_map/ppermute | solution.py:952
  406.3 11.7 %collective-permute-start.12 = (bf16[24,256,256]{2,1,0:T(8,128)(2,1)}, bf16[24,256,256]{2,1,0:T(8,128)(2,1)S(1)}, u32[]{:S(2)}, u32[]{:S(2)}) collective-permute-start(bf16[24,256,256]{2,1,0:T(8,128)(2,1)} %get-tuple-element.125), channel_id=1, source_target_pairs={{0,4},{4,0},{8,12},{12,8},{16,20},{20,16},{24,28},{28,24},{1,5},{5... | collective-permute-start | bytes 9437192 | tf_op jit(solution)/shard_map/ppermute | solution.py:952
  414.6 35.2 %collective-permute-start.13 = (bf16[6,256,256]{2,1,0:T(8,128)(2,1)}, bf16[6,256,256]{2,1,0:T(8,128)(2,1)}, u32[]{:S(2)}, u32[]{:S(2)}) collective-permute-start(bf16[6,256,256]{2,1,0:T(8,128)(2,1)} %get-tuple-element.128), channel_id=1, source_target_pairs={{0,24},{4,28},{8,16},{12,20},{16,8},{20,12},{24,0},{28,4},{1,25},{... | collective-permute-start | bytes 2359304 | tf_op jit(solution)/shard_map/ppermute | solution.py:952
  416.5 35.2 %collective-permute-start.17 = (bf16[6,256,256]{2,1,0:T(8,128)(2,1)}, bf16[6,256,256]{2,1,0:T(8,128)(2,1)}, u32[]{:S(2)}, u32[]{:S(2)}) collective-permute-start(bf16[6,256,256]{2,1,0:T(8,128)(2,1)} %get-tuple-element.134), channel_id=1, source_target_pairs={{0,8},{4,12},{8,0},{12,4},{16,24},{20,28},{24,16},{28,20},{1,9},{5... | collective-permute-start | bytes 2359304 | tf_op jit(solution)/shard_map/ppermute | solution.py:952
  416.9 35.3 %collective-permute-start.18 = (bf16[6,256,256]{2,1,0:T(8,128)(2,1)}, bf16[6,256,256]{2,1,0:T(8,128)(2,1)}, u32[]{:S(2)}, u32[]{:S(2)}) collective-permute-start(bf16[6,256,256]{2,1,0:T(8,128)(2,1)} %get-tuple-element.135), channel_id=1, source_target_pairs={{0,16},{4,20},{8,24},{12,28},{16,0},{20,4},{24,8},{28,12},{1,17},{... | collective-permute-start | bytes 2359304 | tf_op jit(solution)/shard_map/ppermute | solution.py:952
  471.6 58.8 %collective-permute-start.19 = (bf16[24,256,256]{2,1,0:T(8,128)(2,1)}, bf16[24,256,256]{2,1,0:T(8,128)(2,1)S(1)}, u32[]{:S(2)}, u32[]{:S(2)}) collective-permute-start(bf16[24,256,256]{2,1,0:T(8,128)(2,1)} %get-tuple-element.141), channel_id=1, source_target_pairs={{0,4},{4,0},{8,12},{12,8},{16,20},{20,16},{24,28},{28,24},{1,5},{5... | collective-permute-start | bytes 9437192 | tf_op jit(solution)/shard_map/ppermute | solution.py:952
  474.9 50.3 %collective-permute-start.10 = (bf16[512,2048]{1,0:T(8,128)(2,1)}, bf16[512,2048]{1,0:T(8,128)(2,1)}, u32[]{:S(2)}, u32[]{:S(2)}) collective-permute-start(bf16[512,2048]{1,0:T(8,128)(2,1)} %constant_dynamic-slice_fusion), channel_id=1, source_target_pairs={{0,1},{1,2},{2,3},{3,0},{4,5},{5,6},{6,7},{7,4},{8,9},{9,10},{10,1... | collective-permute-start | bytes 6291464 | tf_op jit(solution)/shard_map/ppermute | solution.py:947
  484.9 53.9 %collective-permute-start.14 = (bf16[6,256,256]{2,1,0:T(8,128)(2,1)}, bf16[6,256,256]{2,1,0:T(8,128)(2,1)}, u32[]{:S(2)}, u32[]{:S(2)}) collective-permute-start(bf16[6,256,256]{2,1,0:T(8,128)(2,1)} %get-tuple-element.129), channel_id=1, source_target_pairs={{0,8},{4,12},{8,0},{12,4},{16,24},{20,28},{24,16},{28,20},{1,9},{5... | collective-permute-start | bytes 2359304 | tf_op jit(solution)/shard_map/ppermute | solution.py:952
  486.0 52.9 %collective-permute-start.15 = (bf16[6,256,256]{2,1,0:T(8,128)(2,1)}, bf16[6,256,256]{2,1,0:T(8,128)(2,1)}, u32[]{:S(2)}, u32[]{:S(2)}) collective-permute-start(bf16[6,256,256]{2,1,0:T(8,128)(2,1)} %get-tuple-element.131), channel_id=1, source_target_pairs={{0,16},{4,20},{8,24},{12,28},{16,0},{20,4},{24,8},{28,12},{1,17},{... | collective-permute-start | bytes 2359304 | tf_op jit(solution)/shard_map/ppermute | solution.py:952
  487.4 49.5 %collective-permute-start.16 = (bf16[6,256,256]{2,1,0:T(8,128)(2,1)}, bf16[6,256,256]{2,1,0:T(8,128)(2,1)}, u32[]{:S(2)}, u32[]{:S(2)}) collective-permute-start(bf16[6,256,256]{2,1,0:T(8,128)(2,1)} %get-tuple-element.133.refs_13_), channel_id=1, source_target_pairs={{0,24},{4,28},{8,16},{12,20},{16,8},{20,12},{24,0},{28,4},{1,25},{... | collective-permute-start | bytes 2359304 | tf_op jit(solution)/shard_map/ppermute | solution.py:952
  525.2 43.4 %collective-permute-start.21 = (bf16[24,256,256]{2,1,0:T(8,128)(2,1)}, bf16[24,256,256]{2,1,0:T(8,128)(2,1)}, u32[]{:S(2)}, u32[]{:S(2)}) collective-permute-start(bf16[24,256,256]{2,1,0:T(8,128)(2,1)} %get-tuple-element.153), channel_id=1, source_target_pairs={{0,4},{4,0},{8,12},{12,8},{16,20},{20,16},{24,28},{28,24},{1,5},{5... | collective-permute-start | bytes 9437192 | tf_op jit(solution)/shard_map/ppermute | solution.py:952
  530.4 78.9 %collective-permute-start.11 = (bf16[512,2048]{1,0:T(8,128)(2,1)}, bf16[512,2048]{1,0:T(8,128)(2,1)}, u32[]{:S(2)}, u32[]{:S(2)}) collective-permute-start(bf16[512,2048]{1,0:T(8,128)(2,1)} %add_convert_fusion.1.refs_17_), channel_id=1, source_target_pairs={{0,1},{1,2},{2,3},{3,0},{4,5},{5,6},{6,7},{7,4},{8,9},{9,10},{10,1... | collective-permute-start | bytes 6291464 | tf_op jit(solution)/shard_map/ppermute | solution.py:947
  536.9 36.5 %collective-permute-start.22 = (bf16[6,256,256]{2,1,0:T(8,128)(2,1)}, bf16[6,256,256]{2,1,0:T(8,128)(2,1)S(1)}, u32[]{:S(2)}, u32[]{:S(2)}) collective-permute-start(bf16[6,256,256]{2,1,0:T(8,128)(2,1)} %get-tuple-element.143.refs_17_), channel_id=1, source_target_pairs={{0,24},{4,28},{8,16},{12,20},{16,8},{20,12},{24,0},{28,4},{1,25},{... | collective-permute-start | bytes 2359304 | tf_op jit(solution)/shard_map/ppermute | solution.py:952
  567.0 47.8 %collective-permute-start.26 = (bf16[6,256,256]{2,1,0:T(8,128)(2,1)}, bf16[6,256,256]{2,1,0:T(8,128)(2,1)}, u32[]{:S(2)}, u32[]{:S(2)}) collective-permute-start(bf16[6,256,256]{2,1,0:T(8,128)(2,1)} %get-tuple-element.163), channel_id=1, source_target_pairs={{0,8},{4,12},{8,0},{12,4},{16,24},{20,28},{24,16},{28,20},{1,9},{5... | collective-permute-start | bytes 2359304 | tf_op jit(solution)/shard_map/ppermute | solution.py:952
  567.4 48.2 %collective-permute-start.27 = (bf16[6,256,256]{2,1,0:T(8,128)(2,1)}, bf16[6,256,256]{2,1,0:T(8,128)(2,1)}, u32[]{:S(2)}, u32[]{:S(2)}) collective-permute-start(bf16[6,256,256]{2,1,0:T(8,128)(2,1)} %get-tuple-element.165), channel_id=1, source_target_pairs={{0,16},{4,20},{8,24},{12,28},{16,0},{20,4},{24,8},{28,12},{1,17},{... | collective-permute-start | bytes 2359304 | tf_op jit(solution)/shard_map/ppermute | solution.py:952
  574.4 71.8 %collective-permute-start.23 = (bf16[6,256,256]{2,1,0:T(8,128)(2,1)}, bf16[6,256,256]{2,1,0:T(8,128)(2,1)S(1)}, u32[]{:S(2)}, u32[]{:S(2)}) collective-permute-start(bf16[6,256,256]{2,1,0:T(8,128)(2,1)} %get-tuple-element.156), channel_id=1, source_target_pairs={{0,8},{4,12},{8,0},{12,4},{16,24},{20,28},{24,16},{28,20},{1,9},{5... | collective-permute-start | bytes 2359304 | tf_op jit(solution)/shard_map/ppermute | solution.py:952
  575.4 70.7 %collective-permute-start.24 = (bf16[6,256,256]{2,1,0:T(8,128)(2,1)}, bf16[6,256,256]{2,1,0:T(8,128)(2,1)}, u32[]{:S(2)}, u32[]{:S(2)}) collective-permute-start(bf16[6,256,256]{2,1,0:T(8,128)(2,1)} %get-tuple-element.158), channel_id=1, source_target_pairs={{0,16},{4,20},{8,24},{12,28},{16,0},{20,4},{24,8},{28,12},{1,17},{... | collective-permute-start | bytes 2359304 | tf_op jit(solution)/shard_map/ppermute | solution.py:952
  576.9 67.1 %reduce-scatter.8.cloned.1.call-start = ((), (), s32[]{:S(2)}) async-start(), calls=%async_computation.6 | async-start | bytes 40960 | tf_op jit(solution)/shard_map/reduce_scatter | solution.py:1133
  609.3 36.9 %collective-permute-start.25 = (bf16[6,256,256]{2,1,0:T(8,128)(2,1)}, bf16[6,256,256]{2,1,0:T(8,128)(2,1)}, u32[]{:S(2)}, u32[]{:S(2)}) collective-permute-start(bf16[6,256,256]{2,1,0:T(8,128)(2,1)} %get-tuple-element.160.refs_17_), channel_id=1, source_target_pairs={{0,24},{4,28},{8,16},{12,20},{16,8},{20,12},{24,0},{28,4},{1,25},{... | collective-permute-start | bytes 2359304 | tf_op jit(solution)/shard_map/ppermute | solution.py:952
  614.8 59.9 %collective-permute-start.20 = (bf16[512,2048]{1,0:T(8,128)(2,1)S(1)}, bf16[512,2048]{1,0:T(8,128)(2,1)}, u32[]{:S(2)}, u32[]{:S(2)}) collective-permute-start(bf16[512,2048]{1,0:T(8,128)(2,1)S(1)} %add_convert_fusion.refs_18_), channel_id=1, source_target_pairs={{0,1},{1,2},{2,3},{3,0},{4,5},{5,6},{6,7},{7,4},{8,9},{9,10},{10,1... | collective-permute-start | bytes 6291464 | tf_op jit(solution)/shard_map/ppermute | solution.py:947
  (24 other events, 443.6 us)
Sparse Core Ops, SparseCore 0:
  14.1 128.2 all-gather.1
  323.5 144.7 reduce-scatter.3
  577.0 31.6 reduce-scatter.5
  614.9 18.8 reduce-scatter.7

commit v7 on v6

--- a/solution.py
+++ b/solution.py
@@ -708,16 +708,18 @@
 def pair_sum(kept, received, chip, chips):
     rows, size, _ = kept.shape
     part = rows // chips
+    tile = next(each for each in (3, 2, 1) if part % each == 0)
+    pieces = part // tile
     spec = lambda away: pl.BlockSpec(
-        (part, size, size), lambda i, chip: (jnp.bitwise_xor(chip[0], away), 0, 0)
-    )
-    plain = pl.BlockSpec((part, size, size), lambda i, chip: (0, 0, 0))
+        (tile, size, size), lambda i, chip: (jnp.bitwise_xor(chip[0], away) * pieces + i, 0, 0)
+    )
+    plain = pl.BlockSpec((tile, size, size), lambda i, chip: (i, 0, 0))
     dtypes = [jnp.float32] + [jnp.bfloat16] * (chips - 1)
     return pl.pallas_call(
         pair_sum_kernel,
         grid_spec=pltpu.PrefetchScalarGridSpec(
             num_scalar_prefetch=1,
-            grid=(1,),
+            grid=(pieces,),
             in_specs=[spec(away) for away in range(chips)] * 2,
             out_specs=[plain] * chips,
         ),

time: 697 us -> 696 us (level)
  no operation moved by 1% of the time
where the time goes in v7:
time: 696 us; the launch traced here: 687 us
  Pallas kernels  430 us (62%)
  waiting for transfers between devices  158 us (23%)
  other arithmetic  29.9 us (4%)
  starting transfers between devices  29.5 us (4%)
  local copies, waits for them, and re-layouts  24.6 us (4%)
  between operations  15.3 us (2%)
    ppermute x9, waiting for transfers between devices, onward(): lax.ppermute(part, axis, [(each, (each + 1) % ways) for each in range(way...  115 us
    pallas_call x4, Pallas kernels, shampoo(): pl.pallas_call(functools.partial(shampoo_kernel, count, len(grads), held...  112 us
    pallas_call x4, Pallas kernels, weight_grads(): pl.pallas_call(functools.partial(weight_grad_kernel, tuple(steps), len(wa...  78.1 us
    pallas_call x2, Pallas kernels, feed_back(): pl.pallas_call(functools.partial(feed_back_kernel, offsets, owned, first_...  72.7 us
    pallas_call x1, Pallas kernels, feed_forward(): pl.pallas_call(functools.partial(feed_kernel, offsets, owned), grid=(toke...  57.1 us
    pallas_call x1, Pallas kernels, project_qkv(): pl.pallas_call(functools.partial(qkv_kernel, heads, owned, ways), grid_sp...  32.9 us
    all_gather x1, waiting for transfers between devices, shards(): blocks = lax.all_gather(rows16, 'dp', axis=0, tiled=True)  25.8 us
    pallas_call x1, Pallas kernels, qkv_back(): pl.pallas_call(functools.partial(qkv_back_kernel, owned, len(waits)), gri...  25.1 us
  transfers between devices with their start and end apart: 32, of which 9 were waited for; matrix products, arithmetic and copies ran while one was open for 6% of the time, Pallas kernels for 62%

profile of v7, /device:TPU:0, one launch (start us, length us, event | category | flops | bytes accessed | tf_op | source)
XLA Modules:
  0.0 686.8 jit_solution(2579760282374293793)
XLA Ops:
  8.9 3.2 convert.20
  14.6 3.0 collective-permute-start
  17.7 47.8 %collective-permute-done.refs_1_ = bf16[512,2048]{1,0:T(8,128)(2,1)} collective-permute-done((bf16[512,2048]{1,0:T(8,128)(2,1)S(1)}, bf16[512,2048]{1,0:T(8,128)(2,1)}, u32[]{:S(2)}, u32[]{:S(2)}) %collective-permute-start) | collective-permute-done | bytes 2097184 | tf_op jit(solution)/shard_map/ppermute | solution.py:949
  65.5 48.8 %collective-permute-done.1.refs_2_ = bf16[512,2048]{1,0:T(8,128)(2,1)} collective-permute-done((bf16[512,2048]{1,0:T(8,128)(2,1)}, bf16[512,2048]{1,0:T(8,128)(2,1)}, u32[]{:S(2)}, u32[]{:S(2)}) %collective-permute-start.1) | collective-permute-done | bytes 2097184 | tf_op jit(solution)/shard_map/ppermute | solution.py:949
  116.7 25.8 %all-gather.2.cloned.1.call-done.refs_4_.blocks_ref.refs_8_.refs_6_ = bf16[49280,256]{1,0:T(8,128)(2,1)} async-done(((bf16[6160,256]{1,0:T(8,128)(2,1)}), bf16[49280,256]{1,0:T(8,128)(2,1)}) %all-gather.2.cloned.1.call-update) | async-done | bytes 25231376 | tf_op jit(solution)/shard_map/all_gather | solution.py:998
  148.8 13.8 %collective-permute-done.3 = bf16[8,384]{1,0:T(8,128)(2,1)S(1)} collective-permute-done((bf16[8,384]{1,0:T(8,128)(2,1)S(1)}, bf16[8,384]{1,0:T(8,128)(2,1)S(1)}, u32[]{:S(2)}, u32[]{:S(2)}) %collective-permute-start.3) | collective-permute-done | bytes 6176 | tf_op jit(solution)/shard_map/ppermute | solution.py:1013
  171.1 32.9 %qkv.1 = (bf16[2048,1536]{1,0:T(8,128)(2,1)}, bf16[2048,2048]{1,0:T(8,128)(2,1)}, bf16[2048,2048]{1,0:T(8,128)(2,1)}, bf16[2048,2048]{1,0:T(8,128)(2,1)}, bf16[2...) custom-call(s32[1]{0:T(128)} %bitcast.1.rank_ref, bf16[512,2048]{1,0:T(8,128)(2,1)} %refs_2_.1, ...), custom_call_target="tpu_custom_call" | custom-call | flops 12884901888 | bytes 46137344 | tf_op jit(solution)/shard_map/qkv/pallas_call | solution.py:188
  204.1 10.8 %attend.1 = (bf16[2048,512]{1,0:T(8,128)(2,1)}, bf16[512,2048]{1,0:T(8,128)(2,1)}) custom-call(bf16[2048,1536]{1,0:T(8,128)(2,1)} %get-tuple-element.96.query_ref.key_ref.value_ref, bf16[2048,1536]{1,0:T(8,128)(2,1)} %get-tuple-element.96.query_ref.key_ref.value_ref, bf16[2048,1536]{1,0:T(8,128)(2,1)} %get-tuple-element.96.query_ref.key_ref.value_ref, ...), custom_call_target="tpu_custom_call" | custom-call | flops 3221225472 | bytes 8388608 | tf_op jit(solution)/shard_map/attend/pallas_call | solution.py:239
  215.6 57.1 %feed.1 = (bf16[2048,2048]{1,0:T(8,128)(2,1)}, bf16[2048,2048]{1,0:T(8,128)(2,1)}, bf16[2048,2048]{1,0:T(8,128)(2,1)}) custom-call(bf16[2048,2048]{1,0:T(8,128)(2,1)} %get-tuple-element.95.x_ref, bf16[2048,512]{1,0:T(8,128)(2,1)} %get-tuple-element.97.attended_ref, bf16[49280,256]{1,0:T(8,128)(2,1)} %all-gather.2.cloned.1.call-done.refs_4_.blocks_ref.refs_8_.refs_6_, ...), custom_call_target="tpu_custom_call" | custom-call | flops 38654705664 | bytes 58720256 | tf_op jit(solution)/shard_map/feed/pallas_call | solution.py:379
  274.7 47.8 %feed_back.2 = (bf16[2048,2048]{1,0:T(8,128)(2,1)}, bf16[2048,512]{1,0:T(8,128)(2,1)}, bf16[2048,2048]{1,0:T(8,128)(2,1)}, bf16[2048,2048]{1,0:T(8,128)(2,1)}, f32[24,2048]{1,0:T(8,128)}, /*index=5*/f32[8,2048]{1,0:T(8,128)}) custom-call(s32[1]{0:T(128)} %bitcast.1.rank_ref, bf16[512,2048]{1,0:T(8,128)(2,1)} %refs_0_.3, ...), custom_call_target="tpu_custom_call" | custom-call | flops 28991029248 | bytes 60817408 | tf_op jit(solution)/shard_map/feed_back/pallas_call | solution.py:485
  324.9 24.8 %feed_back.3 = (bf16[2048,2048]{1,0:T(8,128)(2,1)}, bf16[2048,512]{1,0:T(8,128)(2,1)}, bf16[2048,2048]{1,0:T(8,128)(2,1)}, bf16[2048,2048]{1,0:T(8,128)(2,1)}, f32[24,2048]{1,0:T(8,128)}, /*index=5*/f32[8,2048]{1,0:T(8,128)}) custom-call(s32[1]{0:T(128)} %bitcast.1.rank_ref, ...), custom_call_target="tpu_custom_call", output_to_operand_aliasing={{0}: (9, {}), {1}: (10, {}), {2}: (11, {}), {3}: (12, {})} | custom-call | flops 9663676416 | bytes 31457280 | tf_op jit(solution)/shard_map/feed_back/pallas_call | solution.py:485
  349.7 17.1 %attend_back.1.refs_6_.d_qkv_ref = bf16[2048,1536]{1,0:T(8,128)(2,1)} custom-call(bf16[2048,1536]{1,0:T(8,128)(2,1)} %get-tuple-element.96.query_ref.key_ref.value_ref, bf16[2048,1536]{1,0:T(8,128)(2,1)} %get-tuple-element.96.query_ref.key_ref.value_ref, bf16[2048,1536]{1,0:T(8,128)(2,1)} %get-tuple-element.96.query_ref.key_ref.value_ref, ...), custom_call_target="tpu_custom_call" | custom-call | flops 7516192768 | bytes 16777216 | tf_op jit(solution)/shard_map/attend_back/pallas_call | solution.py:306
  366.8 19.4 %weight_grads.4 = (bf16[24,256,256]{2,1,0:T(8,128)(2,1)}, bf16[24,256,256]{2,1,0:T(8,128)(2,1)}) custom-call(s32[1]{0:T(128)} %bitcast.13.core_ref, bf16[2048,2048]{1,0:T(8,128)(2,1)} %get-tuple-element.114.refs_0_, bf16[2048,2048]{1,0:T(8,128)(2,1)} %get-tuple-element.115.refs_1_, bf16[2048,2048]{1,0:T(8,128)(2,1)} %get-tuple-element.116.refs_2_, ...), custom_call_target="tpu_custom_call" | custom-call | flops 12884901888 | bytes 25769804 | tf_op jit(solution)/shard_map/weight_grads/pallas_call | solution.py:680
  386.2 20.1 %weight_grads.5 = (bf16[24,256,256]{2,1,0:T(8,128)(2,1)}, bf16[24,256,256]{2,1,0:T(8,128)(2,1)}) custom-call(s32[1]{0:T(128)} %bitcast.13.core_ref, bf16[2048,2048]{1,0:T(8,128)(2,1)} %get-tuple-element.114.refs_0_, bf16[2048,2048]{1,0:T(8,128)(2,1)} %get-tuple-element.115.refs_1_, bf16[2048,2048]{1,0:T(8,128)(2,1)} %get-tuple-element.116.refs_2_, ...), custom_call_target="tpu_custom_call" | custom-call | flops 12884901888 | bytes 25769804 | tf_op jit(solution)/shard_map/weight_grads/pallas_call | solution.py:680
  409.6 4.4 pair_sum.4
  419.3 4.5 pair_sum.5
  423.7 25.1 %qkv_back.1 = (bf16[2048,2048]{1,0:T(8,128)(2,1)}, f32[16,2048]{1,0:T(8,128)}, f32[8,1536]{1,0:T(8,128)}) custom-call(bf16[2048,1536]{1,0:T(8,128)(2,1)} %attend_back.1.refs_6_.d_qkv_ref, bf16[2048,2048]{1,0:T(8,128)(2,1)} %get-tuple-element.113.part_ref, bf16[2048,2048]{1,0:T(8,128)(2,1)} %get-tuple-element.103.refs_5_.refs_3_.tokens_ref, ...), custom_call_target="tpu_custom_call" | custom-call | flops 12884901888 | bytes 46137344 | tf_op jit(solution)/shard_map/qkv_back/pallas_call | solution.py:559
  451.7 19.3 %weight_grads.6 = (bf16[24,256,256]{2,1,0:T(8,128)(2,1)}, bf16[24,256,256]{2,1,0:T(8,128)(2,1)}) custom-call(s32[1]{0:T(128)} %bitcast.13.core_ref, bf16[2048,2048]{1,0:T(8,128)(2,1)} %get-tuple-element.114.refs_0_, bf16[2048,2048]{1,0:T(8,128)(2,1)} %get-tuple-element.115.refs_1_, bf16[2048,2048]{1,0:T(8,128)(2,1)} %get-tuple-element.116.refs_2_, ...), custom_call_target="tpu_custom_call" | custom-call | flops 12884901888 | bytes 25769804 | tf_op jit(solution)/shard_map/weight_grads/pallas_call | solution.py:680
  471.2 3.2 constant_dynamic-slice_fusion
  474.4 2.7 collective-permute-start.10
  487.9 19.3 %weight_grads.7 = (bf16[24,256,256]{2,1,0:T(8,128)(2,1)}, bf16[24,256,256]{2,1,0:T(8,128)(2,1)}) custom-call(s32[1]{0:T(128)} %bitcast.13.core_ref, bf16[2048,2048]{1,0:T(8,128)(2,1)} %get-tuple-element.114.refs_0_, bf16[2048,2048]{1,0:T(8,128)(2,1)} %get-tuple-element.115.refs_1_, bf16[2048,2048]{1,0:T(8,128)(2,1)} %get-tuple-element.116.refs_2_, ...), custom_call_target="tpu_custom_call" | custom-call | flops 12884901888 | bytes 25769804 | tf_op jit(solution)/shard_map/weight_grads/pallas_call | solution.py:680
  507.2 17.5 %collective-permute-done.10 = bf16[512,2048]{1,0:T(8,128)(2,1)} collective-permute-done((bf16[512,2048]{1,0:T(8,128)(2,1)}, bf16[512,2048]{1,0:T(8,128)(2,1)}, u32[]{:S(2)}, u32[]{:S(2)}) %collective-permute-start.10) | collective-permute-done | bytes 2097184 | tf_op jit(solution)/shard_map/ppermute | solution.py:949
  525.4 4.5 add_convert_fusion.1.refs_17_
  531.5 4.4 pair_sum.6
  537.9 28.0 %shampoo.4 = (f32[24,256,256]{2,1,0:T(8,128)}, f32[24,256,256]{2,1,0:T(8,128)}, f32[24,256,256]{2,1,0:T(8,128)}, f32[24,256,256]{2,1,0:T(8,128)}) custom-call(s32[6]{0:T(128)} %broadcast_select_fusion.2.places_ref, f32[6,256,256]{2,1,0:T(8,128)} %get-tuple-element.122.refs_0_, bf16[6,256,256]{2,1,0:T(8,128)(2,1)} %collective-permute-done.17.refs_1_.refs_9_.refs_7_, ...), custom_call_target="tpu_custom_call" | custom-call | flops 26172456960 | bytes 11796480 | tf_op jit(solution)/shard_map/shampoo/pallas_call | solution.py:905
  567.5 4.5 pair_sum.7
  575.7 28.1 %shampoo.5 = (f32[24,256,256]{2,1,0:T(8,128)}, f32[24,256,256]{2,1,0:T(8,128)}, f32[24,256,256]{2,1,0:T(8,128)}, f32[24,256,256]{2,1,0:T(8,128)}) custom-call(s32[6]{0:T(128)} %broadcast_select_fusion.3.places_ref, f32[6,256,256]{2,1,0:T(8,128)} %get-tuple-element.126.refs_8_.refs_0_, ...), custom_call_target="tpu_custom_call", output_to_operand_aliasing={{0}: (14, {}), {1}: (15, {}), {2}: (16, {}), {3}: (17, {})} | custom-call | flops 26172456960 | bytes 11796480 | tf_op jit(solution)/shard_map/shampoo/pallas_call | solution.py:905
  603.8 4.1 multiply_convert_fusion.refs_17_
  608.8 3.0 add_convert_fusion.refs_18_
  614.3 27.7 %shampoo.6 = (f32[24,256,256]{2,1,0:T(8,128)}, f32[24,256,256]{2,1,0:T(8,128)}, f32[24,256,256]{2,1,0:T(8,128)}, f32[24,256,256]{2,1,0:T(8,128)}) custom-call(s32[6]{0:T(128)} %broadcast_select_fusion.places_ref, f32[6,256,256]{2,1,0:T(8,128)} %get-tuple-element.161.refs_0_, ...), custom_call_target="tpu_custom_call", output_to_operand_aliasing={{0}: (14, {}), {1}: (15, {}), {2}: (16, {}), {3}: (17, {})} | custom-call | flops 26172456960 | bytes 11796480 | tf_op jit(solution)/shard_map/shampoo/pallas_call | solution.py:905
  645.6 27.7 %shampoo.7 = (f32[24,256,256]{2,1,0:T(8,128)}, f32[24,256,256]{2,1,0:T(8,128)}, f32[24,256,256]{2,1,0:T(8,128)}, f32[24,256,256]{2,1,0:T(8,128)}) custom-call(s32[6]{0:T(128)} %broadcast_select_fusion.1.places_ref, f32[6,256,256]{2,1,0:T(8,128)} %get-tuple-element.154.refs_0_, ...), custom_call_target="tpu_custom_call", output_to_operand_aliasing={{0}: (14, {}), {1}: (15, {}), {2}: (16, {}), {3}: (17, {})} | custom-call | flops 26172456960 | bytes 11796480 | tf_op jit(solution)/shard_map/shampoo/pallas_call | solution.py:905
  673.4 6.7 input_gradient.1
  (188 shorter events, 64.2 us)
Async XLA Ops:
  7.2 135.3 %all-gather.2.cloned.1.call-start = ((), (), s32[]{:S(2)}) async-start(), calls=%async_computation.3 | async-start | bytes 28385280 | tf_op jit(solution)/shard_map/all_gather | solution.py:998
  14.0 561.5 %reduce-scatter.4.cloned.1.call-start = ((), (), s32[]{:S(2)}) async-start(), calls=%async_computation.4 | async-start | bytes 10485760 | tf_op jit(solution)/shard_map/reduce_scatter | solution.py:1058
  14.6 50.8 %collective-permute-start = (bf16[512,2048]{1,0:T(8,128)(2,1)S(1)}, bf16[512,2048]{1,0:T(8,128)(2,1)}, u32[]{:S(2)}, u32[]{:S(2)}) collective-permute-start(bf16[512,2048]{1,0:T(8,128)(2,1)S(1)} %copy-done.2), channel_id=1, source_target_pairs={{0,1},{1,2},{2,3},{3,0},{4,5},{5,6},{6,7},{7,4},{8,9},{9,10},{10,1... | collective-permute-start | bytes 6291464 | tf_op jit(solution)/shard_map/ppermute | solution.py:949
  65.4 48.9 %collective-permute-start.1 = (bf16[512,2048]{1,0:T(8,128)(2,1)}, bf16[512,2048]{1,0:T(8,128)(2,1)}, u32[]{:S(2)}, u32[]{:S(2)}) collective-permute-start(bf16[512,2048]{1,0:T(8,128)(2,1)} %collective-permute-done.refs_1_), channel_id=1, source_target_pairs={{0,1},{1,2},{2,3},{3,0},{4,5},{5,6},{6,7},{7,4},{8,9},{9,10},{10,1... | collective-permute-start | bytes 6291464 | tf_op jit(solution)/shard_map/ppermute | solution.py:949
  114.3 48.4 %collective-permute-start.2 = (bf16[512,2048]{1,0:T(8,128)(2,1)}, bf16[512,2048]{1,0:T(8,128)(2,1)}, u32[]{:S(2)}, u32[]{:S(2)}) collective-permute-start(bf16[512,2048]{1,0:T(8,128)(2,1)} %collective-permute-done.1.refs_2_), channel_id=1, source_target_pairs={{0,1},{1,2},{2,3},{3,0},{4,5},{5,6},{6,7},{7,4},{8,9},{9,10},{10,1... | collective-permute-start | bytes 6291464 | tf_op jit(solution)/shard_map/ppermute | solution.py:949
  143.4 19.2 %collective-permute-start.3 = (bf16[8,384]{1,0:T(8,128)(2,1)S(1)}, bf16[8,384]{1,0:T(8,128)(2,1)S(1)}, u32[]{:S(2)}, u32[]{:S(2)}) collective-permute-start(bf16[8,384]{1,0:T(8,128)(2,1)S(1)} %slice.75), channel_id=1, source_target_pairs={{0,1},{1,2},{2,3},{3,0},{4,5},{5,6},{6,7},{7,4},{8,9},{9,10},{10,1... | collective-permute-start | bytes 18440 | tf_op jit(solution)/shard_map/ppermute | solution.py:1013
  144.9 17.8 %collective-permute-start.4 = (bf16[8,384]{1,0:T(8,128)(2,1)S(1)}, bf16[8,384]{1,0:T(8,128)(2,1)S(1)}, u32[]{:S(2)}, u32[]{:S(2)}) collective-permute-start(bf16[8,384]{1,0:T(8,128)(2,1)S(1)} %slice.75), channel_id=1, source_target_pairs={{0,2},{1,3},{2,0},{3,1},{4,6},{5,7},{6,4},{7,5},{8,10},{9,11},{10,... | collective-permute-start | bytes 18440 | tf_op jit(solution)/shard_map/ppermute | solution.py:1013
  147.3 15.4 %collective-permute-start.5 = (bf16[8,384]{1,0:T(8,128)(2,1)S(1)}, bf16[8,384]{1,0:T(8,128)(2,1)S(1)}, u32[]{:S(2)}, u32[]{:S(2)}) collective-permute-start(bf16[8,384]{1,0:T(8,128)(2,1)S(1)} %slice.75), channel_id=1, source_target_pairs={{0,3},{1,0},{2,1},{3,2},{4,7},{5,4},{6,5},{7,6},{8,11},{9,8},{10,9... | collective-permute-start | bytes 18440 | tf_op jit(solution)/shard_map/ppermute | solution.py:1013
  162.7 52.1 %collective-permute-start.6 = (bf16[512,2048]{1,0:T(8,128)(2,1)}, bf16[512,2048]{1,0:T(8,128)(2,1)}, u32[]{:S(2)}, u32[]{:S(2)}) collective-permute-start(bf16[512,2048]{1,0:T(8,128)(2,1)} %refs_0_.3), channel_id=1, source_target_pairs={{0,1},{1,2},{2,3},{3,0},{4,5},{5,6},{6,7},{7,4},{8,9},{9,10},{10,1... | collective-permute-start | bytes 6291464 | tf_op jit(solution)/shard_map/ppermute | solution.py:949
  214.9 57.9 %collective-permute-start.7 = (bf16[512,2048]{1,0:T(8,128)(2,1)}, bf16[512,2048]{1,0:T(8,128)(2,1)S(1)}, u32[]{:S(2)}, u32[]{:S(2)}) collective-permute-start(bf16[512,2048]{1,0:T(8,128)(2,1)} %collective-permute-done.6.refs_1_), channel_id=1, source_target_pairs={{0,1},{1,2},{2,3},{3,0},{4,5},{5,6},{6,7},{7,4},{8,9},{9,10},{10,1... | collective-permute-start | bytes 6291464 | tf_op jit(solution)/shard_map/ppermute | solution.py:949
  274.1 49.3 %collective-permute-start.8 = (bf16[512,2048]{1,0:T(8,128)(2,1)}, bf16[512,2048]{1,0:T(8,128)(2,1)S(1)}, u32[]{:S(2)}, u32[]{:S(2)}) collective-permute-start(bf16[512,2048]{1,0:T(8,128)(2,1)} %copy-done.20), channel_id=1, source_target_pairs={{0,1},{1,2},{2,3},{3,0},{4,5},{5,6},{6,7},{7,4},{8,9},{9,10},{10,1... | collective-permute-start | bytes 6291464 | tf_op jit(solution)/shard_map/ppermute | solution.py:949
  324.7 287.2 %reduce-scatter.6.cloned.1.call-start = ((), (), s32[]{:S(2)}) async-start(), calls=%async_computation.5 | async-start | bytes 73728 | tf_op jit(solution)/shard_map/reduce_scatter | solution.py:1125
  386.1 23.5 %collective-permute-start.9 = (bf16[24,256,256]{2,1,0:T(8,128)(2,1)}, bf16[24,256,256]{2,1,0:T(8,128)(2,1)}, u32[]{:S(2)}, u32[]{:S(2)}) collective-permute-start(bf16[24,256,256]{2,1,0:T(8,128)(2,1)} %get-tuple-element.121), channel_id=1, source_target_pairs={{0,4},{4,0},{8,12},{12,8},{16,20},{20,16},{24,28},{28,24},{1,5},{5... | collective-permute-start | bytes 9437192 | tf_op jit(solution)/shard_map/ppermute | solution.py:954
  406.3 11.3 %collective-permute-start.12 = (bf16[24,256,256]{2,1,0:T(8,128)(2,1)}, bf16[24,256,256]{2,1,0:T(8,128)(2,1)S(1)}, u32[]{:S(2)}, u32[]{:S(2)}) collective-permute-start(bf16[24,256,256]{2,1,0:T(8,128)(2,1)} %get-tuple-element.125), channel_id=1, source_target_pairs={{0,4},{4,0},{8,12},{12,8},{16,20},{20,16},{24,28},{28,24},{1,5},{5... | collective-permute-start | bytes 9437192 | tf_op jit(solution)/shard_map/ppermute | solution.py:954
  414.1 34.8 %collective-permute-start.13 = (bf16[6,256,256]{2,1,0:T(8,128)(2,1)}, bf16[6,256,256]{2,1,0:T(8,128)(2,1)}, u32[]{:S(2)}, u32[]{:S(2)}) collective-permute-start(bf16[6,256,256]{2,1,0:T(8,128)(2,1)} %get-tuple-element.128), channel_id=1, source_target_pairs={{0,24},{4,28},{8,16},{12,20},{16,8},{20,12},{24,0},{28,4},{1,25},{... | collective-permute-start | bytes 2359304 | tf_op jit(solution)/shard_map/ppermute | solution.py:954
  416.0 35.2 %collective-permute-start.17 = (bf16[6,256,256]{2,1,0:T(8,128)(2,1)}, bf16[6,256,256]{2,1,0:T(8,128)(2,1)}, u32[]{:S(2)}, u32[]{:S(2)}) collective-permute-start(bf16[6,256,256]{2,1,0:T(8,128)(2,1)} %get-tuple-element.134), channel_id=1, source_target_pairs={{0,8},{4,12},{8,0},{12,4},{16,24},{20,28},{24,16},{28,20},{1,9},{5... | collective-permute-start | bytes 2359304 | tf_op jit(solution)/shard_map/ppermute | solution.py:954
  416.5 35.3 %collective-permute-start.18 = (bf16[6,256,256]{2,1,0:T(8,128)(2,1)}, bf16[6,256,256]{2,1,0:T(8,128)(2,1)}, u32[]{:S(2)}, u32[]{:S(2)}) collective-permute-start(bf16[6,256,256]{2,1,0:T(8,128)(2,1)} %get-tuple-element.135), channel_id=1, source_target_pairs={{0,16},{4,20},{8,24},{12,28},{16,0},{20,4},{24,8},{28,12},{1,17},{... | collective-permute-start | bytes 2359304 | tf_op jit(solution)/shard_map/ppermute | solution.py:954
  471.1 58.8 %collective-permute-start.19 = (bf16[24,256,256]{2,1,0:T(8,128)(2,1)}, bf16[24,256,256]{2,1,0:T(8,128)(2,1)S(1)}, u32[]{:S(2)}, u32[]{:S(2)}) collective-permute-start(bf16[24,256,256]{2,1,0:T(8,128)(2,1)} %get-tuple-element.141), channel_id=1, source_target_pairs={{0,4},{4,0},{8,12},{12,8},{16,20},{20,16},{24,28},{28,24},{1,5},{5... | collective-permute-start | bytes 9437192 | tf_op jit(solution)/shard_map/ppermute | solution.py:954
  474.4 50.3 %collective-permute-start.10 = (bf16[512,2048]{1,0:T(8,128)(2,1)}, bf16[512,2048]{1,0:T(8,128)(2,1)}, u32[]{:S(2)}, u32[]{:S(2)}) collective-permute-start(bf16[512,2048]{1,0:T(8,128)(2,1)} %constant_dynamic-slice_fusion), channel_id=1, source_target_pairs={{0,1},{1,2},{2,3},{3,0},{4,5},{5,6},{6,7},{7,4},{8,9},{9,10},{10,1... | collective-permute-start | bytes 6291464 | tf_op jit(solution)/shard_map/ppermute | solution.py:949
  484.4 53.6 %collective-permute-start.14 = (bf16[6,256,256]{2,1,0:T(8,128)(2,1)}, bf16[6,256,256]{2,1,0:T(8,128)(2,1)}, u32[]{:S(2)}, u32[]{:S(2)}) collective-permute-start(bf16[6,256,256]{2,1,0:T(8,128)(2,1)} %get-tuple-element.129), channel_id=1, source_target_pairs={{0,8},{4,12},{8,0},{12,4},{16,24},{20,28},{24,16},{28,20},{1,9},{5... | collective-permute-start | bytes 2359304 | tf_op jit(solution)/shard_map/ppermute | solution.py:954
  485.5 52.4 %collective-permute-start.15 = (bf16[6,256,256]{2,1,0:T(8,128)(2,1)}, bf16[6,256,256]{2,1,0:T(8,128)(2,1)}, u32[]{:S(2)}, u32[]{:S(2)}) collective-permute-start(bf16[6,256,256]{2,1,0:T(8,128)(2,1)} %get-tuple-element.131), channel_id=1, source_target_pairs={{0,16},{4,20},{8,24},{12,28},{16,0},{20,4},{24,8},{28,12},{1,17},{... | collective-permute-start | bytes 2359304 | tf_op jit(solution)/shard_map/ppermute | solution.py:954
  486.9 49.0 %collective-permute-start.16 = (bf16[6,256,256]{2,1,0:T(8,128)(2,1)}, bf16[6,256,256]{2,1,0:T(8,128)(2,1)}, u32[]{:S(2)}, u32[]{:S(2)}) collective-permute-start(bf16[6,256,256]{2,1,0:T(8,128)(2,1)} %get-tuple-element.133.refs_13_), channel_id=1, source_target_pairs={{0,24},{4,28},{8,16},{12,20},{16,8},{20,12},{24,0},{28,4},{1,25},{... | collective-permute-start | bytes 2359304 | tf_op jit(solution)/shard_map/ppermute | solution.py:954
  524.7 42.8 %collective-permute-start.21 = (bf16[24,256,256]{2,1,0:T(8,128)(2,1)}, bf16[24,256,256]{2,1,0:T(8,128)(2,1)}, u32[]{:S(2)}, u32[]{:S(2)}) collective-permute-start(bf16[24,256,256]{2,1,0:T(8,128)(2,1)} %get-tuple-element.153), channel_id=1, source_target_pairs={{0,4},{4,0},{8,12},{12,8},{16,20},{20,16},{24,28},{28,24},{1,5},{5... | collective-permute-start | bytes 9437192 | tf_op jit(solution)/shard_map/ppermute | solution.py:954
  529.9 78.1 %collective-permute-start.11 = (bf16[512,2048]{1,0:T(8,128)(2,1)}, bf16[512,2048]{1,0:T(8,128)(2,1)}, u32[]{:S(2)}, u32[]{:S(2)}) collective-permute-start(bf16[512,2048]{1,0:T(8,128)(2,1)} %add_convert_fusion.1.refs_17_), channel_id=1, source_target_pairs={{0,1},{1,2},{2,3},{3,0},{4,5},{5,6},{6,7},{7,4},{8,9},{9,10},{10,1... | collective-permute-start | bytes 6291464 | tf_op jit(solution)/shard_map/ppermute | solution.py:949
  535.9 36.1 %collective-permute-start.22 = (bf16[6,256,256]{2,1,0:T(8,128)(2,1)}, bf16[6,256,256]{2,1,0:T(8,128)(2,1)S(1)}, u32[]{:S(2)}, u32[]{:S(2)}) collective-permute-start(bf16[6,256,256]{2,1,0:T(8,128)(2,1)} %get-tuple-element.143.refs_17_), channel_id=1, source_target_pairs={{0,24},{4,28},{8,16},{12,20},{16,8},{20,12},{24,0},{28,4},{1,25},{... | collective-permute-start | bytes 2359304 | tf_op jit(solution)/shard_map/ppermute | solution.py:954
  566.0 47.5 %collective-permute-start.26 = (bf16[6,256,256]{2,1,0:T(8,128)(2,1)}, bf16[6,256,256]{2,1,0:T(8,128)(2,1)}, u32[]{:S(2)}, u32[]{:S(2)}) collective-permute-start(bf16[6,256,256]{2,1,0:T(8,128)(2,1)} %get-tuple-element.163), channel_id=1, source_target_pairs={{0,8},{4,12},{8,0},{12,4},{16,24},{20,28},{24,16},{28,20},{1,9},{5... | collective-permute-start | bytes 2359304 | tf_op jit(solution)/shard_map/ppermute | solution.py:954
  566.4 47.8 %collective-permute-start.27 = (bf16[6,256,256]{2,1,0:T(8,128)(2,1)}, bf16[6,256,256]{2,1,0:T(8,128)(2,1)}, u32[]{:S(2)}, u32[]{:S(2)}) collective-permute-start(bf16[6,256,256]{2,1,0:T(8,128)(2,1)} %get-tuple-element.165), channel_id=1, source_target_pairs={{0,16},{4,20},{8,24},{12,28},{16,0},{20,4},{24,8},{28,12},{1,17},{... | collective-permute-start | bytes 2359304 | tf_op jit(solution)/shard_map/ppermute | solution.py:954
  573.0 71.8 %collective-permute-start.23 = (bf16[6,256,256]{2,1,0:T(8,128)(2,1)}, bf16[6,256,256]{2,1,0:T(8,128)(2,1)S(1)}, u32[]{:S(2)}, u32[]{:S(2)}) collective-permute-start(bf16[6,256,256]{2,1,0:T(8,128)(2,1)} %get-tuple-element.156), channel_id=1, source_target_pairs={{0,8},{4,12},{8,0},{12,4},{16,24},{20,28},{24,16},{28,20},{1,9},{5... | collective-permute-start | bytes 2359304 | tf_op jit(solution)/shard_map/ppermute | solution.py:954
  574.1 70.7 %collective-permute-start.24 = (bf16[6,256,256]{2,1,0:T(8,128)(2,1)}, bf16[6,256,256]{2,1,0:T(8,128)(2,1)}, u32[]{:S(2)}, u32[]{:S(2)}) collective-permute-start(bf16[6,256,256]{2,1,0:T(8,128)(2,1)} %get-tuple-element.158), channel_id=1, source_target_pairs={{0,16},{4,20},{8,24},{12,28},{16,0},{20,4},{24,8},{28,12},{1,17},{... | collective-permute-start | bytes 2359304 | tf_op jit(solution)/shard_map/ppermute | solution.py:954
  575.6 67.1 %reduce-scatter.8.cloned.1.call-start = ((), (), s32[]{:S(2)}) async-start(), calls=%async_computation.6 | async-start | bytes 40960 | tf_op jit(solution)/shard_map/reduce_scatter | solution.py:1135
  607.9 36.8 %collective-permute-start.25 = (bf16[6,256,256]{2,1,0:T(8,128)(2,1)}, bf16[6,256,256]{2,1,0:T(8,128)(2,1)}, u32[]{:S(2)}, u32[]{:S(2)}) collective-permute-start(bf16[6,256,256]{2,1,0:T(8,128)(2,1)} %get-tuple-element.160.refs_17_), channel_id=1, source_target_pairs={{0,24},{4,28},{8,16},{12,20},{16,8},{20,12},{24,0},{28,4},{1,25},{... | collective-permute-start | bytes 2359304 | tf_op jit(solution)/shard_map/ppermute | solution.py:954
  613.5 59.9 %collective-permute-start.20 = (bf16[512,2048]{1,0:T(8,128)(2,1)S(1)}, bf16[512,2048]{1,0:T(8,128)(2,1)}, u32[]{:S(2)}, u32[]{:S(2)}) collective-permute-start(bf16[512,2048]{1,0:T(8,128)(2,1)S(1)} %add_convert_fusion.refs_18_), channel_id=1, source_target_pairs={{0,1},{1,2},{2,3},{3,0},{4,5},{5,6},{6,7},{7,4},{8,9},{9,10},{10,1... | collective-permute-start | bytes 6291464 | tf_op jit(solution)/shard_map/ppermute | solution.py:949
  (24 other events, 443.6 us)
Sparse Core Ops, SparseCore 0:
  14.1 128.2 all-gather.1
  323.5 144.7 reduce-scatter.3
  575.7 31.6 reduce-scatter.5
  613.6 18.9 reduce-scatter.7
